TPU v7x, 32 devices: a whole 2x2x4 slice. The times are simulated.
32 devices in a mesh: groups: 2 (over y), expert: 4 (over z), decode: 4 (over x, core), tensor: 1.
Axes of the slice: x: 2, y: 2, z: 4, core: 2. Of those that a mesh axis runs over, the one named last changes fastest.
Arguments:
- resid: bfloat16 [1024, 2560], P(('groups', 'expert')), parts along dimension 0, may hold values from -6 to 6
- moe_gain: float32 [2560], replicated, may hold values from 0.25 to 1.75
- attn_gain: float32 [2560], replicated, may hold values from 0.25 to 1.75
- gate_score: float32 [1024], P(('groups', 'expert')), parts along dimension 0, may hold values from 0.2 to 1
- expert_ids: int32 [1024, 1], P(('groups', 'expert')), parts along dimension 0, may hold values from 0 to 1
- w_gate: bfloat16 [4, 2560, 2048], P('expert', None, ('decode', 'tensor')), may hold values from -0.125 to 0.125
- w_up: bfloat16 [4, 2560, 2048], P('expert', None, ('decode', 'tensor')), may hold values from -0.125 to 0.125
- w_down: bfloat16 [4, 2048, 2560], P('expert', ('decode', 'tensor')), may hold values from -0.09375 to 0.09375
- shared_gate: bfloat16 [2560, 4096], P('expert', ('decode', 'tensor')), may hold values from -0.125 to 0.125
- shared_up: bfloat16 [2560, 4096], P('expert', ('decode', 'tensor')), may hold values from -0.125 to 0.125
- shared_down: bfloat16 [4096, 2560], P(('decode', 'tensor'), 'expert'), may hold values from -0.09375 to 0.09375
- w_kv: bfloat16 [2560, 2048], P('expert', ('decode', 'tensor')), may hold values from -0.125 to 0.125
- req_owner: int32 [8, 4], P(('groups', 'expert')), parts along dimension 0, may hold values from 0 to 3, each once within a row
- req_blocks: int32 [8, 4], P(('groups', 'expert')), parts along dimension 0, may hold values from 1 to 4, 8 in all within a row
Outputs:
- layer_out: bfloat16 [1024, 2560], P(('groups', 'expert'), ('decode', 'tensor')), parts along dimension 0
- kv_handed: bfloat16 [8, 4, 64, 4, 512], P(('groups', 'expert'), 'decode', None, None, 'tensor'), parts along dimension 0
There are 2 independent parts, one for each index of `groups`. A program takes and returns all parts, laid end to end along the dimension named above; an argument that names none is the same for every part. Nothing has to cross between parts.
Inputs may be any that keep to these rules, and one draw needn't show every extreme that they name: `req_owner`: each shard's requests go to distinct decode owners. `req_blocks`: the 4 requests of a shard hold 8 blocks together.
All inputs are finite; a program needn't handle non-finite values.
Results may differ from a plain program's by a relative error of at most 0.018.
Values may be sent and summed in bfloat16 or wider, within the bound.
No kernel may reach another device: no remote copies, remote signals or barrier semaphores. Data moves between devices by JAX's collectives and lax.ppermute only.
A program may use at most 64 MiB of HBM per device.

v0:
```python
import jax
import jax.numpy as jnp
from jax import lax
from jax.sharding import PartitionSpec as P

BLOCK = 16
QCAP = 4


def rms_scale(values, gain):
    return values * lax.rsqrt(jnp.mean(values * values, axis=-1, keepdims=True) + 1e-05) * gain


def unpermute(slot_values, row_index):
    padded = jnp.concatenate(
        [slot_values, jnp.zeros((1, slot_values.shape[1]), jnp.float32)], axis=0
    )
    return padded[row_index]


def on_device(
    resid,
    moe_gain,
    attn_gain,
    gate_score,
    expert_ids,
    w_gate,
    w_up,
    w_down,
    shared_gate,
    shared_up,
    shared_down,
    w_kv,
    req_owner,
    req_blocks,
):
    tok_rows, feature_width = resid.shape
    expert_count = lax.axis_size("expert")
    pair_count = expert_count // 2
    capacity = 2 * tok_rows // pair_count
    group_size = lax.axis_size(("decode", "tensor"))
    piece_width = feature_width // group_size
    feature_start = lax.axis_index(("decode", "tensor")) * piece_width
    moe_in = rms_scale(resid.astype(jnp.float32), moe_gain).astype(jnp.bfloat16)
    routes = expert_ids[:, 0]
    onehot = (routes[:, None] == jnp.arange(pair_count, dtype=jnp.int32)[None, :]).astype(jnp.int32)
    slots = jnp.sum((jnp.cumsum(onehot, axis=0) - 1) * onehot, axis=1)
    kept = slots < capacity
    position = routes * capacity + slots
    row_index = jnp.where(kept, position, pair_count * capacity)
    selector = (
        position[None, :] == jnp.arange(pair_count * capacity, dtype=jnp.int32)[:, None]
    ) & kept[None, :]
    select_bf = selector.astype(jnp.bfloat16)
    packed = jnp.dot(select_bf, moe_in, preferred_element_type=jnp.float32).astype(jnp.bfloat16)
    packed = packed.reshape(pair_count, capacity, feature_width)
    outgoing = jnp.repeat(packed, 2, axis=0)
    incoming = lax.all_to_all(outgoing, "expert", split_axis=0, concat_axis=0, tiled=True)
    flat_in = incoming.reshape(expert_count * capacity, feature_width)
    gate_val = jnp.dot(flat_in, w_gate[0], preferred_element_type=jnp.float32)
    up_val = jnp.dot(flat_in, w_up[0], preferred_element_type=jnp.float32)
    hidden = (jax.nn.silu(gate_val) * up_val).astype(jnp.bfloat16)
    partial_flat = jnp.dot(hidden, w_down[0], preferred_element_type=jnp.float32).astype(
        jnp.bfloat16
    )
    returned = lax.all_to_all(
        partial_flat.reshape(expert_count, capacity, feature_width),
        "expert",
        split_axis=0,
        concat_axis=0,
        tiled=True,
    )
    pair_sums = jnp.sum(
        returned.reshape(pair_count, 2, capacity, feature_width).astype(jnp.float32), axis=1
    )
    routed_full = (
        unpermute(pair_sums.reshape(pair_count * capacity, feature_width), row_index)
        * gate_score[:, None]
    )
    columns = moe_in
    shared_gate_val = jnp.dot(
        columns,
        lax.all_gather(shared_gate, "expert", axis=0, tiled=True),
        preferred_element_type=jnp.float32,
    )
    shared_up_val = jnp.dot(
        columns,
        lax.all_gather(shared_up, "expert", axis=0, tiled=True),
        preferred_element_type=jnp.float32,
    )
    shared_hidden = (jax.nn.silu(shared_gate_val) * shared_up_val).astype(jnp.bfloat16)
    shared_out = jnp.dot(
        shared_hidden,
        lax.all_gather(shared_down, "expert", axis=1, tiled=True),
        preferred_element_type=jnp.float32,
    )
    total_terms = routed_full + shared_out
    summed_share = lax.psum_scatter(
        total_terms.astype(jnp.bfloat16), ("decode", "tensor"), scatter_dimension=1, tiled=True
    ).astype(jnp.float32)
    resid_share = lax.dynamic_slice_in_dim(resid, feature_start, piece_width, 1)
    layer_out = (resid_share.astype(jnp.float32) + summed_share).astype(jnp.bfloat16)
    full_rows = lax.all_gather(layer_out, ("decode", "tensor"), axis=1, tiled=True)
    attn_in = rms_scale(full_rows.astype(jnp.float32), attn_gain).astype(jnp.bfloat16)
    kv_width = w_kv.shape[1]
    columns = attn_in
    key_value = jnp.dot(
        columns,
        lax.all_gather(w_kv, "expert", axis=0, tiled=True),
        preferred_element_type=jnp.float32,
    ).astype(jnp.bfloat16)
    owner_count = req_owner.shape[1]
    block_count = tok_rows // BLOCK
    owners = req_owner[0]
    counts = req_blocks[0]
    starts = jnp.cumsum(counts) - counts
    owner_index = jnp.arange(owner_count, dtype=jnp.int32)
    slot_index = jnp.arange(QCAP, dtype=jnp.int32)
    block_index = jnp.arange(block_count, dtype=jnp.int32)
    chosen = owners[:, None, None, None] == owner_index[None, :, None, None]
    chosen = chosen & (slot_index[None, None, :, None] < counts[:, None, None, None])
    chosen = chosen & (
        block_index[None, None, None, :]
        == starts[:, None, None, None] + slot_index[None, None, :, None]
    )
    choose = jnp.sum(chosen.astype(jnp.int32), axis=0).astype(jnp.bfloat16)
    kv_blocks = key_value.reshape(block_count, BLOCK, kv_width)
    sending = jnp.einsum(
        "oqb,bjw->qjow", choose, kv_blocks, preferred_element_type=jnp.float32
    ).astype(jnp.bfloat16)
    sending = sending.reshape(QCAP * BLOCK, owner_count, kv_width)
    received = lax.all_to_all(sending, "decode", split_axis=1, concat_axis=1, tiled=True)
    kv_handed = received.reshape(1, 1, QCAP * BLOCK, owner_count, kv_width)
    return (layer_out, kv_handed)


def solution(mesh):
    return jax.shard_map(
        on_device,
        mesh=mesh,
        in_specs=(
            P(("groups", "expert"), None),
            P(),
            P(),
            P(("groups", "expert")),
            P(("groups", "expert"), None),
            P("expert", None, ("decode", "tensor")),
            P("expert", None, ("decode", "tensor")),
            P("expert", ("decode", "tensor"), None),
            P("expert", ("decode", "tensor")),
            P("expert", ("decode", "tensor")),
            P(("decode", "tensor"), "expert"),
            P("expert", ("decode", "tensor")),
            P(("groups", "expert"), None),
            P(("groups", "expert"), None),
        ),
        out_specs=(
            P(("groups", "expert"), ("decode", "tensor")),
            P(("groups", "expert"), "decode", None, None, "tensor"),
        ),
        check_vma=False,
    )
```

profile of v0, /device:TPU:0, one launch (start us, length us, event | category | flops | bytes accessed | tf_op | source)
XLA Modules:
  0.0 506.8 jit_solution(15398212137151211010)
XLA Ops:
  7.3 0.7 all-gather.5.cloned.1.call-update
  8.0 0.7 all-gather.7.cloned.1.call-update
  9.2 0.2 fusion.9
  9.4 0.6 convolution_convert_fusion.1
  10.0 1.7 broadcast_in_dim.6
  11.7 6.3 %all-to-all-start = ((bf16[4,128,2560]{2,1,0:T(8,128)(2,1)}), bf16[4,128,2560]{2,1,0:T(8,128)(2,1)}, u32[]{:S(2)}, u32[]{:S(2)}) async-start(bf16[4,128,2560]{2,1,0:T(8,128)(2,1)} %bitcast.58), calls=%async_computation | async-start | bytes 5242880 | tf_op jit(solution)/shard_map/all_to_all | solution.py:58
  18.0 0.7 all-gather.9.cloned.1.call-update
  18.7 125.5 %all-to-all-done = bf16[4,128,2560]{2,1,0:T(8,128)(2,1)} async-done(((bf16[4,128,2560]{2,1,0:T(8,128)(2,1)}), bf16[4,128,2560]{2,1,0:T(8,128)(2,1)}, u32[]{:S(2)}, u32[]{:S(2)}) %all-to-all-start) | async-done | bytes 2621472 | tf_op jit(solution)/shard_map/all_to_all | solution.py:58
  144.2 5.1 fusion.4
  149.3 7.2 %convolution_convert_fusion = bf16[512,2560]{1,0:T(8,128)(2,1)} fusion(bf16[1,512,2560]{2,1,0:T(8,128)(2,1)S(1)} %copy-done, bf16[512,2560]{1,0:T(8,128)(2,1)} %bitcast.3, bf16[1,2560,512]{2,1,0:T(8,128)(2,1)} %param.20, f32[512,512]{1,0:T(8,128)} %fusion.4), kind=kOutput, calls=%fused_computation.2 | convolution fusion | flops 2687238144 | bytes 11534336 | tf_op jit(solution)/shard_map/dot_general | solution.py:63
  156.5 4.6 all-to-all-start.1
  161.2 118.5 %all-to-all-done.1 = bf16[4,128,2560]{2,1,0:T(8,128)(2,1)} async-done(((bf16[4,128,2560]{2,1,0:T(8,128)(2,1)}), bf16[4,128,2560]{2,1,0:T(8,128)(2,1)}, u32[]{:S(2)}, u32[]{:S(2)}) %all-to-all-start.1) | async-done | bytes 2621472 | tf_op jit(solution)/shard_map/all_to_all | solution.py:66
  279.6 2.5 convert_reduce_fusion
  282.2 1.8 concatenate.3
  283.9 4.4 gather_fusion
  288.3 4.2 fusion.45
  292.5 10.1 %all-gather.7.cloned.1.call-done = bf16[2560,1024]{1,0:T(8,128)(2,1)} async-done(((bf16[640,1024]{1,0:T(8,128)(2,1)}), bf16[2560,1024]{1,0:T(8,128)(2,1)}) %all-gather.7.cloned.1.call-update) | async-done | bytes 5242896 | tf_op jit(solution)/shard_map/all_gather | solution.py:88
  302.6 98.9 %all-gather.9.cloned.1.call-done = bf16[1024,2560]{1,0:T(8,128)(2,1)} async-done(((bf16[1024,640]{1,0:T(8,128)(2,1)}), bf16[1024,2560]{1,0:T(8,128)(2,1)}) %all-gather.9.cloned.1.call-update) | async-done | bytes 5242896 | tf_op jit(solution)/shard_map/all_gather | solution.py:94
  401.5 7.1 %fusion = bf16[128,2560]{1,0:T(8,128)(2,1)} fusion(bf16[1024,2560]{1,0:T(8,128)(2,1)} %all-gather.9.cloned.1.call-done, f32[128,2560]{1,0:T(8,128)} %gather_fusion, f32[128]{0:T(128)S(1)} %copy-done.8, bf16[2560,1024]{1,0:T(8,128)(2,1)} %all-gather.7.cloned.1.call-done, f32[128,1024]{1,0:T(8,128)} %fusion.45, bf16[128,2560]{1,0:T(8,128)(2,1)S(1)} %copy-done.1, ...), kind=kOutput, calls=%fused_computation.5 | convolution fusion | flops 1345257472 | bytes 13642752 | tf_op jit(solution)/shard_map/dot_general | solution.py:92
  408.5 2.2 copy.29
  410.8 0.5 all-gather.11.cloned.1.call-update
  411.4 0.2 reduce-window.8
  412.0 19.8 %reduce-scatter.4.cloned.1.call-done = bf16[640,128]{1,0:T(8,128)(2,1)} async-done(((bf16[2560,128]{1,0:T(8,128)(2,1)}), bf16[640,128]{1,0:T(8,128)(2,1)}) %reduce-scatter.4.cloned.1.call-update) | async-done | bytes 163856
  431.7 1.1 copy.30
  432.9 0.7 copy-done.2
  433.5 7.5 %all_gather.18 = bf16[128,2560]{1,0:T(8,128)(2,1)S(1)} all-gather(bf16[128,640]{1,0:T(8,128)(2,1)S(1)} %add_convert_fusion), channel_id=1, replica_groups=mesh['groups'=2,'expert'=4,'decode'=4,'tensor'=1] {'decode','tensor'}, dimensions={1}, use_global_device_ids=true | all-gather | bytes 819200 | tf_op jit(solution)/shard_map/all_gather | solution.py:103
  441.0 0.2 fusion.12
  441.3 46.8 %all-gather.11.cloned.1.call-done = bf16[2560,512]{1,0:T(8,128)(2,1)} async-done(((bf16[640,512]{1,0:T(8,128)(2,1)}), bf16[2560,512]{1,0:T(8,128)(2,1)}) %all-gather.11.cloned.1.call-update) | async-done | bytes 2621456 | tf_op jit(solution)/shard_map/all_gather | solution.py:109
  488.0 2.3 convolution_convert_fusion.3
  490.3 0.3 fusion.19
  490.8 8.6 %all_to_all.15 = bf16[64,4,512]{2,0,1:T(8,128)(2,1)S(1)} all-to-all(bf16[64,4,512]{2,0,1:T(8,128)(2,1)S(1)} %bitcast.63), channel_id=1, replica_groups=mesh['groups'=2,'expert'=4,'decode'=4,'tensor'=1] {'decode'}, dimensions={1} | all-to-all | bytes 524288 | tf_op jit(solution)/shard_map/all_to_all | solution.py:132
  499.4 0.9 copy.25
  (41 shorter events, 1.3 us)
Async XLA Ops:
  7.2 142.2 %copy-start = (bf16[1,512,2560]{2,1,0:T(8,128)(2,1)S(1)}, bf16[1,512,2560]{2,1,0:T(8,128)(2,1)}, u32[]{:S(2)}) copy-start(bf16[1,512,2560]{2,1,0:T(8,128)(2,1)} %param.21) | copy-start | bytes 7864324
  7.2 1.5 copy-start.4
  7.2 2.0 copy-start.1
  7.2 2.2 copy-start.3
  7.2 281.1 %all-gather.5.cloned.1.call-start = ((), (), s32[]{:S(2)}) async-start(), calls=%async_computation.4 | async-start | bytes 6553600 | tf_op jit(solution)/shard_map/all_gather | solution.py:83
  7.9 294.7 %all-gather.7.cloned.1.call-start = ((), (), s32[]{:S(2)}) async-start(), calls=%async_computation.5 | async-start | bytes 6553600 | tf_op jit(solution)/shard_map/all_gather | solution.py:88
  11.7 132.6 %all-to-all-start = ((bf16[4,128,2560]{2,1,0:T(8,128)(2,1)}), bf16[4,128,2560]{2,1,0:T(8,128)(2,1)}, u32[]{:S(2)}, u32[]{:S(2)}) async-start(bf16[4,128,2560]{2,1,0:T(8,128)(2,1)} %bitcast.58), calls=%async_computation | async-start | bytes 5242880 | tf_op jit(solution)/shard_map/all_to_all | solution.py:58
  18.0 383.5 %all-gather.9.cloned.1.call-start = ((), (), s32[]{:S(2)}) async-start(), calls=%async_computation.6 | async-start | bytes 6553600 | tf_op jit(solution)/shard_map/all_gather | solution.py:94
  156.5 123.1 %all-to-all-start.1 = ((bf16[4,128,2560]{2,1,0:T(8,128)(2,1)}), bf16[4,128,2560]{2,1,0:T(8,128)(2,1)}, u32[]{:S(2)}, u32[]{:S(2)}) async-start(bf16[4,128,2560]{2,1,0:T(8,128)(2,1)} %bitcast.61), calls=%async_computation.1 | async-start | bytes 5242880 | tf_op jit(solution)/shard_map/all_to_all | solution.py:66
  161.1 270.6 %reduce-scatter.4.cloned.1.call-start = ((), (), s32[]{:S(2)}) async-start(), calls=%async_computation.8 | async-start | bytes 819200
  288.3 113.2 %copy-start.8 = (f32[128]{0:T(128)S(1)}, f32[128]{0:T(128)}, u32[]{:S(2)}) copy-start(f32[128]{0:T(128)} %param.17) | copy-start | bytes 1540
  408.5 2.8 copy-start.5
  408.5 3.0 copy-start.6
  408.5 79.5 %copy-start.7 = (f32[2560]{0:T(1024)S(1)}, f32[2560]{0:T(1024)}, u32[]{:S(2)}) copy-start(f32[2560]{0:T(1024)} %param.16) | copy-start | bytes 30724
  410.8 77.2 %all-gather.11.cloned.1.call-start = ((), (), s32[]{:S(2)}) async-start(), calls=%async_computation.7 | async-start | bytes 3276800 | tf_op jit(solution)/shard_map/all_gather | solution.py:109
  432.9 0.7 copy-start.2
Sparse Core Ops, SparseCore 0:
  9.6 152.4 all-gather.4
  163.7 138.8 all-gather.6
  304.2 97.2 all-gather.8
  410.9 20.8 reduce-scatter.3
  433.2 54.8 all-gather.10
where the time goes:
time: 507 us
  waiting for transfers between devices  422 us (83%)
  matrix products  26.7 us (5%)
  blocking collectives  16.1 us (3%)
  between operations  14 us (3%)
  local copies, waits for them, and re-layouts  12.8 us (3%)
  starting transfers between devices  11.1 us (2%)
    all_to_all x1, waiting for transfers between devices, on_device(): lax.all_to_all(outgoing, 'expert', split_axis=0, concat_axis=0, tiled=True)  126 us
    all_to_all x1, waiting for transfers between devices, on_device(): lax.all_to_all(partial_flat.reshape(expert_count, capacity, feature_width...  118 us
    all_gather x1, waiting for transfers between devices, on_device(): lax.all_gather(shared_down, 'expert', axis=1, tiled=True)  98.9 us
    all_gather x1, waiting for transfers between devices, on_device(): lax.all_gather(w_kv, 'expert', axis=0, tiled=True)  46.8 us
    unnamed x6, waiting for transfers between devices  22.4 us
  transfers between devices with their start and end apart: 7, of which 6 were waited for; matrix products, arithmetic and copies ran while one was open for 6% of the time, Pallas kernels for 0%

commit v1 on v0

--- a/solution.py
+++ b/solution.py
@@ -18,7 +18,34 @@
     return padded[row_index]
 
 
-def on_device(
+def hand_over(key_value, req_owner, req_blocks):
+    tok_rows, kv_width = key_value.shape
+    owner_count = req_owner.shape[1]
+    block_count = tok_rows // BLOCK
+    owners = req_owner[0]
+    counts = req_blocks[0]
+    starts = jnp.cumsum(counts) - counts
+    owner_index = jnp.arange(owner_count, dtype=jnp.int32)
+    slot_index = jnp.arange(QCAP, dtype=jnp.int32)
+    block_index = jnp.arange(block_count, dtype=jnp.int32)
+    chosen = owners[:, None, None, None] == owner_index[None, :, None, None]
+    chosen = chosen & (slot_index[None, None, :, None] < counts[:, None, None, None])
+    chosen = chosen & (
+        block_index[None, None, None, :]
+        == starts[:, None, None, None] + slot_index[None, None, :, None]
+    )
+    choose = jnp.sum(chosen.astype(jnp.int32), axis=0).astype(jnp.bfloat16)
+    kv_blocks = key_value.reshape(block_count, BLOCK, kv_width)
+    sending = jnp.einsum(
+        "oqb,bjw->qjow", choose, kv_blocks, preferred_element_type=jnp.float32
+    ).astype(jnp.bfloat16)
+    sending = sending.reshape(QCAP * BLOCK, owner_count, kv_width)
+    received = lax.all_to_all(sending, "decode", split_axis=1, concat_axis=1, tiled=True)
+    kv_handed = received.reshape(1, 1, QCAP * BLOCK, owner_count, kv_width)
+    return kv_handed
+
+
+def wide_plan(
     resid,
     moe_gain,
     attn_gain,
@@ -109,29 +136,178 @@
         lax.all_gather(w_kv, "expert", axis=0, tiled=True),
         preferred_element_type=jnp.float32,
     ).astype(jnp.bfloat16)
-    owner_count = req_owner.shape[1]
-    block_count = tok_rows // BLOCK
-    owners = req_owner[0]
-    counts = req_blocks[0]
-    starts = jnp.cumsum(counts) - counts
-    owner_index = jnp.arange(owner_count, dtype=jnp.int32)
-    slot_index = jnp.arange(QCAP, dtype=jnp.int32)
-    block_index = jnp.arange(block_count, dtype=jnp.int32)
-    chosen = owners[:, None, None, None] == owner_index[None, :, None, None]
-    chosen = chosen & (slot_index[None, None, :, None] < counts[:, None, None, None])
-    chosen = chosen & (
-        block_index[None, None, None, :]
-        == starts[:, None, None, None] + slot_index[None, None, :, None]
-    )
-    choose = jnp.sum(chosen.astype(jnp.int32), axis=0).astype(jnp.bfloat16)
-    kv_blocks = key_value.reshape(block_count, BLOCK, kv_width)
-    sending = jnp.einsum(
-        "oqb,bjw->qjow", choose, kv_blocks, preferred_element_type=jnp.float32
-    ).astype(jnp.bfloat16)
-    sending = sending.reshape(QCAP * BLOCK, owner_count, kv_width)
-    received = lax.all_to_all(sending, "decode", split_axis=1, concat_axis=1, tiled=True)
-    kv_handed = received.reshape(1, 1, QCAP * BLOCK, owner_count, kv_width)
-    return (layer_out, kv_handed)
+    return layer_out, hand_over(key_value, req_owner, req_blocks)
+
+
+SWAP_CORE = [(0, 1), (1, 0), (2, 3), (3, 2)]
+SWAP_CHIP = [(0, 2), (2, 0), (1, 3), (3, 1)]
+SWAP_GROUP = [(0, 1), (1, 0)]
+
+
+def to_shift(values, shift):
+    count = lax.axis_size("expert")
+    return lax.ppermute(values, "expert", [(i, (i + shift) % count) for i in range(count)])
+
+
+def place(target, values, row, column):
+    return lax.dynamic_update_slice(target, values, (row, column))
+
+
+def near_plan(
+    resid,
+    moe_gain,
+    attn_gain,
+    gate_score,
+    expert_ids,
+    w_gate,
+    w_up,
+    w_down,
+    shared_gate,
+    shared_up,
+    shared_down,
+    w_kv,
+    req_owner,
+    req_blocks,
+):
+    bf16, f32 = jnp.bfloat16, jnp.float32
+    rows, width = resid.shape
+    expert_count = lax.axis_size("expert")
+    pair_count = expert_count // 2
+    capacity = 2 * rows // pair_count
+    group_size = lax.axis_size("decode")
+    piece = width // group_size
+    zone = lax.axis_index("expert")
+    slot = lax.axis_index("decode")
+    group = lax.axis_index("groups")
+    near_rows = shared_gate.shape[0]
+    half_rows = near_rows // 2
+    hidden_piece = shared_gate.shape[1] // expert_count
+    half_hidden = hidden_piece // 2
+    shifts = (2, 1, 3)
+
+    moe_in = rms_scale(resid.astype(f32), moe_gain).astype(bf16)
+    mine = lax.dynamic_slice_in_dim(moe_in, slot * piece, piece, 1)
+
+    routes = expert_ids[:, 0]
+    onehot = (routes[:, None] == jnp.arange(pair_count, dtype=jnp.int32)[None, :]).astype(jnp.int32)
+    slots = jnp.sum((jnp.cumsum(onehot, axis=0) - 1) * onehot, axis=1)
+    kept = slots < capacity
+    scale = jnp.where(kept, gate_score, 0.0)
+    picks = jnp.where(
+        routes[None, :] == jnp.arange(pair_count, dtype=jnp.int32)[:, None], scale[None, :], 0.0
+    )
+    all_picks = lax.all_gather(picks, "expert", axis=0)
+    my_picks = lax.dynamic_index_in_dim(all_picks, zone // 2, 1, keepdims=False)
+
+    arrived = {s: to_shift(mine, s) for s in shifts}
+    blocks = {0: moe_in}
+    for s in shifts:
+        own = arrived[s]
+        across = lax.ppermute(own, "decode", SWAP_CHIP)
+        beside = lax.ppermute(own, "decode", SWAP_CORE)
+        far = lax.ppermute(across, "decode", SWAP_CORE)
+        block = jnp.zeros((rows, width), bf16)
+        for j, part in ((0, own), (2, across), (1, beside), (3, far)):
+            block = place(block, part, 0, (slot ^ j) * piece)
+        blocks[s] = block
+    tokens = jnp.concatenate([blocks[s] for s in range(expert_count)], axis=0)
+
+    def gate_up(row, count, owner):
+        return jnp.concatenate(
+            [
+                lax.dynamic_slice(w, (row, owner * hidden_piece), (count, hidden_piece))
+                for w in (shared_gate, shared_up)
+            ],
+            axis=1,
+        )
+
+    near_weights = jnp.zeros((width, 2 * hidden_piece), bf16)
+    near_weights = place(near_weights, gate_up(0, near_rows, zone), zone * near_rows, 0)
+    for s in shifts:
+        sent = gate_up(group * half_rows, half_rows, (zone + s) % expert_count)
+        got = to_shift(sent, s)
+        other = lax.ppermute(got, "groups", SWAP_GROUP)
+        base = ((zone - s) % expert_count) * near_rows
+        near_weights = place(near_weights, got, base + group * half_rows, 0)
+        near_weights = place(near_weights, other, base + (1 - group) * half_rows, 0)
+
+    down = jnp.zeros((group_size * hidden_piece, piece), bf16)
+    for k in range(group_size):
+        target = slot ^ k
+        sent = lax.dynamic_slice(
+            shared_down, (target * hidden_piece + group * half_hidden, 0), (half_hidden, piece)
+        )
+        pairs = [
+            (z * group_size + d, (d ^ k) * group_size + z)
+            for z in range(expert_count)
+            for d in range(group_size)
+        ]
+        got = lax.ppermute(sent, ("expert", "decode"), pairs)
+        other = lax.ppermute(got, "groups", SWAP_GROUP)
+        base = (zone ^ k) * hidden_piece
+        down = place(down, got, base + group * half_hidden, 0)
+        down = place(down, other, base + (1 - group) * half_hidden, 0)
+
+    kv_weights = lax.all_gather(w_kv, "expert", axis=0, tiled=True)
+
+    gate_val = jnp.dot(tokens, w_gate[0], preferred_element_type=f32)
+    up_val = jnp.dot(tokens, w_up[0], preferred_element_type=f32)
+    hidden = (jax.nn.silu(gate_val) * up_val).astype(bf16)
+    row_scale = jnp.concatenate(
+        [
+            lax.dynamic_index_in_dim(my_picks, (zone - s) % expert_count, 0, keepdims=False)
+            for s in range(expert_count)
+        ]
+    )
+    partial = (
+        jnp.dot(hidden, w_down[0], preferred_element_type=f32) * row_scale[:, None]
+    ).astype(bf16)
+
+    def part_of(j):
+        return lax.dynamic_slice_in_dim(partial, (slot ^ j) * piece, piece, 1)
+
+    beside = lax.ppermute(jnp.concatenate([part_of(1), part_of(3)], axis=1), "decode", SWAP_CORE)
+    keep = part_of(0).astype(f32) + beside[:, :piece].astype(f32)
+    pass_on = (part_of(2).astype(f32) + beside[:, piece:].astype(f32)).astype(bf16)
+    routed = keep + lax.ppermute(pass_on, "decode", SWAP_CHIP).astype(f32)
+
+    both = jnp.dot(tokens, near_weights, preferred_element_type=f32)
+    own = (jax.nn.silu(both[:, :hidden_piece]) * both[:, hidden_piece:]).astype(bf16)
+    across = lax.ppermute(own, "decode", SWAP_CHIP)
+    beside = lax.ppermute(own, "decode", SWAP_CORE)
+    far = lax.ppermute(across, "decode", SWAP_CORE)
+    shared_hidden = jnp.zeros((expert_count * rows, group_size * hidden_piece), bf16)
+    for j, part in ((0, own), (2, across), (1, beside), (3, far)):
+        shared_hidden = place(shared_hidden, part, 0, (slot ^ j) * hidden_piece)
+    total = routed + jnp.dot(shared_hidden, down, preferred_element_type=f32)
+
+    summed = total[:rows]
+    sending = total.astype(bf16)
+    for s in shifts:
+        summed = summed + to_shift(sending[s * rows : (s + 1) * rows], -s).astype(f32)
+    resid_share = lax.dynamic_slice_in_dim(resid, slot * piece, piece, 1)
+    layer_out = (resid_share.astype(f32) + summed).astype(bf16)
+
+    across = lax.ppermute(layer_out, "decode", SWAP_CHIP)
+    beside = lax.ppermute(layer_out, "decode", SWAP_CORE)
+    far = lax.ppermute(across, "decode", SWAP_CORE)
+    full_rows = jnp.zeros((rows, width), bf16)
+    for j, part in ((0, layer_out), (2, across), (1, beside), (3, far)):
+        full_rows = place(full_rows, part, 0, (slot ^ j) * piece)
+    attn_in = rms_scale(full_rows.astype(f32), attn_gain).astype(bf16)
+    key_value = jnp.dot(attn_in, kv_weights, preferred_element_type=f32).astype(bf16)
+    return layer_out, hand_over(key_value, req_owner, req_blocks)
+
+
+def on_device(*operands):
+    resid = operands[0]
+    zones = lax.axis_size("expert")
+    holders = lax.axis_size("decode")
+    fits = 2 * resid.shape[0] // (zones // 2) >= resid.shape[0]
+    square = zones == holders == 4 and lax.axis_size("tensor") == 1
+    if fits and square and lax.axis_size("groups") == 2:
+        return near_plan(*operands)
+    return wide_plan(*operands)
 
 
 def solution(mesh):

time: 507 us -> 252 us (0.50)
  waiting for transfers between devices: 422 us -> 53.3 us
  starting transfers between devices: 11.1 us -> 80.9 us
  local copies, waits for them, and re-layouts: 12.8 us -> 35.4 us
  blocking collectives: 16.1 us -> 37.5 us
  matrix products: 26.7 us -> 17.9 us
  other arithmetic: 4.03 us -> 11 us
    all_to_all x2 -> x0, waiting for transfers between devices: 244 us -> none  [the longest x1 126 us: on_device(): lax.all_to_all(outgoing, 'expert', split_axis=0, concat_axis=0, tiled=True)]
    all_gather x4 -> x1, waiting for transfers between devices: 156 us -> 0.02 us  [near_plan(): kv_weights = lax.all_gather(w_kv, 'expert', axis=0, tiled=True)]
    ppermute x0 -> x37, starting transfers between devices: none -> 80.9 us  [the longest x9 49.8 us: to_shift(): lax.ppermute(values, 'expert', [(i, (i + shift) % count) for i in range(c...]
    ppermute x0 -> x37, waiting for transfers between devices: none -> 53.2 us  [the longest x9 13.2 us: to_shift(): lax.ppermute(values, 'expert', [(i, (i + shift) % count) for i in range(c...]
    unnamed x6 -> x1, waiting for transfers between devices: 22.4 us -> 0.02 us
    dynamic_update_slice x0 -> x32, local copies, waits for them, and re-layouts: none -> 21.9 us  [place(): return lax.dynamic_update_slice(target, values, (row, column))]
    all_gather x1, blocking collectives: 7.49 us -> 29.1 us  [near_plan(): all_picks = lax.all_gather(picks, 'expert', axis=0)]
    all_to_all x2 -> x0, starting transfers between devices: 10.9 us -> none  [the longest x1 6.32 us: on_device(): lax.all_to_all(outgoing, 'expert', split_axis=0, concat_axis=0, tiled=True)]
  transfers between devices with their start and end apart: 7 -> 38, of which waited for: 6 -> 14; matrix products, arithmetic and copies ran while one was open for 6% -> 22% of each run, Pallas kernels for 0% -> 0%
where the time goes in v1:
time: 252 us; the launch traced here: 251 us
  starting transfers between devices  80.9 us (32%)
  waiting for transfers between devices  53.3 us (21%)
  blocking collectives  37.5 us (15%)
  local copies, waits for them, and re-layouts  35.4 us (14%)
  matrix products  17.9 us (7%)
  between operations  14.8 us (6%)
  other arithmetic  11 us (4%)
    ppermute x9, starting transfers between devices, to_shift(): lax.ppermute(values, 'expert', [(i, (i + shift) % count) for i in range(c...  49.8 us
    all_gather x1, blocking collectives, near_plan(): all_picks = lax.all_gather(picks, 'expert', axis=0)  29.1 us
    dynamic_update_slice x32, local copies, waits for them, and re-layouts, place(): return lax.dynamic_update_slice(target, values, (row, column))  21.9 us
    ppermute x9, waiting for transfers between devices, to_shift(): lax.ppermute(values, 'expert', [(i, (i + shift) % count) for i in range(c...  13.2 us
    ppermute x7, waiting for transfers between devices, near_plan(): other = lax.ppermute(got, 'groups', SWAP_GROUP)  11.8 us
    ppermute x4, starting transfers between devices, near_plan(): across = lax.ppermute(own, 'decode', SWAP_CHIP)  11.4 us
    ppermute x1, waiting for transfers between devices, near_plan(): routed = keep + lax.ppermute(pass_on, 'decode', SWAP_CHIP).astype(f32)  11.2 us
    ppermute x4, starting transfers between devices, near_plan(): got = lax.ppermute(sent, ('expert', 'decode'), pairs)  11 us
  transfers between devices with their start and end apart: 38, of which 14 were waited for; matrix products, arithmetic and copies ran while one was open for 22% of the time, Pallas kernels for 0%

profile of v1, /device:TPU:0, one launch (start us, length us, event | category | flops | bytes accessed | tf_op | source)
XLA Modules:
  0.0 250.8 jit_solution(12144221785655313877)
XLA Ops:
  11.5 5.0 %collective-permute-start.8 = (bf16[128,640]{1,0:T(8,128)(2,1)}, bf16[128,640]{1,0:T(8,128)(2,1)}, u32[]{:S(2)}, u32[]{:S(2)}) collective-permute-start(bf16[128,640]{1,0:T(8,128)(2,1)} %constant_dynamic-slice_fusion.12), channel_id=1, source_target_pairs={{0,12},{4,0},{8,4},{12,8},{1,13},{5,1},{9,5},{13,9},{2,14},{6,2},{... | collective-permute-start | bytes 491528 | tf_op jit(solution)/shard_map/ppermute | solution.py:149
  17.6 2.1 fusion.37
  20.4 1.9 collective-permute-start.14
  27.8 29.1 %all_gather.7 = f32[4,2,128]{2,1,0:T(2,128)S(1)} all-gather(f32[1,2,128]{2,1,0:T(2,128)S(1)} %compare_select_fusion.1), channel_id=1, replica_groups=mesh['groups'=2,'expert'=4,'decode'=4,'tensor'=1] {'expert'}, dimensions={0}, use_global_device_ids=true | all-gather | bytes 5120 | tf_op jit(solution)/shard_map/all_gather | solution.py:199
  62.4 36.5 %collective-permute-start.18 = (bf16[320,512]{1,0:T(8,128)(2,1)}, bf16[320,512]{1,0:T(8,128)(2,1)}, u32[]{:S(2)}, u32[]{:S(2)}) collective-permute-start(bf16[320,512]{1,0:T(8,128)(2,1)} %pad_maximum_fusion.4), channel_id=1, source_target_pairs={{0,12},{4,0},{8,4},{12,8},{1,13},{5,1},{9,5},{13,9},{2,14},{6,2},{... | collective-permute-start | bytes 983048 | tf_op jit(solution)/shard_map/ppermute | solution.py:149
  101.7 4.1 %collective-permute-start.9 = (bf16[128,640]{1,0:T(8,128)(2,1)}, bf16[128,640]{1,0:T(8,128)(2,1)S(1)}, u32[]{:S(2)}, u32[]{:S(2)}) collective-permute-start(bf16[128,640]{1,0:T(8,128)(2,1)} %collective-permute-done.8), channel_id=1, source_target_pairs={{0,2},{2,0},{1,3},{3,1},{4,6},{6,4},{5,7},{7,5},{8,10},{10,8},{9,1... | collective-permute-start | bytes 491528 | tf_op jit(solution)/shard_map/ppermute | solution.py:206
  106.8 5.1 %collective-permute-start.5 = (bf16[128,640]{1,0:T(8,128)(2,1)}, bf16[128,640]{1,0:T(8,128)(2,1)S(1)}, u32[]{:S(2)}, u32[]{:S(2)}) collective-permute-start(bf16[128,640]{1,0:T(8,128)(2,1)} %collective-permute-done.4), channel_id=1, source_target_pairs={{0,2},{2,0},{1,3},{3,1},{4,6},{6,4},{5,7},{7,5},{8,10},{10,8},{9,1... | collective-permute-start | bytes 491528 | tf_op jit(solution)/shard_map/ppermute | solution.py:206
  115.4 2.1 collective-permute-start.1
  117.9 4.7 %collective-permute-done.1 = bf16[128,640]{1,0:T(8,128)(2,1)S(1)} collective-permute-done((bf16[128,640]{1,0:T(8,128)(2,1)}, bf16[128,640]{1,0:T(8,128)(2,1)S(1)}, u32[]{:S(2)}, u32[]{:S(2)}) %collective-permute-start.1) | collective-permute-done | bytes 163872 | tf_op jit(solution)/shard_map/ppermute | solution.py:206
  122.6 1.7 collective-permute-start.25
  126.2 2.7 %collective-permute-start.27 = (bf16[128,640]{1,0:T(8,128)(2,1)S(1)}, bf16[128,640]{1,0:T(8,128)(2,1)}, u32[]{:S(2)}, u32[]{:S(2)}) collective-permute-start(bf16[128,640]{1,0:T(8,128)(2,1)S(1)} %copy-done.11), channel_id=1, source_target_pairs={{0,8},{1,12},{2,0},{3,4},{4,9},{5,13},{6,1},{7,5},{8,10},{9,14},{1... | collective-permute-start | bytes 491528 | tf_op jit(solution)/shard_map/ppermute | solution.py:245
  130.6 5.9 %collective-permute-start.29 = (bf16[128,640]{1,0:T(8,128)(2,1)S(1)}, bf16[128,640]{1,0:T(8,128)(2,1)}, u32[]{:S(2)}, u32[]{:S(2)}) collective-permute-start(bf16[128,640]{1,0:T(8,128)(2,1)S(1)} %get-tuple-element.14), channel_id=1, source_target_pairs={{0,12},{1,8},{2,4},{3,0},{4,13},{5,9},{6,5},{7,1},{8,14},{9,10},{1... | collective-permute-start | bytes 491528 | tf_op jit(solution)/shard_map/ppermute | solution.py:245
  137.8 3.9 %collective-permute-done.26 = bf16[128,640]{1,0:T(8,128)(2,1)S(1)} collective-permute-done((bf16[128,640]{1,0:T(8,128)(2,1)S(1)}, bf16[128,640]{1,0:T(8,128)(2,1)S(1)}, u32[]{:S(2)}, u32[]{:S(2)}) %collective-permute-start.26) | collective-permute-done | bytes 163872 | tf_op jit(solution)/shard_map/ppermute | solution.py:246
  150.2 2.5 %fusion.1 = f32[512,512]{1,0:T(8,128)} fusion(bf16[1,2560,512]{2,1,0:T(8,128)(2,1)S(1)} %copy-done.17, bf16[128,2560]{1,0:T(8,128)(2,1)S(1)} %constant_dynamic-update-slice_fusion.22, bf16[128,2560]{1,0:T(8,128)(2,1)S(1)} %constant_dynamic-update-slice_fusion.26, bf16[128,2560]{1,0:T(8,128)(2,1)S(1)} %constant_dynamic-update-slice_fusion.30, ...), kind=kOutput, calls=%fused_computation.3 | convolution fusion | flops 1352663040 | bytes 6291456 | tf_op jit(solution)/shard_map/dot_general | solution.py:254
  152.7 7.2 %multiply_convert_fusion = bf16[512,2560]{1,0:T(8,128)(2,1)} fusion(bf16[1,512,2560]{2,1,0:T(8,128)(2,1)S(1)} %copy-done, f32[512]{0:T(512)S(1)} %pad_maximum_fusion.5, f32[512,512]{1,0:T(8,128)} %fusion.1, bf16[1,2560,512]{2,1,0:T(8,128)(2,1)} %param.19, bf16[128,2560]{1,0:T(8,128)(2,1)} %copy-done.4, bf16[128,2560]{1,0:T(8,128)(2,1)} %copy-done.6, ...), kind=kOutput, calls=%fused_computation | convolution fusion | flops 2699034624 | bytes 11536384 | tf_op jit(solution)/shard_map/dot_general | solution.py:263
  164.3 1.7 constant_dynamic-update-slice_fusion.19
  166.0 3.5 %collective-permute-done.17 = bf16[320,512]{1,0:T(8,128)(2,1)} collective-permute-done((bf16[320,512]{1,0:T(8,128)(2,1)}, bf16[320,512]{1,0:T(8,128)(2,1)}, u32[]{:S(2)}, u32[]{:S(2)}) %collective-permute-start.17) | collective-permute-done | bytes 327712 | tf_op jit(solution)/shard_map/ppermute | solution.py:229
  169.6 1.7 constant_dynamic-update-slice_fusion.18
  171.3 1.7 constant_dynamic-update-slice_fusion.17
  173.1 3.1 %collective-permute-done.19 = bf16[320,512]{1,0:T(8,128)(2,1)} collective-permute-done((bf16[320,512]{1,0:T(8,128)(2,1)}, bf16[320,512]{1,0:T(8,128)(2,1)}, u32[]{:S(2)}, u32[]{:S(2)}) %collective-permute-start.19) | collective-permute-done | bytes 327712 | tf_op jit(solution)/shard_map/ppermute | solution.py:229
  176.2 1.7 constant_dynamic-update-slice_fusion.16
  178.0 3.3 %fusion.34 = f32[512,512]{1,0:T(8,128)S(1)} fusion(bf16[2560,512]{1,0:T(8,128)(2,1)} %constant_dynamic-update-slice_fusion.16, bf16[128,2560]{1,0:T(8,128)(2,1)S(1)} %copy-done.5, bf16[128,2560]{1,0:T(8,128)(2,1)S(1)} %copy-done.7, bf16[128,2560]{1,0:T(8,128)(2,1)S(1)} %copy-done.9, bf16[128,2560]{1,0:T(8,128)(2,1)S(1)} %copy-done.3), kind=kOutput, calls=%fused_computation.108 | convolution fusion | flops 1352663040 | bytes 6291456 | tf_op jit(solution)/shard_map/dot_general | solution.py:274
  187.1 3.7 %collective-permute-done.20 = bf16[512,256]{1,0:T(8,128)(2,1)S(1)} collective-permute-done((bf16[512,256]{1,0:T(8,128)(2,1)S(1)}, bf16[512,256]{1,0:T(8,128)(2,1)S(1)}, u32[]{:S(2)}, u32[]{:S(2)}) %collective-permute-start.20) | collective-permute-done | bytes 262176 | tf_op jit(solution)/shard_map/ppermute | solution.py:276
  192.4 11.2 %collective-permute-done.13 = bf16[512,640]{1,0:T(8,128)(2,1)S(1)} collective-permute-done((bf16[512,640]{1,0:T(8,128)(2,1)S(1)}, bf16[512,640]{1,0:T(8,128)(2,1)S(1)}, u32[]{:S(2)}, u32[]{:S(2)}) %collective-permute-start.13) | collective-permute-done | bytes 655392 | tf_op jit(solution)/shard_map/ppermute | solution.py:272
  203.6 2.4 fusion.40
  206.0 1.9 collective-permute-start.33
  207.9 2.0 collective-permute-start.32
  210.0 5.1 %collective-permute-done.33 = bf16[128,640]{1,0:T(8,128)(2,1)S(1)} collective-permute-done((bf16[128,640]{1,0:T(8,128)(2,1)S(1)}, bf16[128,640]{1,0:T(8,128)(2,1)S(1)}, u32[]{:S(2)}, u32[]{:S(2)}) %collective-permute-start.33) | collective-permute-done | bytes 163872 | tf_op jit(solution)/shard_map/ppermute | solution.py:149
  216.0 7.1 %collective-permute-done.31 = bf16[128,640]{1,0:T(8,128)(2,1)S(1)} collective-permute-done((bf16[128,640]{1,0:T(8,128)(2,1)S(1)}, bf16[128,640]{1,0:T(8,128)(2,1)S(1)}, u32[]{:S(2)}, u32[]{:S(2)}) %collective-permute-start.31) | collective-permute-done | bytes 163872 | tf_op jit(solution)/shard_map/ppermute | solution.py:149
  225.3 4.9 %collective-permute-done.34 = bf16[128,640]{1,0:T(8,128)(2,1)S(1)} collective-permute-done((bf16[128,640]{1,0:T(8,128)(2,1)S(1)}, bf16[128,640]{1,0:T(8,128)(2,1)S(1)}, u32[]{:S(2)}, u32[]{:S(2)}) %collective-permute-start.34) | collective-permute-done | bytes 163872 | tf_op jit(solution)/shard_map/ppermute | solution.py:291
  231.9 2.3 convolution_convert_fusion.1
  234.7 8.4 %all_to_all.5 = bf16[64,4,512]{2,0,1:T(8,128)(2,1)S(1)} all-to-all(bf16[64,4,512]{2,0,1:T(8,128)(2,1)S(1)} %bitcast.42), channel_id=1, replica_groups=mesh['groups'=2,'expert'=4,'decode'=4,'tensor'=1] {'decode'}, dimensions={1} | all-to-all | bytes 524288 | tf_op jit(solution)/shard_map/all_to_all | solution.py:43
  (167 shorter events, 55.5 us)
Async XLA Ops:
  7.2 224.7 %all-gather.2.cloned.1.call-start = ((), (), s32[]{:S(2)}) async-start(), calls=%async_computation.1 | async-start | bytes 3276800 | tf_op jit(solution)/shard_map/all_gather | solution.py:251
  11.5 50.9 %collective-permute-start.8 = (bf16[128,640]{1,0:T(8,128)(2,1)}, bf16[128,640]{1,0:T(8,128)(2,1)}, u32[]{:S(2)}, u32[]{:S(2)}) collective-permute-start(bf16[128,640]{1,0:T(8,128)(2,1)} %constant_dynamic-slice_fusion.12), channel_id=1, source_target_pairs={{0,12},{4,0},{8,4},{12,8},{1,13},{5,1},{9,5},{13,9},{2,14},{6,2},{... | collective-permute-start | bytes 491528 | tf_op jit(solution)/shard_map/ppermute | solution.py:149
  16.6 83.3 %collective-permute-start.4 = (bf16[128,640]{1,0:T(8,128)(2,1)}, bf16[128,640]{1,0:T(8,128)(2,1)}, u32[]{:S(2)}, u32[]{:S(2)}) collective-permute-start(bf16[128,640]{1,0:T(8,128)(2,1)} %constant_dynamic-slice_fusion.12), channel_id=1, source_target_pairs={{0,8},{4,12},{8,0},{12,4},{1,9},{5,13},{9,1},{13,5},{2,10},{6,14},... | collective-permute-start | bytes 491528 | tf_op jit(solution)/shard_map/ppermute | solution.py:149
  16.6 85.1 %collective-permute-start = (bf16[128,640]{1,0:T(8,128)(2,1)}, bf16[128,640]{1,0:T(8,128)(2,1)}, u32[]{:S(2)}, u32[]{:S(2)}) collective-permute-start(bf16[128,640]{1,0:T(8,128)(2,1)} %constant_dynamic-slice_fusion.12), channel_id=1, source_target_pairs={{0,4},{4,8},{8,12},{12,0},{1,5},{5,9},{9,13},{13,1},{2,6},{6,10},{... | collective-permute-start | bytes 491528 | tf_op jit(solution)/shard_map/ppermute | solution.py:149
  20.4 105.7 %collective-permute-start.14 = (bf16[320,512]{1,0:T(8,128)(2,1)}, bf16[320,512]{1,0:T(8,128)(2,1)}, u32[]{:S(2)}, u32[]{:S(2)}) collective-permute-start(bf16[320,512]{1,0:T(8,128)(2,1)} %pad_maximum_fusion.2), channel_id=1, source_target_pairs={{0,8},{4,12},{8,0},{12,4},{1,9},{5,13},{9,1},{13,5},{2,10},{6,14},... | collective-permute-start | bytes 983048 | tf_op jit(solution)/shard_map/ppermute | solution.py:149
  23.1 123.7 %collective-permute-start.16 = (bf16[320,512]{1,0:T(8,128)(2,1)}, bf16[320,512]{1,0:T(8,128)(2,1)}, u32[]{:S(2)}, u32[]{:S(2)}) collective-permute-start(bf16[320,512]{1,0:T(8,128)(2,1)} %pad_maximum_fusion.3), channel_id=1, source_target_pairs={{0,4},{4,8},{8,12},{12,0},{1,5},{5,9},{9,13},{13,1},{2,6},{6,10},{... | collective-permute-start | bytes 983048 | tf_op jit(solution)/shard_map/ppermute | solution.py:149
  62.4 84.8 %collective-permute-start.18 = (bf16[320,512]{1,0:T(8,128)(2,1)}, bf16[320,512]{1,0:T(8,128)(2,1)}, u32[]{:S(2)}, u32[]{:S(2)}) collective-permute-start(bf16[320,512]{1,0:T(8,128)(2,1)} %pad_maximum_fusion.4), channel_id=1, source_target_pairs={{0,12},{4,0},{8,4},{12,8},{1,13},{5,1},{9,5},{13,9},{2,14},{6,2},{... | collective-permute-start | bytes 983048 | tf_op jit(solution)/shard_map/ppermute | solution.py:149
  99.9 6.9 %collective-permute-start.23 = (bf16[128,640]{1,0:T(8,128)(2,1)S(1)}, bf16[128,640]{1,0:T(8,128)(2,1)S(1)}, u32[]{:S(2)}, u32[]{:S(2)}) collective-permute-start(bf16[128,640]{1,0:T(8,128)(2,1)S(1)} %get-tuple-element.16), channel_id=1, source_target_pairs={{0,0},{1,4},{2,8},{3,12},{4,1},{5,5},{6,9},{7,13},{8,2},{9,6},{10,... | collective-permute-start | bytes 491528 | tf_op jit(solution)/shard_map/ppermute | solution.py:245
  101.7 12.1 %collective-permute-start.9 = (bf16[128,640]{1,0:T(8,128)(2,1)}, bf16[128,640]{1,0:T(8,128)(2,1)S(1)}, u32[]{:S(2)}, u32[]{:S(2)}) collective-permute-start(bf16[128,640]{1,0:T(8,128)(2,1)} %collective-permute-done.8), channel_id=1, source_target_pairs={{0,2},{2,0},{1,3},{3,1},{4,6},{6,4},{5,7},{7,5},{8,10},{10,8},{9,1... | collective-permute-start | bytes 491528 | tf_op jit(solution)/shard_map/ppermute | solution.py:206
  106.8 8.6 %collective-permute-start.5 = (bf16[128,640]{1,0:T(8,128)(2,1)}, bf16[128,640]{1,0:T(8,128)(2,1)S(1)}, u32[]{:S(2)}, u32[]{:S(2)}) collective-permute-start(bf16[128,640]{1,0:T(8,128)(2,1)} %collective-permute-done.4), channel_id=1, source_target_pairs={{0,2},{2,0},{1,3},{3,1},{4,6},{6,4},{5,7},{7,5},{8,10},{10,8},{9,1... | collective-permute-start | bytes 491528 | tf_op jit(solution)/shard_map/ppermute | solution.py:206
  115.4 7.2 %collective-permute-start.1 = (bf16[128,640]{1,0:T(8,128)(2,1)}, bf16[128,640]{1,0:T(8,128)(2,1)S(1)}, u32[]{:S(2)}, u32[]{:S(2)}) collective-permute-start(bf16[128,640]{1,0:T(8,128)(2,1)} %collective-permute-done), channel_id=1, source_target_pairs={{0,2},{2,0},{1,3},{3,1},{4,6},{6,4},{5,7},{7,5},{8,10},{10,8},{9,1... | collective-permute-start | bytes 491528 | tf_op jit(solution)/shard_map/ppermute | solution.py:206
  117.6 6.8 %collective-permute-start.2 = (bf16[128,640]{1,0:T(8,128)(2,1)}, bf16[128,640]{1,0:T(8,128)(2,1)S(1)}, u32[]{:S(2)}, u32[]{:S(2)}) collective-permute-start(bf16[128,640]{1,0:T(8,128)(2,1)} %collective-permute-done), channel_id=1, source_target_pairs={{0,1},{1,0},{2,3},{3,2},{4,5},{5,4},{6,7},{7,6},{8,9},{9,8},{10,11... | collective-permute-start | bytes 491528 | tf_op jit(solution)/shard_map/ppermute | solution.py:207
  122.6 8.0 %collective-permute-start.25 = (bf16[128,640]{1,0:T(8,128)(2,1)S(1)}, bf16[128,640]{1,0:T(8,128)(2,1)S(1)}, u32[]{:S(2)}, u32[]{:S(2)}) collective-permute-start(bf16[128,640]{1,0:T(8,128)(2,1)S(1)} %copy-done.12), channel_id=1, source_target_pairs={{0,4},{1,0},{2,12},{3,8},{4,5},{5,1},{6,13},{7,9},{8,6},{9,2},{10,... | collective-permute-start | bytes 491528 | tf_op jit(solution)/shard_map/ppermute | solution.py:245
  124.4 12.1 %collective-permute-start.24 = (bf16[128,640]{1,0:T(8,128)(2,1)S(1)}, bf16[128,640]{1,0:T(8,128)(2,1)S(1)}, u32[]{:S(2)}, u32[]{:S(2)}) collective-permute-start(bf16[128,640]{1,0:T(8,128)(2,1)S(1)} %collective-permute-done.23), channel_id=1, source_target_pairs={{0,16},{16,0},{1,17},{17,1},{2,18},{18,2},{3,19},{19,3},{4,20},{20... | collective-permute-start | bytes 491528 | tf_op jit(solution)/shard_map/ppermute | solution.py:246
  126.2 16.3 %collective-permute-start.27 = (bf16[128,640]{1,0:T(8,128)(2,1)S(1)}, bf16[128,640]{1,0:T(8,128)(2,1)}, u32[]{:S(2)}, u32[]{:S(2)}) collective-permute-start(bf16[128,640]{1,0:T(8,128)(2,1)S(1)} %copy-done.11), channel_id=1, source_target_pairs={{0,8},{1,12},{2,0},{3,4},{4,9},{5,13},{6,1},{7,5},{8,10},{9,14},{1... | collective-permute-start | bytes 491528 | tf_op jit(solution)/shard_map/ppermute | solution.py:245
  130.6 14.1 %collective-permute-start.29 = (bf16[128,640]{1,0:T(8,128)(2,1)S(1)}, bf16[128,640]{1,0:T(8,128)(2,1)}, u32[]{:S(2)}, u32[]{:S(2)}) collective-permute-start(bf16[128,640]{1,0:T(8,128)(2,1)S(1)} %get-tuple-element.14), channel_id=1, source_target_pairs={{0,12},{1,8},{2,4},{3,0},{4,13},{5,9},{6,5},{7,1},{8,14},{9,10},{1... | collective-permute-start | bytes 491528 | tf_op jit(solution)/shard_map/ppermute | solution.py:245
  136.5 5.3 %collective-permute-start.26 = (bf16[128,640]{1,0:T(8,128)(2,1)S(1)}, bf16[128,640]{1,0:T(8,128)(2,1)S(1)}, u32[]{:S(2)}, u32[]{:S(2)}) collective-permute-start(bf16[128,640]{1,0:T(8,128)(2,1)S(1)} %collective-permute-done.25), channel_id=1, source_target_pairs={{0,16},{16,0},{1,17},{17,1},{2,18},{18,2},{3,19},{19,3},{4,20},{20... | collective-permute-start | bytes 491528 | tf_op jit(solution)/shard_map/ppermute | solution.py:246
  144.6 4.3 %collective-permute-start.3 = (bf16[128,640]{1,0:T(8,128)(2,1)S(1)}, bf16[128,640]{1,0:T(8,128)(2,1)S(1)}, u32[]{:S(2)}, u32[]{:S(2)}) collective-permute-start(bf16[128,640]{1,0:T(8,128)(2,1)S(1)} %collective-permute-done.1), channel_id=1, source_target_pairs={{0,1},{1,0},{2,3},{3,2},{4,5},{5,4},{6,7},{7,6},{8,9},{9,8},{10,11... | collective-permute-start | bytes 491528 | tf_op jit(solution)/shard_map/ppermute | solution.py:208
  144.6 39.2 %collective-permute-start.28 = (bf16[128,640]{1,0:T(8,128)(2,1)}, bf16[128,640]{1,0:T(8,128)(2,1)}, u32[]{:S(2)}, u32[]{:S(2)}) collective-permute-start(bf16[128,640]{1,0:T(8,128)(2,1)} %collective-permute-done.27), channel_id=1, source_target_pairs={{0,16},{16,0},{1,17},{17,1},{2,18},{18,2},{3,19},{19,3},{4,20},{20... | collective-permute-start | bytes 491528 | tf_op jit(solution)/shard_map/ppermute | solution.py:246
  145.1 45.7 %collective-permute-start.30 = (bf16[128,640]{1,0:T(8,128)(2,1)}, bf16[128,640]{1,0:T(8,128)(2,1)S(1)}, u32[]{:S(2)}, u32[]{:S(2)}) collective-permute-start(bf16[128,640]{1,0:T(8,128)(2,1)} %collective-permute-done.29), channel_id=1, source_target_pairs={{0,16},{16,0},{1,17},{17,1},{2,18},{18,2},{3,19},{19,3},{4,20},{20... | collective-permute-start | bytes 491528 | tf_op jit(solution)/shard_map/ppermute | solution.py:246
  146.8 15.8 %collective-permute-start.15 = (bf16[320,512]{1,0:T(8,128)(2,1)}, bf16[320,512]{1,0:T(8,128)(2,1)}, u32[]{:S(2)}, u32[]{:S(2)}) collective-permute-start(bf16[320,512]{1,0:T(8,128)(2,1)} %collective-permute-done.14), channel_id=1, source_target_pairs={{0,16},{16,0},{1,17},{17,1},{2,18},{18,2},{3,19},{19,3},{4,20},{20... | collective-permute-start | bytes 983048 | tf_op jit(solution)/shard_map/ppermute | solution.py:229
  147.2 22.3 %collective-permute-start.17 = (bf16[320,512]{1,0:T(8,128)(2,1)}, bf16[320,512]{1,0:T(8,128)(2,1)}, u32[]{:S(2)}, u32[]{:S(2)}) collective-permute-start(bf16[320,512]{1,0:T(8,128)(2,1)} %collective-permute-done.16), channel_id=1, source_target_pairs={{0,16},{16,0},{1,17},{17,1},{2,18},{18,2},{3,19},{19,3},{4,20},{20... | collective-permute-start | bytes 983048 | tf_op jit(solution)/shard_map/ppermute | solution.py:229
  148.9 27.3 %collective-permute-start.19 = (bf16[320,512]{1,0:T(8,128)(2,1)}, bf16[320,512]{1,0:T(8,128)(2,1)}, u32[]{:S(2)}, u32[]{:S(2)}) collective-permute-start(bf16[320,512]{1,0:T(8,128)(2,1)} %collective-permute-done.18), channel_id=1, source_target_pairs={{0,16},{16,0},{1,17},{17,1},{2,18},{18,2},{3,19},{19,3},{4,20},{20... | collective-permute-start | bytes 983048 | tf_op jit(solution)/shard_map/ppermute | solution.py:229
  162.6 19.1 %collective-permute-start.12 = (bf16[512,1280]{1,0:T(8,128)(2,1)S(1)}, bf16[512,1280]{1,0:T(8,128)(2,1)S(1)}, u32[]{:S(2)}, u32[]{:S(2)}) collective-permute-start(bf16[512,1280]{1,0:T(8,128)(2,1)S(1)} %pad_maximum_fusion.1), channel_id=1, source_target_pairs={{0,1},{1,0},{2,3},{3,2},{4,5},{5,4},{6,7},{7,6},{8,9},{9,8},{10,11... | collective-permute-start | bytes 3932168 | tf_op jit(solution)/shard_map/ppermute | solution.py:269
  181.5 9.3 %collective-permute-start.20 = (bf16[512,256]{1,0:T(8,128)(2,1)S(1)}, bf16[512,256]{1,0:T(8,128)(2,1)S(1)}, u32[]{:S(2)}, u32[]{:S(2)}) collective-permute-start(bf16[512,256]{1,0:T(8,128)(2,1)S(1)} %get-tuple-element.11), channel_id=1, source_target_pairs={{0,2},{2,0},{1,3},{3,1},{4,6},{6,4},{5,7},{7,5},{8,10},{10,8},{9,1... | collective-permute-start | bytes 786440 | tf_op jit(solution)/shard_map/ppermute | solution.py:276
  183.1 20.5 %collective-permute-start.13 = (bf16[512,640]{1,0:T(8,128)(2,1)S(1)}, bf16[512,640]{1,0:T(8,128)(2,1)S(1)}, u32[]{:S(2)}, u32[]{:S(2)}) collective-permute-start(bf16[512,640]{1,0:T(8,128)(2,1)S(1)} %add_convert_fusion), channel_id=1, source_target_pairs={{0,2},{2,0},{1,3},{3,1},{4,6},{6,4},{5,7},{7,5},{8,10},{10,8},{9,1... | collective-permute-start | bytes 1966088 | tf_op jit(solution)/shard_map/ppermute | solution.py:272
  185.5 6.1 %collective-permute-start.21 = (bf16[512,256]{1,0:T(8,128)(2,1)S(1)}, bf16[512,256]{1,0:T(8,128)(2,1)S(1)}, u32[]{:S(2)}, u32[]{:S(2)}) collective-permute-start(bf16[512,256]{1,0:T(8,128)(2,1)S(1)} %get-tuple-element.11), channel_id=1, source_target_pairs={{0,1},{1,0},{2,3},{3,2},{4,5},{5,4},{6,7},{7,6},{8,9},{9,8},{10,11... | collective-permute-start | bytes 786440 | tf_op jit(solution)/shard_map/ppermute | solution.py:277
  206.0 9.0 %collective-permute-start.33 = (bf16[128,640]{1,0:T(8,128)(2,1)S(1)}, bf16[128,640]{1,0:T(8,128)(2,1)S(1)}, u32[]{:S(2)}, u32[]{:S(2)}) collective-permute-start(bf16[128,640]{1,0:T(8,128)(2,1)S(1)} %get-tuple-element.25), channel_id=1, source_target_pairs={{0,4},{4,8},{8,12},{12,0},{1,5},{5,9},{9,13},{13,1},{2,6},{6,10},{... | collective-permute-start | bytes 491528 | tf_op jit(solution)/shard_map/ppermute | solution.py:149
  207.9 8.2 %collective-permute-start.32 = (bf16[128,640]{1,0:T(8,128)(2,1)S(1)}, bf16[128,640]{1,0:T(8,128)(2,1)S(1)}, u32[]{:S(2)}, u32[]{:S(2)}) collective-permute-start(bf16[128,640]{1,0:T(8,128)(2,1)S(1)} %get-tuple-element.26), channel_id=1, source_target_pairs={{0,12},{4,0},{8,4},{12,8},{1,13},{5,1},{9,5},{13,9},{2,14},{6,2},{... | collective-permute-start | bytes 491528 | tf_op jit(solution)/shard_map/ppermute | solution.py:149
  209.9 13.3 %collective-permute-start.31 = (bf16[128,640]{1,0:T(8,128)(2,1)S(1)}, bf16[128,640]{1,0:T(8,128)(2,1)S(1)}, u32[]{:S(2)}, u32[]{:S(2)}) collective-permute-start(bf16[128,640]{1,0:T(8,128)(2,1)S(1)} %get-tuple-element.24), channel_id=1, source_target_pairs={{0,8},{4,12},{8,0},{12,4},{1,9},{5,13},{9,1},{13,5},{2,10},{6,14},... | collective-permute-start | bytes 491528 | tf_op jit(solution)/shard_map/ppermute | solution.py:149
  224.3 5.9 %collective-permute-start.34 = (bf16[128,640]{1,0:T(8,128)(2,1)S(1)}, bf16[128,640]{1,0:T(8,128)(2,1)S(1)}, u32[]{:S(2)}, u32[]{:S(2)}) collective-permute-start(bf16[128,640]{1,0:T(8,128)(2,1)S(1)} %get-tuple-element.9), channel_id=1, source_target_pairs={{0,2},{2,0},{1,3},{3,1},{4,6},{6,4},{5,7},{7,5},{8,10},{10,8},{9,1... | collective-permute-start | bytes 491528 | tf_op jit(solution)/shard_map/ppermute | solution.py:291
  225.2 5.0 %collective-permute-start.35 = (bf16[128,640]{1,0:T(8,128)(2,1)S(1)}, bf16[128,640]{1,0:T(8,128)(2,1)S(1)}, u32[]{:S(2)}, u32[]{:S(2)}) collective-permute-start(bf16[128,640]{1,0:T(8,128)(2,1)S(1)} %get-tuple-element.9), channel_id=1, source_target_pairs={{0,1},{1,0},{2,3},{3,2},{4,5},{5,4},{6,7},{7,6},{8,9},{9,8},{10,11... | collective-permute-start | bytes 491528 | tf_op jit(solution)/shard_map/ppermute | solution.py:292
  (26 other events, 455.4 us)
Sparse Core Ops, SparseCore 0:
  24.7 70.0 all-gather.1

commit v2 on v0

--- a/solution.py
+++ b/solution.py
@@ -1,6 +1,8 @@
 import jax
 import jax.numpy as jnp
 from jax import lax
+from jax.experimental import pallas as pl
+from jax.experimental.pallas import tpu as pltpu
 from jax.sharding import PartitionSpec as P
 
 BLOCK = 16
@@ -18,7 +20,34 @@
     return padded[row_index]
 
 
-def on_device(
+def hand_over(key_value, req_owner, req_blocks):
+    tok_rows, kv_width = key_value.shape
+    owner_count = req_owner.shape[1]
+    block_count = tok_rows // BLOCK
+    owners = req_owner[0]
+    counts = req_blocks[0]
+    starts = jnp.cumsum(counts) - counts
+    owner_index = jnp.arange(owner_count, dtype=jnp.int32)
+    slot_index = jnp.arange(QCAP, dtype=jnp.int32)
+    block_index = jnp.arange(block_count, dtype=jnp.int32)
+    chosen = owners[:, None, None, None] == owner_index[None, :, None, None]
+    chosen = chosen & (slot_index[None, None, :, None] < counts[:, None, None, None])
+    chosen = chosen & (
+        block_index[None, None, None, :]
+        == starts[:, None, None, None] + slot_index[None, None, :, None]
+    )
+    choose = jnp.sum(chosen.astype(jnp.int32), axis=0).astype(jnp.bfloat16)
+    kv_blocks = key_value.reshape(block_count, BLOCK, kv_width)
+    sending = jnp.einsum(
+        "oqb,bjw->qjow", choose, kv_blocks, preferred_element_type=jnp.float32
+    ).astype(jnp.bfloat16)
+    sending = sending.reshape(QCAP * BLOCK, owner_count, kv_width)
+    received = lax.all_to_all(sending, "decode", split_axis=1, concat_axis=1, tiled=True)
+    kv_handed = received.reshape(1, 1, QCAP * BLOCK, owner_count, kv_width)
+    return kv_handed
+
+
+def wide_plan(
     resid,
     moe_gain,
     attn_gain,
@@ -109,29 +138,394 @@
         lax.all_gather(w_kv, "expert", axis=0, tiled=True),
         preferred_element_type=jnp.float32,
     ).astype(jnp.bfloat16)
-    owner_count = req_owner.shape[1]
-    block_count = tok_rows // BLOCK
-    owners = req_owner[0]
-    counts = req_blocks[0]
-    starts = jnp.cumsum(counts) - counts
-    owner_index = jnp.arange(owner_count, dtype=jnp.int32)
-    slot_index = jnp.arange(QCAP, dtype=jnp.int32)
-    block_index = jnp.arange(block_count, dtype=jnp.int32)
-    chosen = owners[:, None, None, None] == owner_index[None, :, None, None]
-    chosen = chosen & (slot_index[None, None, :, None] < counts[:, None, None, None])
-    chosen = chosen & (
-        block_index[None, None, None, :]
-        == starts[:, None, None, None] + slot_index[None, None, :, None]
-    )
-    choose = jnp.sum(chosen.astype(jnp.int32), axis=0).astype(jnp.bfloat16)
-    kv_blocks = key_value.reshape(block_count, BLOCK, kv_width)
-    sending = jnp.einsum(
-        "oqb,bjw->qjow", choose, kv_blocks, preferred_element_type=jnp.float32
-    ).astype(jnp.bfloat16)
-    sending = sending.reshape(QCAP * BLOCK, owner_count, kv_width)
-    received = lax.all_to_all(sending, "decode", split_axis=1, concat_axis=1, tiled=True)
-    kv_handed = received.reshape(1, 1, QCAP * BLOCK, owner_count, kv_width)
-    return (layer_out, kv_handed)
+    return layer_out, hand_over(key_value, req_owner, req_blocks)
+
+
+SWAP_CORE = [(0, 1), (1, 0), (2, 3), (3, 2)]
+SWAP_CHIP = [(0, 2), (2, 0), (1, 3), (3, 1)]
+SWAP_FAR = [(0, 3), (3, 0), (1, 2), (2, 1)]
+SWAP_GROUP = [(0, 1), (1, 0)]
+SHIFTS = (2, 1, 3)
+BF16 = jnp.bfloat16
+F32 = jnp.float32
+VMEM = pl.BlockSpec(memory_space=pltpu.VMEM)
+SMEM = pl.BlockSpec(memory_space=pltpu.SMEM)
+ANY = pl.BlockSpec(memory_space=pl.ANY)
+META = 16
+
+
+def call(body, outs, in_specs, scratch=(), flops=0, moved=0, name=None):
+    return pl.pallas_call(
+        body,
+        out_shape=[jax.ShapeDtypeStruct(shape, kind) for shape, kind in outs],
+        in_specs=in_specs,
+        out_specs=[VMEM] * len(outs),
+        scratch_shapes=list(scratch),
+        compiler_params=pltpu.CompilerParams(vmem_limit_bytes=48 << 20),
+        cost_estimate=pl.CostEstimate(flops=flops, bytes_accessed=moved, transcendentals=0),
+        name=name,
+    )
+
+
+def to_shift(values, shift):
+    count = lax.axis_size("expert")
+    return lax.ppermute(values, "expert", [(i, (i + shift) % count) for i in range(count)])
+
+
+def after(values, *others):
+    return lax.optimization_barrier((values,) + others)[0]
+
+
+def spread(values):
+    across = lax.ppermute(values, "decode", SWAP_CHIP)
+    beside = lax.ppermute(values, "decode", SWAP_CORE)
+    far = lax.ppermute(across, "decode", SWAP_CORE)
+    return values, beside, across, far
+
+
+def lanes(index, size):
+    return pl.ds(pl.multiple_of(index * size, 128), size)
+
+
+def dot(a, b):
+    return jnp.dot(a, b, preferred_element_type=F32)
+
+
+def norm_kernel(capacity, place, resid, gain, score, ids_row, ids_column, moe_in, message):
+    rows, width = resid.shape
+    piece = message.shape[1]
+    values = resid[...].astype(F32)
+    power = jnp.mean(values * values, axis=-1, keepdims=True)
+    moe_in[...] = (values * lax.rsqrt(power + 1e-05) * gain[...]).astype(BF16)
+    message[:rows, :] = moe_in[:, lanes(place[1], piece)]
+    earlier = lax.broadcasted_iota(jnp.int32, (rows, rows), 0) < lax.broadcasted_iota(
+        jnp.int32, (rows, rows), 1
+    )
+    same = (ids_column[...] == ids_row[...]) & earlier
+    slots = jnp.sum(same.astype(F32), axis=0, keepdims=True)
+    scale = jnp.where(slots < capacity, score[...], 0.0)
+    high = scale.astype(BF16)
+    rest = scale - high.astype(F32)
+    middle = rest.astype(BF16)
+    low = (rest - middle.astype(F32)).astype(BF16)
+    message[rows:, :] = jnp.zeros((META, piece), BF16)
+    for i, part in enumerate((high, middle, low, ids_row[...].astype(F32).astype(BF16))):
+        message[rows:, i * rows : (i + 1) * rows] = jnp.broadcast_to(part, (META, rows))
+
+
+def pack_kernel(place, gate, up, down, own, *rest):
+    messages, downs, sem = rest[:3], rest[3:7], rest[7]
+    zone, slot, group = place[0], place[1], place[2]
+    count = 4
+    near = gate.shape[0]
+    hidden = gate.shape[1] // count
+    half = hidden // 2
+    copies = []
+
+    def move(source, target):
+        copies.append(pltpu.make_async_copy(source, target, sem.at[len(copies)]))
+
+    for i, shift in enumerate(SHIFTS):
+        start = lax.rem(zone + shift, count) * hidden + group * half
+        for j, weights in enumerate((gate, up)):
+            move(
+                weights.at[:, pl.ds(pl.multiple_of(start, 128), half)],
+                messages[i].at[:, j * half : (j + 1) * half],
+            )
+    for k in range(count):
+        start = (slot ^ k) * hidden + group * half
+        move(down.at[pl.ds(pl.multiple_of(start, 128), half), :], downs[k])
+    for part in range(2):
+        start = zone * hidden + (group ^ part) * half
+        for j, weights in enumerate((gate, up)):
+            move(
+                weights.at[:, pl.ds(pl.multiple_of(start, 128), half)],
+                own.at[:, (2 * part + j) * half : (2 * part + j + 1) * half],
+            )
+    for copy in copies:
+        copy.start()
+    for copy in copies:
+        copy.wait()
+
+
+def routed_kernel(place, moe_in, own, *rest):
+    pieces = rest[:12]
+    gate, up, down, tokens, send, keep, hidden = rest[12:]
+    zone, slot = place[0], place[1]
+    rows = moe_in.shape[0]
+    piece = own.shape[1]
+    tokens[:rows, :] = moe_in[...]
+    for i, shift in enumerate(SHIFTS):
+        for j in range(4):
+            tokens[shift * rows : (shift + 1) * rows, lanes(slot ^ j, piece)] = pieces[4 * i + j][
+                :rows, :
+            ]
+    width = hidden.shape[1]
+    step = 256
+    for n in range(width // step):
+        cols = slice(n * step, (n + 1) * step)
+        gate_val = dot(tokens[...], gate[0, :, cols])
+        up_val = dot(tokens[...], up[0, :, cols])
+        hidden[:, cols] = (gate_val / (1.0 + jnp.exp(-gate_val)) * up_val).astype(BF16)
+    diagonal = lax.broadcasted_iota(jnp.int32, (rows, rows), 0) == lax.broadcasted_iota(
+        jnp.int32, (rows, rows), 1
+    )
+    mine = (zone // 2).astype(F32)
+    scales = []
+    for shift in range(4):
+        source = own if shift == 0 else pieces[4 * SHIFTS.index(shift)]
+        info = source[rows : rows + META, :].astype(F32)[:1]
+        value = info[:, :rows] + info[:, rows : 2 * rows] + info[:, 2 * rows : 3 * rows]
+        value = jnp.where(info[:, 3 * rows : 4 * rows] == mine, value, 0.0)
+        scales.append(
+            jnp.sum(jnp.where(diagonal, value, 0.0), axis=1, keepdims=True)
+        )
+    scale = jnp.concatenate(scales, axis=0)
+    for target, first, parts in ((send, 1, (1, 3)), (keep, 0, (0, 2))):
+        for i, j in enumerate(parts):
+            value = dot(hidden[...], down[0, :, lanes(slot ^ j, piece)]) * scale
+            target[:, i * piece : (i + 1) * piece] = value.astype(BF16)
+
+
+def gate_up_kernel(place, tokens, own, *rest):
+    got, other, hidden = rest[:3], rest[3:6], rest[6]
+    zone, group = place[0], place[2]
+    near = own.shape[0]
+    width = own.shape[1] // 2
+    half = width // 2
+    for part, pieces in ((0, got), (1, other)):
+        both = dot(tokens[:, lanes(zone, near)], own[:, part * width : (part + 1) * width])
+        for i, shift in enumerate(SHIFTS):
+            source = lax.rem(zone - shift + 4, 4)
+            both = both + dot(tokens[:, lanes(source, near)], pieces[i][...])
+        gate_val, up_val = both[:, :half], both[:, half:]
+        hidden[:, lanes(group ^ part, half)] = (
+            gate_val / (1.0 + jnp.exp(-gate_val)) * up_val
+        ).astype(BF16)
+
+
+def down_kernel(place, keep, crossed, *rest):
+    pieces, got, other = rest[:4], rest[4:8], rest[8:12]
+    own, sends, hidden, weights = rest[12], rest[13:16], rest[16], rest[17]
+    zone, slot, group = place[0], place[1], place[2]
+    width = pieces[0].shape[1]
+    half = width // 2
+    rows = own.shape[0]
+    for j in range(4):
+        hidden[:, lanes(slot ^ j, width)] = pieces[j][...]
+    for k in range(4):
+        base = (zone ^ k) * width
+        weights[pl.ds(pl.multiple_of(base + group * half, 128), half), :] = got[k][...]
+        weights[pl.ds(pl.multiple_of(base + (1 - group) * half, 128), half), :] = other[k][...]
+    for block in range(4):
+        span = slice(block * rows, (block + 1) * rows)
+        value = keep[span, :].astype(F32) + crossed[span, :].astype(F32)
+        value = value + dot(hidden[span, :], weights[...])
+        if block == 0:
+            own[...] = value
+        else:
+            sends[SHIFTS.index(block)][...] = value.astype(BF16)
+
+
+def layer_kernel(place, resid, own, a, b, c, out):
+    piece = own.shape[1]
+    value = own[...] + a[...].astype(F32) + b[...].astype(F32) + c[...].astype(F32)
+    value = value + resid[:, lanes(place[1], piece)].astype(F32)
+    out[...] = value.astype(BF16)
+
+
+def kv_kernel(place, owner, blocks, gain, a, b, c, d, mine, theirs, *rest):
+    outs, full, key_value = rest[:4], rest[4], rest[5]
+    slot, group = place[1], place[2]
+    piece = a.shape[1]
+    for j, part in enumerate((a, b, c, d)):
+        full[:, lanes(slot ^ j, piece)] = part[...].astype(F32)
+    values = full[...]
+    power = jnp.mean(values * values, axis=-1, keepdims=True)
+    attn_in = (values * lax.rsqrt(power + 1e-05) * gain[...]).astype(BF16)
+    half = mine.shape[1]
+    for part, weights in ((0, mine), (1, theirs)):
+        key_value[:, lanes(group ^ part, half)] = dot(attn_in, weights[...]).astype(BF16)
+    held = full.shape[0] // BLOCK
+    width = key_value.shape[1]
+    for j in range(4):
+        start, amount, begin = 0, 0, 0
+        for r in range(4):
+            here = owner[0, r] == (slot ^ j)
+            amount = jnp.where(here, blocks[0, r], amount)
+            begin = jnp.where(here, start, begin)
+            start = start + blocks[0, r]
+        for q in range(QCAP):
+            row = jnp.clip(begin + q, 0, held - 1) * BLOCK
+            chosen = key_value[pl.ds(pl.multiple_of(row, BLOCK), BLOCK), :]
+            outs[j][q * BLOCK : (q + 1) * BLOCK, :] = jnp.where(
+                q < amount, chosen, jnp.zeros((BLOCK, width), BF16)
+            )
+
+
+def hand_kernel(place, a, b, c, d, out):
+    parts = [part[...].astype(F32) for part in (a, b, c, d)]
+    ordered = []
+    for source in range(4):
+        j = place[1] ^ source
+        value = jnp.where(j == 0, parts[0], parts[1])
+        ordered.append(jnp.where(j < 2, value, jnp.where(j == 2, parts[2], parts[3])))
+    out[...] = jnp.stack(ordered, axis=1).astype(BF16)
+
+
+def near_plan(
+    resid,
+    moe_gain,
+    attn_gain,
+    gate_score,
+    expert_ids,
+    w_gate,
+    w_up,
+    w_down,
+    shared_gate,
+    shared_up,
+    shared_down,
+    w_kv,
+    req_owner,
+    req_blocks,
+):
+    rows, width = resid.shape
+    zones = lax.axis_size("expert")
+    slots = lax.axis_size("decode")
+    capacity = 2 * rows // (zones // 2)
+    piece = width // slots
+    near = shared_gate.shape[0]
+    hidden = shared_gate.shape[1] // zones
+    half = hidden // 2
+    total_rows = zones * rows
+    routed_width = w_gate.shape[2]
+    kv_width = w_kv.shape[1]
+    group = lax.axis_index("groups")
+    place = jnp.stack(
+        [lax.axis_index("expert"), lax.axis_index("decode"), group]
+    ).astype(jnp.int32)
+
+    moe_in, message = call(
+        lambda *refs: norm_kernel(capacity, *refs),
+        [((rows, width), BF16), ((rows + META, piece), BF16)],
+        [SMEM] + [VMEM] * 5,
+        name="norm",
+    )(
+        place,
+        resid,
+        moe_gain.reshape(1, width),
+        gate_score.reshape(1, rows),
+        expert_ids.reshape(1, rows),
+        expert_ids,
+    )
+    packed = call(
+        pack_kernel,
+        [((near, 2 * hidden), BF16)] + [((near, hidden), BF16)] * 3 + [((half, piece), BF16)] * 4,
+        [SMEM] + [ANY] * 3,
+        [pltpu.SemaphoreType.DMA((14,))],
+        name="pack",
+    )(place, shared_gate, shared_up, shared_down)
+    own_weights, weight_messages, down_messages = packed[0], packed[1:4], packed[4:8]
+
+    arrived = [to_shift(message, s) for s in SHIFTS]
+    pieces = [part for values in arrived for part in spread(values)]
+
+    got = [to_shift(values, s) for values, s in zip(weight_messages, SHIFTS)]
+    other = [lax.ppermute(values, "groups", SWAP_GROUP) for values in got]
+
+    down_got, down_other = [], []
+    down_messages = lax.optimization_barrier(tuple(down_messages) + (got[0],))[:4]
+    for k in range(slots):
+        pairs = [
+            (z * slots + d, (d ^ k) * slots + z) for z in range(zones) for d in range(slots)
+        ]
+        values = lax.ppermute(down_messages[k], ("expert", "decode"), pairs)
+        down_got.append(values)
+        down_other.append(lax.ppermute(values, "groups", SWAP_GROUP))
+
+    kv_half = lax.dynamic_slice_in_dim(w_kv, group * (kv_width // 2), kv_width // 2, 1)
+    kv_half = after(kv_half, arrived[0])
+    kv_mine = lax.all_gather(kv_half, "expert", axis=0, tiled=True)
+    kv_theirs = lax.ppermute(kv_mine, "groups", SWAP_GROUP)
+
+    tokens, send, keep = call(
+        routed_kernel,
+        [((total_rows, width), BF16), ((total_rows, 2 * piece), BF16), ((total_rows, 2 * piece), BF16)],
+        [SMEM] + [VMEM] * 17,
+        [pltpu.VMEM((total_rows, routed_width), BF16)],
+        flops=6 * total_rows * width * routed_width,
+        moved=14 << 20,
+        name="routed",
+    )(place, moe_in, message, *pieces, w_gate, w_up, w_down)
+    beside = lax.ppermute(send, "decode", SWAP_CORE)
+    keep_sum = keep.astype(F32) + beside.astype(F32)
+    crossed = lax.ppermute(keep_sum[:, piece:].astype(BF16), "decode", SWAP_CHIP)
+
+    (shared_hidden,) = call(
+        gate_up_kernel,
+        [((total_rows, hidden), BF16)],
+        [SMEM] + [VMEM] * 8,
+        flops=4 * total_rows * width * hidden,
+        moved=6 << 20,
+        name="gate_up",
+    )(place, tokens, own_weights, *got, *other)
+    hidden_pieces = spread(shared_hidden)
+    summed = call(
+        down_kernel,
+        [((rows, piece), F32)] + [((rows, piece), BF16)] * 3,
+        [SMEM] + [VMEM] * 14,
+        [
+            pltpu.VMEM((total_rows, slots * hidden), BF16),
+            pltpu.VMEM((slots * hidden, piece), BF16),
+        ],
+        flops=2 * total_rows * slots * hidden * piece,
+        moved=5 << 20,
+        name="down",
+    )(place, keep_sum[:, :piece], crossed, *hidden_pieces, *down_got, *down_other)
+    returned = [to_shift(values, -s) for values, s in zip(summed[1:], SHIFTS)]
+    (layer_out,) = call(
+        layer_kernel, [((rows, piece), BF16)], [SMEM] + [VMEM] * 5, name="layer"
+    )(place, resid, summed[0], *returned)
+
+    handed = call(
+        kv_kernel,
+        [((QCAP * BLOCK, kv_width), BF16)] * 4,
+        [SMEM] * 3 + [VMEM] * 7,
+        [pltpu.VMEM((rows, width), F32), pltpu.VMEM((rows, kv_width), BF16)],
+        flops=2 * rows * width * kv_width,
+        moved=4 << 20,
+        name="kv",
+    )(
+        place,
+        req_owner,
+        req_blocks,
+        attn_gain.reshape(1, width),
+        *spread(layer_out),
+        kv_mine,
+        kv_theirs,
+    )
+    received = [handed[0]] + [
+        lax.ppermute(values, "decode", pairs)
+        for values, pairs in zip(handed[1:], (SWAP_CORE, SWAP_CHIP, SWAP_FAR))
+    ]
+    (kv_handed,) = call(
+        hand_kernel,
+        [((QCAP * BLOCK, slots, kv_width), BF16)],
+        [SMEM] + [VMEM] * 4,
+        name="hand",
+    )(place, *received)
+    return layer_out, kv_handed[None, None]
+
+
+def on_device(*operands):
+    resid = operands[0]
+    zones = lax.axis_size("expert")
+    holders = lax.axis_size("decode")
+    fits = 2 * resid.shape[0] // (zones // 2) >= resid.shape[0]
+    square = zones == holders == 4 and lax.axis_size("tensor") == 1
+    if fits and square and lax.axis_size("groups") == 2:
+        return near_plan(*operands)
+    return wide_plan(*operands)
 
 
 def solution(mesh):

time: 507 us -> 207 us (0.41)
  waiting for transfers between devices: 422 us -> 89.6 us
  starting transfers between devices: 11.1 us -> 64.9 us
  matrix products: 26.7 us -> 0 us
  Pallas kernels: 0 us -> 22.1 us
  blocking collectives: 16.1 us -> 0 us
    all_to_all x2 -> x0, waiting for transfers between devices: 244 us -> none  [the longest x1 126 us: on_device(): lax.all_to_all(outgoing, 'expert', split_axis=0, concat_axis=0, tiled=True)]
    all_gather x4 -> x1, waiting for transfers between devices: 156 us -> 0.01 us  [near_plan(): kv_mine = lax.all_gather(kv_half, 'expert', axis=0, tiled=True)]
    ppermute x0 -> x41, waiting for transfers between devices: none -> 89.6 us  [the longest x9 40.4 us: to_shift(): lax.ppermute(values, 'expert', [(i, (i + shift) % count) for i in range(c...]
    ppermute x0 -> x41, starting transfers between devices: none -> 64.9 us  [the longest x9 20.7 us: to_shift(): lax.ppermute(values, 'expert', [(i, (i + shift) % count) for i in range(c...]
    dot_general x7 -> x0, matrix products: 26.7 us -> none  [the longest x1 7.19 us: on_device(): jnp.dot(hidden, w_down[0], preferred_element_type=jnp.float32)]
    unnamed x6 -> x1, waiting for transfers between devices: 22.4 us -> 0.02 us
    pallas_call x0 -> x8, Pallas kernels: none -> 22.1 us  [the longest x1 8.9 us: near_plan(): call(routed_kernel, [((total_rows, width), BF16), ((total_rows, 2 * piece...]
    all_to_all x2 -> x0, starting transfers between devices: 10.9 us -> none  [the longest x1 6.32 us: on_device(): lax.all_to_all(outgoing, 'expert', split_axis=0, concat_axis=0, tiled=True)]
  transfers between devices with their start and end apart: 7 -> 42, of which waited for: 6 -> 17; matrix products, arithmetic and copies ran while one was open for 6% -> 1% of each run, Pallas kernels for 0% -> 9%
where the time goes in v2:
time: 207 us; the launch traced here: 206 us
  waiting for transfers between devices  89.6 us (43%)
  starting transfers between devices  64.9 us (31%)
  Pallas kernels  22.1 us (11%)
  between operations  14.3 us (7%)
  local copies, waits for them, and re-layouts  13.6 us (7%)
    ppermute x9, waiting for transfers between devices, to_shift(): lax.ppermute(values, 'expert', [(i, (i + shift) % count) for i in range(c...  40.4 us
    ppermute x4, waiting for transfers between devices, near_plan(): down_other.append(lax.ppermute(values, 'groups', SWAP_GROUP))  26.7 us
    ppermute x9, starting transfers between devices, to_shift(): lax.ppermute(values, 'expert', [(i, (i + shift) % count) for i in range(c...  20.7 us
    ppermute x5, waiting for transfers between devices, spread(): across = lax.ppermute(values, 'decode', SWAP_CHIP)  13.5 us
    unnamed x51, local copies, waits for them, and re-layouts  11.9 us
    ppermute x5, starting transfers between devices, spread(): across = lax.ppermute(values, 'decode', SWAP_CHIP)  10.9 us
    ppermute x4, starting transfers between devices, near_plan(): values = lax.ppermute(down_messages[k], ('expert', 'decode'), pairs)  9.87 us
    pallas_call x1, Pallas kernels, near_plan(): call(routed_kernel, [((total_rows, width), BF16), ((total_rows, 2 * piece...  8.9 us
  transfers between devices with their start and end apart: 42, of which 17 were waited for; matrix products, arithmetic and copies ran while one was open for 1% of the time, Pallas kernels for 9%

profile of v2, /device:TPU:0, one launch (start us, length us, event | category | flops | bytes accessed | tf_op | source)
XLA Modules:
  0.0 206.4 jit_solution(4727600624372409664)
XLA Ops:
  12.1 4.1 %collective-permute-start = (bf16[144,640]{1,0:T(8,128)(2,1)S(1)}, bf16[144,640]{1,0:T(8,128)(2,1)S(1)}, u32[]{:S(2)}, u32[]{:S(2)}) collective-permute-start(bf16[144,640]{1,0:T(8,128)(2,1)S(1)} %get-tuple-element.29.own), channel_id=1, source_target_pairs={{0,8},{4,12},{8,0},{12,4},{1,9},{5,13},{9,1},{13,5},{2,10},{6,14},... | collective-permute-start | bytes 552968 | tf_op jit(solution)/shard_map/ppermute | solution.py:172
  17.8 2.2 %collective-permute-start.8 = (bf16[144,640]{1,0:T(8,128)(2,1)S(1)}, bf16[144,640]{1,0:T(8,128)(2,1)S(1)}, u32[]{:S(2)}, u32[]{:S(2)}) collective-permute-start(bf16[144,640]{1,0:T(8,128)(2,1)S(1)} %get-tuple-element.29.own), channel_id=1, source_target_pairs={{0,12},{4,0},{8,4},{12,8},{1,13},{5,1},{9,5},{13,9},{2,14},{6,2},{... | collective-permute-start | bytes 552968 | tf_op jit(solution)/shard_map/ppermute | solution.py:172
  20.0 9.6 %collective-permute-done.rest_0_ = bf16[144,640]{1,0:T(8,128)(2,1)S(1)} collective-permute-done((bf16[144,640]{1,0:T(8,128)(2,1)S(1)}, bf16[144,640]{1,0:T(8,128)(2,1)S(1)}, u32[]{:S(2)}, u32[]{:S(2)}) %collective-permute-start) | collective-permute-done | bytes 184352 | tf_op jit(solution)/shard_map/ppermute | solution.py:172
  29.6 1.8 collective-permute-start.2
  31.6 1.8 collective-permute-start.10
  37.7 3.3 %collective-permute-done.6.rest_6_ = bf16[144,640]{1,0:T(8,128)(2,1)S(1)} collective-permute-done((bf16[144,640]{1,0:T(8,128)(2,1)S(1)}, bf16[144,640]{1,0:T(8,128)(2,1)S(1)}, u32[]{:S(2)}, u32[]{:S(2)}) %collective-permute-start.6) | collective-permute-done | bytes 184352 | tf_op jit(solution)/shard_map/ppermute | solution.py:180
  41.7 3.0 %collective-permute-done.10.rest_10_ = bf16[144,640]{1,0:T(8,128)(2,1)S(1)} collective-permute-done((bf16[144,640]{1,0:T(8,128)(2,1)S(1)}, bf16[144,640]{1,0:T(8,128)(2,1)S(1)}, u32[]{:S(2)}, u32[]{:S(2)}) %collective-permute-start.10) | collective-permute-done | bytes 184352 | tf_op jit(solution)/shard_map/ppermute | solution.py:180
  49.8 8.9 %routed.1 = (bf16[512,2560]{1,0:T(8,128)(2,1)}, bf16[512,1280]{1,0:T(8,128)(2,1)S(1)}, bf16[512,1280]{1,0:T(8,128)(2,1)S(1)}) custom-call(s32[3]{0:T(128)S(1)} %pad_add_fusion.refs_0_.place, bf16[128,2560]{1,0:T(8,128)(2,1)S(1)} %get-tuple-element.28.moe_in, bf16[144,640]{1,0:T(8,128)(2,1)S(1)} %get-tuple-element.29.own, ...), custom_call_target="tpu_custom_call" | custom-call | flops 4026531840 | bytes 14680064 | tf_op jit(solution)/shard_map/routed/pallas_call | solution.py:451
  58.8 2.8 %pack.1 = (bf16[640,512]{1,0:T(8,128)(2,1)S(1)}, bf16[640,256]{1,0:T(8,128)(2,1)S(1)}, bf16[640,256]{1,0:T(8,128)(2,1)S(1)}, bf16[640,256]{1,0:T(8,128)(2,1)S(1)...) custom-call(s32[3]{0:T(128)S(1)} %pad_add_fusion.refs_0_.place, ...), custom_call_target="tpu_custom_call" | custom-call | tf_op jit(solution)/shard_map/pack/pallas_call | solution.py:421
  63.5 3.8 %collective-permute-start.16 = (bf16[640,256]{1,0:T(8,128)(2,1)S(1)}, bf16[640,256]{1,0:T(8,128)(2,1)}, u32[]{:S(2)}, u32[]{:S(2)}) collective-permute-start(bf16[640,256]{1,0:T(8,128)(2,1)S(1)} %get-tuple-element.36), channel_id=1, source_target_pairs={{0,12},{4,0},{8,4},{12,8},{1,13},{5,1},{9,5},{13,9},{2,14},{6,2},{... | collective-permute-start | bytes 983048 | tf_op jit(solution)/shard_map/ppermute | solution.py:172
  67.3 22.1 %collective-permute-done.14.rest_0_ = bf16[640,256]{1,0:T(8,128)(2,1)S(1)} collective-permute-done((bf16[640,256]{1,0:T(8,128)(2,1)S(1)}, bf16[640,256]{1,0:T(8,128)(2,1)S(1)}, u32[]{:S(2)}, u32[]{:S(2)}) %collective-permute-start.14) | collective-permute-done | bytes 327712 | tf_op jit(solution)/shard_map/ppermute | solution.py:172
  91.5 3.1 %collective-permute-start.24 = (bf16[128,640]{1,0:T(8,128)(2,1)}, bf16[128,640]{1,0:T(8,128)(2,1)}, u32[]{:S(2)}, u32[]{:S(2)}) collective-permute-start(bf16[128,640]{1,0:T(8,128)(2,1)} %get-tuple-element.42), channel_id=1, source_target_pairs={{0,4},{1,0},{2,12},{3,8},{4,5},{5,1},{6,13},{7,9},{8,6},{9,2},{10,... | collective-permute-start | bytes 491528 | tf_op jit(solution)/shard_map/ppermute | solution.py:442
  94.7 6.1 %collective-permute-start.25 = (bf16[128,640]{1,0:T(8,128)(2,1)}, bf16[128,640]{1,0:T(8,128)(2,1)}, u32[]{:S(2)}, u32[]{:S(2)}) collective-permute-start(bf16[128,640]{1,0:T(8,128)(2,1)} %get-tuple-element.43), channel_id=1, source_target_pairs={{0,8},{1,12},{2,0},{3,4},{4,9},{5,13},{6,1},{7,5},{8,10},{9,14},{1... | collective-permute-start | bytes 491528 | tf_op jit(solution)/shard_map/ppermute | solution.py:442
  100.8 1.9 collective-permute-start.18
  103.5 1.9 collective-permute-start.37
  105.5 1.7 convert_add_fusion
  107.3 3.4 %collective-permute-done.18.rest_4_ = bf16[640,256]{1,0:T(8,128)(2,1)} collective-permute-done((bf16[640,256]{1,0:T(8,128)(2,1)S(1)}, bf16[640,256]{1,0:T(8,128)(2,1)}, u32[]{:S(2)}, u32[]{:S(2)}) %collective-permute-start.18) | collective-permute-done | bytes 327712 | tf_op jit(solution)/shard_map/ppermute | solution.py:434
  110.7 8.5 %collective-permute-start.13 = (bf16[512,640]{1,0:T(8,128)(2,1)S(1)}, bf16[512,640]{1,0:T(8,128)(2,1)S(1)}, u32[]{:S(2)}, u32[]{:S(2)}) collective-permute-start(bf16[512,640]{1,0:T(8,128)(2,1)S(1)} %slice.12), channel_id=1, source_target_pairs={{0,2},{2,0},{1,3},{3,1},{4,6},{6,4},{5,7},{7,5},{8,10},{10,8},{9,1... | collective-permute-start | bytes 1966088 | tf_op jit(solution)/shard_map/ppermute | solution.py:462
  119.2 3.0 %gate_up.1.rest_0_ = bf16[512,256]{1,0:T(8,128)(2,1)S(1)} custom-call(s32[3]{0:T(128)S(1)} %pad_add_fusion.refs_0_.place, bf16[512,2560]{1,0:T(8,128)(2,1)S(1)} %copy-done.1, bf16[640,512]{1,0:T(8,128)(2,1)S(1)} %get-tuple-element.33.own, bf16[640,256]{1,0:T(8,128)(2,1)S(1)} %collective-permute-done.14.rest_0_, ...), custom_call_target="tpu_custom_call" | custom-call | flops 1342177280 | bytes 6291456 | tf_op jit(solution)/shard_map/gate_up/pallas_call | solution.py:464
  122.3 7.1 %collective-permute-start.21 = (bf16[512,256]{1,0:T(8,128)(2,1)S(1)}, bf16[512,256]{1,0:T(8,128)(2,1)S(1)}, u32[]{:S(2)}, u32[]{:S(2)}) collective-permute-start(bf16[512,256]{1,0:T(8,128)(2,1)S(1)} %gate_up.1.rest_0_), channel_id=1, source_target_pairs={{0,2},{2,0},{1,3},{3,1},{4,6},{6,4},{5,7},{7,5},{8,10},{10,8},{9,1... | collective-permute-start | bytes 786440 | tf_op jit(solution)/shard_map/ppermute | solution.py:180
  131.4 18.0 %collective-permute-done.27.rest_8_ = bf16[128,640]{1,0:T(8,128)(2,1)S(1)} collective-permute-done((bf16[128,640]{1,0:T(8,128)(2,1)S(1)}, bf16[128,640]{1,0:T(8,128)(2,1)S(1)}, u32[]{:S(2)}, u32[]{:S(2)}) %collective-permute-start.27) | collective-permute-done | bytes 163872 | tf_op jit(solution)/shard_map/ppermute | solution.py:444
  149.4 2.5 %collective-permute-start.29 = (bf16[128,640]{1,0:T(8,128)(2,1)}, bf16[128,640]{1,0:T(8,128)(2,1)S(1)}, u32[]{:S(2)}, u32[]{:S(2)}) collective-permute-start(bf16[128,640]{1,0:T(8,128)(2,1)} %collective-permute-done.25.rest_6_), channel_id=1, source_target_pairs={{0,16},{16,0},{1,17},{17,1},{2,18},{18,2},{3,19},{19,3},{4,20},{20... | collective-permute-start | bytes 491528 | tf_op jit(solution)/shard_map/ppermute | solution.py:444
  153.5 3.1 %collective-permute-done.29.rest_10_ = bf16[128,640]{1,0:T(8,128)(2,1)S(1)} collective-permute-done((bf16[128,640]{1,0:T(8,128)(2,1)}, bf16[128,640]{1,0:T(8,128)(2,1)S(1)}, u32[]{:S(2)}, u32[]{:S(2)}) %collective-permute-start.29) | collective-permute-done | bytes 163872 | tf_op jit(solution)/shard_map/ppermute | solution.py:444
  156.6 1.9 collective-permute-start.30
  158.6 4.4 %collective-permute-done.30.rest_11_ = bf16[128,640]{1,0:T(8,128)(2,1)S(1)} collective-permute-done((bf16[128,640]{1,0:T(8,128)(2,1)S(1)}, bf16[128,640]{1,0:T(8,128)(2,1)S(1)}, u32[]{:S(2)}, u32[]{:S(2)}) %collective-permute-start.30) | collective-permute-done | bytes 163872 | tf_op jit(solution)/shard_map/ppermute | solution.py:444
  163.0 2.2 %down.3 = (f32[128,640]{1,0:T(8,128)S(1)}, bf16[128,640]{1,0:T(8,128)(2,1)S(1)}, bf16[128,640]{1,0:T(8,128)(2,1)S(1)}, bf16[128,640]{1,0:T(8,128)(2,1)S(1)}) custom-call(s32[3]{0:T(128)S(1)} %pad_add_fusion.refs_0_.place, f32[512,640]{1,0:T(8,128)S(1)} %slice.9.keep, bf16[512,640]{1,0:T(8,128)(2,1)S(1)} %collective-permute-done.13.crossed, ...), custom_call_target="tpu_custom_call" | custom-call | flops 671088640 | bytes 5242880 | tf_op jit(solution)/shard_map/down/pallas_call | solution.py:473
  165.3 5.7 %collective-permute-start.31 = (bf16[128,640]{1,0:T(8,128)(2,1)S(1)}, bf16[128,640]{1,0:T(8,128)(2,1)S(1)}, u32[]{:S(2)}, u32[]{:S(2)}) collective-permute-start(bf16[128,640]{1,0:T(8,128)(2,1)S(1)} %get-tuple-element.46), channel_id=1, source_target_pairs={{0,8},{4,12},{8,0},{12,4},{1,9},{5,13},{9,1},{13,5},{2,10},{6,14},... | collective-permute-start | bytes 491528 | tf_op jit(solution)/shard_map/ppermute | solution.py:172
  171.0 2.0 collective-permute-start.33
  173.1 6.6 %collective-permute-done.31.a = bf16[128,640]{1,0:T(8,128)(2,1)S(1)} collective-permute-done((bf16[128,640]{1,0:T(8,128)(2,1)S(1)}, bf16[128,640]{1,0:T(8,128)(2,1)S(1)}, u32[]{:S(2)}, u32[]{:S(2)}) %collective-permute-start.31) | collective-permute-done | bytes 163872 | tf_op jit(solution)/shard_map/ppermute | solution.py:172
  179.7 2.1 %collective-permute-done.32.b = bf16[128,640]{1,0:T(8,128)(2,1)S(1)} collective-permute-done((bf16[128,640]{1,0:T(8,128)(2,1)S(1)}, bf16[128,640]{1,0:T(8,128)(2,1)S(1)}, u32[]{:S(2)}, u32[]{:S(2)}) %collective-permute-start.32) | collective-permute-done | bytes 163872 | tf_op jit(solution)/shard_map/ppermute | solution.py:172
  183.1 5.7 %collective-permute-done.35.c = bf16[128,640]{1,0:T(8,128)(2,1)S(1)} collective-permute-done((bf16[128,640]{1,0:T(8,128)(2,1)}, bf16[128,640]{1,0:T(8,128)(2,1)S(1)}, u32[]{:S(2)}, u32[]{:S(2)}) %collective-permute-start.35) | collective-permute-done | bytes 163872 | tf_op jit(solution)/shard_map/ppermute | solution.py:180
  194.4 3.2 %collective-permute-done.39.c = bf16[64,512]{1,0:T(8,128)(2,1)S(1)} collective-permute-done((bf16[64,512]{1,0:T(8,128)(2,1)S(1)}, bf16[64,512]{1,0:T(8,128)(2,1)S(1)}, u32[]{:S(2)}, u32[]{:S(2)}) %collective-permute-start.39) | collective-permute-done | bytes 65568 | tf_op jit(solution)/shard_map/ppermute | solution.py:508
  (119 shorter events, 34.2 us)
Async XLA Ops:
  7.2 96.3 %all-gather.2.cloned.1.call-start = ((), (), s32[]{:S(2)}) async-start(), calls=%async_computation | async-start | bytes 1638400 | tf_op jit(solution)/shard_map/all_gather | solution.py:448
  12.1 17.5 %collective-permute-start = (bf16[144,640]{1,0:T(8,128)(2,1)S(1)}, bf16[144,640]{1,0:T(8,128)(2,1)S(1)}, u32[]{:S(2)}, u32[]{:S(2)}) collective-permute-start(bf16[144,640]{1,0:T(8,128)(2,1)S(1)} %get-tuple-element.29.own), channel_id=1, source_target_pairs={{0,8},{4,12},{8,0},{12,4},{1,9},{5,13},{9,1},{13,5},{2,10},{6,14},... | collective-permute-start | bytes 552968 | tf_op jit(solution)/shard_map/ppermute | solution.py:172
  16.2 15.3 %collective-permute-start.4 = (bf16[144,640]{1,0:T(8,128)(2,1)S(1)}, bf16[144,640]{1,0:T(8,128)(2,1)S(1)}, u32[]{:S(2)}, u32[]{:S(2)}) collective-permute-start(bf16[144,640]{1,0:T(8,128)(2,1)S(1)} %get-tuple-element.29.own), channel_id=1, source_target_pairs={{0,4},{4,8},{8,12},{12,0},{1,5},{5,9},{9,13},{13,1},{2,6},{6,10},{... | collective-permute-start | bytes 552968 | tf_op jit(solution)/shard_map/ppermute | solution.py:172
  17.8 13.9 %collective-permute-start.8 = (bf16[144,640]{1,0:T(8,128)(2,1)S(1)}, bf16[144,640]{1,0:T(8,128)(2,1)S(1)}, u32[]{:S(2)}, u32[]{:S(2)}) collective-permute-start(bf16[144,640]{1,0:T(8,128)(2,1)S(1)} %get-tuple-element.29.own), channel_id=1, source_target_pairs={{0,12},{4,0},{8,4},{12,8},{1,13},{5,1},{9,5},{13,9},{2,14},{6,2},{... | collective-permute-start | bytes 552968 | tf_op jit(solution)/shard_map/ppermute | solution.py:172
  29.6 7.4 %collective-permute-start.2 = (bf16[144,640]{1,0:T(8,128)(2,1)S(1)}, bf16[144,640]{1,0:T(8,128)(2,1)S(1)}, u32[]{:S(2)}, u32[]{:S(2)}) collective-permute-start(bf16[144,640]{1,0:T(8,128)(2,1)S(1)} %collective-permute-done.rest_0_), channel_id=1, source_target_pairs={{0,2},{2,0},{1,3},{3,1},{4,6},{6,4},{5,7},{7,5},{8,10},{10,8},{9,1... | collective-permute-start | bytes 552968 | tf_op jit(solution)/shard_map/ppermute | solution.py:180
  31.4 9.5 %collective-permute-start.6 = (bf16[144,640]{1,0:T(8,128)(2,1)S(1)}, bf16[144,640]{1,0:T(8,128)(2,1)S(1)}, u32[]{:S(2)}, u32[]{:S(2)}) collective-permute-start(bf16[144,640]{1,0:T(8,128)(2,1)S(1)} %collective-permute-done.4.rest_4_), channel_id=1, source_target_pairs={{0,2},{2,0},{1,3},{3,1},{4,6},{6,4},{5,7},{7,5},{8,10},{10,8},{9,1... | collective-permute-start | bytes 552968 | tf_op jit(solution)/shard_map/ppermute | solution.py:180
  31.6 13.0 %collective-permute-start.10 = (bf16[144,640]{1,0:T(8,128)(2,1)S(1)}, bf16[144,640]{1,0:T(8,128)(2,1)S(1)}, u32[]{:S(2)}, u32[]{:S(2)}) collective-permute-start(bf16[144,640]{1,0:T(8,128)(2,1)S(1)} %collective-permute-done.8.rest_8_), channel_id=1, source_target_pairs={{0,2},{2,0},{1,3},{3,1},{4,6},{6,4},{5,7},{7,5},{8,10},{10,8},{9,1... | collective-permute-start | bytes 552968 | tf_op jit(solution)/shard_map/ppermute | solution.py:180
  34.2 11.1 %collective-permute-start.5 = (bf16[144,640]{1,0:T(8,128)(2,1)S(1)}, bf16[144,640]{1,0:T(8,128)(2,1)S(1)}, u32[]{:S(2)}, u32[]{:S(2)}) collective-permute-start(bf16[144,640]{1,0:T(8,128)(2,1)S(1)} %collective-permute-done.4.rest_4_), channel_id=1, source_target_pairs={{0,1},{1,0},{2,3},{3,2},{4,5},{5,4},{6,7},{7,6},{8,9},{9,8},{10,11... | collective-permute-start | bytes 552968 | tf_op jit(solution)/shard_map/ppermute | solution.py:181
  35.0 10.3 %collective-permute-start.9 = (bf16[144,640]{1,0:T(8,128)(2,1)S(1)}, bf16[144,640]{1,0:T(8,128)(2,1)S(1)}, u32[]{:S(2)}, u32[]{:S(2)}) collective-permute-start(bf16[144,640]{1,0:T(8,128)(2,1)S(1)} %collective-permute-done.8.rest_8_), channel_id=1, source_target_pairs={{0,1},{1,0},{2,3},{3,2},{4,5},{5,4},{6,7},{7,6},{8,9},{9,8},{10,11... | collective-permute-start | bytes 552968 | tf_op jit(solution)/shard_map/ppermute | solution.py:181
  37.0 8.3 %collective-permute-start.3 = (bf16[144,640]{1,0:T(8,128)(2,1)S(1)}, bf16[144,640]{1,0:T(8,128)(2,1)S(1)}, u32[]{:S(2)}, u32[]{:S(2)}) collective-permute-start(bf16[144,640]{1,0:T(8,128)(2,1)S(1)} %collective-permute-done.2.rest_2_), channel_id=1, source_target_pairs={{0,1},{1,0},{2,3},{3,2},{4,5},{5,4},{6,7},{7,6},{8,9},{9,8},{10,11... | collective-permute-start | bytes 552968 | tf_op jit(solution)/shard_map/ppermute | solution.py:182
  58.7 44.8 %collective-permute-start.12 = (bf16[512,1280]{1,0:T(8,128)(2,1)S(1)}, bf16[512,1280]{1,0:T(8,128)(2,1)}, u32[]{:S(2)}, u32[]{:S(2)}) collective-permute-start(bf16[512,1280]{1,0:T(8,128)(2,1)S(1)} %get-tuple-element.31), channel_id=1, source_target_pairs={{0,1},{1,0},{2,3},{3,2},{4,5},{5,4},{6,7},{7,6},{8,9},{9,8},{10,11... | collective-permute-start | bytes 3932168 | tf_op jit(solution)/shard_map/ppermute | solution.py:460
  62.3 27.1 %collective-permute-start.14 = (bf16[640,256]{1,0:T(8,128)(2,1)S(1)}, bf16[640,256]{1,0:T(8,128)(2,1)S(1)}, u32[]{:S(2)}, u32[]{:S(2)}) collective-permute-start(bf16[640,256]{1,0:T(8,128)(2,1)S(1)} %get-tuple-element.34), channel_id=1, source_target_pairs={{0,8},{4,12},{8,0},{12,4},{1,9},{5,13},{9,1},{13,5},{2,10},{6,14},... | collective-permute-start | bytes 983048 | tf_op jit(solution)/shard_map/ppermute | solution.py:172
  63.5 28.1 %collective-permute-start.15 = (bf16[640,256]{1,0:T(8,128)(2,1)S(1)}, bf16[640,256]{1,0:T(8,128)(2,1)S(1)}, u32[]{:S(2)}, u32[]{:S(2)}) collective-permute-start(bf16[640,256]{1,0:T(8,128)(2,1)S(1)} %get-tuple-element.35), channel_id=1, source_target_pairs={{0,4},{4,8},{8,12},{12,0},{1,5},{5,9},{9,13},{13,1},{2,6},{6,10},{... | collective-permute-start | bytes 983048 | tf_op jit(solution)/shard_map/ppermute | solution.py:172
  63.5 31.2 %collective-permute-start.16 = (bf16[640,256]{1,0:T(8,128)(2,1)S(1)}, bf16[640,256]{1,0:T(8,128)(2,1)}, u32[]{:S(2)}, u32[]{:S(2)}) collective-permute-start(bf16[640,256]{1,0:T(8,128)(2,1)S(1)} %get-tuple-element.36), channel_id=1, source_target_pairs={{0,12},{4,0},{8,4},{12,8},{1,13},{5,1},{9,5},{13,9},{2,14},{6,2},{... | collective-permute-start | bytes 983048 | tf_op jit(solution)/shard_map/ppermute | solution.py:172
  89.4 13.3 %collective-permute-start.17 = (bf16[640,256]{1,0:T(8,128)(2,1)S(1)}, bf16[640,256]{1,0:T(8,128)(2,1)S(1)}, u32[]{:S(2)}, u32[]{:S(2)}) collective-permute-start(bf16[640,256]{1,0:T(8,128)(2,1)S(1)} %collective-permute-done.14.rest_0_), channel_id=1, source_target_pairs={{0,16},{16,0},{1,17},{17,1},{2,18},{18,2},{3,19},{19,3},{4,20},{20... | collective-permute-start | bytes 983048 | tf_op jit(solution)/shard_map/ppermute | solution.py:434
  90.9 9.9 %collective-permute-start.23 = (bf16[128,640]{1,0:T(8,128)(2,1)S(1)}, bf16[128,640]{1,0:T(8,128)(2,1)S(1)}, u32[]{:S(2)}, u32[]{:S(2)}) collective-permute-start(bf16[128,640]{1,0:T(8,128)(2,1)S(1)} %get-tuple-element.41), channel_id=1, source_target_pairs={{0,0},{1,4},{2,8},{3,12},{4,1},{5,5},{6,9},{7,13},{8,2},{9,6},{10,... | collective-permute-start | bytes 491528 | tf_op jit(solution)/shard_map/ppermute | solution.py:442
  91.5 30.7 %collective-permute-start.24 = (bf16[128,640]{1,0:T(8,128)(2,1)}, bf16[128,640]{1,0:T(8,128)(2,1)}, u32[]{:S(2)}, u32[]{:S(2)}) collective-permute-start(bf16[128,640]{1,0:T(8,128)(2,1)} %get-tuple-element.42), channel_id=1, source_target_pairs={{0,4},{1,0},{2,12},{3,8},{4,5},{5,1},{6,13},{7,9},{8,6},{9,2},{10,... | collective-permute-start | bytes 491528 | tf_op jit(solution)/shard_map/ppermute | solution.py:442
  94.7 34.7 %collective-permute-start.25 = (bf16[128,640]{1,0:T(8,128)(2,1)}, bf16[128,640]{1,0:T(8,128)(2,1)}, u32[]{:S(2)}, u32[]{:S(2)}) collective-permute-start(bf16[128,640]{1,0:T(8,128)(2,1)} %get-tuple-element.43), channel_id=1, source_target_pairs={{0,8},{1,12},{2,0},{3,4},{4,9},{5,13},{6,1},{7,5},{8,10},{9,14},{1... | collective-permute-start | bytes 491528 | tf_op jit(solution)/shard_map/ppermute | solution.py:442
  100.8 10.0 %collective-permute-start.18 = (bf16[640,256]{1,0:T(8,128)(2,1)S(1)}, bf16[640,256]{1,0:T(8,128)(2,1)}, u32[]{:S(2)}, u32[]{:S(2)}) collective-permute-start(bf16[640,256]{1,0:T(8,128)(2,1)S(1)} %collective-permute-done.15.rest_1_), channel_id=1, source_target_pairs={{0,16},{16,0},{1,17},{17,1},{2,18},{18,2},{3,19},{19,3},{4,20},{20... | collective-permute-start | bytes 983048 | tf_op jit(solution)/shard_map/ppermute | solution.py:434
  103.4 15.8 %collective-permute-start.19 = (bf16[640,256]{1,0:T(8,128)(2,1)}, bf16[640,256]{1,0:T(8,128)(2,1)}, u32[]{:S(2)}, u32[]{:S(2)}) collective-permute-start(bf16[640,256]{1,0:T(8,128)(2,1)} %collective-permute-done.16.rest_2_), channel_id=1, source_target_pairs={{0,16},{16,0},{1,17},{17,1},{2,18},{18,2},{3,19},{19,3},{4,20},{20... | collective-permute-start | bytes 983048 | tf_op jit(solution)/shard_map/ppermute | solution.py:434
  103.5 86.7 %collective-permute-start.37 = (bf16[2560,256]{1,0:T(8,128)(2,1)}, bf16[2560,256]{1,0:T(8,128)(2,1)S(1)}, u32[]{:S(2)}, u32[]{:S(2)}) collective-permute-start(bf16[2560,256]{1,0:T(8,128)(2,1)} %all-gather.2.cloned.1.call-done.mine), channel_id=1, source_target_pairs={{0,16},{16,0},{1,17},{17,1},{2,18},{18,2},{3,19},{19,3},{4,20},{20... | collective-permute-start | bytes 3932168 | tf_op jit(solution)/shard_map/ppermute | solution.py:449
  110.7 52.3 %collective-permute-start.13 = (bf16[512,640]{1,0:T(8,128)(2,1)S(1)}, bf16[512,640]{1,0:T(8,128)(2,1)S(1)}, u32[]{:S(2)}, u32[]{:S(2)}) collective-permute-start(bf16[512,640]{1,0:T(8,128)(2,1)S(1)} %slice.12), channel_id=1, source_target_pairs={{0,2},{2,0},{1,3},{3,1},{4,6},{6,4},{5,7},{7,5},{8,10},{10,8},{9,1... | collective-permute-start | bytes 1966088 | tf_op jit(solution)/shard_map/ppermute | solution.py:462
  119.2 11.6 %collective-permute-start.26 = (bf16[128,640]{1,0:T(8,128)(2,1)S(1)}, bf16[128,640]{1,0:T(8,128)(2,1)S(1)}, u32[]{:S(2)}, u32[]{:S(2)}) collective-permute-start(bf16[128,640]{1,0:T(8,128)(2,1)S(1)} %copy-done.23), channel_id=1, source_target_pairs={{0,12},{1,8},{2,4},{3,0},{4,13},{5,9},{6,5},{7,1},{8,14},{9,10},{1... | collective-permute-start | bytes 491528 | tf_op jit(solution)/shard_map/ppermute | solution.py:442
  122.3 31.1 %collective-permute-start.21 = (bf16[512,256]{1,0:T(8,128)(2,1)S(1)}, bf16[512,256]{1,0:T(8,128)(2,1)S(1)}, u32[]{:S(2)}, u32[]{:S(2)}) collective-permute-start(bf16[512,256]{1,0:T(8,128)(2,1)S(1)} %gate_up.1.rest_0_), channel_id=1, source_target_pairs={{0,2},{2,0},{1,3},{3,1},{4,6},{6,4},{5,7},{7,5},{8,10},{10,8},{9,1... | collective-permute-start | bytes 786440 | tf_op jit(solution)/shard_map/ppermute | solution.py:180
  129.3 20.0 %collective-permute-start.27 = (bf16[128,640]{1,0:T(8,128)(2,1)S(1)}, bf16[128,640]{1,0:T(8,128)(2,1)S(1)}, u32[]{:S(2)}, u32[]{:S(2)}) collective-permute-start(bf16[128,640]{1,0:T(8,128)(2,1)S(1)} %collective-permute-done.23.rest_4_), channel_id=1, source_target_pairs={{0,16},{16,0},{1,17},{17,1},{2,18},{18,2},{3,19},{19,3},{4,20},{20... | collective-permute-start | bytes 491528 | tf_op jit(solution)/shard_map/ppermute | solution.py:444
  130.8 22.2 %collective-permute-start.28 = (bf16[128,640]{1,0:T(8,128)(2,1)}, bf16[128,640]{1,0:T(8,128)(2,1)S(1)}, u32[]{:S(2)}, u32[]{:S(2)}) collective-permute-start(bf16[128,640]{1,0:T(8,128)(2,1)} %collective-permute-done.24.rest_5_), channel_id=1, source_target_pairs={{0,16},{16,0},{1,17},{17,1},{2,18},{18,2},{3,19},{19,3},{4,20},{20... | collective-permute-start | bytes 491528 | tf_op jit(solution)/shard_map/ppermute | solution.py:444
  149.4 7.2 %collective-permute-start.29 = (bf16[128,640]{1,0:T(8,128)(2,1)}, bf16[128,640]{1,0:T(8,128)(2,1)S(1)}, u32[]{:S(2)}, u32[]{:S(2)}) collective-permute-start(bf16[128,640]{1,0:T(8,128)(2,1)} %collective-permute-done.25.rest_6_), channel_id=1, source_target_pairs={{0,16},{16,0},{1,17},{17,1},{2,18},{18,2},{3,19},{19,3},{4,20},{20... | collective-permute-start | bytes 491528 | tf_op jit(solution)/shard_map/ppermute | solution.py:444
  153.0 10.1 %collective-permute-start.20 = (bf16[512,256]{1,0:T(8,128)(2,1)S(1)}, bf16[512,256]{1,0:T(8,128)(2,1)S(1)}, u32[]{:S(2)}, u32[]{:S(2)}) collective-permute-start(bf16[512,256]{1,0:T(8,128)(2,1)S(1)} %gate_up.1.rest_0_), channel_id=1, source_target_pairs={{0,1},{1,0},{2,3},{3,2},{4,5},{5,4},{6,7},{7,6},{8,9},{9,8},{10,11... | collective-permute-start | bytes 786440 | tf_op jit(solution)/shard_map/ppermute | solution.py:181
  153.3 9.7 %collective-permute-start.22 = (bf16[512,256]{1,0:T(8,128)(2,1)S(1)}, bf16[512,256]{1,0:T(8,128)(2,1)S(1)}, u32[]{:S(2)}, u32[]{:S(2)}) collective-permute-start(bf16[512,256]{1,0:T(8,128)(2,1)S(1)} %collective-permute-done.21.rest_2_), channel_id=1, source_target_pairs={{0,1},{1,0},{2,3},{3,2},{4,5},{5,4},{6,7},{7,6},{8,9},{9,8},{10,11... | collective-permute-start | bytes 786440 | tf_op jit(solution)/shard_map/ppermute | solution.py:182
  165.3 14.4 %collective-permute-start.31 = (bf16[128,640]{1,0:T(8,128)(2,1)S(1)}, bf16[128,640]{1,0:T(8,128)(2,1)S(1)}, u32[]{:S(2)}, u32[]{:S(2)}) collective-permute-start(bf16[128,640]{1,0:T(8,128)(2,1)S(1)} %get-tuple-element.46), channel_id=1, source_target_pairs={{0,8},{4,12},{8,0},{12,4},{1,9},{5,13},{9,1},{13,5},{2,10},{6,14},... | collective-permute-start | bytes 491528 | tf_op jit(solution)/shard_map/ppermute | solution.py:172
  171.0 10.7 %collective-permute-start.32 = (bf16[128,640]{1,0:T(8,128)(2,1)S(1)}, bf16[128,640]{1,0:T(8,128)(2,1)S(1)}, u32[]{:S(2)}, u32[]{:S(2)}) collective-permute-start(bf16[128,640]{1,0:T(8,128)(2,1)S(1)} %get-tuple-element.47), channel_id=1, source_target_pairs={{0,12},{4,0},{8,4},{12,8},{1,13},{5,1},{9,5},{13,9},{2,14},{6,2},{... | collective-permute-start | bytes 491528 | tf_op jit(solution)/shard_map/ppermute | solution.py:172
  171.0 10.7 %collective-permute-start.33 = (bf16[128,640]{1,0:T(8,128)(2,1)S(1)}, bf16[128,640]{1,0:T(8,128)(2,1)S(1)}, u32[]{:S(2)}, u32[]{:S(2)}) collective-permute-start(bf16[128,640]{1,0:T(8,128)(2,1)S(1)} %get-tuple-element.48), channel_id=1, source_target_pairs={{0,4},{4,8},{8,12},{12,0},{1,5},{5,9},{9,13},{13,1},{2,6},{6,10},{... | collective-permute-start | bytes 491528 | tf_op jit(solution)/shard_map/ppermute | solution.py:172
  (35 other events, 256.4 us)
Sparse Core Ops, SparseCore 0:
  34.4 49.6 all-gather.1

commit v3 on v2

--- a/solution.py
+++ b/solution.py
@@ -154,14 +154,14 @@
 META = 16
 
 
-def call(body, outs, in_specs, scratch=(), flops=0, moved=0, name=None):
+def call(body, outs, in_specs, scratch=(), flops=0, moved=0, name=None, vmem=8):
     return pl.pallas_call(
         body,
         out_shape=[jax.ShapeDtypeStruct(shape, kind) for shape, kind in outs],
         in_specs=in_specs,
         out_specs=[VMEM] * len(outs),
         scratch_shapes=list(scratch),
-        compiler_params=pltpu.CompilerParams(vmem_limit_bytes=48 << 20),
+        compiler_params=pltpu.CompilerParams(vmem_limit_bytes=vmem << 20),
         cost_estimate=pl.CostEstimate(flops=flops, bytes_accessed=moved, transcendentals=0),
         name=name,
     )
@@ -191,33 +191,12 @@
     return jnp.dot(a, b, preferred_element_type=F32)
 
 
-def norm_kernel(capacity, place, resid, gain, score, ids_row, ids_column, moe_in, message):
-    rows, width = resid.shape
-    piece = message.shape[1]
-    values = resid[...].astype(F32)
-    power = jnp.mean(values * values, axis=-1, keepdims=True)
-    moe_in[...] = (values * lax.rsqrt(power + 1e-05) * gain[...]).astype(BF16)
-    message[:rows, :] = moe_in[:, lanes(place[1], piece)]
-    earlier = lax.broadcasted_iota(jnp.int32, (rows, rows), 0) < lax.broadcasted_iota(
-        jnp.int32, (rows, rows), 1
-    )
-    same = (ids_column[...] == ids_row[...]) & earlier
-    slots = jnp.sum(same.astype(F32), axis=0, keepdims=True)
-    scale = jnp.where(slots < capacity, score[...], 0.0)
-    high = scale.astype(BF16)
-    rest = scale - high.astype(F32)
-    middle = rest.astype(BF16)
-    low = (rest - middle.astype(F32)).astype(BF16)
-    message[rows:, :] = jnp.zeros((META, piece), BF16)
-    for i, part in enumerate((high, middle, low, ids_row[...].astype(F32).astype(BF16))):
-        message[rows:, i * rows : (i + 1) * rows] = jnp.broadcast_to(part, (META, rows))
-
-
-def pack_kernel(place, gate, up, down, own, *rest):
-    messages, downs, sem = rest[:3], rest[3:7], rest[7]
+def first_kernel(
+    capacity, place, resid, gain, score, ids, gate, up, down, kv, moe_in, message, share, own, *rest
+):
+    messages, downs, kv_half, sem = rest[:3], rest[3:7], rest[7], rest[8]
     zone, slot, group = place[0], place[1], place[2]
     count = 4
-    near = gate.shape[0]
     hidden = gate.shape[1] // count
     half = hidden // 2
     copies = []
@@ -235,6 +214,8 @@
     for k in range(count):
         start = (slot ^ k) * hidden + group * half
         move(down.at[pl.ds(pl.multiple_of(start, 128), half), :], downs[k])
+    start = group * kv_half.shape[1]
+    move(kv.at[:, pl.ds(pl.multiple_of(start, 128), kv_half.shape[1])], kv_half)
     for part in range(2):
         start = zone * hidden + (group ^ part) * half
         for j, weights in enumerate((gate, up)):
@@ -244,16 +225,42 @@
             )
     for copy in copies:
         copy.start()
+
+    rows, width = resid.shape
+    piece = message.shape[1]
+    values = resid[...].astype(F32)
+    power = jnp.mean(values * values, axis=-1, keepdims=True)
+    moe_in[...] = (values * lax.rsqrt(power + 1e-05) * gain[...]).astype(BF16)
+    message[:rows, :] = moe_in[:, lanes(slot, piece)]
+    share[...] = resid[:, lanes(slot, piece)]
+    first = lax.broadcasted_iota(jnp.int32, (rows, rows), 0)
+    second = lax.broadcasted_iota(jnp.int32, (rows, rows), 1)
+    across = jnp.broadcast_to(ids[...].astype(F32), (rows, rows))
+    along = jnp.sum(jnp.where(first == second, across, 0.0), axis=1, keepdims=True)
+    same = (along == across) & (first < second)
+    slots = jnp.sum(jnp.where(same, 1.0, 0.0), axis=0, keepdims=True)
+    scale = jnp.where(slots < capacity, score[...], 0.0)
+    high = scale.astype(BF16)
+    rest = scale - high.astype(F32)
+    middle = rest.astype(BF16)
+    low = (rest - middle.astype(F32)).astype(BF16)
+    message[rows:, :] = jnp.zeros((META, piece), BF16)
+    for i, part in enumerate((high, middle, low, ids[...].astype(F32).astype(BF16))):
+        message[rows:, i * rows : (i + 1) * rows] = jnp.broadcast_to(part, (META, rows))
     for copy in copies:
         copy.wait()
 
 
-def routed_kernel(place, moe_in, own, *rest):
+def silu(values):
+    return values / (1.0 + jnp.exp(-values))
+
+
+def routed_up_kernel(place, moe_in, *rest):
     pieces = rest[:12]
-    gate, up, down, tokens, send, keep, hidden = rest[12:]
-    zone, slot = place[0], place[1]
+    gate, up, tokens, hidden = rest[12:]
+    slot = place[1]
     rows = moe_in.shape[0]
-    piece = own.shape[1]
+    piece = pieces[0].shape[1]
     tokens[:rows, :] = moe_in[...]
     for i, shift in enumerate(SHIFTS):
         for j in range(4):
@@ -266,42 +273,51 @@
         cols = slice(n * step, (n + 1) * step)
         gate_val = dot(tokens[...], gate[0, :, cols])
         up_val = dot(tokens[...], up[0, :, cols])
-        hidden[:, cols] = (gate_val / (1.0 + jnp.exp(-gate_val)) * up_val).astype(BF16)
+        hidden[:, cols] = (silu(gate_val) * up_val).astype(BF16)
+
+
+def routed_down_kernel(place, hidden, *rest):
+    messages, down, send, keep = rest[:4], rest[4], rest[5], rest[6]
+    zone, slot = place[0], place[1]
+    rows = messages[0].shape[0] - META
+    piece = messages[0].shape[1]
     diagonal = lax.broadcasted_iota(jnp.int32, (rows, rows), 0) == lax.broadcasted_iota(
         jnp.int32, (rows, rows), 1
     )
     mine = (zone // 2).astype(F32)
     scales = []
-    for shift in range(4):
-        source = own if shift == 0 else pieces[4 * SHIFTS.index(shift)]
+    for source in messages:
         info = source[rows : rows + META, :].astype(F32)[:1]
         value = info[:, :rows] + info[:, rows : 2 * rows] + info[:, 2 * rows : 3 * rows]
         value = jnp.where(info[:, 3 * rows : 4 * rows] == mine, value, 0.0)
-        scales.append(
-            jnp.sum(jnp.where(diagonal, value, 0.0), axis=1, keepdims=True)
-        )
+        scales.append(jnp.sum(jnp.where(diagonal, value, 0.0), axis=1, keepdims=True))
     scale = jnp.concatenate(scales, axis=0)
-    for target, first, parts in ((send, 1, (1, 3)), (keep, 0, (0, 2))):
+    for target, parts in ((send, (1, 3)), (keep, (0, 2))):
         for i, j in enumerate(parts):
             value = dot(hidden[...], down[0, :, lanes(slot ^ j, piece)]) * scale
             target[:, i * piece : (i + 1) * piece] = value.astype(BF16)
 
 
-def gate_up_kernel(place, tokens, own, *rest):
-    got, other, hidden = rest[:3], rest[3:6], rest[6]
-    zone, group = place[0], place[2]
+def gate_up_half(place, tokens, own, pieces, part):
+    zone = place[0]
     near = own.shape[0]
     width = own.shape[1] // 2
     half = width // 2
-    for part, pieces in ((0, got), (1, other)):
-        both = dot(tokens[:, lanes(zone, near)], own[:, part * width : (part + 1) * width])
-        for i, shift in enumerate(SHIFTS):
-            source = lax.rem(zone - shift + 4, 4)
-            both = both + dot(tokens[:, lanes(source, near)], pieces[i][...])
-        gate_val, up_val = both[:, :half], both[:, half:]
-        hidden[:, lanes(group ^ part, half)] = (
-            gate_val / (1.0 + jnp.exp(-gate_val)) * up_val
-        ).astype(BF16)
+    both = dot(tokens[:, lanes(zone, near)], own[:, part * width : (part + 1) * width])
+    for i, shift in enumerate(SHIFTS):
+        source = lax.rem(zone - shift + 4, 4)
+        both = both + dot(tokens[:, lanes(source, near)], pieces[i][...])
+    return (silu(both[:, :half]) * both[:, half:]).astype(BF16)
+
+
+def gate_up_first_kernel(place, tokens, own, a, b, c, hidden):
+    hidden[...] = gate_up_half(place, tokens, own, (a, b, c), 0)
+
+
+def gate_up_second_kernel(place, tokens, own, first, a, b, c, hidden):
+    half = first.shape[1]
+    hidden[:, lanes(place[2], half)] = first[...]
+    hidden[:, lanes(1 - place[2], half)] = gate_up_half(place, tokens, own, (a, b, c), 1)
 
 
 def down_kernel(place, keep, crossed, *rest):
@@ -327,25 +343,30 @@
             sends[SHIFTS.index(block)][...] = value.astype(BF16)
 
 
-def layer_kernel(place, resid, own, a, b, c, out):
-    piece = own.shape[1]
+def layer_kernel(resid, own, a, b, c, out):
     value = own[...] + a[...].astype(F32) + b[...].astype(F32) + c[...].astype(F32)
-    value = value + resid[:, lanes(place[1], piece)].astype(F32)
+    value = value + resid[...].astype(F32)
     out[...] = value.astype(BF16)
 
 
-def kv_kernel(place, owner, blocks, gain, a, b, c, d, mine, theirs, *rest):
-    outs, full, key_value = rest[:4], rest[4], rest[5]
-    slot, group = place[1], place[2]
+def kv_kernel(place, owner, blocks, gain, a, b, c, d, own, *rest):
+    got, other, outs = rest[:3], rest[3:6], rest[6:10]
+    full, key_value, ready = rest[10:]
+    zone, slot, group = place[0], place[1], place[2]
     piece = a.shape[1]
     for j, part in enumerate((a, b, c, d)):
         full[:, lanes(slot ^ j, piece)] = part[...].astype(F32)
     values = full[...]
     power = jnp.mean(values * values, axis=-1, keepdims=True)
-    attn_in = (values * lax.rsqrt(power + 1e-05) * gain[...]).astype(BF16)
-    half = mine.shape[1]
-    for part, weights in ((0, mine), (1, theirs)):
-        key_value[:, lanes(group ^ part, half)] = dot(attn_in, weights[...]).astype(BF16)
+    ready[...] = (values * lax.rsqrt(power + 1e-05) * gain[...]).astype(BF16)
+    near = own.shape[0]
+    half = own.shape[1] // 2
+    for part, pieces in ((0, got), (1, other)):
+        value = dot(ready[:, lanes(zone, near)], own[:, lanes(group ^ part, half)])
+        for i, shift in enumerate(SHIFTS):
+            source = lax.rem(zone - shift + 4, 4)
+            value = value + dot(ready[:, lanes(source, near)], pieces[i][...])
+        key_value[:, lanes(group ^ part, half)] = value.astype(BF16)
     held = full.shape[0] // BLOCK
     width = key_value.shape[1]
     for j in range(4):
@@ -405,27 +426,35 @@
         [lax.axis_index("expert"), lax.axis_index("decode"), group]
     ).astype(jnp.int32)
 
-    moe_in, message = call(
-        lambda *refs: norm_kernel(capacity, *refs),
-        [((rows, width), BF16), ((rows + META, piece), BF16)],
-        [SMEM] + [VMEM] * 5,
-        name="norm",
+    first = call(
+        lambda *refs: first_kernel(capacity, *refs),
+        [
+            ((rows, width), BF16),
+            ((rows + META, piece), BF16),
+            ((rows, piece), BF16),
+            ((near, 2 * hidden), BF16),
+        ]
+        + [((near, hidden), BF16)] * 3
+        + [((half, piece), BF16)] * 4
+        + [((near, kv_width // 2), BF16)],
+        [SMEM] + [VMEM] * 4 + [ANY] * 4,
+        [pltpu.SemaphoreType.DMA((15,))],
+        moved=6 << 20,
+        name="first",
+        vmem=58,
     )(
         place,
         resid,
         moe_gain.reshape(1, width),
         gate_score.reshape(1, rows),
         expert_ids.reshape(1, rows),
-        expert_ids,
-    )
-    packed = call(
-        pack_kernel,
-        [((near, 2 * hidden), BF16)] + [((near, hidden), BF16)] * 3 + [((half, piece), BF16)] * 4,
-        [SMEM] + [ANY] * 3,
-        [pltpu.SemaphoreType.DMA((14,))],
-        name="pack",
-    )(place, shared_gate, shared_up, shared_down)
-    own_weights, weight_messages, down_messages = packed[0], packed[1:4], packed[4:8]
+        shared_gate,
+        shared_up,
+        shared_down,
+        w_kv,
+    )
+    moe_in, message, resid_share, own_weights = first[:4]
+    weight_messages, down_messages, kv_half = first[4:7], first[7:11], first[11]
 
     arrived = [to_shift(message, s) for s in SHIFTS]
     pieces = [part for values in arrived for part in spread(values)]
@@ -434,7 +463,7 @@
     other = [lax.ppermute(values, "groups", SWAP_GROUP) for values in got]
 
     down_got, down_other = [], []
-    down_messages = lax.optimization_barrier(tuple(down_messages) + (got[0],))[:4]
+    down_messages = lax.optimization_barrier(tuple(down_messages) + tuple(got) + (other[0],))[:4]
     for k in range(slots):
         pairs = [
             (z * slots + d, (d ^ k) * slots + z) for z in range(zones) for d in range(slots)
@@ -443,32 +472,56 @@
         down_got.append(values)
         down_other.append(lax.ppermute(values, "groups", SWAP_GROUP))
 
-    kv_half = lax.dynamic_slice_in_dim(w_kv, group * (kv_width // 2), kv_width // 2, 1)
-    kv_half = after(kv_half, arrived[0])
-    kv_mine = lax.all_gather(kv_half, "expert", axis=0, tiled=True)
-    kv_theirs = lax.ppermute(kv_mine, "groups", SWAP_GROUP)
-
-    tokens, send, keep = call(
-        routed_kernel,
-        [((total_rows, width), BF16), ((total_rows, 2 * piece), BF16), ((total_rows, 2 * piece), BF16)],
-        [SMEM] + [VMEM] * 17,
-        [pltpu.VMEM((total_rows, routed_width), BF16)],
-        flops=6 * total_rows * width * routed_width,
-        moved=14 << 20,
-        name="routed",
-    )(place, moe_in, message, *pieces, w_gate, w_up, w_down)
+    kv_half = after(kv_half, *got)
+    kv_got = [to_shift(kv_half, s) for s in SHIFTS]
+    kv_other = [lax.ppermute(values, "groups", SWAP_GROUP) for values in kv_got]
+
+    tokens, routed_hidden = call(
+        routed_up_kernel,
+        [((total_rows, width), BF16), ((total_rows, routed_width), BF16)],
+        [SMEM] + [VMEM] * 15,
+        flops=4 * total_rows * width * routed_width,
+        moved=10 << 20,
+        name="routed_up",
+        vmem=22,
+    )(after(place, got[0]), moe_in, *pieces, w_gate, w_up)
+    send, keep = call(
+        routed_down_kernel,
+        [((total_rows, 2 * piece), BF16), ((total_rows, 2 * piece), BF16)],
+        [SMEM] + [VMEM] * 6,
+        flops=2 * total_rows * width * routed_width,
+        moved=6 << 20,
+        name="routed_down",
+        vmem=16,
+    )(
+        after(place, other[0], *got),
+        routed_hidden,
+        message,
+        *[arrived[SHIFTS.index(s)] for s in range(1, zones)],
+        w_down,
+    )
     beside = lax.ppermute(send, "decode", SWAP_CORE)
     keep_sum = keep.astype(F32) + beside.astype(F32)
     crossed = lax.ppermute(keep_sum[:, piece:].astype(BF16), "decode", SWAP_CHIP)
 
+    (first_half,) = call(
+        gate_up_first_kernel,
+        [((total_rows, half), BF16)],
+        [SMEM] + [VMEM] * 5,
+        flops=2 * total_rows * width * hidden,
+        moved=4 << 20,
+        name="gate_up_first",
+        vmem=12,
+    )(place, tokens, own_weights, *got)
     (shared_hidden,) = call(
-        gate_up_kernel,
+        gate_up_second_kernel,
         [((total_rows, hidden), BF16)],
-        [SMEM] + [VMEM] * 8,
-        flops=4 * total_rows * width * hidden,
-        moved=6 << 20,
-        name="gate_up",
-    )(place, tokens, own_weights, *got, *other)
+        [SMEM] + [VMEM] * 6,
+        flops=2 * total_rows * width * hidden,
+        moved=4 << 20,
+        name="gate_up_second",
+        vmem=12,
+    )(after(place, kv_got[0]), tokens, own_weights, first_half, *other)
     hidden_pieces = spread(shared_hidden)
     summed = call(
         down_kernel,
@@ -478,31 +531,34 @@
             pltpu.VMEM((total_rows, slots * hidden), BF16),
             pltpu.VMEM((slots * hidden, piece), BF16),
         ],
-        flops=2 * total_rows * slots * hidden * piece,
-        moved=5 << 20,
         name="down",
-    )(place, keep_sum[:, :piece], crossed, *hidden_pieces, *down_got, *down_other)
+        vmem=14,
+    )(after(place, *kv_got), keep_sum[:, :piece], crossed, *hidden_pieces, *down_got, *down_other)
     returned = [to_shift(values, -s) for values, s in zip(summed[1:], SHIFTS)]
     (layer_out,) = call(
-        layer_kernel, [((rows, piece), BF16)], [SMEM] + [VMEM] * 5, name="layer"
-    )(place, resid, summed[0], *returned)
+        layer_kernel, [((rows, piece), BF16)], [VMEM] * 5, name="layer"
+    )(resid_share, summed[0], *returned)
 
     handed = call(
         kv_kernel,
         [((QCAP * BLOCK, kv_width), BF16)] * 4,
-        [SMEM] * 3 + [VMEM] * 7,
-        [pltpu.VMEM((rows, width), F32), pltpu.VMEM((rows, kv_width), BF16)],
-        flops=2 * rows * width * kv_width,
-        moved=4 << 20,
+        [SMEM] * 3 + [VMEM] * 12,
+        [
+            pltpu.VMEM((rows, width), F32),
+            pltpu.VMEM((rows, kv_width), BF16),
+            pltpu.VMEM((rows, width), BF16),
+        ],
         name="kv",
+        vmem=10,
     )(
         place,
         req_owner,
         req_blocks,
         attn_gain.reshape(1, width),
         *spread(layer_out),
-        kv_mine,
-        kv_theirs,
+        w_kv,
+        *kv_got,
+        *kv_other,
     )
     received = [handed[0]] + [
         lax.ppermute(values, "decode", pairs)

time: 207 us -> 174 us (0.84)
  between operations: 14.3 us -> 0.99 us
  starting transfers between devices: 64.9 us -> 52.7 us
  local copies, waits for them, and re-layouts: 13.6 us -> 3.54 us
  waiting for transfers between devices: 89.6 us -> 94.7 us
    ppermute x4, waiting for transfers between devices: 26.7 us -> 10.6 us  [near_plan(): down_other.append(lax.ppermute(values, 'groups', SWAP_GROUP))]
    ppermute x9 -> x12, waiting for transfers between devices: 40.4 us -> 54.8 us  [to_shift(): lax.ppermute(values, 'expert', [(i, (i + shift) % count) for i in range(c...]
    unnamed x51 -> x36, local copies, waits for them, and re-layouts: 11.9 us -> 2.07 us
    ppermute x4, waiting for transfers between devices: 0.01 us -> 9.14 us  [near_plan(): values = lax.ppermute(down_messages[k], ('expert', 'decode'), pairs)]
    ppermute x1, starting transfers between devices: 8.46 us -> 1.23 us  [near_plan(): lax.ppermute(keep_sum[:, piece:].astype(BF16), 'decode', SWAP_CHIP)]
    ppermute x1 -> x3, waiting for transfers between devices: 0.01 us -> 5.14 us  [near_plan(): kv_other = [lax.ppermute(values, 'groups', SWAP_GROUP) for values in kv_got]]
    ppermute x5, starting transfers between devices: 10.9 us -> 6.18 us  [spread(): across = lax.ppermute(values, 'decode', SWAP_CHIP)]
    ppermute x3, waiting for transfers between devices: 3.45 us -> 0.01 us  [near_plan(): other = [lax.ppermute(values, 'groups', SWAP_GROUP) for values in got]]
  transfers between devices with their start and end apart: 42 -> 46, of which waited for: 17 -> 19; matrix products, arithmetic and copies ran while one was open for 1% -> 0% of each run, Pallas kernels for 9% -> 4%
where the time goes in v3:
time: 174 us; the launch traced here: 173 us
  waiting for transfers between devices  94.7 us (54%)
  starting transfers between devices  52.7 us (30%)
  Pallas kernels  20.3 us (12%)
  local copies, waits for them, and re-layouts  3.54 us (2%)
    ppermute x12, waiting for transfers between devices, to_shift(): lax.ppermute(values, 'expert', [(i, (i + shift) % count) for i in range(c...  54.8 us
    ppermute x12, starting transfers between devices, to_shift(): lax.ppermute(values, 'expert', [(i, (i + shift) % count) for i in range(c...  18.5 us
    ppermute x4, starting transfers between devices, near_plan(): values = lax.ppermute(down_messages[k], ('expert', 'decode'), pairs)  12 us
    ppermute x5, waiting for transfers between devices, spread(): across = lax.ppermute(values, 'decode', SWAP_CHIP)  11.4 us
    ppermute x4, waiting for transfers between devices, near_plan(): down_other.append(lax.ppermute(values, 'groups', SWAP_GROUP))  10.6 us
    ppermute x4, waiting for transfers between devices, near_plan(): values = lax.ppermute(down_messages[k], ('expert', 'decode'), pairs)  9.14 us
    ppermute x5, starting transfers between devices, spread(): across = lax.ppermute(values, 'decode', SWAP_CHIP)  6.18 us
    pallas_call x1, Pallas kernels, near_plan(): call(lambda *refs: first_kernel(capacity, *refs), [((rows, width), BF16),...  5.59 us
  transfers between devices with their start and end apart: 46, of which 19 were waited for; matrix products, arithmetic and copies ran while one was open for 0% of the time, Pallas kernels for 4%

profile of v3, /device:TPU:0, one launch (start us, length us, event | category | flops | bytes accessed | tf_op | source)
XLA Modules:
  0.0 173.3 jit_solution(2227179815410532993)
XLA Ops:
  2.6 5.6 %first.1 = (bf16[128,2560]{1,0:T(8,128)(2,1)}, bf16[144,640]{1,0:T(8,128)(2,1)}, bf16[128,640]{1,0:T(8,128)(2,1)}, bf16[640,512]{1,0:T(8,128)(2,1)}, bf16[640,25...) custom-call(s32[3]{0:T(128)} %pad_add_fusion.refs_0_.place, ...), custom_call_target="tpu_custom_call" | custom-call | bytes 6291456 | tf_op jit(solution)/shard_map/first/pallas_call | solution.py:429
  8.2 4.1 %collective-permute-start.7 = (bf16[144,640]{1,0:T(8,128)(2,1)}, bf16[144,640]{1,0:T(8,128)(2,1)S(1)}, u32[]{:S(2)}, u32[]{:S(2)}) collective-permute-start(bf16[144,640]{1,0:T(8,128)(2,1)} %get-tuple-element.45.rest_0_), channel_id=1, source_target_pairs={{0,8},{4,12},{8,0},{12,4},{1,9},{5,13},{9,1},{13,5},{2,10},{6,14},... | collective-permute-start | bytes 552968 | tf_op jit(solution)/shard_map/ppermute | solution.py:172
  14.2 2.0 %collective-permute-start.15 = (bf16[144,640]{1,0:T(8,128)(2,1)}, bf16[144,640]{1,0:T(8,128)(2,1)S(1)}, u32[]{:S(2)}, u32[]{:S(2)}) collective-permute-start(bf16[144,640]{1,0:T(8,128)(2,1)} %get-tuple-element.45.rest_0_), channel_id=1, source_target_pairs={{0,12},{4,0},{8,4},{12,8},{1,13},{5,1},{9,5},{13,9},{2,14},{6,2},{... | collective-permute-start | bytes 552968 | tf_op jit(solution)/shard_map/ppermute | solution.py:172
  16.3 16.7 %collective-permute-done.7.rest_0_.rest_2_ = bf16[144,640]{1,0:T(8,128)(2,1)S(1)} collective-permute-done((bf16[144,640]{1,0:T(8,128)(2,1)}, bf16[144,640]{1,0:T(8,128)(2,1)S(1)}, u32[]{:S(2)}, u32[]{:S(2)}) %collective-permute-start.7) | collective-permute-done | bytes 184352 | tf_op jit(solution)/shard_map/ppermute | solution.py:172
  33.0 1.8 %collective-permute-start.9 = (bf16[144,640]{1,0:T(8,128)(2,1)S(1)}, bf16[144,640]{1,0:T(8,128)(2,1)S(1)}, u32[]{:S(2)}, u32[]{:S(2)}) collective-permute-start(bf16[144,640]{1,0:T(8,128)(2,1)S(1)} %collective-permute-done.7.rest_0_.rest_2_), channel_id=1, source_target_pairs={{0,2},{2,0},{1,3},{3,1},{4,6},{6,4},{5,7},{7,5},{8,10},{10,8},{9,1... | collective-permute-start | bytes 552968 | tf_op jit(solution)/shard_map/ppermute | solution.py:180
  35.0 1.8 %collective-permute-start.17 = (bf16[144,640]{1,0:T(8,128)(2,1)S(1)}, bf16[144,640]{1,0:T(8,128)(2,1)S(1)}, u32[]{:S(2)}, u32[]{:S(2)}) collective-permute-start(bf16[144,640]{1,0:T(8,128)(2,1)S(1)} %collective-permute-done.15.rest_8_.rest_3_), channel_id=1, source_target_pairs={{0,2},{2,0},{1,3},{3,1},{4,6},{6,4},{5,7},{7,5},{8,10},{10,8},{9,1... | collective-permute-start | bytes 552968 | tf_op jit(solution)/shard_map/ppermute | solution.py:180
  36.8 3.1 %collective-permute-done.a = bf16[640,256]{1,0:T(8,128)(2,1)S(1)} collective-permute-done((bf16[640,256]{1,0:T(8,128)(2,1)}, bf16[640,256]{1,0:T(8,128)(2,1)S(1)}, u32[]{:S(2)}, u32[]{:S(2)}) %collective-permute-start) | collective-permute-done | bytes 327712 | tf_op jit(solution)/shard_map/ppermute | solution.py:172
  40.5 3.3 %collective-permute-done.13.rest_6_ = bf16[144,640]{1,0:T(8,128)(2,1)S(1)} collective-permute-done((bf16[144,640]{1,0:T(8,128)(2,1)S(1)}, bf16[144,640]{1,0:T(8,128)(2,1)S(1)}, u32[]{:S(2)}, u32[]{:S(2)}) %collective-permute-start.13) | collective-permute-done | bytes 184352 | tf_op jit(solution)/shard_map/ppermute | solution.py:180
  43.9 2.0 %collective-permute-done.17.rest_10_ = bf16[144,640]{1,0:T(8,128)(2,1)S(1)} collective-permute-done((bf16[144,640]{1,0:T(8,128)(2,1)S(1)}, bf16[144,640]{1,0:T(8,128)(2,1)S(1)}, u32[]{:S(2)}, u32[]{:S(2)}) %collective-permute-start.17) | collective-permute-done | bytes 184352 | tf_op jit(solution)/shard_map/ppermute | solution.py:180
  46.4 3.6 %collective-permute-start.1 = (bf16[640,256]{1,0:T(8,128)(2,1)}, bf16[640,256]{1,0:T(8,128)(2,1)S(1)}, u32[]{:S(2)}, u32[]{:S(2)}) collective-permute-start(bf16[640,256]{1,0:T(8,128)(2,1)} %get-tuple-element.38), channel_id=1, source_target_pairs={{0,4},{4,8},{8,12},{12,0},{1,5},{5,9},{9,13},{13,1},{2,6},{6,10},{... | collective-permute-start | bytes 983048 | tf_op jit(solution)/shard_map/ppermute | solution.py:172
  52.6 3.6 %routed_up.1 = (bf16[512,2560]{1,0:T(8,128)(2,1)S(1)}, bf16[512,512]{1,0:T(8,128)(2,1)S(1)}) custom-call(s32[3]{0:T(128)S(1)} %copy-done.4, bf16[128,2560]{1,0:T(8,128)(2,1)S(1)} %copy-done.10, bf16[144,640]{1,0:T(8,128)(2,1)S(1)} %collective-permute-done.7.rest_0_.rest_2_, bf16[144,640]{1,0:T(8,128)(2,1)S(1)} %collective-permute-done.8.rest_1_, ...), custom_call_target="tpu_custom_call" | custom-call | flops 2684354560 | bytes 10485760 | tf_op jit(solution)/shard_map/routed_up/pallas_call | solution.py:479
  56.2 2.8 %collective-permute-done.1.b = bf16[640,256]{1,0:T(8,128)(2,1)S(1)} collective-permute-done((bf16[640,256]{1,0:T(8,128)(2,1)}, bf16[640,256]{1,0:T(8,128)(2,1)S(1)}, u32[]{:S(2)}, u32[]{:S(2)}) %collective-permute-start.1) | collective-permute-done | bytes 327712 | tf_op jit(solution)/shard_map/ppermute | solution.py:172
  59.0 6.1 %collective-permute-done.2.c = bf16[640,256]{1,0:T(8,128)(2,1)S(1)} collective-permute-done((bf16[640,256]{1,0:T(8,128)(2,1)}, bf16[640,256]{1,0:T(8,128)(2,1)S(1)}, u32[]{:S(2)}, u32[]{:S(2)}) %collective-permute-start.2) | collective-permute-done | bytes 327712 | tf_op jit(solution)/shard_map/ppermute | solution.py:172
  65.1 2.4 %routed_down.1 = (bf16[512,1280]{1,0:T(8,128)(2,1)S(1)}, bf16[512,1280]{1,0:T(8,128)(2,1)S(1)}) custom-call(s32[3]{0:T(128)S(1)} %copy-done.4, bf16[512,512]{1,0:T(8,128)(2,1)S(1)} %get-tuple-element.46.hidden, bf16[144,640]{1,0:T(8,128)(2,1)S(1)} %copy-done.11, bf16[144,640]{1,0:T(8,128)(2,1)S(1)} %collective-permute-done.11.rest_4_.rest_1_, ...), custom_call_target="tpu_custom_call" | custom-call | flops 1342177280 | bytes 6291456 | tf_op jit(solution)/shard_map/routed_down/pallas_call | solution.py:488
  68.3 3.6 %collective-permute-start.4 = (bf16[640,256]{1,0:T(8,128)(2,1)S(1)}, bf16[640,256]{1,0:T(8,128)(2,1)S(1)}, u32[]{:S(2)}, u32[]{:S(2)}) collective-permute-start(bf16[640,256]{1,0:T(8,128)(2,1)S(1)} %copy-done.13), channel_id=1, source_target_pairs={{0,4},{4,8},{8,12},{12,0},{1,5},{5,9},{9,13},{13,1},{2,6},{6,10},{... | collective-permute-start | bytes 983048 | tf_op jit(solution)/shard_map/ppermute | solution.py:172
  74.6 18.6 %collective-permute-done.3.rest_0_ = bf16[640,256]{1,0:T(8,128)(2,1)S(1)} collective-permute-done((bf16[640,256]{1,0:T(8,128)(2,1)S(1)}, bf16[640,256]{1,0:T(8,128)(2,1)S(1)}, u32[]{:S(2)}, u32[]{:S(2)}) %collective-permute-start.3) | collective-permute-done | bytes 327712 | tf_op jit(solution)/shard_map/ppermute | solution.py:172
  98.2 2.3 %collective-permute-start.24 = (bf16[512,256]{1,0:T(8,128)(2,1)S(1)}, bf16[512,256]{1,0:T(8,128)(2,1)S(1)}, u32[]{:S(2)}, u32[]{:S(2)}) collective-permute-start(bf16[512,256]{1,0:T(8,128)(2,1)S(1)} %gate_up_second.1.rest_0_), channel_id=1, source_target_pairs={{0,2},{2,0},{1,3},{3,1},{4,6},{6,4},{5,7},{7,5},{8,10},{10,8},{9,1... | collective-permute-start | bytes 786440 | tf_op jit(solution)/shard_map/ppermute | solution.py:180
  100.6 3.6 %collective-permute-start.28 = (bf16[128,640]{1,0:T(8,128)(2,1)S(1)}, bf16[128,640]{1,0:T(8,128)(2,1)S(1)}, u32[]{:S(2)}, u32[]{:S(2)}) collective-permute-start(bf16[128,640]{1,0:T(8,128)(2,1)S(1)} %copy-done.15), channel_id=1, source_target_pairs={{0,8},{1,12},{2,0},{3,4},{4,9},{5,13},{6,1},{7,5},{8,10},{9,14},{1... | collective-permute-start | bytes 491528 | tf_op jit(solution)/shard_map/ppermute | solution.py:471
  104.8 7.7 %collective-permute-start.29 = (bf16[128,640]{1,0:T(8,128)(2,1)S(1)}, bf16[128,640]{1,0:T(8,128)(2,1)S(1)}, u32[]{:S(2)}, u32[]{:S(2)}) collective-permute-start(bf16[128,640]{1,0:T(8,128)(2,1)S(1)} %copy-done.14), channel_id=1, source_target_pairs={{0,12},{1,8},{2,4},{3,0},{4,13},{5,9},{6,5},{7,1},{8,14},{9,10},{1... | collective-permute-start | bytes 491528 | tf_op jit(solution)/shard_map/ppermute | solution.py:471
  112.5 9.1 %collective-permute-done.28.rest_6_ = bf16[128,640]{1,0:T(8,128)(2,1)S(1)} collective-permute-done((bf16[128,640]{1,0:T(8,128)(2,1)S(1)}, bf16[128,640]{1,0:T(8,128)(2,1)S(1)}, u32[]{:S(2)}, u32[]{:S(2)}) %collective-permute-start.28) | collective-permute-done | bytes 163872 | tf_op jit(solution)/shard_map/ppermute | solution.py:471
  125.0 2.9 %collective-permute-done.30.rest_8_ = bf16[128,640]{1,0:T(8,128)(2,1)S(1)} collective-permute-done((bf16[128,640]{1,0:T(8,128)(2,1)S(1)}, bf16[128,640]{1,0:T(8,128)(2,1)S(1)}, u32[]{:S(2)}, u32[]{:S(2)}) %collective-permute-start.30) | collective-permute-done | bytes 163872 | tf_op jit(solution)/shard_map/ppermute | solution.py:473
  127.9 1.7 collective-permute-start.33
  129.8 1.6 collective-permute-done.31.rest_9_
  131.4 3.5 %collective-permute-done.32.rest_10_ = bf16[128,640]{1,0:T(8,128)(2,1)S(1)} collective-permute-done((bf16[128,640]{1,0:T(8,128)(2,1)S(1)}, bf16[128,640]{1,0:T(8,128)(2,1)S(1)}, u32[]{:S(2)}, u32[]{:S(2)}) %collective-permute-start.32) | collective-permute-done | bytes 163872 | tf_op jit(solution)/shard_map/ppermute | solution.py:473
  135.0 2.5 %collective-permute-done.33.rest_11_ = bf16[128,640]{1,0:T(8,128)(2,1)S(1)} collective-permute-done((bf16[128,640]{1,0:T(8,128)(2,1)S(1)}, bf16[128,640]{1,0:T(8,128)(2,1)S(1)}, u32[]{:S(2)}, u32[]{:S(2)}) %collective-permute-start.33) | collective-permute-done | bytes 163872 | tf_op jit(solution)/shard_map/ppermute | solution.py:473
  137.5 1.8 %down.1 = (f32[128,640]{1,0:T(8,128)S(1)}, bf16[128,640]{1,0:T(8,128)(2,1)S(1)}, bf16[128,640]{1,0:T(8,128)(2,1)S(1)}, bf16[128,640]{1,0:T(8,128)(2,1)S(1)}) custom-call(s32[3]{0:T(128)S(1)} %copy-done.4, f32[512,640]{1,0:T(8,128)S(1)} %slice.9.keep, bf16[512,640]{1,0:T(8,128)(2,1)S(1)} %collective-permute-done.20.crossed, ...), custom_call_target="tpu_custom_call" | custom-call | tf_op jit(solution)/shard_map/down/pallas_call | solution.py:526
  139.4 2.0 %collective-permute-start.36 = (bf16[128,640]{1,0:T(8,128)(2,1)S(1)}, bf16[128,640]{1,0:T(8,128)(2,1)S(1)}, u32[]{:S(2)}, u32[]{:S(2)}) collective-permute-start(bf16[128,640]{1,0:T(8,128)(2,1)S(1)} %get-tuple-element.63), channel_id=1, source_target_pairs={{0,4},{4,8},{8,12},{12,0},{1,5},{5,9},{9,13},{13,1},{2,6},{6,10},{... | collective-permute-start | bytes 491528 | tf_op jit(solution)/shard_map/ppermute | solution.py:172
  143.5 7.4 %collective-permute-done.34.a = bf16[128,640]{1,0:T(8,128)(2,1)S(1)} collective-permute-done((bf16[128,640]{1,0:T(8,128)(2,1)S(1)}, bf16[128,640]{1,0:T(8,128)(2,1)S(1)}, u32[]{:S(2)}, u32[]{:S(2)}) %collective-permute-start.34) | collective-permute-done | bytes 163872 | tf_op jit(solution)/shard_map/ppermute | solution.py:172
  153.0 5.5 %collective-permute-done.38.c = bf16[128,640]{1,0:T(8,128)(2,1)S(1)} collective-permute-done((bf16[128,640]{1,0:T(8,128)(2,1)}, bf16[128,640]{1,0:T(8,128)(2,1)S(1)}, u32[]{:S(2)}, u32[]{:S(2)}) %collective-permute-start.38) | collective-permute-done | bytes 163872 | tf_op jit(solution)/shard_map/ppermute | solution.py:180
  159.1 4.6 %collective-permute-done.42.rest_5_ = bf16[640,256]{1,0:T(8,128)(2,1)S(1)} collective-permute-done((bf16[640,256]{1,0:T(8,128)(2,1)S(1)}, bf16[640,256]{1,0:T(8,128)(2,1)S(1)}, u32[]{:S(2)}, u32[]{:S(2)}) %collective-permute-start.42) | collective-permute-done | bytes 327712 | tf_op jit(solution)/shard_map/ppermute | solution.py:477
  168.0 3.1 %collective-permute-done.44.c = bf16[64,512]{1,0:T(8,128)(2,1)S(1)} collective-permute-done((bf16[64,512]{1,0:T(8,128)(2,1)S(1)}, bf16[64,512]{1,0:T(8,128)(2,1)S(1)}, u32[]{:S(2)}, u32[]{:S(2)}) %collective-permute-start.44) | collective-permute-done | bytes 65568 | tf_op jit(solution)/shard_map/ppermute | solution.py:564
  171.6 1.7 hand.1
  (111 shorter events, 29.9 us)
Async XLA Ops:
  8.2 24.7 %collective-permute-start.7 = (bf16[144,640]{1,0:T(8,128)(2,1)}, bf16[144,640]{1,0:T(8,128)(2,1)S(1)}, u32[]{:S(2)}, u32[]{:S(2)}) collective-permute-start(bf16[144,640]{1,0:T(8,128)(2,1)} %get-tuple-element.45.rest_0_), channel_id=1, source_target_pairs={{0,8},{4,12},{8,0},{12,4},{1,9},{5,13},{9,1},{13,5},{2,10},{6,14},... | collective-permute-start | bytes 552968 | tf_op jit(solution)/shard_map/ppermute | solution.py:172
  12.3 22.5 %collective-permute-start.11 = (bf16[144,640]{1,0:T(8,128)(2,1)}, bf16[144,640]{1,0:T(8,128)(2,1)S(1)}, u32[]{:S(2)}, u32[]{:S(2)}) collective-permute-start(bf16[144,640]{1,0:T(8,128)(2,1)} %get-tuple-element.45.rest_0_), channel_id=1, source_target_pairs={{0,4},{4,8},{8,12},{12,0},{1,5},{5,9},{9,13},{13,1},{2,6},{6,10},{... | collective-permute-start | bytes 552968 | tf_op jit(solution)/shard_map/ppermute | solution.py:172
  13.9 26.1 %collective-permute-start = (bf16[640,256]{1,0:T(8,128)(2,1)}, bf16[640,256]{1,0:T(8,128)(2,1)S(1)}, u32[]{:S(2)}, u32[]{:S(2)}) collective-permute-start(bf16[640,256]{1,0:T(8,128)(2,1)} %get-tuple-element.37), channel_id=1, source_target_pairs={{0,8},{4,12},{8,0},{12,4},{1,9},{5,13},{9,1},{13,5},{2,10},{6,14},... | collective-permute-start | bytes 983048 | tf_op jit(solution)/shard_map/ppermute | solution.py:172
  14.2 20.8 %collective-permute-start.15 = (bf16[144,640]{1,0:T(8,128)(2,1)}, bf16[144,640]{1,0:T(8,128)(2,1)S(1)}, u32[]{:S(2)}, u32[]{:S(2)}) collective-permute-start(bf16[144,640]{1,0:T(8,128)(2,1)} %get-tuple-element.45.rest_0_), channel_id=1, source_target_pairs={{0,12},{4,0},{8,4},{12,8},{1,13},{5,1},{9,5},{13,9},{2,14},{6,2},{... | collective-permute-start | bytes 552968 | tf_op jit(solution)/shard_map/ppermute | solution.py:172
  34.8 9.1 %collective-permute-start.13 = (bf16[144,640]{1,0:T(8,128)(2,1)S(1)}, bf16[144,640]{1,0:T(8,128)(2,1)S(1)}, u32[]{:S(2)}, u32[]{:S(2)}) collective-permute-start(bf16[144,640]{1,0:T(8,128)(2,1)S(1)} %collective-permute-done.11.rest_4_.rest_1_), channel_id=1, source_target_pairs={{0,2},{2,0},{1,3},{3,1},{4,6},{6,4},{5,7},{7,5},{8,10},{10,8},{9,1... | collective-permute-start | bytes 552968 | tf_op jit(solution)/shard_map/ppermute | solution.py:180
  35.0 10.9 %collective-permute-start.17 = (bf16[144,640]{1,0:T(8,128)(2,1)S(1)}, bf16[144,640]{1,0:T(8,128)(2,1)S(1)}, u32[]{:S(2)}, u32[]{:S(2)}) collective-permute-start(bf16[144,640]{1,0:T(8,128)(2,1)S(1)} %collective-permute-done.15.rest_8_.rest_3_), channel_id=1, source_target_pairs={{0,2},{2,0},{1,3},{3,1},{4,6},{6,4},{5,7},{7,5},{8,10},{10,8},{9,1... | collective-permute-start | bytes 552968 | tf_op jit(solution)/shard_map/ppermute | solution.py:180
  36.8 9.0 %collective-permute-start.12 = (bf16[144,640]{1,0:T(8,128)(2,1)S(1)}, bf16[144,640]{1,0:T(8,128)(2,1)S(1)}, u32[]{:S(2)}, u32[]{:S(2)}) collective-permute-start(bf16[144,640]{1,0:T(8,128)(2,1)S(1)} %collective-permute-done.11.rest_4_.rest_1_), channel_id=1, source_target_pairs={{0,1},{1,0},{2,3},{3,2},{4,5},{5,4},{6,7},{7,6},{8,9},{9,8},{10,11... | collective-permute-start | bytes 552968 | tf_op jit(solution)/shard_map/ppermute | solution.py:181
  40.5 9.5 %collective-permute-start.8 = (bf16[144,640]{1,0:T(8,128)(2,1)S(1)}, bf16[144,640]{1,0:T(8,128)(2,1)S(1)}, u32[]{:S(2)}, u32[]{:S(2)}) collective-permute-start(bf16[144,640]{1,0:T(8,128)(2,1)S(1)} %collective-permute-done.7.rest_0_.rest_2_), channel_id=1, source_target_pairs={{0,1},{1,0},{2,3},{3,2},{4,5},{5,4},{6,7},{7,6},{8,9},{9,8},{10,11... | collective-permute-start | bytes 552968 | tf_op jit(solution)/shard_map/ppermute | solution.py:181
  46.4 12.6 %collective-permute-start.1 = (bf16[640,256]{1,0:T(8,128)(2,1)}, bf16[640,256]{1,0:T(8,128)(2,1)S(1)}, u32[]{:S(2)}, u32[]{:S(2)}) collective-permute-start(bf16[640,256]{1,0:T(8,128)(2,1)} %get-tuple-element.38), channel_id=1, source_target_pairs={{0,4},{4,8},{8,12},{12,0},{1,5},{5,9},{9,13},{13,1},{2,6},{6,10},{... | collective-permute-start | bytes 983048 | tf_op jit(solution)/shard_map/ppermute | solution.py:172
  50.0 15.1 %collective-permute-start.2 = (bf16[640,256]{1,0:T(8,128)(2,1)}, bf16[640,256]{1,0:T(8,128)(2,1)S(1)}, u32[]{:S(2)}, u32[]{:S(2)}) collective-permute-start(bf16[640,256]{1,0:T(8,128)(2,1)} %get-tuple-element.39), channel_id=1, source_target_pairs={{0,12},{4,0},{8,4},{12,8},{1,13},{5,1},{9,5},{13,9},{2,14},{6,2},{... | collective-permute-start | bytes 983048 | tf_op jit(solution)/shard_map/ppermute | solution.py:172
  50.2 14.9 %collective-permute-start.6 = (bf16[640,256]{1,0:T(8,128)(2,1)S(1)}, bf16[640,256]{1,0:T(8,128)(2,1)S(1)}, u32[]{:S(2)}, u32[]{:S(2)}) collective-permute-start(bf16[640,256]{1,0:T(8,128)(2,1)S(1)} %collective-permute-done.a), channel_id=1, source_target_pairs={{0,16},{16,0},{1,17},{17,1},{2,18},{18,2},{3,19},{19,3},{4,20},{20... | collective-permute-start | bytes 983048 | tf_op jit(solution)/shard_map/ppermute | solution.py:463
  67.6 25.6 %collective-permute-start.3 = (bf16[640,256]{1,0:T(8,128)(2,1)S(1)}, bf16[640,256]{1,0:T(8,128)(2,1)S(1)}, u32[]{:S(2)}, u32[]{:S(2)}) collective-permute-start(bf16[640,256]{1,0:T(8,128)(2,1)S(1)} %copy-done.13), channel_id=1, source_target_pairs={{0,8},{4,12},{8,0},{12,4},{1,9},{5,13},{9,1},{13,5},{2,10},{6,14},... | collective-permute-start | bytes 983048 | tf_op jit(solution)/shard_map/ppermute | solution.py:172
  68.3 32.3 %collective-permute-start.4 = (bf16[640,256]{1,0:T(8,128)(2,1)S(1)}, bf16[640,256]{1,0:T(8,128)(2,1)S(1)}, u32[]{:S(2)}, u32[]{:S(2)}) collective-permute-start(bf16[640,256]{1,0:T(8,128)(2,1)S(1)} %copy-done.13), channel_id=1, source_target_pairs={{0,4},{4,8},{8,12},{12,0},{1,5},{5,9},{9,13},{13,1},{2,6},{6,10},{... | collective-permute-start | bytes 983048 | tf_op jit(solution)/shard_map/ppermute | solution.py:172
  71.9 28.7 %collective-permute-start.5 = (bf16[640,256]{1,0:T(8,128)(2,1)S(1)}, bf16[640,256]{1,0:T(8,128)(2,1)S(1)}, u32[]{:S(2)}, u32[]{:S(2)}) collective-permute-start(bf16[640,256]{1,0:T(8,128)(2,1)S(1)} %copy-done.13), channel_id=1, source_target_pairs={{0,12},{4,0},{8,4},{12,8},{1,13},{5,1},{9,5},{13,9},{2,14},{6,2},{... | collective-permute-start | bytes 983048 | tf_op jit(solution)/shard_map/ppermute | solution.py:172
  72.1 22.3 %collective-permute-start.21 = (bf16[640,256]{1,0:T(8,128)(2,1)S(1)}, bf16[640,256]{1,0:T(8,128)(2,1)S(1)}, u32[]{:S(2)}, u32[]{:S(2)}) collective-permute-start(bf16[640,256]{1,0:T(8,128)(2,1)S(1)} %collective-permute-done.1.b), channel_id=1, source_target_pairs={{0,16},{16,0},{1,17},{17,1},{2,18},{18,2},{3,19},{19,3},{4,20},{20... | collective-permute-start | bytes 983048 | tf_op jit(solution)/shard_map/ppermute | solution.py:463
  73.4 23.3 %collective-permute-start.22 = (bf16[640,256]{1,0:T(8,128)(2,1)S(1)}, bf16[640,256]{1,0:T(8,128)(2,1)S(1)}, u32[]{:S(2)}, u32[]{:S(2)}) collective-permute-start(bf16[640,256]{1,0:T(8,128)(2,1)S(1)} %collective-permute-done.2.c), channel_id=1, source_target_pairs={{0,16},{16,0},{1,17},{17,1},{2,18},{18,2},{3,19},{19,3},{4,20},{20... | collective-permute-start | bytes 983048 | tf_op jit(solution)/shard_map/ppermute | solution.py:463
  93.2 44.3 %collective-permute-start.20 = (bf16[512,640]{1,0:T(8,128)(2,1)S(1)}, bf16[512,640]{1,0:T(8,128)(2,1)S(1)}, u32[]{:S(2)}, u32[]{:S(2)}) collective-permute-start(bf16[512,640]{1,0:T(8,128)(2,1)S(1)} %slice.12), channel_id=1, source_target_pairs={{0,2},{2,0},{1,3},{3,1},{4,6},{6,4},{5,7},{7,5},{8,10},{10,8},{9,1... | collective-permute-start | bytes 1966088 | tf_op jit(solution)/shard_map/ppermute | solution.py:505
  94.4 9.7 %collective-permute-start.26 = (bf16[128,640]{1,0:T(8,128)(2,1)S(1)}, bf16[128,640]{1,0:T(8,128)(2,1)S(1)}, u32[]{:S(2)}, u32[]{:S(2)}) collective-permute-start(bf16[128,640]{1,0:T(8,128)(2,1)S(1)} %copy-done.17), channel_id=1, source_target_pairs={{0,0},{1,4},{2,8},{3,12},{4,1},{5,5},{6,9},{7,13},{8,2},{9,6},{10,... | collective-permute-start | bytes 491528 | tf_op jit(solution)/shard_map/ppermute | solution.py:471
  98.2 24.7 %collective-permute-start.24 = (bf16[512,256]{1,0:T(8,128)(2,1)S(1)}, bf16[512,256]{1,0:T(8,128)(2,1)S(1)}, u32[]{:S(2)}, u32[]{:S(2)}) collective-permute-start(bf16[512,256]{1,0:T(8,128)(2,1)S(1)} %gate_up_second.1.rest_0_), channel_id=1, source_target_pairs={{0,2},{2,0},{1,3},{3,1},{4,6},{6,4},{5,7},{7,5},{8,10},{10,8},{9,1... | collective-permute-start | bytes 786440 | tf_op jit(solution)/shard_map/ppermute | solution.py:180
  100.6 21.1 %collective-permute-start.28 = (bf16[128,640]{1,0:T(8,128)(2,1)S(1)}, bf16[128,640]{1,0:T(8,128)(2,1)S(1)}, u32[]{:S(2)}, u32[]{:S(2)}) collective-permute-start(bf16[128,640]{1,0:T(8,128)(2,1)S(1)} %copy-done.15), channel_id=1, source_target_pairs={{0,8},{1,12},{2,0},{3,4},{4,9},{5,13},{6,1},{7,5},{8,10},{9,14},{1... | collective-permute-start | bytes 491528 | tf_op jit(solution)/shard_map/ppermute | solution.py:471
  104.1 19.6 %collective-permute-start.23 = (bf16[512,256]{1,0:T(8,128)(2,1)S(1)}, bf16[512,256]{1,0:T(8,128)(2,1)S(1)}, u32[]{:S(2)}, u32[]{:S(2)}) collective-permute-start(bf16[512,256]{1,0:T(8,128)(2,1)S(1)} %gate_up_second.1.rest_0_), channel_id=1, source_target_pairs={{0,1},{1,0},{2,3},{3,2},{4,5},{5,4},{6,7},{7,6},{8,9},{9,8},{10,11... | collective-permute-start | bytes 786440 | tf_op jit(solution)/shard_map/ppermute | solution.py:181
  104.8 18.1 %collective-permute-start.29 = (bf16[128,640]{1,0:T(8,128)(2,1)S(1)}, bf16[128,640]{1,0:T(8,128)(2,1)S(1)}, u32[]{:S(2)}, u32[]{:S(2)}) collective-permute-start(bf16[128,640]{1,0:T(8,128)(2,1)S(1)} %copy-done.14), channel_id=1, source_target_pairs={{0,12},{1,8},{2,4},{3,0},{4,13},{5,9},{6,5},{7,1},{8,14},{9,10},{1... | collective-permute-start | bytes 491528 | tf_op jit(solution)/shard_map/ppermute | solution.py:471
  122.9 14.6 %collective-permute-start.25 = (bf16[512,256]{1,0:T(8,128)(2,1)S(1)}, bf16[512,256]{1,0:T(8,128)(2,1)S(1)}, u32[]{:S(2)}, u32[]{:S(2)}) collective-permute-start(bf16[512,256]{1,0:T(8,128)(2,1)S(1)} %collective-permute-done.24.rest_2_), channel_id=1, source_target_pairs={{0,1},{1,0},{2,3},{3,2},{4,5},{5,4},{6,7},{7,6},{8,9},{9,8},{10,11... | collective-permute-start | bytes 786440 | tf_op jit(solution)/shard_map/ppermute | solution.py:182
  123.7 11.2 %collective-permute-start.32 = (bf16[128,640]{1,0:T(8,128)(2,1)S(1)}, bf16[128,640]{1,0:T(8,128)(2,1)S(1)}, u32[]{:S(2)}, u32[]{:S(2)}) collective-permute-start(bf16[128,640]{1,0:T(8,128)(2,1)S(1)} %collective-permute-done.28.rest_6_), channel_id=1, source_target_pairs={{0,16},{16,0},{1,17},{17,1},{2,18},{18,2},{3,19},{19,3},{4,20},{20... | collective-permute-start | bytes 491528 | tf_op jit(solution)/shard_map/ppermute | solution.py:473
  127.9 9.6 %collective-permute-start.33 = (bf16[128,640]{1,0:T(8,128)(2,1)S(1)}, bf16[128,640]{1,0:T(8,128)(2,1)S(1)}, u32[]{:S(2)}, u32[]{:S(2)}) collective-permute-start(bf16[128,640]{1,0:T(8,128)(2,1)S(1)} %collective-permute-done.29.rest_7_), channel_id=1, source_target_pairs={{0,16},{16,0},{1,17},{17,1},{2,18},{18,2},{3,19},{19,3},{4,20},{20... | collective-permute-start | bytes 491528 | tf_op jit(solution)/shard_map/ppermute | solution.py:473
  139.3 11.6 %collective-permute-start.34 = (bf16[128,640]{1,0:T(8,128)(2,1)S(1)}, bf16[128,640]{1,0:T(8,128)(2,1)S(1)}, u32[]{:S(2)}, u32[]{:S(2)}) collective-permute-start(bf16[128,640]{1,0:T(8,128)(2,1)S(1)} %get-tuple-element.61), channel_id=1, source_target_pairs={{0,8},{4,12},{8,0},{12,4},{1,9},{5,13},{9,1},{13,5},{2,10},{6,14},... | collective-permute-start | bytes 491528 | tf_op jit(solution)/shard_map/ppermute | solution.py:172
  139.4 12.8 %collective-permute-start.35 = (bf16[128,640]{1,0:T(8,128)(2,1)S(1)}, bf16[128,640]{1,0:T(8,128)(2,1)S(1)}, u32[]{:S(2)}, u32[]{:S(2)}) collective-permute-start(bf16[128,640]{1,0:T(8,128)(2,1)S(1)} %get-tuple-element.62), channel_id=1, source_target_pairs={{0,12},{4,0},{8,4},{12,8},{1,13},{5,1},{9,5},{13,9},{2,14},{6,2},{... | collective-permute-start | bytes 491528 | tf_op jit(solution)/shard_map/ppermute | solution.py:172
  139.4 12.8 %collective-permute-start.36 = (bf16[128,640]{1,0:T(8,128)(2,1)S(1)}, bf16[128,640]{1,0:T(8,128)(2,1)S(1)}, u32[]{:S(2)}, u32[]{:S(2)}) collective-permute-start(bf16[128,640]{1,0:T(8,128)(2,1)S(1)} %get-tuple-element.63), channel_id=1, source_target_pairs={{0,4},{4,8},{8,12},{12,0},{1,5},{5,9},{9,13},{13,1},{2,6},{6,10},{... | collective-permute-start | bytes 491528 | tf_op jit(solution)/shard_map/ppermute | solution.py:172
  141.4 17.1 %collective-permute-start.40 = (bf16[640,256]{1,0:T(8,128)(2,1)S(1)}, bf16[640,256]{1,0:T(8,128)(2,1)S(1)}, u32[]{:S(2)}, u32[]{:S(2)}) collective-permute-start(bf16[640,256]{1,0:T(8,128)(2,1)S(1)} %collective-permute-done.3.rest_0_), channel_id=1, source_target_pairs={{0,16},{16,0},{1,17},{17,1},{2,18},{18,2},{3,19},{19,3},{4,20},{20... | collective-permute-start | bytes 983048 | tf_op jit(solution)/shard_map/ppermute | solution.py:477
  142.7 16.4 %collective-permute-start.41 = (bf16[640,256]{1,0:T(8,128)(2,1)S(1)}, bf16[640,256]{1,0:T(8,128)(2,1)S(1)}, u32[]{:S(2)}, u32[]{:S(2)}) collective-permute-start(bf16[640,256]{1,0:T(8,128)(2,1)S(1)} %collective-permute-done.4.rest_1_), channel_id=1, source_target_pairs={{0,16},{16,0},{1,17},{17,1},{2,18},{18,2},{3,19},{19,3},{4,20},{20... | collective-permute-start | bytes 983048 | tf_op jit(solution)/shard_map/ppermute | solution.py:477
  150.9 12.8 %collective-permute-start.42 = (bf16[640,256]{1,0:T(8,128)(2,1)S(1)}, bf16[640,256]{1,0:T(8,128)(2,1)S(1)}, u32[]{:S(2)}, u32[]{:S(2)}) collective-permute-start(bf16[640,256]{1,0:T(8,128)(2,1)S(1)} %collective-permute-done.5.rest_2_), channel_id=1, source_target_pairs={{0,16},{16,0},{1,17},{17,1},{2,18},{18,2},{3,19},{19,3},{4,20},{20... | collective-permute-start | bytes 983048 | tf_op jit(solution)/shard_map/ppermute | solution.py:477
  153.0 10.7 %collective-permute-start.37 = (bf16[128,640]{1,0:T(8,128)(2,1)}, bf16[128,640]{1,0:T(8,128)(2,1)S(1)}, u32[]{:S(2)}, u32[]{:S(2)}) collective-permute-start(bf16[128,640]{1,0:T(8,128)(2,1)} %layer.1.a), channel_id=1, source_target_pairs={{0,1},{1,0},{2,3},{3,2},{4,5},{5,4},{6,7},{7,6},{8,9},{9,8},{10,11... | collective-permute-start | bytes 491528 | tf_op jit(solution)/shard_map/ppermute | solution.py:181
  (32 other events, 455.4 us)

commit v4 on v3

--- a/solution.py
+++ b/solution.py
@@ -176,6 +176,10 @@
     return lax.optimization_barrier((values,) + others)[0]
 
 
+def swap_groups(values):
+    return lax.ppermute(values, "groups", SWAP_GROUP)
+
+
 def spread(values):
     across = lax.ppermute(values, "decode", SWAP_CHIP)
     beside = lax.ppermute(values, "decode", SWAP_CORE)
@@ -194,7 +198,7 @@
 def first_kernel(
     capacity, place, resid, gain, score, ids, gate, up, down, kv, moe_in, message, share, own, *rest
 ):
-    messages, downs, kv_half, sem = rest[:3], rest[3:7], rest[7], rest[8]
+    messages, downs, kv_half, own_down, sem = rest[:3], rest[3:6], rest[6], rest[7], rest[8]
     zone, slot, group = place[0], place[1], place[2]
     count = 4
     hidden = gate.shape[1] // count
@@ -211,9 +215,10 @@
                 weights.at[:, pl.ds(pl.multiple_of(start, 128), half)],
                 messages[i].at[:, j * half : (j + 1) * half],
             )
-    for k in range(count):
-        start = (slot ^ k) * hidden + group * half
-        move(down.at[pl.ds(pl.multiple_of(start, 128), half), :], downs[k])
+    for i, shift in enumerate(SHIFTS):
+        start = lax.rem(zone + shift, count) * hidden + group * half
+        move(down.at[pl.ds(pl.multiple_of(start, 128), half), :], downs[i])
+    move(down.at[pl.ds(pl.multiple_of(zone * hidden, 128), hidden), :], own_down)
     start = group * kv_half.shape[1]
     move(kv.at[:, pl.ds(pl.multiple_of(start, 128), kv_half.shape[1])], kv_half)
     for part in range(2):
@@ -255,18 +260,38 @@
     return values / (1.0 + jnp.exp(-values))
 
 
-def routed_up_kernel(place, moe_in, *rest):
-    pieces = rest[:12]
-    gate, up, tokens, hidden = rest[12:]
+def join_kernel(*refs):
+    out, row = refs[-1], 0
+    for part in refs[:-1]:
+        out[row : row + part.shape[0], :] = part[...]
+        row += part.shape[0]
+
+
+def join(*parts):
+    rows = sum(part.shape[0] for part in parts)
+    return call(
+        join_kernel, [((rows, parts[0].shape[1]), BF16)], [VMEM] * len(parts), name="join"
+    )(*parts)[0]
+
+
+def half_kernel(place, moe_in, *rest):
+    own, across, out = rest[:3], rest[3:6], rest[6]
+    rows = moe_in.shape[0]
+    piece = out.shape[1] // 2
+    out[:rows, :piece] = moe_in[:, lanes(place[1], piece)]
+    out[:rows, piece:] = moe_in[:, lanes(place[1] ^ 2, piece)]
+    for i, shift in enumerate(SHIFTS):
+        span = slice(shift * rows, (shift + 1) * rows)
+        out[span, :piece] = own[i][:rows, :]
+        out[span, piece:] = across[i][:rows, :]
+
+
+def routed_up_kernel(place, mine, theirs, gate, up, tokens, hidden):
     slot = place[1]
-    rows = moe_in.shape[0]
-    piece = pieces[0].shape[1]
-    tokens[:rows, :] = moe_in[...]
-    for i, shift in enumerate(SHIFTS):
-        for j in range(4):
-            tokens[shift * rows : (shift + 1) * rows, lanes(slot ^ j, piece)] = pieces[4 * i + j][
-                :rows, :
-            ]
+    piece = mine.shape[1] // 2
+    for j in range(4):
+        source = theirs if j % 2 else mine
+        tokens[:, lanes(slot ^ j, piece)] = source[:, (j // 2) * piece : (j // 2 + 1) * piece]
     width = hidden.shape[1]
     step = 256
     for n in range(width // step):
@@ -277,8 +302,8 @@
 
 
 def routed_down_kernel(place, hidden, *rest):
-    messages, down, send, keep = rest[:4], rest[4], rest[5], rest[6]
-    zone, slot = place[0], place[1]
+    messages, down, out = rest[:4], rest[4], rest[5]
+    zone = place[0]
     rows = messages[0].shape[0] - META
     piece = messages[0].shape[1]
     diagonal = lax.broadcasted_iota(jnp.int32, (rows, rows), 0) == lax.broadcasted_iota(
@@ -292,10 +317,9 @@
         value = jnp.where(info[:, 3 * rows : 4 * rows] == mine, value, 0.0)
         scales.append(jnp.sum(jnp.where(diagonal, value, 0.0), axis=1, keepdims=True))
     scale = jnp.concatenate(scales, axis=0)
-    for target, parts in ((send, (1, 3)), (keep, (0, 2))):
-        for i, j in enumerate(parts):
-            value = dot(hidden[...], down[0, :, lanes(slot ^ j, piece)]) * scale
-            target[:, i * piece : (i + 1) * piece] = value.astype(BF16)
+    for n in range(out.shape[1] // piece):
+        cols = slice(n * piece, (n + 1) * piece)
+        out[:, cols] = (dot(hidden[...], down[0, :, cols]) * scale).astype(BF16)
 
 
 def gate_up_half(place, tokens, own, pieces, part):
@@ -314,44 +338,56 @@
     hidden[...] = gate_up_half(place, tokens, own, (a, b, c), 0)
 
 
-def gate_up_second_kernel(place, tokens, own, first, a, b, c, hidden):
+def gate_up_second_kernel(place, tokens, own, first, rest, hidden):
     half = first.shape[1]
+    near = own.shape[0]
+    a, b, c = [rest.at[i * near : (i + 1) * near, :] for i in range(3)]
     hidden[:, lanes(place[2], half)] = first[...]
     hidden[:, lanes(1 - place[2], half)] = gate_up_half(place, tokens, own, (a, b, c), 1)
 
 
-def down_kernel(place, keep, crossed, *rest):
-    pieces, got, other = rest[:4], rest[4:8], rest[8:12]
-    own, sends, hidden, weights = rest[12], rest[13:16], rest[16], rest[17]
+def down_kernel(place, routed, hidden, own, other, a, b, c, send, keep, weights):
     zone, slot, group = place[0], place[1], place[2]
-    width = pieces[0].shape[1]
-    half = width // 2
-    rows = own.shape[0]
-    for j in range(4):
-        hidden[:, lanes(slot ^ j, width)] = pieces[j][...]
-    for k in range(4):
-        base = (zone ^ k) * width
-        weights[pl.ds(pl.multiple_of(base + group * half, 128), half), :] = got[k][...]
-        weights[pl.ds(pl.multiple_of(base + (1 - group) * half, 128), half), :] = other[k][...]
-    for block in range(4):
-        span = slice(block * rows, (block + 1) * rows)
-        value = keep[span, :].astype(F32) + crossed[span, :].astype(F32)
-        value = value + dot(hidden[span, :], weights[...])
-        if block == 0:
-            own[...] = value
-        else:
-            sends[SHIFTS.index(block)][...] = value.astype(BF16)
-
-
-def layer_kernel(resid, own, a, b, c, out):
-    value = own[...] + a[...].astype(F32) + b[...].astype(F32) + c[...].astype(F32)
+    piece = own.shape[1]
+    half = own.shape[0] // 2
+    weights[:, lanes(zone, piece)] = own[...]
+    for i, (shift, part) in enumerate(zip(SHIFTS, (a, b, c))):
+        cols = lanes(lax.rem(zone - shift + 4, 4), piece)
+        weights[pl.ds(pl.multiple_of(group * half, 128), half), cols] = part[...]
+        weights[pl.ds(pl.multiple_of((1 - group) * half, 128), half), cols] = other[
+            i * half : (i + 1) * half, :
+        ]
+    for target, parts in ((send, (1, 3)), (keep, (0, 2))):
+        for i, j in enumerate(parts):
+            cols = lanes(slot ^ j, piece)
+            value = routed[:, cols].astype(F32) + dot(hidden[...], weights[:, cols])
+            target[:, i * piece : (i + 1) * piece] = value.astype(target.dtype)
+
+
+def pass_kernel(keep, beside, *outs):
+    rows, piece = outs[0].shape
+    for shard in range(4):
+        span = slice(shard * rows, (shard + 1) * rows)
+        value = keep[span, :].astype(F32) + beside[span, :].astype(F32)
+        outs[shard][...] = value[:, :piece]
+        outs[4 + shard][...] = value[:, piece:].astype(BF16)
+
+
+def add_kernel(a, b, out):
+    out[...] = (a[...] + b[...].astype(F32)).astype(BF16)
+
+
+def layer_kernel(resid, own, crossed, a, b, c, out):
+    value = own[...] + crossed[...].astype(F32) + a[...].astype(F32) + b[...].astype(F32) + c[...].astype(F32)
     value = value + resid[...].astype(F32)
     out[...] = value.astype(BF16)
 
 
 def kv_kernel(place, owner, blocks, gain, a, b, c, d, own, *rest):
-    got, other, outs = rest[:3], rest[3:6], rest[6:10]
-    full, key_value, ready = rest[10:]
+    got, outs = rest[:3], rest[4:8]
+    full, key_value, ready = rest[8:]
+    rows = own.shape[0]
+    other = [rest[3].at[i * rows : (i + 1) * rows, :] for i in range(3)]
     zone, slot, group = place[0], place[1], place[2]
     piece = a.shape[1]
     for j, part in enumerate((a, b, c, d)):
@@ -435,8 +471,8 @@
             ((near, 2 * hidden), BF16),
         ]
         + [((near, hidden), BF16)] * 3
-        + [((half, piece), BF16)] * 4
-        + [((near, kv_width // 2), BF16)],
+        + [((half, piece), BF16)] * 3
+        + [((near, kv_width // 2), BF16), ((hidden, piece), BF16)],
         [SMEM] + [VMEM] * 4 + [ANY] * 4,
         [pltpu.SemaphoreType.DMA((15,))],
         moved=6 << 20,
@@ -454,55 +490,51 @@
         w_kv,
     )
     moe_in, message, resid_share, own_weights = first[:4]
-    weight_messages, down_messages, kv_half = first[4:7], first[7:11], first[11]
+    weight_messages, down_messages, kv_half, own_down = first[4:7], first[7:10], *first[10:]
 
     arrived = [to_shift(message, s) for s in SHIFTS]
-    pieces = [part for values in arrived for part in spread(values)]
-
     got = [to_shift(values, s) for values, s in zip(weight_messages, SHIFTS)]
-    other = [lax.ppermute(values, "groups", SWAP_GROUP) for values in got]
-
-    down_got, down_other = [], []
-    down_messages = lax.optimization_barrier(tuple(down_messages) + tuple(got) + (other[0],))[:4]
-    for k in range(slots):
-        pairs = [
-            (z * slots + d, (d ^ k) * slots + z) for z in range(zones) for d in range(slots)
-        ]
-        values = lax.ppermute(down_messages[k], ("expert", "decode"), pairs)
-        down_got.append(values)
-        down_other.append(lax.ppermute(values, "groups", SWAP_GROUP))
-
-    kv_half = after(kv_half, *got)
+    joined = join(*got)
+    other = swap_groups(joined)
+
+    across = [lax.ppermute(values, "decode", SWAP_CHIP) for values in arrived]
+    (token_half,) = call(
+        half_kernel,
+        [((total_rows, 2 * piece), BF16)],
+        [SMEM] + [VMEM] * 7,
+        name="half",
+    )(after(place, joined), moe_in, *arrived, *across)
+    token_rest = lax.ppermute(token_half, "decode", SWAP_CORE)
+
+    down_got = [to_shift(values, s) for values, s in zip(down_messages, SHIFTS)]
+    down_other = swap_groups(join(*down_got))
+
+    kv_half = after(kv_half, *down_got)
     kv_got = [to_shift(kv_half, s) for s in SHIFTS]
-    kv_other = [lax.ppermute(values, "groups", SWAP_GROUP) for values in kv_got]
-
     tokens, routed_hidden = call(
         routed_up_kernel,
         [((total_rows, width), BF16), ((total_rows, routed_width), BF16)],
-        [SMEM] + [VMEM] * 15,
+        [SMEM] + [VMEM] * 4,
         flops=4 * total_rows * width * routed_width,
         moved=10 << 20,
         name="routed_up",
         vmem=22,
-    )(after(place, got[0]), moe_in, *pieces, w_gate, w_up)
-    send, keep = call(
+    )(place, token_half, token_rest, w_gate, w_up)
+    (routed,) = call(
         routed_down_kernel,
-        [((total_rows, 2 * piece), BF16), ((total_rows, 2 * piece), BF16)],
+        [((total_rows, width), BF16)],
         [SMEM] + [VMEM] * 6,
         flops=2 * total_rows * width * routed_width,
         moved=6 << 20,
         name="routed_down",
         vmem=16,
     )(
-        after(place, other[0], *got),
+        place,
         routed_hidden,
         message,
         *[arrived[SHIFTS.index(s)] for s in range(1, zones)],
         w_down,
     )
-    beside = lax.ppermute(send, "decode", SWAP_CORE)
-    keep_sum = keep.astype(F32) + beside.astype(F32)
-    crossed = lax.ppermute(keep_sum[:, piece:].astype(BF16), "decode", SWAP_CHIP)
 
     (first_half,) = call(
         gate_up_first_kernel,
@@ -516,33 +548,44 @@
     (shared_hidden,) = call(
         gate_up_second_kernel,
         [((total_rows, hidden), BF16)],
-        [SMEM] + [VMEM] * 6,
+        [SMEM] + [VMEM] * 4,
         flops=2 * total_rows * width * hidden,
         moved=4 << 20,
         name="gate_up_second",
         vmem=12,
-    )(after(place, kv_got[0]), tokens, own_weights, first_half, *other)
-    hidden_pieces = spread(shared_hidden)
-    summed = call(
+    )(after(place, *down_got), tokens, own_weights, first_half, other)
+    kv_joined = join(*lax.optimization_barrier(tuple(kv_got) + (routed, shared_hidden))[:3])
+    send, keep = call(
         down_kernel,
-        [((rows, piece), F32)] + [((rows, piece), BF16)] * 3,
-        [SMEM] + [VMEM] * 14,
-        [
-            pltpu.VMEM((total_rows, slots * hidden), BF16),
-            pltpu.VMEM((slots * hidden, piece), BF16),
-        ],
+        [((total_rows, 2 * piece), BF16), ((total_rows, 2 * piece), F32)],
+        [SMEM] + [VMEM] * 7,
+        [pltpu.VMEM((hidden, width), BF16)],
         name="down",
         vmem=14,
-    )(after(place, *kv_got), keep_sum[:, :piece], crossed, *hidden_pieces, *down_got, *down_other)
-    returned = [to_shift(values, -s) for values, s in zip(summed[1:], SHIFTS)]
+    )(after(place, kv_joined), routed, shared_hidden, own_down, down_other, *down_got)
+    beside = lax.ppermute(send, "decode", SWAP_CORE)
+    kv_other = swap_groups(kv_joined)
+    passed = call(
+        pass_kernel,
+        [((rows, piece), F32)] * 4 + [((rows, piece), BF16)] * 4,
+        [VMEM] * 2,
+        name="pass",
+    )(keep, beside)
+    crossed = {s: lax.ppermute(passed[4 + s], "decode", SWAP_CHIP) for s in SHIFTS + (0,)}
+    returned = []
+    for s in SHIFTS:
+        (summed,) = call(add_kernel, [((rows, piece), BF16)], [VMEM] * 2, name="add")(
+            passed[s], crossed[s]
+        )
+        returned.append(to_shift(summed, -s))
     (layer_out,) = call(
-        layer_kernel, [((rows, piece), BF16)], [VMEM] * 5, name="layer"
-    )(resid_share, summed[0], *returned)
+        layer_kernel, [((rows, piece), BF16)], [VMEM] * 6, name="layer"
+    )(resid_share, passed[0], crossed[0], *returned)
 
     handed = call(
         kv_kernel,
         [((QCAP * BLOCK, kv_width), BF16)] * 4,
-        [SMEM] * 3 + [VMEM] * 12,
+        [SMEM] * 3 + [VMEM] * 10,
         [
             pltpu.VMEM((rows, width), F32),
             pltpu.VMEM((rows, kv_width), BF16),
@@ -558,7 +601,7 @@
         *spread(layer_out),
         w_kv,
         *kv_got,
-        *kv_other,
+        kv_other,
     )
     received = [handed[0]] + [
         lax.ppermute(values, "decode", pairs)

time: 174 us -> 160 us (0.920)
  waiting for transfers between devices: 94.7 us -> 74.2 us
  starting transfers between devices: 52.7 us -> 60.2 us
    ppermute x12 -> x15, starting transfers between devices: 18.5 us -> 45.6 us  [to_shift(): lax.ppermute(values, 'expert', [(i, (i + shift) % count) for i in range(c...]
    ppermute x15 -> x11, waiting for transfers between devices: 24.9 us -> 3.8 us  [the longest x4 3.78 us: near_plan(): lax.ppermute(passed[4 + s], 'decode', SWAP_CHIP)]
    ppermute x15 -> x11, starting transfers between devices: 24.9 us -> 11.1 us  [the longest x4 4.12 us: near_plan(): lax.ppermute(passed[4 + s], 'decode', SWAP_CHIP)]
    ppermute x5 -> x1, waiting for transfers between devices: 11.4 us -> 4.04 us  [spread(): across = lax.ppermute(values, 'decode', SWAP_CHIP)]
    ppermute x5 -> x1, starting transfers between devices: 6.18 us -> 1.53 us  [spread(): across = lax.ppermute(values, 'decode', SWAP_CHIP)]
    ppermute x12 -> x15, waiting for transfers between devices: 54.8 us -> 58.5 us  [to_shift(): lax.ppermute(values, 'expert', [(i, (i + shift) % count) for i in range(c...]
    ppermute x1, waiting for transfers between devices: 0.01 us -> 2.45 us  [near_plan(): beside = lax.ppermute(send, 'decode', SWAP_CORE)]
    pallas_call x3 -> x11, Pallas kernels: 4.92 us -> 6.06 us  [the longest x1 2.4 us: near_plan(): call(routed_down_kernel, [((total_rows, width), BF16)], [SMEM] + [VMEM] *...]
  transfers between devices with their start and end apart: 46 -> 33, of which waited for: 19 -> 14; matrix products, arithmetic and copies ran while one was open for 0% -> 0% of each run, Pallas kernels for 4% -> 7%
where the time goes in v4:
time: 160 us; the launch traced here: 159 us
  waiting for transfers between devices  74.2 us (46%)
  starting transfers between devices  60.2 us (38%)
  Pallas kernels  20.8 us (13%)
  local copies, waits for them, and re-layouts  2.47 us (2%)
    ppermute x15, waiting for transfers between devices, to_shift(): lax.ppermute(values, 'expert', [(i, (i + shift) % count) for i in range(c...  58.5 us
    ppermute x15, starting transfers between devices, to_shift(): lax.ppermute(values, 'expert', [(i, (i + shift) % count) for i in range(c...  45.6 us
    pallas_call x1, Pallas kernels, near_plan(): call(lambda *refs: first_kernel(capacity, *refs), [((rows, width), BF16),...  5 us
    ppermute x4, starting transfers between devices, near_plan(): lax.ppermute(passed[4 + s], 'decode', SWAP_CHIP)  4.12 us
    ppermute x3, starting transfers between devices, near_plan(): across = [lax.ppermute(values, 'decode', SWAP_CHIP) for values in arrived]  4.09 us
    ppermute x1, waiting for transfers between devices, spread(): across = lax.ppermute(values, 'decode', SWAP_CHIP)  4.04 us
    ppermute x3, waiting for transfers between devices, near_plan(): lax.ppermute(values, 'decode', pairs)  4.01 us
    ppermute x4, waiting for transfers between devices, near_plan(): lax.ppermute(passed[4 + s], 'decode', SWAP_CHIP)  3.78 us
  transfers between devices with their start and end apart: 33, of which 14 were waited for; matrix products, arithmetic and copies ran while one was open for 0% of the time, Pallas kernels for 7%

profile of v4, /device:TPU:0, one launch (start us, length us, event | category | flops | bytes accessed | tf_op | source)
XLA Modules:
  0.0 159.2 jit_solution(7702350385193454249)
XLA Ops:
  2.5 5.0 %first.1 = (bf16[128,2560]{1,0:T(8,128)(2,1)}, bf16[144,640]{1,0:T(8,128)(2,1)}, bf16[128,640]{1,0:T(8,128)(2,1)}, bf16[640,512]{1,0:T(8,128)(2,1)}, bf16[640,25...) custom-call(s32[3]{0:T(128)} %pad_add_fusion.refs_0_.place, ...), custom_call_target="tpu_custom_call" | custom-call | bytes 6291456 | tf_op jit(solution)/shard_map/first/pallas_call | solution.py:465
  7.6 4.1 %collective-permute-start.9 = (bf16[144,640]{1,0:T(8,128)(2,1)}, bf16[144,640]{1,0:T(8,128)(2,1)S(1)}, u32[]{:S(2)}, u32[]{:S(2)}) collective-permute-start(bf16[144,640]{1,0:T(8,128)(2,1)} %get-tuple-element.48.rest_0_), channel_id=1, source_target_pairs={{0,8},{4,12},{8,0},{12,4},{1,9},{5,13},{9,1},{13,5},{2,10},{6,14},... | collective-permute-start | bytes 552968 | tf_op jit(solution)/shard_map/ppermute | solution.py:172
  11.8 1.8 %collective-permute-start.10 = (bf16[144,640]{1,0:T(8,128)(2,1)}, bf16[144,640]{1,0:T(8,128)(2,1)S(1)}, u32[]{:S(2)}, u32[]{:S(2)}) collective-permute-start(bf16[144,640]{1,0:T(8,128)(2,1)} %get-tuple-element.48.rest_0_), channel_id=1, source_target_pairs={{0,4},{4,8},{8,12},{12,0},{1,5},{5,9},{9,13},{13,1},{2,6},{6,10},{... | collective-permute-start | bytes 552968 | tf_op jit(solution)/shard_map/ppermute | solution.py:172
  13.6 2.0 %collective-permute-start.11 = (bf16[144,640]{1,0:T(8,128)(2,1)}, bf16[144,640]{1,0:T(8,128)(2,1)S(1)}, u32[]{:S(2)}, u32[]{:S(2)}) collective-permute-start(bf16[144,640]{1,0:T(8,128)(2,1)} %get-tuple-element.48.rest_0_), channel_id=1, source_target_pairs={{0,12},{4,0},{8,4},{12,8},{1,13},{5,1},{9,5},{13,9},{2,14},{6,2},{... | collective-permute-start | bytes 552968 | tf_op jit(solution)/shard_map/ppermute | solution.py:172
  15.6 17.5 %collective-permute-done.9.rest_0_.rest_2_ = bf16[144,640]{1,0:T(8,128)(2,1)S(1)} collective-permute-done((bf16[144,640]{1,0:T(8,128)(2,1)}, bf16[144,640]{1,0:T(8,128)(2,1)S(1)}, u32[]{:S(2)}, u32[]{:S(2)}) %collective-permute-start.9) | collective-permute-done | bytes 184352 | tf_op jit(solution)/shard_map/ppermute | solution.py:172
  33.1 2.2 %collective-permute-start.12 = (bf16[144,640]{1,0:T(8,128)(2,1)S(1)}, bf16[144,640]{1,0:T(8,128)(2,1)S(1)}, u32[]{:S(2)}, u32[]{:S(2)}) collective-permute-start(bf16[144,640]{1,0:T(8,128)(2,1)S(1)} %collective-permute-done.9.rest_0_.rest_2_), channel_id=1, source_target_pairs={{0,2},{2,0},{1,3},{3,1},{4,6},{6,4},{5,7},{7,5},{8,10},{10,8},{9,1... | collective-permute-start | bytes 552968 | tf_op jit(solution)/shard_map/ppermute | solution.py:500
  35.4 11.0 %collective-permute-done.6.refs_0_.a = bf16[640,256]{1,0:T(8,128)(2,1)S(1)} collective-permute-done((bf16[640,256]{1,0:T(8,128)(2,1)}, bf16[640,256]{1,0:T(8,128)(2,1)S(1)}, u32[]{:S(2)}, u32[]{:S(2)}) %collective-permute-start.6) | collective-permute-done | bytes 327712 | tf_op jit(solution)/shard_map/ppermute | solution.py:172
  46.4 1.8 %collective-permute-start.14 = (bf16[144,640]{1,0:T(8,128)(2,1)S(1)}, bf16[144,640]{1,0:T(8,128)(2,1)S(1)}, u32[]{:S(2)}, u32[]{:S(2)}) collective-permute-start(bf16[144,640]{1,0:T(8,128)(2,1)S(1)} %collective-permute-done.11.rest_2_.rest_3_), channel_id=1, source_target_pairs={{0,2},{2,0},{1,3},{3,1},{4,6},{6,4},{5,7},{7,5},{8,10},{10,8},{9,1... | collective-permute-start | bytes 552968 | tf_op jit(solution)/shard_map/ppermute | solution.py:500
  48.2 4.3 %collective-permute-done.8.refs_2_.c = bf16[640,256]{1,0:T(8,128)(2,1)S(1)} collective-permute-done((bf16[640,256]{1,0:T(8,128)(2,1)}, bf16[640,256]{1,0:T(8,128)(2,1)S(1)}, u32[]{:S(2)}, u32[]{:S(2)}) %collective-permute-start.8) | collective-permute-done | bytes 327712 | tf_op jit(solution)/shard_map/ppermute | solution.py:172
  53.4 1.6 %collective-permute-start.16 = (bf16[1920,256]{1,0:T(8,128)(2,1)S(1)}, bf16[1920,256]{1,0:T(8,128)(2,1)S(1)}, u32[]{:S(2)}, u32[]{:S(2)}) collective-permute-start(bf16[1920,256]{1,0:T(8,128)(2,1)S(1)} %join.3), channel_id=1, source_target_pairs={{0,16},{16,0},{1,17},{17,1},{2,18},{18,2},{3,19},{19,3},{4,20},{20... | collective-permute-start | bytes 2949128 | tf_op jit(solution)/shard_map/ppermute | solution.py:180
  55.0 13.9 %collective-permute-start = (bf16[128,640]{1,0:T(8,128)(2,1)}, bf16[128,640]{1,0:T(8,128)(2,1)S(1)}, u32[]{:S(2)}, u32[]{:S(2)}) collective-permute-start(bf16[128,640]{1,0:T(8,128)(2,1)} %get-tuple-element.39), channel_id=1, source_target_pairs={{0,8},{4,12},{8,0},{12,4},{1,9},{5,13},{9,1},{13,5},{2,10},{6,14},... | collective-permute-start | bytes 491528 | tf_op jit(solution)/shard_map/ppermute | solution.py:172
  68.9 3.8 %collective-permute-start.2 = (bf16[128,640]{1,0:T(8,128)(2,1)}, bf16[128,640]{1,0:T(8,128)(2,1)S(1)}, u32[]{:S(2)}, u32[]{:S(2)}) collective-permute-start(bf16[128,640]{1,0:T(8,128)(2,1)} %get-tuple-element.41), channel_id=1, source_target_pairs={{0,12},{4,0},{8,4},{12,8},{1,13},{5,1},{9,5},{13,9},{2,14},{6,2},{... | collective-permute-start | bytes 491528 | tf_op jit(solution)/shard_map/ppermute | solution.py:172
  72.7 8.3 %collective-permute-done.refs_0_.a = bf16[128,640]{1,0:T(8,128)(2,1)S(1)} collective-permute-done((bf16[128,640]{1,0:T(8,128)(2,1)}, bf16[128,640]{1,0:T(8,128)(2,1)S(1)}, u32[]{:S(2)}, u32[]{:S(2)}) %collective-permute-start) | collective-permute-done | bytes 163872 | tf_op jit(solution)/shard_map/ppermute | solution.py:172
  81.8 2.1 %collective-permute-start.3 = (bf16[640,256]{1,0:T(8,128)(2,1)}, bf16[640,256]{1,0:T(8,128)(2,1)S(1)}, u32[]{:S(2)}, u32[]{:S(2)}) collective-permute-start(bf16[640,256]{1,0:T(8,128)(2,1)} %get-tuple-element.42), channel_id=1, source_target_pairs={{0,8},{4,12},{8,0},{12,4},{1,9},{5,13},{9,1},{13,5},{2,10},{6,14},... | collective-permute-start | bytes 983048 | tf_op jit(solution)/shard_map/ppermute | solution.py:172
  84.9 2.8 %collective-permute-start.5 = (bf16[640,256]{1,0:T(8,128)(2,1)}, bf16[640,256]{1,0:T(8,128)(2,1)S(1)}, u32[]{:S(2)}, u32[]{:S(2)}) collective-permute-start(bf16[640,256]{1,0:T(8,128)(2,1)} %get-tuple-element.42), channel_id=1, source_target_pairs={{0,12},{4,0},{8,4},{12,8},{1,13},{5,1},{9,5},{13,9},{2,14},{6,2},{... | collective-permute-start | bytes 983048 | tf_op jit(solution)/shard_map/ppermute | solution.py:172
  88.3 3.6 %routed_up.1 = (bf16[512,2560]{1,0:T(8,128)(2,1)S(1)}, bf16[512,512]{1,0:T(8,128)(2,1)S(1)}) custom-call(s32[3]{0:T(128)S(1)} %copy-done.8, bf16[512,1280]{1,0:T(8,128)(2,1)S(1)} %half.1.mine, bf16[512,1280]{1,0:T(8,128)(2,1)S(1)} %collective-permute-done.15.theirs, bf16[1,2560,512]{2,1,0:T(8,128)(2,1)S(1)} %copy-done.11, bf16[1,2560,512]{2,1,0:T(8,128)(2,1)S(1)} %copy-done.12), custom_call_target="tpu_custom_call" | custom-call | flops 2684354560 | bytes 10485760 | tf_op jit(solution)/shard_map/routed_up/pallas_call | solution.py:514
  92.0 1.5 gate_up_first.1.first
  93.5 1.5 gate_up_second.1.hidden
  95.2 2.4 %routed_down.1.routed = bf16[512,2560]{1,0:T(8,128)(2,1)S(1)} custom-call(s32[3]{0:T(128)S(1)} %copy-done.8, bf16[512,512]{1,0:T(8,128)(2,1)S(1)} %get-tuple-element.49.hidden, bf16[144,640]{1,0:T(8,128)(2,1)S(1)} %copy-done.6, bf16[144,640]{1,0:T(8,128)(2,1)S(1)} %collective-permute-done.10.rest_1_, ...), custom_call_target="tpu_custom_call" | custom-call | flops 1342177280 | bytes 6291456 | tf_op jit(solution)/shard_map/routed_down/pallas_call | solution.py:523
  97.7 9.9 %collective-permute-done.3.refs_0_.rest_0_ = bf16[640,256]{1,0:T(8,128)(2,1)S(1)} collective-permute-done((bf16[640,256]{1,0:T(8,128)(2,1)}, bf16[640,256]{1,0:T(8,128)(2,1)S(1)}, u32[]{:S(2)}, u32[]{:S(2)}) %collective-permute-start.3) | collective-permute-done | bytes 327712 | tf_op jit(solution)/shard_map/ppermute | solution.py:172
  107.7 1.7 %down.1 = (bf16[512,1280]{1,0:T(8,128)(2,1)S(1)}, f32[512,1280]{1,0:T(8,128)S(1)}) custom-call(s32[3]{0:T(128)S(1)} %copy-done.8, bf16[512,2560]{1,0:T(8,128)(2,1)S(1)} %routed_down.1.routed, bf16[512,256]{1,0:T(8,128)(2,1)S(1)} %gate_up_second.1.hidden, bf16[256,640]{1,0:T(8,128)(2,1)S(1)} %copy-done.5, bf16[384,640]{1,0:T(8,128)(2,1)S(1)} %collective-permute-done.17.other, ...), custom_call_target="tpu_custom_call" | custom-call | tf_op jit(solution)/shard_map/down/pallas_call | solution.py:558
  110.0 2.5 %collective-permute-done.18.beside = bf16[512,1280]{1,0:T(8,128)(2,1)S(1)} collective-permute-done((bf16[512,1280]{1,0:T(8,128)(2,1)S(1)}, bf16[512,1280]{1,0:T(8,128)(2,1)S(1)}, u32[]{:S(2)}, u32[]{:S(2)}) %collective-permute-start.18) | collective-permute-done | bytes 1310752 | tf_op jit(solution)/shard_map/ppermute | solution.py:566
  112.7 1.6 collective-permute-start.24
  116.8 3.0 %collective-permute-done.24.b = bf16[128,640]{1,0:T(8,128)(2,1)S(1)} collective-permute-done((bf16[128,640]{1,0:T(8,128)(2,1)S(1)}, bf16[128,640]{1,0:T(8,128)(2,1)S(1)}, u32[]{:S(2)}, u32[]{:S(2)}) %collective-permute-start.24) | collective-permute-done | bytes 163872 | tf_op jit(solution)/shard_map/ppermute | solution.py:574
  119.9 5.9 %collective-permute-start.25 = (bf16[128,640]{1,0:T(8,128)(2,1)S(1)}, bf16[128,640]{1,0:T(8,128)(2,1)S(1)}, u32[]{:S(2)}, u32[]{:S(2)}) collective-permute-start(bf16[128,640]{1,0:T(8,128)(2,1)S(1)} %add.9), channel_id=1, source_target_pairs={{0,4},{4,8},{8,12},{12,0},{1,5},{5,9},{9,13},{13,1},{2,6},{6,10},{... | collective-permute-start | bytes 491528 | tf_op jit(solution)/shard_map/ppermute | solution.py:172
  126.9 7.8 %collective-permute-start.21 = (bf16[128,640]{1,0:T(8,128)(2,1)S(1)}, bf16[128,640]{1,0:T(8,128)(2,1)S(1)}, u32[]{:S(2)}, u32[]{:S(2)}) collective-permute-start(bf16[128,640]{1,0:T(8,128)(2,1)S(1)} %add.7), channel_id=1, source_target_pairs={{0,8},{4,12},{8,0},{12,4},{1,9},{5,13},{9,1},{13,5},{2,10},{6,14},... | collective-permute-start | bytes 491528 | tf_op jit(solution)/shard_map/ppermute | solution.py:172
  134.7 6.8 %collective-permute-done.21.a = bf16[128,640]{1,0:T(8,128)(2,1)S(1)} collective-permute-done((bf16[128,640]{1,0:T(8,128)(2,1)S(1)}, bf16[128,640]{1,0:T(8,128)(2,1)S(1)}, u32[]{:S(2)}, u32[]{:S(2)}) %collective-permute-start.21) | collective-permute-done | bytes 163872 | tf_op jit(solution)/shard_map/ppermute | solution.py:172
  142.3 1.5 collective-permute-start.27
  143.8 4.0 %collective-permute-done.27.c = bf16[128,640]{1,0:T(8,128)(2,1)S(1)} collective-permute-done((bf16[128,640]{1,0:T(8,128)(2,1)}, bf16[128,640]{1,0:T(8,128)(2,1)S(1)}, u32[]{:S(2)}, u32[]{:S(2)}) %collective-permute-start.27) | collective-permute-done | bytes 163872 | tf_op jit(solution)/shard_map/ppermute | solution.py:184
  151.8 1.6 %collective-permute-start.31 = (bf16[64,512]{1,0:T(8,128)(2,1)S(1)}, bf16[64,512]{1,0:T(8,128)(2,1)S(1)}, u32[]{:S(2)}, u32[]{:S(2)}) collective-permute-start(bf16[64,512]{1,0:T(8,128)(2,1)S(1)} %get-tuple-element.70), channel_id=1, source_target_pairs={{0,2},{2,0},{1,3},{3,1},{4,6},{6,4},{5,7},{7,5},{8,10},{10,8},{9,1... | collective-permute-start | bytes 196616 | tf_op jit(solution)/shard_map/ppermute | solution.py:607
  153.5 2.6 %collective-permute-done.31.c = bf16[64,512]{1,0:T(8,128)(2,1)S(1)} collective-permute-done((bf16[64,512]{1,0:T(8,128)(2,1)S(1)}, bf16[64,512]{1,0:T(8,128)(2,1)S(1)}, u32[]{:S(2)}, u32[]{:S(2)}) %collective-permute-start.31) | collective-permute-done | bytes 65568 | tf_op jit(solution)/shard_map/ppermute | solution.py:607
  157.5 1.7 %hand.1 = bf16[64,4,512]{2,1,0:T(4,128)(2,1)} custom-call(s32[3]{0:T(128)S(1)} %copy-done.8, bf16[64,512]{1,0:T(8,128)(2,1)S(1)} %get-tuple-element.68.a, bf16[64,512]{1,0:T(8,128)(2,1)S(1)} %collective-permute-done.30.b, bf16[64,512]{1,0:T(8,128)(2,1)S(1)} %collective-permute-done.31.c, bf16[64,512]{1,0:T(8,128)(2,1)S(1)} %collective-permute-done.32.d), custom_call_target="tpu_custom_call" | custom-call | tf_op jit(solution)/shard_map/hand/pallas_call | solution.py:610
  (82 shorter events, 16.4 us)
Async XLA Ops:
  7.6 25.5 %collective-permute-start.9 = (bf16[144,640]{1,0:T(8,128)(2,1)}, bf16[144,640]{1,0:T(8,128)(2,1)S(1)}, u32[]{:S(2)}, u32[]{:S(2)}) collective-permute-start(bf16[144,640]{1,0:T(8,128)(2,1)} %get-tuple-element.48.rest_0_), channel_id=1, source_target_pairs={{0,8},{4,12},{8,0},{12,4},{1,9},{5,13},{9,1},{13,5},{2,10},{6,14},... | collective-permute-start | bytes 552968 | tf_op jit(solution)/shard_map/ppermute | solution.py:172
  11.7 34.7 %collective-permute-start.6 = (bf16[640,256]{1,0:T(8,128)(2,1)}, bf16[640,256]{1,0:T(8,128)(2,1)S(1)}, u32[]{:S(2)}, u32[]{:S(2)}) collective-permute-start(bf16[640,256]{1,0:T(8,128)(2,1)} %get-tuple-element.43), channel_id=1, source_target_pairs={{0,8},{4,12},{8,0},{12,4},{1,9},{5,13},{9,1},{13,5},{2,10},{6,14},... | collective-permute-start | bytes 983048 | tf_op jit(solution)/shard_map/ppermute | solution.py:172
  11.8 21.3 %collective-permute-start.10 = (bf16[144,640]{1,0:T(8,128)(2,1)}, bf16[144,640]{1,0:T(8,128)(2,1)S(1)}, u32[]{:S(2)}, u32[]{:S(2)}) collective-permute-start(bf16[144,640]{1,0:T(8,128)(2,1)} %get-tuple-element.48.rest_0_), channel_id=1, source_target_pairs={{0,4},{4,8},{8,12},{12,0},{1,5},{5,9},{9,13},{13,1},{2,6},{6,10},{... | collective-permute-start | bytes 552968 | tf_op jit(solution)/shard_map/ppermute | solution.py:172
  13.6 21.7 %collective-permute-start.11 = (bf16[144,640]{1,0:T(8,128)(2,1)}, bf16[144,640]{1,0:T(8,128)(2,1)S(1)}, u32[]{:S(2)}, u32[]{:S(2)}) collective-permute-start(bf16[144,640]{1,0:T(8,128)(2,1)} %get-tuple-element.48.rest_0_), channel_id=1, source_target_pairs={{0,12},{4,0},{8,4},{12,8},{1,13},{5,1},{9,5},{13,9},{2,14},{6,2},{... | collective-permute-start | bytes 552968 | tf_op jit(solution)/shard_map/ppermute | solution.py:172
  15.6 32.6 %collective-permute-start.7 = (bf16[640,256]{1,0:T(8,128)(2,1)}, bf16[640,256]{1,0:T(8,128)(2,1)S(1)}, u32[]{:S(2)}, u32[]{:S(2)}) collective-permute-start(bf16[640,256]{1,0:T(8,128)(2,1)} %get-tuple-element.44), channel_id=1, source_target_pairs={{0,4},{4,8},{8,12},{12,0},{1,5},{5,9},{9,13},{13,1},{2,6},{6,10},{... | collective-permute-start | bytes 983048 | tf_op jit(solution)/shard_map/ppermute | solution.py:172
  33.1 19.4 %collective-permute-start.8 = (bf16[640,256]{1,0:T(8,128)(2,1)}, bf16[640,256]{1,0:T(8,128)(2,1)S(1)}, u32[]{:S(2)}, u32[]{:S(2)}) collective-permute-start(bf16[640,256]{1,0:T(8,128)(2,1)} %get-tuple-element.45), channel_id=1, source_target_pairs={{0,12},{4,0},{8,4},{12,8},{1,13},{5,1},{9,5},{13,9},{2,14},{6,2},{... | collective-permute-start | bytes 983048 | tf_op jit(solution)/shard_map/ppermute | solution.py:172
  33.1 19.5 %collective-permute-start.12 = (bf16[144,640]{1,0:T(8,128)(2,1)S(1)}, bf16[144,640]{1,0:T(8,128)(2,1)S(1)}, u32[]{:S(2)}, u32[]{:S(2)}) collective-permute-start(bf16[144,640]{1,0:T(8,128)(2,1)S(1)} %collective-permute-done.9.rest_0_.rest_2_), channel_id=1, source_target_pairs={{0,2},{2,0},{1,3},{3,1},{4,6},{6,4},{5,7},{7,5},{8,10},{10,8},{9,1... | collective-permute-start | bytes 552968 | tf_op jit(solution)/shard_map/ppermute | solution.py:500
  35.3 17.3 %collective-permute-start.13 = (bf16[144,640]{1,0:T(8,128)(2,1)S(1)}, bf16[144,640]{1,0:T(8,128)(2,1)S(1)}, u32[]{:S(2)}, u32[]{:S(2)}) collective-permute-start(bf16[144,640]{1,0:T(8,128)(2,1)S(1)} %collective-permute-done.10.rest_1_), channel_id=1, source_target_pairs={{0,2},{2,0},{1,3},{3,1},{4,6},{6,4},{5,7},{7,5},{8,10},{10,8},{9,1... | collective-permute-start | bytes 552968 | tf_op jit(solution)/shard_map/ppermute | solution.py:500
  46.4 6.2 %collective-permute-start.14 = (bf16[144,640]{1,0:T(8,128)(2,1)S(1)}, bf16[144,640]{1,0:T(8,128)(2,1)S(1)}, u32[]{:S(2)}, u32[]{:S(2)}) collective-permute-start(bf16[144,640]{1,0:T(8,128)(2,1)S(1)} %collective-permute-done.11.rest_2_.rest_3_), channel_id=1, source_target_pairs={{0,2},{2,0},{1,3},{3,1},{4,6},{6,4},{5,7},{7,5},{8,10},{10,8},{9,1... | collective-permute-start | bytes 552968 | tf_op jit(solution)/shard_map/ppermute | solution.py:500
  53.3 34.5 %collective-permute-start.15 = (bf16[512,1280]{1,0:T(8,128)(2,1)S(1)}, bf16[512,1280]{1,0:T(8,128)(2,1)S(1)}, u32[]{:S(2)}, u32[]{:S(2)}) collective-permute-start(bf16[512,1280]{1,0:T(8,128)(2,1)S(1)} %half.1.mine), channel_id=1, source_target_pairs={{0,1},{1,0},{2,3},{3,2},{4,5},{5,4},{6,7},{7,6},{8,9},{9,8},{10,11... | collective-permute-start | bytes 3932168 | tf_op jit(solution)/shard_map/ppermute | solution.py:507
  53.4 40.1 %collective-permute-start.16 = (bf16[1920,256]{1,0:T(8,128)(2,1)S(1)}, bf16[1920,256]{1,0:T(8,128)(2,1)S(1)}, u32[]{:S(2)}, u32[]{:S(2)}) collective-permute-start(bf16[1920,256]{1,0:T(8,128)(2,1)S(1)} %join.3), channel_id=1, source_target_pairs={{0,16},{16,0},{1,17},{17,1},{2,18},{18,2},{3,19},{19,3},{4,20},{20... | collective-permute-start | bytes 2949128 | tf_op jit(solution)/shard_map/ppermute | solution.py:180
  55.0 26.0 %collective-permute-start = (bf16[128,640]{1,0:T(8,128)(2,1)}, bf16[128,640]{1,0:T(8,128)(2,1)S(1)}, u32[]{:S(2)}, u32[]{:S(2)}) collective-permute-start(bf16[128,640]{1,0:T(8,128)(2,1)} %get-tuple-element.39), channel_id=1, source_target_pairs={{0,8},{4,12},{8,0},{12,4},{1,9},{5,13},{9,1},{13,5},{2,10},{6,14},... | collective-permute-start | bytes 491528 | tf_op jit(solution)/shard_map/ppermute | solution.py:172
  68.9 12.1 %collective-permute-start.1 = (bf16[128,640]{1,0:T(8,128)(2,1)}, bf16[128,640]{1,0:T(8,128)(2,1)S(1)}, u32[]{:S(2)}, u32[]{:S(2)}) collective-permute-start(bf16[128,640]{1,0:T(8,128)(2,1)} %get-tuple-element.40), channel_id=1, source_target_pairs={{0,4},{4,8},{8,12},{12,0},{1,5},{5,9},{9,13},{13,1},{2,6},{6,10},{... | collective-permute-start | bytes 491528 | tf_op jit(solution)/shard_map/ppermute | solution.py:172
  68.9 12.9 %collective-permute-start.2 = (bf16[128,640]{1,0:T(8,128)(2,1)}, bf16[128,640]{1,0:T(8,128)(2,1)S(1)}, u32[]{:S(2)}, u32[]{:S(2)}) collective-permute-start(bf16[128,640]{1,0:T(8,128)(2,1)} %get-tuple-element.41), channel_id=1, source_target_pairs={{0,12},{4,0},{8,4},{12,8},{1,13},{5,1},{9,5},{13,9},{2,14},{6,2},{... | collective-permute-start | bytes 491528 | tf_op jit(solution)/shard_map/ppermute | solution.py:172
  81.8 25.8 %collective-permute-start.3 = (bf16[640,256]{1,0:T(8,128)(2,1)}, bf16[640,256]{1,0:T(8,128)(2,1)S(1)}, u32[]{:S(2)}, u32[]{:S(2)}) collective-permute-start(bf16[640,256]{1,0:T(8,128)(2,1)} %get-tuple-element.42), channel_id=1, source_target_pairs={{0,8},{4,12},{8,0},{12,4},{1,9},{5,13},{9,1},{13,5},{2,10},{6,14},... | collective-permute-start | bytes 983048 | tf_op jit(solution)/shard_map/ppermute | solution.py:172
  83.9 23.7 %collective-permute-start.4 = (bf16[640,256]{1,0:T(8,128)(2,1)}, bf16[640,256]{1,0:T(8,128)(2,1)S(1)}, u32[]{:S(2)}, u32[]{:S(2)}) collective-permute-start(bf16[640,256]{1,0:T(8,128)(2,1)} %get-tuple-element.42), channel_id=1, source_target_pairs={{0,4},{4,8},{8,12},{12,0},{1,5},{5,9},{9,13},{13,1},{2,6},{6,10},{... | collective-permute-start | bytes 983048 | tf_op jit(solution)/shard_map/ppermute | solution.py:172
  84.9 22.7 %collective-permute-start.5 = (bf16[640,256]{1,0:T(8,128)(2,1)}, bf16[640,256]{1,0:T(8,128)(2,1)S(1)}, u32[]{:S(2)}, u32[]{:S(2)}) collective-permute-start(bf16[640,256]{1,0:T(8,128)(2,1)} %get-tuple-element.42), channel_id=1, source_target_pairs={{0,12},{4,0},{8,4},{12,8},{1,13},{5,1},{9,5},{13,9},{2,14},{6,2},{... | collective-permute-start | bytes 983048 | tf_op jit(solution)/shard_map/ppermute | solution.py:172
  87.8 19.9 %collective-permute-start.17 = (bf16[384,640]{1,0:T(8,128)(2,1)S(1)}, bf16[384,640]{1,0:T(8,128)(2,1)S(1)}, u32[]{:S(2)}, u32[]{:S(2)}) collective-permute-start(bf16[384,640]{1,0:T(8,128)(2,1)S(1)} %join.5), channel_id=1, source_target_pairs={{0,16},{16,0},{1,17},{17,1},{2,18},{18,2},{3,19},{19,3},{4,20},{20... | collective-permute-start | bytes 1474568 | tf_op jit(solution)/shard_map/ppermute | solution.py:180
  109.3 3.1 %collective-permute-start.18 = (bf16[512,1280]{1,0:T(8,128)(2,1)S(1)}, bf16[512,1280]{1,0:T(8,128)(2,1)S(1)}, u32[]{:S(2)}, u32[]{:S(2)}) collective-permute-start(bf16[512,1280]{1,0:T(8,128)(2,1)S(1)} %get-tuple-element.59), channel_id=1, source_target_pairs={{0,1},{1,0},{2,3},{3,2},{4,5},{5,4},{6,7},{7,6},{8,9},{9,8},{10,11... | collective-permute-start | bytes 3932168 | tf_op jit(solution)/shard_map/ppermute | solution.py:566
  109.4 38.4 %collective-permute-start.29 = (bf16[1920,256]{1,0:T(8,128)(2,1)S(1)}, bf16[1920,256]{1,0:T(8,128)(2,1)S(1)}, u32[]{:S(2)}, u32[]{:S(2)}) collective-permute-start(bf16[1920,256]{1,0:T(8,128)(2,1)S(1)} %join.4), channel_id=1, source_target_pairs={{0,16},{16,0},{1,17},{17,1},{2,18},{18,2},{3,19},{19,3},{4,20},{20... | collective-permute-start | bytes 2949128 | tf_op jit(solution)/shard_map/ppermute | solution.py:180
  112.7 7.1 %collective-permute-start.24 = (bf16[128,640]{1,0:T(8,128)(2,1)S(1)}, bf16[128,640]{1,0:T(8,128)(2,1)S(1)}, u32[]{:S(2)}, u32[]{:S(2)}) collective-permute-start(bf16[128,640]{1,0:T(8,128)(2,1)S(1)} %get-tuple-element.67), channel_id=1, source_target_pairs={{0,2},{2,0},{1,3},{3,1},{4,6},{6,4},{5,7},{7,5},{8,10},{10,8},{9,1... | collective-permute-start | bytes 491528 | tf_op jit(solution)/shard_map/ppermute | solution.py:574
  114.3 11.5 %collective-permute-start.22 = (bf16[128,640]{1,0:T(8,128)(2,1)S(1)}, bf16[128,640]{1,0:T(8,128)(2,1)S(1)}, u32[]{:S(2)}, u32[]{:S(2)}) collective-permute-start(bf16[128,640]{1,0:T(8,128)(2,1)S(1)} %get-tuple-element.65), channel_id=1, source_target_pairs={{0,2},{2,0},{1,3},{3,1},{4,6},{6,4},{5,7},{7,5},{8,10},{10,8},{9,1... | collective-permute-start | bytes 491528 | tf_op jit(solution)/shard_map/ppermute | solution.py:574
  114.8 12.0 %collective-permute-start.20 = (bf16[128,640]{1,0:T(8,128)(2,1)S(1)}, bf16[128,640]{1,0:T(8,128)(2,1)S(1)}, u32[]{:S(2)}, u32[]{:S(2)}) collective-permute-start(bf16[128,640]{1,0:T(8,128)(2,1)S(1)} %get-tuple-element.63), channel_id=1, source_target_pairs={{0,2},{2,0},{1,3},{3,1},{4,6},{6,4},{5,7},{7,5},{8,10},{10,8},{9,1... | collective-permute-start | bytes 491528 | tf_op jit(solution)/shard_map/ppermute | solution.py:574
  116.3 18.3 %collective-permute-start.19 = (bf16[128,640]{1,0:T(8,128)(2,1)S(1)}, bf16[128,640]{1,0:T(8,128)(2,1)S(1)}, u32[]{:S(2)}, u32[]{:S(2)}) collective-permute-start(bf16[128,640]{1,0:T(8,128)(2,1)S(1)} %get-tuple-element.61), channel_id=1, source_target_pairs={{0,2},{2,0},{1,3},{3,1},{4,6},{6,4},{5,7},{7,5},{8,10},{10,8},{9,1... | collective-permute-start | bytes 491528 | tf_op jit(solution)/shard_map/ppermute | solution.py:574
  119.9 14.8 %collective-permute-start.25 = (bf16[128,640]{1,0:T(8,128)(2,1)S(1)}, bf16[128,640]{1,0:T(8,128)(2,1)S(1)}, u32[]{:S(2)}, u32[]{:S(2)}) collective-permute-start(bf16[128,640]{1,0:T(8,128)(2,1)S(1)} %add.9), channel_id=1, source_target_pairs={{0,4},{4,8},{8,12},{12,0},{1,5},{5,9},{9,13},{13,1},{2,6},{6,10},{... | collective-permute-start | bytes 491528 | tf_op jit(solution)/shard_map/ppermute | solution.py:172
  125.9 8.8 %collective-permute-start.23 = (bf16[128,640]{1,0:T(8,128)(2,1)S(1)}, bf16[128,640]{1,0:T(8,128)(2,1)S(1)}, u32[]{:S(2)}, u32[]{:S(2)}) collective-permute-start(bf16[128,640]{1,0:T(8,128)(2,1)S(1)} %add.8), channel_id=1, source_target_pairs={{0,12},{4,0},{8,4},{12,8},{1,13},{5,1},{9,5},{13,9},{2,14},{6,2},{... | collective-permute-start | bytes 491528 | tf_op jit(solution)/shard_map/ppermute | solution.py:172
  126.9 14.6 %collective-permute-start.21 = (bf16[128,640]{1,0:T(8,128)(2,1)S(1)}, bf16[128,640]{1,0:T(8,128)(2,1)S(1)}, u32[]{:S(2)}, u32[]{:S(2)}) collective-permute-start(bf16[128,640]{1,0:T(8,128)(2,1)S(1)} %add.7), channel_id=1, source_target_pairs={{0,8},{4,12},{8,0},{12,4},{1,9},{5,13},{9,1},{13,5},{2,10},{6,14},... | collective-permute-start | bytes 491528 | tf_op jit(solution)/shard_map/ppermute | solution.py:172
  142.3 5.6 %collective-permute-start.27 = (bf16[128,640]{1,0:T(8,128)(2,1)}, bf16[128,640]{1,0:T(8,128)(2,1)S(1)}, u32[]{:S(2)}, u32[]{:S(2)}) collective-permute-start(bf16[128,640]{1,0:T(8,128)(2,1)} %layer.1.a), channel_id=1, source_target_pairs={{0,2},{2,0},{1,3},{3,1},{4,6},{6,4},{5,7},{7,5},{8,10},{10,8},{9,1... | collective-permute-start | bytes 491528 | tf_op jit(solution)/shard_map/ppermute | solution.py:184
  143.8 4.1 %collective-permute-start.26 = (bf16[128,640]{1,0:T(8,128)(2,1)}, bf16[128,640]{1,0:T(8,128)(2,1)S(1)}, u32[]{:S(2)}, u32[]{:S(2)}) collective-permute-start(bf16[128,640]{1,0:T(8,128)(2,1)} %layer.1.a), channel_id=1, source_target_pairs={{0,1},{1,0},{2,3},{3,2},{4,5},{5,4},{6,7},{7,6},{8,9},{9,8},{10,11... | collective-permute-start | bytes 491528 | tf_op jit(solution)/shard_map/ppermute | solution.py:185
  151.6 1.9 %collective-permute-start.30 = (bf16[64,512]{1,0:T(8,128)(2,1)S(1)}, bf16[64,512]{1,0:T(8,128)(2,1)S(1)}, u32[]{:S(2)}, u32[]{:S(2)}) collective-permute-start(bf16[64,512]{1,0:T(8,128)(2,1)S(1)} %get-tuple-element.69), channel_id=1, source_target_pairs={{0,1},{1,0},{2,3},{3,2},{4,5},{5,4},{6,7},{7,6},{8,9},{9,8},{10,11... | collective-permute-start | bytes 196616 | tf_op jit(solution)/shard_map/ppermute | solution.py:607
  151.8 4.4 %collective-permute-start.31 = (bf16[64,512]{1,0:T(8,128)(2,1)S(1)}, bf16[64,512]{1,0:T(8,128)(2,1)S(1)}, u32[]{:S(2)}, u32[]{:S(2)}) collective-permute-start(bf16[64,512]{1,0:T(8,128)(2,1)S(1)} %get-tuple-element.70), channel_id=1, source_target_pairs={{0,2},{2,0},{1,3},{3,1},{4,6},{6,4},{5,7},{7,5},{8,10},{10,8},{9,1... | collective-permute-start | bytes 196616 | tf_op jit(solution)/shard_map/ppermute | solution.py:607
  153.4 4.1 %collective-permute-start.32 = (bf16[64,512]{1,0:T(8,128)(2,1)S(1)}, bf16[64,512]{1,0:T(8,128)(2,1)S(1)}, u32[]{:S(2)}, u32[]{:S(2)}) collective-permute-start(bf16[64,512]{1,0:T(8,128)(2,1)S(1)} %get-tuple-element.71), channel_id=1, source_target_pairs={{0,3},{3,0},{1,2},{2,1},{4,7},{7,4},{5,6},{6,5},{8,11},{11,8},{9,1... | collective-permute-start | bytes 196616 | tf_op jit(solution)/shard_map/ppermute | solution.py:607
  (15 other events, 302.7 us)

commit v5 on v4

--- a/solution.py
+++ b/solution.py
@@ -198,7 +198,8 @@
 def first_kernel(
     capacity, place, resid, gain, score, ids, gate, up, down, kv, moe_in, message, share, own, *rest
 ):
-    messages, downs, kv_half, own_down, sem = rest[:3], rest[3:6], rest[6], rest[7], rest[8]
+    messages, both, kv_half, own_down, sem = rest[:3], rest[3:6], rest[6], rest[7], rest[8]
+    top = message.shape[0]
     zone, slot, group = place[0], place[1], place[2]
     count = 4
     hidden = gate.shape[1] // count
@@ -217,7 +218,7 @@
             )
     for i, shift in enumerate(SHIFTS):
         start = lax.rem(zone + shift, count) * hidden + group * half
-        move(down.at[pl.ds(pl.multiple_of(start, 128), half), :], downs[i])
+        move(down.at[pl.ds(pl.multiple_of(start, 128), half), :], both[i].at[top:, :])
     move(down.at[pl.ds(pl.multiple_of(zone * hidden, 128), hidden), :], own_down)
     start = group * kv_half.shape[1]
     move(kv.at[:, pl.ds(pl.multiple_of(start, 128), kv_half.shape[1])], kv_half)
@@ -235,7 +236,7 @@
     piece = message.shape[1]
     values = resid[...].astype(F32)
     power = jnp.mean(values * values, axis=-1, keepdims=True)
-    moe_in[...] = (values * lax.rsqrt(power + 1e-05) * gain[...]).astype(BF16)
+    moe_in[...] = (values * lax.rsqrt(power + 1e-05) * gain[...][None, :]).astype(BF16)
     message[:rows, :] = moe_in[:, lanes(slot, piece)]
     share[...] = resid[:, lanes(slot, piece)]
     first = lax.broadcasted_iota(jnp.int32, (rows, rows), 0)
@@ -252,6 +253,8 @@
     message[rows:, :] = jnp.zeros((META, piece), BF16)
     for i, part in enumerate((high, middle, low, ids[...].astype(F32).astype(BF16))):
         message[rows:, i * rows : (i + 1) * rows] = jnp.broadcast_to(part, (META, rows))
+    for target in both:
+        target[:top, :] = message[...]
     for copy in copies:
         copy.wait()
 
@@ -394,7 +397,7 @@
         full[:, lanes(slot ^ j, piece)] = part[...].astype(F32)
     values = full[...]
     power = jnp.mean(values * values, axis=-1, keepdims=True)
-    ready[...] = (values * lax.rsqrt(power + 1e-05) * gain[...]).astype(BF16)
+    ready[...] = (values * lax.rsqrt(power + 1e-05) * gain[...][None, :]).astype(BF16)
     near = own.shape[0]
     half = own.shape[1] // 2
     for part, pieces in ((0, got), (1, other)):
@@ -471,7 +474,7 @@
             ((near, 2 * hidden), BF16),
         ]
         + [((near, hidden), BF16)] * 3
-        + [((half, piece), BF16)] * 3
+        + [((rows + META + half, piece), BF16)] * 3
         + [((near, kv_width // 2), BF16), ((hidden, piece), BF16)],
         [SMEM] + [VMEM] * 4 + [ANY] * 4,
         [pltpu.SemaphoreType.DMA((15,))],
@@ -481,7 +484,7 @@
     )(
         place,
         resid,
-        moe_gain.reshape(1, width),
+        moe_gain,
         gate_score.reshape(1, rows),
         expert_ids.reshape(1, rows),
         shared_gate,
@@ -490,12 +493,17 @@
         w_kv,
     )
     moe_in, message, resid_share, own_weights = first[:4]
-    weight_messages, down_messages, kv_half, own_down = first[4:7], first[7:10], *first[10:]
-
-    arrived = [to_shift(message, s) for s in SHIFTS]
+    weight_messages, mixed_messages, kv_half, own_down = first[4:7], first[7:10], *first[10:]
+
+    mixed = [to_shift(values, s) for values, s in zip(mixed_messages, SHIFTS)]
+    top = rows + META
+    arrived = [values[:top] for values in mixed]
     got = [to_shift(values, s) for values, s in zip(weight_messages, SHIFTS)]
     joined = join(*got)
     other = swap_groups(joined)
+
+    down_got = [values[top:] for values in mixed]
+    down_other = swap_groups(join(*down_got))
 
     across = [lax.ppermute(values, "decode", SWAP_CHIP) for values in arrived]
     (token_half,) = call(
@@ -506,10 +514,7 @@
     )(after(place, joined), moe_in, *arrived, *across)
     token_rest = lax.ppermute(token_half, "decode", SWAP_CORE)
 
-    down_got = [to_shift(values, s) for values, s in zip(down_messages, SHIFTS)]
-    down_other = swap_groups(join(*down_got))
-
-    kv_half = after(kv_half, *down_got)
+    kv_half = after(kv_half, joined)
     kv_got = [to_shift(kv_half, s) for s in SHIFTS]
     tokens, routed_hidden = call(
         routed_up_kernel,
@@ -544,7 +549,7 @@
         moved=4 << 20,
         name="gate_up_first",
         vmem=12,
-    )(place, tokens, own_weights, *got)
+    )(after(place, routed), tokens, own_weights, *got)
     (shared_hidden,) = call(
         gate_up_second_kernel,
         [((total_rows, hidden), BF16)],
@@ -553,7 +558,7 @@
         moved=4 << 20,
         name="gate_up_second",
         vmem=12,
-    )(after(place, *down_got), tokens, own_weights, first_half, other)
+    )(place, tokens, own_weights, first_half, other)
     kv_joined = join(*lax.optimization_barrier(tuple(kv_got) + (routed, shared_hidden))[:3])
     send, keep = call(
         down_kernel,
@@ -597,7 +602,7 @@
         place,
         req_owner,
         req_blocks,
-        attn_gain.reshape(1, width),
+        attn_gain,
         *spread(layer_out),
         w_kv,
         *kv_got,

time: 160 us -> 153 us (0.956)
  starting transfers between devices: 60.2 us -> 43.5 us
  waiting for transfers between devices: 74.2 us -> 85.7 us
    ppermute x15 -> x12, starting transfers between devices: 45.6 us -> 27.6 us  [to_shift(): lax.ppermute(values, 'expert', [(i, (i + shift) % count) for i in range(c...]
    ppermute x3, waiting for transfers between devices: 0.01 us -> 17.2 us  [swap_groups(): return lax.ppermute(values, 'groups', SWAP_GROUP)]
    ppermute x15 -> x12, waiting for transfers between devices: 58.5 us -> 46.4 us  [to_shift(): lax.ppermute(values, 'expert', [(i, (i + shift) % count) for i in range(c...]
    ppermute x4, waiting for transfers between devices: 3.78 us -> 8.28 us  [near_plan(): lax.ppermute(passed[4 + s], 'decode', SWAP_CHIP)]
    ppermute x3, waiting for transfers between devices: 0.01 us -> 3 us  [near_plan(): across = [lax.ppermute(values, 'decode', SWAP_CHIP) for values in arrived]]
  transfers between devices with their start and end apart: 33 -> 30, of which waited for: 14 -> 19; matrix products, arithmetic and copies ran while one was open for 0% -> 0% of each run, Pallas kernels for 7% -> 7%
where the time goes in v5:
time: 153 us
  waiting for transfers between devices  85.7 us (56%)
  starting transfers between devices  43.5 us (28%)
  Pallas kernels  20.9 us (14%)
    ppermute x12, waiting for transfers between devices, to_shift(): lax.ppermute(values, 'expert', [(i, (i + shift) % count) for i in range(c...  46.4 us
    ppermute x12, starting transfers between devices, to_shift(): lax.ppermute(values, 'expert', [(i, (i + shift) % count) for i in range(c...  27.6 us
    ppermute x3, waiting for transfers between devices, swap_groups(): return lax.ppermute(values, 'groups', SWAP_GROUP)  17.2 us
    ppermute x4, waiting for transfers between devices, near_plan(): lax.ppermute(passed[4 + s], 'decode', SWAP_CHIP)  8.28 us
    pallas_call x1, Pallas kernels, near_plan(): call(lambda *refs: first_kernel(capacity, *refs), [((rows, width), BF16),...  5.2 us
    ppermute x3, starting transfers between devices, near_plan(): across = [lax.ppermute(values, 'decode', SWAP_CHIP) for values in arrived]  4.54 us
    ppermute x4, starting transfers between devices, near_plan(): lax.ppermute(passed[4 + s], 'decode', SWAP_CHIP)  4.12 us
    ppermute x1, waiting for transfers between devices, spread(): across = lax.ppermute(values, 'decode', SWAP_CHIP)  4.07 us
  transfers between devices with their start and end apart: 30, of which 19 were waited for; matrix products, arithmetic and copies ran while one was open for 0% of the time, Pallas kernels for 7%

profile of v5, /device:TPU:0, one launch (start us, length us, event | category | flops | bytes accessed | tf_op | source)
XLA Modules:
  0.0 152.7 jit_solution(201891924503529140)
XLA Ops:
  1.3 5.2 %first.1 = (bf16[128,2560]{1,0:T(8,128)(2,1)}, bf16[144,640]{1,0:T(8,128)(2,1)}, bf16[128,640]{1,0:T(8,128)(2,1)}, bf16[640,512]{1,0:T(8,128)(2,1)}, bf16[640,25...) custom-call(s32[3]{0:T(128)} %pad_add_fusion.refs_0_.place, ...), custom_call_target="tpu_custom_call" | custom-call | bytes 6291456 | tf_op jit(solution)/shard_map/first/pallas_call | solution.py:468
  6.5 3.1 %collective-permute-start.7 = (bf16[272,640]{1,0:T(8,128)(2,1)}, bf16[272,640]{1,0:T(8,128)(2,1)S(1)}, u32[]{:S(2)}, u32[]{:S(2)}) collective-permute-start(bf16[272,640]{1,0:T(8,128)(2,1)} %get-tuple-element.46), channel_id=1, source_target_pairs={{0,4},{4,8},{8,12},{12,0},{1,5},{5,9},{9,13},{13,1},{2,6},{6,10},{... | collective-permute-start | bytes 1044488 | tf_op jit(solution)/shard_map/ppermute | solution.py:172
  9.6 2.1 %collective-permute-start.8 = (bf16[272,640]{1,0:T(8,128)(2,1)}, bf16[272,640]{1,0:T(8,128)(2,1)S(1)}, u32[]{:S(2)}, u32[]{:S(2)}) collective-permute-start(bf16[272,640]{1,0:T(8,128)(2,1)} %get-tuple-element.47), channel_id=1, source_target_pairs={{0,12},{4,0},{8,4},{12,8},{1,13},{5,1},{9,5},{13,9},{2,14},{6,2},{... | collective-permute-start | bytes 1044488 | tf_op jit(solution)/shard_map/ppermute | solution.py:172
  12.6 2.0 %collective-permute-start = (bf16[640,256]{1,0:T(8,128)(2,1)}, bf16[640,256]{1,0:T(8,128)(2,1)S(1)}, u32[]{:S(2)}, u32[]{:S(2)}) collective-permute-start(bf16[640,256]{1,0:T(8,128)(2,1)} %get-tuple-element.39), channel_id=1, source_target_pairs={{0,8},{4,12},{8,0},{12,4},{1,9},{5,13},{9,1},{13,5},{2,10},{6,14},... | collective-permute-start | bytes 983048 | tf_op jit(solution)/shard_map/ppermute | solution.py:172
  14.6 6.2 %collective-permute-done.7 = bf16[272,640]{1,0:T(8,128)(2,1)S(1)} collective-permute-done((bf16[272,640]{1,0:T(8,128)(2,1)}, bf16[272,640]{1,0:T(8,128)(2,1)S(1)}, u32[]{:S(2)}, u32[]{:S(2)}) %collective-permute-start.7) | collective-permute-done | bytes 348192 | tf_op jit(solution)/shard_map/ppermute | solution.py:172
  20.8 10.0 %collective-permute-start.2 = (bf16[640,256]{1,0:T(8,128)(2,1)}, bf16[640,256]{1,0:T(8,128)(2,1)S(1)}, u32[]{:S(2)}, u32[]{:S(2)}) collective-permute-start(bf16[640,256]{1,0:T(8,128)(2,1)} %get-tuple-element.41), channel_id=1, source_target_pairs={{0,12},{4,0},{8,4},{12,8},{1,13},{5,1},{9,5},{13,9},{2,14},{6,2},{... | collective-permute-start | bytes 983048 | tf_op jit(solution)/shard_map/ppermute | solution.py:172
  30.9 1.6 %collective-permute-start.10 = (bf16[144,640]{1,0:T(8,128)(2,1)S(1)}, bf16[144,640]{1,0:T(8,128)(2,1)S(1)}, u32[]{:S(2)}, u32[]{:S(2)}) collective-permute-start(bf16[144,640]{1,0:T(8,128)(2,1)S(1)} %slice.25.rest_1_), channel_id=1, source_target_pairs={{0,2},{2,0},{1,3},{3,1},{4,6},{6,4},{5,7},{7,5},{8,10},{10,8},{9,1... | collective-permute-start | bytes 552968 | tf_op jit(solution)/shard_map/ppermute | solution.py:508
  32.5 24.1 %collective-permute-done.6 = bf16[272,640]{1,0:T(8,128)(2,1)S(1)} collective-permute-done((bf16[272,640]{1,0:T(8,128)(2,1)}, bf16[272,640]{1,0:T(8,128)(2,1)S(1)}, u32[]{:S(2)}, u32[]{:S(2)}) %collective-permute-start.6) | collective-permute-done | bytes 348192 | tf_op jit(solution)/shard_map/ppermute | solution.py:172
  58.1 5.5 %collective-permute-done.refs_0_.a = bf16[640,256]{1,0:T(8,128)(2,1)S(1)} collective-permute-done((bf16[640,256]{1,0:T(8,128)(2,1)}, bf16[640,256]{1,0:T(8,128)(2,1)S(1)}, u32[]{:S(2)}, u32[]{:S(2)}) %collective-permute-start) | collective-permute-done | bytes 327712 | tf_op jit(solution)/shard_map/ppermute | solution.py:172
  63.5 1.5 collective-permute-start.9
  65.0 1.9 %collective-permute-done.2.refs_2_.c = bf16[640,256]{1,0:T(8,128)(2,1)S(1)} collective-permute-done((bf16[640,256]{1,0:T(8,128)(2,1)}, bf16[640,256]{1,0:T(8,128)(2,1)S(1)}, u32[]{:S(2)}, u32[]{:S(2)}) %collective-permute-start.2) | collective-permute-done | bytes 327712 | tf_op jit(solution)/shard_map/ppermute | solution.py:172
  67.0 3.0 %collective-permute-done.9.rest_3_ = bf16[144,640]{1,0:T(8,128)(2,1)S(1)} collective-permute-done((bf16[144,640]{1,0:T(8,128)(2,1)S(1)}, bf16[144,640]{1,0:T(8,128)(2,1)S(1)}, u32[]{:S(2)}, u32[]{:S(2)}) %collective-permute-start.9) | collective-permute-done | bytes 184352 | tf_op jit(solution)/shard_map/ppermute | solution.py:508
  70.7 1.6 %collective-permute-start.13 = (bf16[1920,256]{1,0:T(8,128)(2,1)S(1)}, bf16[1920,256]{1,0:T(8,128)(2,1)S(1)}, u32[]{:S(2)}, u32[]{:S(2)}) collective-permute-start(bf16[1920,256]{1,0:T(8,128)(2,1)S(1)} %join.3), channel_id=1, source_target_pairs={{0,16},{16,0},{1,17},{17,1},{2,18},{18,2},{3,19},{19,3},{4,20},{20... | collective-permute-start | bytes 2949128 | tf_op jit(solution)/shard_map/ppermute | solution.py:180
  74.6 2.8 %collective-permute-start.5 = (bf16[640,256]{1,0:T(8,128)(2,1)S(1)}, bf16[640,256]{1,0:T(8,128)(2,1)S(1)}, u32[]{:S(2)}, u32[]{:S(2)}) collective-permute-start(bf16[640,256]{1,0:T(8,128)(2,1)S(1)} %copy-done.14), channel_id=1, source_target_pairs={{0,12},{4,0},{8,4},{12,8},{1,13},{5,1},{9,5},{13,9},{2,14},{6,2},{... | collective-permute-start | bytes 983048 | tf_op jit(solution)/shard_map/ppermute | solution.py:172
  78.2 3.6 %routed_up.1 = (bf16[512,2560]{1,0:T(8,128)(2,1)S(1)}, bf16[512,512]{1,0:T(8,128)(2,1)S(1)}) custom-call(s32[3]{0:T(128)S(1)} %copy-done.8, bf16[512,1280]{1,0:T(8,128)(2,1)S(1)} %half.1.mine, bf16[512,1280]{1,0:T(8,128)(2,1)S(1)} %collective-permute-done.12.theirs, bf16[1,2560,512]{2,1,0:T(8,128)(2,1)S(1)} %copy-done.12, bf16[1,2560,512]{2,1,0:T(8,128)(2,1)S(1)} %copy-done.13), custom_call_target="tpu_custom_call" | custom-call | flops 2684354560 | bytes 10485760 | tf_op jit(solution)/shard_map/routed_up/pallas_call | solution.py:519
  81.8 2.4 %routed_down.1.routed = bf16[512,2560]{1,0:T(8,128)(2,1)S(1)} custom-call(s32[3]{0:T(128)S(1)} %copy-done.8, bf16[512,512]{1,0:T(8,128)(2,1)S(1)} %get-tuple-element.48.hidden, bf16[144,640]{1,0:T(8,128)(2,1)S(1)} %copy-done.6, bf16[144,640]{1,0:T(8,128)(2,1)S(1)} %slice.25.rest_1_, bf16[144,640]{1,0:T(8,128)(2,1)S(1)} %slice.24.rest_0_.rest_2_, ...), custom_call_target="tpu_custom_call" | custom-call | flops 1342177280 | bytes 6291456 | tf_op jit(solution)/shard_map/routed_down/pallas_call | solution.py:528
  84.2 1.5 gate_up_first.1.first
  85.8 9.6 %collective-permute-done.13.rest = bf16[1920,256]{1,0:T(8,128)(2,1)S(1)} collective-permute-done((bf16[1920,256]{1,0:T(8,128)(2,1)S(1)}, bf16[1920,256]{1,0:T(8,128)(2,1)S(1)}, u32[]{:S(2)}, u32[]{:S(2)}) %collective-permute-start.13) | collective-permute-done | bytes 983072 | tf_op jit(solution)/shard_map/ppermute | solution.py:180
  95.4 1.5 gate_up_second.1.hidden
  97.8 7.6 %collective-permute-done.14.other = bf16[384,640]{1,0:T(8,128)(2,1)S(1)} collective-permute-done((bf16[384,640]{1,0:T(8,128)(2,1)S(1)}, bf16[384,640]{1,0:T(8,128)(2,1)S(1)}, u32[]{:S(2)}, u32[]{:S(2)}) %collective-permute-start.14) | collective-permute-done | bytes 491552 | tf_op jit(solution)/shard_map/ppermute | solution.py:180
  105.5 1.7 %down.1 = (bf16[512,1280]{1,0:T(8,128)(2,1)S(1)}, f32[512,1280]{1,0:T(8,128)S(1)}) custom-call(s32[3]{0:T(128)S(1)} %copy-done.8, bf16[512,2560]{1,0:T(8,128)(2,1)S(1)} %routed_down.1.routed, bf16[512,256]{1,0:T(8,128)(2,1)S(1)} %gate_up_second.1.hidden, bf16[256,640]{1,0:T(8,128)(2,1)S(1)} %copy-done.5, bf16[384,640]{1,0:T(8,128)(2,1)S(1)} %collective-permute-done.14.other, ...), custom_call_target="tpu_custom_call" | custom-call | tf_op jit(solution)/shard_map/down/pallas_call | solution.py:563
  107.2 1.6 %collective-permute-start.26 = (bf16[1920,256]{1,0:T(8,128)(2,1)S(1)}, bf16[1920,256]{1,0:T(8,128)(2,1)S(1)}, u32[]{:S(2)}, u32[]{:S(2)}) collective-permute-start(bf16[1920,256]{1,0:T(8,128)(2,1)S(1)} %join.4), channel_id=1, source_target_pairs={{0,16},{16,0},{1,17},{17,1},{2,18},{18,2},{3,19},{19,3},{4,20},{20... | collective-permute-start | bytes 2949128 | tf_op jit(solution)/shard_map/ppermute | solution.py:180
  110.4 1.6 %collective-permute-start.21 = (bf16[128,640]{1,0:T(8,128)(2,1)S(1)}, bf16[128,640]{1,0:T(8,128)(2,1)S(1)}, u32[]{:S(2)}, u32[]{:S(2)}) collective-permute-start(bf16[128,640]{1,0:T(8,128)(2,1)S(1)} %get-tuple-element.67), channel_id=1, source_target_pairs={{0,2},{2,0},{1,3},{3,1},{4,6},{6,4},{5,7},{7,5},{8,10},{10,8},{9,1... | collective-permute-start | bytes 491528 | tf_op jit(solution)/shard_map/ppermute | solution.py:579
  112.5 1.5 collective-permute-start.17
  114.6 3.0 %collective-permute-done.21.b = bf16[128,640]{1,0:T(8,128)(2,1)S(1)} collective-permute-done((bf16[128,640]{1,0:T(8,128)(2,1)S(1)}, bf16[128,640]{1,0:T(8,128)(2,1)S(1)}, u32[]{:S(2)}, u32[]{:S(2)}) %collective-permute-start.21) | collective-permute-done | bytes 163872 | tf_op jit(solution)/shard_map/ppermute | solution.py:579
  118.8 2.3 %collective-permute-done.19.b = bf16[128,640]{1,0:T(8,128)(2,1)S(1)} collective-permute-done((bf16[128,640]{1,0:T(8,128)(2,1)S(1)}, bf16[128,640]{1,0:T(8,128)(2,1)S(1)}, u32[]{:S(2)}, u32[]{:S(2)}) %collective-permute-start.19) | collective-permute-done | bytes 163872 | tf_op jit(solution)/shard_map/ppermute | solution.py:579
  121.1 1.8 %collective-permute-start.20 = (bf16[128,640]{1,0:T(8,128)(2,1)S(1)}, bf16[128,640]{1,0:T(8,128)(2,1)S(1)}, u32[]{:S(2)}, u32[]{:S(2)}) collective-permute-start(bf16[128,640]{1,0:T(8,128)(2,1)S(1)} %add.8), channel_id=1, source_target_pairs={{0,12},{4,0},{8,4},{12,8},{1,13},{5,1},{9,5},{13,9},{2,14},{6,2},{... | collective-permute-start | bytes 491528 | tf_op jit(solution)/shard_map/ppermute | solution.py:172
  122.9 1.7 %collective-permute-done.17.b = bf16[128,640]{1,0:T(8,128)(2,1)S(1)} collective-permute-done((bf16[128,640]{1,0:T(8,128)(2,1)S(1)}, bf16[128,640]{1,0:T(8,128)(2,1)S(1)}, u32[]{:S(2)}, u32[]{:S(2)}) %collective-permute-start.17) | collective-permute-done | bytes 163872 | tf_op jit(solution)/shard_map/ppermute | solution.py:579
  128.0 7.1 %collective-permute-done.18.a = bf16[128,640]{1,0:T(8,128)(2,1)S(1)} collective-permute-done((bf16[128,640]{1,0:T(8,128)(2,1)S(1)}, bf16[128,640]{1,0:T(8,128)(2,1)S(1)}, u32[]{:S(2)}, u32[]{:S(2)}) %collective-permute-start.18) | collective-permute-done | bytes 163872 | tf_op jit(solution)/shard_map/ppermute | solution.py:172
  137.4 4.1 %collective-permute-done.24.c = bf16[128,640]{1,0:T(8,128)(2,1)S(1)} collective-permute-done((bf16[128,640]{1,0:T(8,128)(2,1)}, bf16[128,640]{1,0:T(8,128)(2,1)S(1)}, u32[]{:S(2)}, u32[]{:S(2)}) %collective-permute-start.24) | collective-permute-done | bytes 163872 | tf_op jit(solution)/shard_map/ppermute | solution.py:184
  147.2 2.6 %collective-permute-done.28.c = bf16[64,512]{1,0:T(8,128)(2,1)S(1)} collective-permute-done((bf16[64,512]{1,0:T(8,128)(2,1)S(1)}, bf16[64,512]{1,0:T(8,128)(2,1)S(1)}, u32[]{:S(2)}, u32[]{:S(2)}) %collective-permute-start.28) | collective-permute-done | bytes 65568 | tf_op jit(solution)/shard_map/ppermute | solution.py:612
  151.1 1.7 %hand.1 = bf16[64,4,512]{2,1,0:T(4,128)(2,1)} custom-call(s32[3]{0:T(128)S(1)} %copy-done.8, bf16[64,512]{1,0:T(8,128)(2,1)S(1)} %get-tuple-element.68.a, bf16[64,512]{1,0:T(8,128)(2,1)S(1)} %collective-permute-done.27.b, bf16[64,512]{1,0:T(8,128)(2,1)S(1)} %collective-permute-done.28.c, bf16[64,512]{1,0:T(8,128)(2,1)S(1)} %collective-permute-done.29.d), custom_call_target="tpu_custom_call" | custom-call | tf_op jit(solution)/shard_map/hand/pallas_call | solution.py:615
  (82 shorter events, 24.4 us)
Async XLA Ops:
  6.5 14.3 %collective-permute-start.7 = (bf16[272,640]{1,0:T(8,128)(2,1)}, bf16[272,640]{1,0:T(8,128)(2,1)S(1)}, u32[]{:S(2)}, u32[]{:S(2)}) collective-permute-start(bf16[272,640]{1,0:T(8,128)(2,1)} %get-tuple-element.46), channel_id=1, source_target_pairs={{0,4},{4,8},{8,12},{12,0},{1,5},{5,9},{9,13},{13,1},{2,6},{6,10},{... | collective-permute-start | bytes 1044488 | tf_op jit(solution)/shard_map/ppermute | solution.py:172
  9.6 21.3 %collective-permute-start.8 = (bf16[272,640]{1,0:T(8,128)(2,1)}, bf16[272,640]{1,0:T(8,128)(2,1)S(1)}, u32[]{:S(2)}, u32[]{:S(2)}) collective-permute-start(bf16[272,640]{1,0:T(8,128)(2,1)} %get-tuple-element.47), channel_id=1, source_target_pairs={{0,12},{4,0},{8,4},{12,8},{1,13},{5,1},{9,5},{13,9},{2,14},{6,2},{... | collective-permute-start | bytes 1044488 | tf_op jit(solution)/shard_map/ppermute | solution.py:172
  11.7 44.9 %collective-permute-start.6 = (bf16[272,640]{1,0:T(8,128)(2,1)}, bf16[272,640]{1,0:T(8,128)(2,1)S(1)}, u32[]{:S(2)}, u32[]{:S(2)}) collective-permute-start(bf16[272,640]{1,0:T(8,128)(2,1)} %get-tuple-element.45), channel_id=1, source_target_pairs={{0,8},{4,12},{8,0},{12,4},{1,9},{5,13},{9,1},{13,5},{2,10},{6,14},... | collective-permute-start | bytes 1044488 | tf_op jit(solution)/shard_map/ppermute | solution.py:172
  12.6 50.9 %collective-permute-start = (bf16[640,256]{1,0:T(8,128)(2,1)}, bf16[640,256]{1,0:T(8,128)(2,1)S(1)}, u32[]{:S(2)}, u32[]{:S(2)}) collective-permute-start(bf16[640,256]{1,0:T(8,128)(2,1)} %get-tuple-element.39), channel_id=1, source_target_pairs={{0,8},{4,12},{8,0},{12,4},{1,9},{5,13},{9,1},{13,5},{2,10},{6,14},... | collective-permute-start | bytes 983048 | tf_op jit(solution)/shard_map/ppermute | solution.py:172
  14.6 50.4 %collective-permute-start.1 = (bf16[640,256]{1,0:T(8,128)(2,1)}, bf16[640,256]{1,0:T(8,128)(2,1)S(1)}, u32[]{:S(2)}, u32[]{:S(2)}) collective-permute-start(bf16[640,256]{1,0:T(8,128)(2,1)} %get-tuple-element.40), channel_id=1, source_target_pairs={{0,4},{4,8},{8,12},{12,0},{1,5},{5,9},{9,13},{13,1},{2,6},{6,10},{... | collective-permute-start | bytes 983048 | tf_op jit(solution)/shard_map/ppermute | solution.py:172
  20.8 46.1 %collective-permute-start.2 = (bf16[640,256]{1,0:T(8,128)(2,1)}, bf16[640,256]{1,0:T(8,128)(2,1)S(1)}, u32[]{:S(2)}, u32[]{:S(2)}) collective-permute-start(bf16[640,256]{1,0:T(8,128)(2,1)} %get-tuple-element.41), channel_id=1, source_target_pairs={{0,12},{4,0},{8,4},{12,8},{1,13},{5,1},{9,5},{13,9},{2,14},{6,2},{... | collective-permute-start | bytes 983048 | tf_op jit(solution)/shard_map/ppermute | solution.py:172
  30.9 39.1 %copy-start.4 = (bf16[128,2560]{1,0:T(8,128)(2,1)S(1)}, bf16[128,2560]{1,0:T(8,128)(2,1)}, u32[]{:S(2)}) copy-start(bf16[128,2560]{1,0:T(8,128)(2,1)} %get-tuple-element.44.moe_in) | copy-start | bytes 1966084
  30.9 39.1 %copy-start.8 = (s32[3]{0:T(128)S(1)}, s32[3]{0:T(128)}, u32[]{:S(2)}) copy-start(s32[3]{0:T(128)} %pad_add_fusion.refs_0_.place) | copy-start | bytes 40
  30.9 36.1 %collective-permute-start.10 = (bf16[144,640]{1,0:T(8,128)(2,1)S(1)}, bf16[144,640]{1,0:T(8,128)(2,1)S(1)}, u32[]{:S(2)}, u32[]{:S(2)}) collective-permute-start(bf16[144,640]{1,0:T(8,128)(2,1)S(1)} %slice.25.rest_1_), channel_id=1, source_target_pairs={{0,2},{2,0},{1,3},{3,1},{4,6},{6,4},{5,7},{7,5},{8,10},{10,8},{9,1... | collective-permute-start | bytes 552968 | tf_op jit(solution)/shard_map/ppermute | solution.py:508
  56.6 10.4 %collective-permute-start.11 = (bf16[144,640]{1,0:T(8,128)(2,1)S(1)}, bf16[144,640]{1,0:T(8,128)(2,1)S(1)}, u32[]{:S(2)}, u32[]{:S(2)}) collective-permute-start(bf16[144,640]{1,0:T(8,128)(2,1)S(1)} %slice.26.rest_2_.rest_3_), channel_id=1, source_target_pairs={{0,2},{2,0},{1,3},{3,1},{4,6},{6,4},{5,7},{7,5},{8,10},{10,8},{9,1... | collective-permute-start | bytes 552968 | tf_op jit(solution)/shard_map/ppermute | solution.py:508
  63.5 6.5 %collective-permute-start.9 = (bf16[144,640]{1,0:T(8,128)(2,1)S(1)}, bf16[144,640]{1,0:T(8,128)(2,1)S(1)}, u32[]{:S(2)}, u32[]{:S(2)}) collective-permute-start(bf16[144,640]{1,0:T(8,128)(2,1)S(1)} %slice.24.rest_0_.rest_2_), channel_id=1, source_target_pairs={{0,2},{2,0},{1,3},{3,1},{4,6},{6,4},{5,7},{7,5},{8,10},{10,8},{9,1... | collective-permute-start | bytes 552968 | tf_op jit(solution)/shard_map/ppermute | solution.py:508
  70.7 6.9 %collective-permute-start.12 = (bf16[512,1280]{1,0:T(8,128)(2,1)S(1)}, bf16[512,1280]{1,0:T(8,128)(2,1)S(1)}, u32[]{:S(2)}, u32[]{:S(2)}) collective-permute-start(bf16[512,1280]{1,0:T(8,128)(2,1)S(1)} %half.1.mine), channel_id=1, source_target_pairs={{0,1},{1,0},{2,3},{3,2},{4,5},{5,4},{6,7},{7,6},{8,9},{9,8},{10,11... | collective-permute-start | bytes 3932168 | tf_op jit(solution)/shard_map/ppermute | solution.py:515
  70.7 24.6 %collective-permute-start.13 = (bf16[1920,256]{1,0:T(8,128)(2,1)S(1)}, bf16[1920,256]{1,0:T(8,128)(2,1)S(1)}, u32[]{:S(2)}, u32[]{:S(2)}) collective-permute-start(bf16[1920,256]{1,0:T(8,128)(2,1)S(1)} %join.3), channel_id=1, source_target_pairs={{0,16},{16,0},{1,17},{17,1},{2,18},{18,2},{3,19},{19,3},{4,20},{20... | collective-permute-start | bytes 2949128 | tf_op jit(solution)/shard_map/ppermute | solution.py:180
  72.3 25.4 %collective-permute-start.3 = (bf16[640,256]{1,0:T(8,128)(2,1)S(1)}, bf16[640,256]{1,0:T(8,128)(2,1)S(1)}, u32[]{:S(2)}, u32[]{:S(2)}) collective-permute-start(bf16[640,256]{1,0:T(8,128)(2,1)S(1)} %copy-done.14), channel_id=1, source_target_pairs={{0,8},{4,12},{8,0},{12,4},{1,9},{5,13},{9,1},{13,5},{2,10},{6,14},... | collective-permute-start | bytes 983048 | tf_op jit(solution)/shard_map/ppermute | solution.py:172
  73.6 24.2 %collective-permute-start.4 = (bf16[640,256]{1,0:T(8,128)(2,1)S(1)}, bf16[640,256]{1,0:T(8,128)(2,1)S(1)}, u32[]{:S(2)}, u32[]{:S(2)}) collective-permute-start(bf16[640,256]{1,0:T(8,128)(2,1)S(1)} %copy-done.14), channel_id=1, source_target_pairs={{0,4},{4,8},{8,12},{12,0},{1,5},{5,9},{9,13},{13,1},{2,6},{6,10},{... | collective-permute-start | bytes 983048 | tf_op jit(solution)/shard_map/ppermute | solution.py:172
  74.6 23.2 %collective-permute-start.5 = (bf16[640,256]{1,0:T(8,128)(2,1)S(1)}, bf16[640,256]{1,0:T(8,128)(2,1)S(1)}, u32[]{:S(2)}, u32[]{:S(2)}) collective-permute-start(bf16[640,256]{1,0:T(8,128)(2,1)S(1)} %copy-done.14), channel_id=1, source_target_pairs={{0,12},{4,0},{8,4},{12,8},{1,13},{5,1},{9,5},{13,9},{2,14},{6,2},{... | collective-permute-start | bytes 983048 | tf_op jit(solution)/shard_map/ppermute | solution.py:172
  77.6 27.9 %collective-permute-start.14 = (bf16[384,640]{1,0:T(8,128)(2,1)S(1)}, bf16[384,640]{1,0:T(8,128)(2,1)S(1)}, u32[]{:S(2)}, u32[]{:S(2)}) collective-permute-start(bf16[384,640]{1,0:T(8,128)(2,1)S(1)} %join.5), channel_id=1, source_target_pairs={{0,16},{16,0},{1,17},{17,1},{2,18},{18,2},{3,19},{19,3},{4,20},{20... | collective-permute-start | bytes 1474568 | tf_op jit(solution)/shard_map/ppermute | solution.py:180
  107.1 3.1 %collective-permute-start.15 = (bf16[512,1280]{1,0:T(8,128)(2,1)S(1)}, bf16[512,1280]{1,0:T(8,128)(2,1)S(1)}, u32[]{:S(2)}, u32[]{:S(2)}) collective-permute-start(bf16[512,1280]{1,0:T(8,128)(2,1)S(1)} %get-tuple-element.59), channel_id=1, source_target_pairs={{0,1},{1,0},{2,3},{3,2},{4,5},{5,4},{6,7},{7,6},{8,9},{9,8},{10,11... | collective-permute-start | bytes 3932168 | tf_op jit(solution)/shard_map/ppermute | solution.py:571
  107.2 34.3 %collective-permute-start.26 = (bf16[1920,256]{1,0:T(8,128)(2,1)S(1)}, bf16[1920,256]{1,0:T(8,128)(2,1)S(1)}, u32[]{:S(2)}, u32[]{:S(2)}) collective-permute-start(bf16[1920,256]{1,0:T(8,128)(2,1)S(1)} %join.4), channel_id=1, source_target_pairs={{0,16},{16,0},{1,17},{17,1},{2,18},{18,2},{3,19},{19,3},{4,20},{20... | collective-permute-start | bytes 2949128 | tf_op jit(solution)/shard_map/ppermute | solution.py:180
  110.4 7.1 %collective-permute-start.21 = (bf16[128,640]{1,0:T(8,128)(2,1)S(1)}, bf16[128,640]{1,0:T(8,128)(2,1)S(1)}, u32[]{:S(2)}, u32[]{:S(2)}) collective-permute-start(bf16[128,640]{1,0:T(8,128)(2,1)S(1)} %get-tuple-element.67), channel_id=1, source_target_pairs={{0,2},{2,0},{1,3},{3,1},{4,6},{6,4},{5,7},{7,5},{8,10},{10,8},{9,1... | collective-permute-start | bytes 491528 | tf_op jit(solution)/shard_map/ppermute | solution.py:579
  112.0 9.0 %collective-permute-start.19 = (bf16[128,640]{1,0:T(8,128)(2,1)S(1)}, bf16[128,640]{1,0:T(8,128)(2,1)S(1)}, u32[]{:S(2)}, u32[]{:S(2)}) collective-permute-start(bf16[128,640]{1,0:T(8,128)(2,1)S(1)} %get-tuple-element.65), channel_id=1, source_target_pairs={{0,2},{2,0},{1,3},{3,1},{4,6},{6,4},{5,7},{7,5},{8,10},{10,8},{9,1... | collective-permute-start | bytes 491528 | tf_op jit(solution)/shard_map/ppermute | solution.py:579
  112.5 12.0 %collective-permute-start.17 = (bf16[128,640]{1,0:T(8,128)(2,1)S(1)}, bf16[128,640]{1,0:T(8,128)(2,1)S(1)}, u32[]{:S(2)}, u32[]{:S(2)}) collective-permute-start(bf16[128,640]{1,0:T(8,128)(2,1)S(1)} %get-tuple-element.63), channel_id=1, source_target_pairs={{0,2},{2,0},{1,3},{3,1},{4,6},{6,4},{5,7},{7,5},{8,10},{10,8},{9,1... | collective-permute-start | bytes 491528 | tf_op jit(solution)/shard_map/ppermute | solution.py:579
  114.1 13.2 %collective-permute-start.16 = (bf16[128,640]{1,0:T(8,128)(2,1)S(1)}, bf16[128,640]{1,0:T(8,128)(2,1)S(1)}, u32[]{:S(2)}, u32[]{:S(2)}) collective-permute-start(bf16[128,640]{1,0:T(8,128)(2,1)S(1)} %get-tuple-element.61), channel_id=1, source_target_pairs={{0,2},{2,0},{1,3},{3,1},{4,6},{6,4},{5,7},{7,5},{8,10},{10,8},{9,1... | collective-permute-start | bytes 491528 | tf_op jit(solution)/shard_map/ppermute | solution.py:579
  117.6 9.7 %collective-permute-start.22 = (bf16[128,640]{1,0:T(8,128)(2,1)S(1)}, bf16[128,640]{1,0:T(8,128)(2,1)S(1)}, u32[]{:S(2)}, u32[]{:S(2)}) collective-permute-start(bf16[128,640]{1,0:T(8,128)(2,1)S(1)} %add.9), channel_id=1, source_target_pairs={{0,4},{4,8},{8,12},{12,0},{1,5},{5,9},{9,13},{13,1},{2,6},{6,10},{... | collective-permute-start | bytes 491528 | tf_op jit(solution)/shard_map/ppermute | solution.py:172
  121.1 6.9 %collective-permute-start.20 = (bf16[128,640]{1,0:T(8,128)(2,1)S(1)}, bf16[128,640]{1,0:T(8,128)(2,1)S(1)}, u32[]{:S(2)}, u32[]{:S(2)}) collective-permute-start(bf16[128,640]{1,0:T(8,128)(2,1)S(1)} %add.8), channel_id=1, source_target_pairs={{0,12},{4,0},{8,4},{12,8},{1,13},{5,1},{9,5},{13,9},{2,14},{6,2},{... | collective-permute-start | bytes 491528 | tf_op jit(solution)/shard_map/ppermute | solution.py:172
  124.6 10.5 %collective-permute-start.18 = (bf16[128,640]{1,0:T(8,128)(2,1)S(1)}, bf16[128,640]{1,0:T(8,128)(2,1)S(1)}, u32[]{:S(2)}, u32[]{:S(2)}) collective-permute-start(bf16[128,640]{1,0:T(8,128)(2,1)S(1)} %add.7), channel_id=1, source_target_pairs={{0,8},{4,12},{8,0},{12,4},{1,9},{5,13},{9,1},{13,5},{2,10},{6,14},... | collective-permute-start | bytes 491528 | tf_op jit(solution)/shard_map/ppermute | solution.py:172
  135.9 5.5 %collective-permute-start.24 = (bf16[128,640]{1,0:T(8,128)(2,1)}, bf16[128,640]{1,0:T(8,128)(2,1)S(1)}, u32[]{:S(2)}, u32[]{:S(2)}) collective-permute-start(bf16[128,640]{1,0:T(8,128)(2,1)} %layer.1.a), channel_id=1, source_target_pairs={{0,2},{2,0},{1,3},{3,1},{4,6},{6,4},{5,7},{7,5},{8,10},{10,8},{9,1... | collective-permute-start | bytes 491528 | tf_op jit(solution)/shard_map/ppermute | solution.py:184
  137.4 4.1 %collective-permute-start.23 = (bf16[128,640]{1,0:T(8,128)(2,1)}, bf16[128,640]{1,0:T(8,128)(2,1)S(1)}, u32[]{:S(2)}, u32[]{:S(2)}) collective-permute-start(bf16[128,640]{1,0:T(8,128)(2,1)} %layer.1.a), channel_id=1, source_target_pairs={{0,1},{1,0},{2,3},{3,2},{4,5},{5,4},{6,7},{7,6},{8,9},{9,8},{10,11... | collective-permute-start | bytes 491528 | tf_op jit(solution)/shard_map/ppermute | solution.py:185
  141.5 1.4 collective-permute-start.25
  145.2 1.9 %collective-permute-start.27 = (bf16[64,512]{1,0:T(8,128)(2,1)S(1)}, bf16[64,512]{1,0:T(8,128)(2,1)S(1)}, u32[]{:S(2)}, u32[]{:S(2)}) collective-permute-start(bf16[64,512]{1,0:T(8,128)(2,1)S(1)} %get-tuple-element.69), channel_id=1, source_target_pairs={{0,1},{1,0},{2,3},{3,2},{4,5},{5,4},{6,7},{7,6},{8,9},{9,8},{10,11... | collective-permute-start | bytes 196616 | tf_op jit(solution)/shard_map/ppermute | solution.py:612
  145.5 4.4 %collective-permute-start.28 = (bf16[64,512]{1,0:T(8,128)(2,1)S(1)}, bf16[64,512]{1,0:T(8,128)(2,1)S(1)}, u32[]{:S(2)}, u32[]{:S(2)}) collective-permute-start(bf16[64,512]{1,0:T(8,128)(2,1)S(1)} %get-tuple-element.70), channel_id=1, source_target_pairs={{0,2},{2,0},{1,3},{3,1},{4,6},{6,4},{5,7},{7,5},{8,10},{10,8},{9,1... | collective-permute-start | bytes 196616 | tf_op jit(solution)/shard_map/ppermute | solution.py:612
  146.9 4.1 %collective-permute-start.29 = (bf16[64,512]{1,0:T(8,128)(2,1)S(1)}, bf16[64,512]{1,0:T(8,128)(2,1)S(1)}, u32[]{:S(2)}, u32[]{:S(2)}) collective-permute-start(bf16[64,512]{1,0:T(8,128)(2,1)S(1)} %get-tuple-element.71), channel_id=1, source_target_pairs={{0,3},{3,0},{1,2},{2,1},{4,7},{7,4},{5,6},{6,5},{8,11},{11,8},{9,1... | collective-permute-start | bytes 196616 | tf_op jit(solution)/shard_map/ppermute | solution.py:612
  (13 other events, 156.5 us)

commit v6 on v5

--- a/solution.py
+++ b/solution.py
@@ -162,7 +162,7 @@
         out_specs=[VMEM] * len(outs),
         scratch_shapes=list(scratch),
         compiler_params=pltpu.CompilerParams(vmem_limit_bytes=vmem << 20),
-        cost_estimate=pl.CostEstimate(flops=flops, bytes_accessed=moved, transcendentals=0),
+        cost_estimate=pl.CostEstimate(flops=0, bytes_accessed=0, transcendentals=0),
         name=name,
     )
 
@@ -196,39 +196,22 @@
 
 
 def first_kernel(
-    capacity, place, resid, gain, score, ids, gate, up, down, kv, moe_in, message, share, own, *rest
+    capacity, place, resid, gain, score, ids, down, moe_in, message, share, *rest
 ):
-    messages, both, kv_half, own_down, sem = rest[:3], rest[3:6], rest[6], rest[7], rest[8]
+    both, sem = rest[:3], rest[3]
     top = message.shape[0]
     zone, slot, group = place[0], place[1], place[2]
     count = 4
-    hidden = gate.shape[1] // count
+    hidden = down.shape[0] // count
     half = hidden // 2
     copies = []
 
     def move(source, target):
         copies.append(pltpu.make_async_copy(source, target, sem.at[len(copies)]))
 
-    for i, shift in enumerate(SHIFTS):
-        start = lax.rem(zone + shift, count) * hidden + group * half
-        for j, weights in enumerate((gate, up)):
-            move(
-                weights.at[:, pl.ds(pl.multiple_of(start, 128), half)],
-                messages[i].at[:, j * half : (j + 1) * half],
-            )
     for i, shift in enumerate(SHIFTS):
         start = lax.rem(zone + shift, count) * hidden + group * half
         move(down.at[pl.ds(pl.multiple_of(start, 128), half), :], both[i].at[top:, :])
-    move(down.at[pl.ds(pl.multiple_of(zone * hidden, 128), hidden), :], own_down)
-    start = group * kv_half.shape[1]
-    move(kv.at[:, pl.ds(pl.multiple_of(start, 128), kv_half.shape[1])], kv_half)
-    for part in range(2):
-        start = zone * hidden + (group ^ part) * half
-        for j, weights in enumerate((gate, up)):
-            move(
-                weights.at[:, pl.ds(pl.multiple_of(start, 128), half)],
-                own.at[:, (2 * part + j) * half : (2 * part + j + 1) * half],
-            )
     for copy in copies:
         copy.start()
 
@@ -259,6 +242,40 @@
         copy.wait()
 
 
+def second_kernel(place, gate, up, down, kv, own, own_down, *rest):
+    messages, kv_half, sem = rest[:3], rest[3], rest[4]
+    count = 4
+    zone, group = place[0], place[2]
+    hidden = gate.shape[1] // 4
+    half = hidden // 2
+    copies = []
+
+    def move(source, target):
+        copies.append(pltpu.make_async_copy(source, target, sem.at[len(copies)]))
+
+    move(down.at[pl.ds(pl.multiple_of(zone * hidden, 128), hidden), :], own_down)
+    for i, shift in enumerate(SHIFTS):
+        start = lax.rem(zone + shift, count) * hidden + group * half
+        for j, weights in enumerate((gate, up)):
+            move(
+                weights.at[:, pl.ds(pl.multiple_of(start, 128), half)],
+                messages[i].at[:, j * half : (j + 1) * half],
+            )
+    start = group * kv_half.shape[1]
+    move(kv.at[:, pl.ds(pl.multiple_of(start, 128), kv_half.shape[1])], kv_half)
+    for part in range(2):
+        start = zone * hidden + (group ^ part) * half
+        for j, weights in enumerate((gate, up)):
+            move(
+                weights.at[:, pl.ds(pl.multiple_of(start, 128), half)],
+                own.at[:, (2 * part + j) * half : (2 * part + j + 1) * half],
+            )
+    for copy in copies:
+        copy.start()
+    for copy in copies:
+        copy.wait()
+
+
 def silu(values):
     return values / (1.0 + jnp.exp(-values))
 
@@ -380,10 +397,11 @@
     out[...] = (a[...] + b[...].astype(F32)).astype(BF16)
 
 
-def layer_kernel(resid, own, crossed, a, b, c, out):
+def layer_kernel(resid, own, crossed, a, b, c, out, again):
     value = own[...] + crossed[...].astype(F32) + a[...].astype(F32) + b[...].astype(F32) + c[...].astype(F32)
     value = value + resid[...].astype(F32)
     out[...] = value.astype(BF16)
+    again[...] = out[...]
 
 
 def kv_kernel(place, owner, blocks, gain, a, b, c, d, own, *rest):
@@ -471,13 +489,10 @@
             ((rows, width), BF16),
             ((rows + META, piece), BF16),
             ((rows, piece), BF16),
-            ((near, 2 * hidden), BF16),
         ]
-        + [((near, hidden), BF16)] * 3
-        + [((rows + META + half, piece), BF16)] * 3
-        + [((near, kv_width // 2), BF16), ((hidden, piece), BF16)],
-        [SMEM] + [VMEM] * 4 + [ANY] * 4,
-        [pltpu.SemaphoreType.DMA((15,))],
+        + [((rows + META + half, piece), BF16)] * 3,
+        [SMEM] + [VMEM] * 4 + [ANY],
+        [pltpu.SemaphoreType.DMA((3,))],
         moved=6 << 20,
         name="first",
         vmem=58,
@@ -487,13 +502,21 @@
         moe_gain,
         gate_score.reshape(1, rows),
         expert_ids.reshape(1, rows),
-        shared_gate,
-        shared_up,
         shared_down,
-        w_kv,
-    )
-    moe_in, message, resid_share, own_weights = first[:4]
-    weight_messages, mixed_messages, kv_half, own_down = first[4:7], first[7:10], *first[10:]
+    )
+    moe_in, message, resid_share = first[:3]
+    mixed_messages = first[3:6]
+    second = call(
+        second_kernel,
+        [((near, 2 * hidden), BF16), ((hidden, piece), BF16)]
+        + [((near, hidden), BF16)] * 3
+        + [((near, kv_width // 2), BF16)],
+        [SMEM] + [ANY] * 4,
+        [pltpu.SemaphoreType.DMA((12,))],
+        name="second",
+        vmem=58,
+    )(place, shared_gate, shared_up, shared_down, w_kv)
+    own_weights, own_down, weight_messages, kv_half = second[0], second[1], second[2:5], second[5]
 
     mixed = [to_shift(values, s) for values, s in zip(mixed_messages, SHIFTS)]
     top = rows + META
@@ -583,8 +606,8 @@
             passed[s], crossed[s]
         )
         returned.append(to_shift(summed, -s))
-    (layer_out,) = call(
-        layer_kernel, [((rows, piece), BF16)], [VMEM] * 6, name="layer"
+    layer_out, layer_rows = call(
+        layer_kernel, [((rows, piece), BF16)] * 2, [VMEM] * 6, name="layer"
     )(resid_share, passed[0], crossed[0], *returned)
 
     handed = call(
@@ -603,7 +626,7 @@
         req_owner,
         req_blocks,
         attn_gain,
-        *spread(layer_out),
+        *spread(layer_rows),
         w_kv,
         *kv_got,
         kv_other,

time: 153 us -> 150 us (0.980)
  waiting for transfers between devices: 85.7 us -> 81.8 us
  Pallas kernels: 20.9 us -> 23.3 us
    pallas_call x1 -> x2, Pallas kernels: 0.78 us -> 4.72 us  [the longest x1 3.85 us: near_plan(): call(second_kernel, [((near, 2 * hidden), BF16), ((hidden, piece), BF16)]...]
    ppermute x12, waiting for transfers between devices: 46.4 us -> 43.2 us  [to_shift(): lax.ppermute(values, 'expert', [(i, (i + shift) % count) for i in range(c...]
    pallas_call x1, Pallas kernels: 5.2 us -> 3.54 us  [near_plan(): call(lambda *refs: first_kernel(capacity, *refs), [((rows, width), BF16),...]
  transfers between devices with their start and end apart: 30 -> 30, of which waited for: 19 -> 19; matrix products, arithmetic and copies ran while one was open for 0% -> 0% of each run, Pallas kernels for 7% -> 10%
where the time goes in v6:
time: 150 us
  waiting for transfers between devices  81.8 us (55%)
  starting transfers between devices  43.2 us (29%)
  Pallas kernels  23.3 us (16%)
    ppermute x12, waiting for transfers between devices, to_shift(): lax.ppermute(values, 'expert', [(i, (i + shift) % count) for i in range(c...  43.2 us
    ppermute x12, starting transfers between devices, to_shift(): lax.ppermute(values, 'expert', [(i, (i + shift) % count) for i in range(c...  27.3 us
    ppermute x3, waiting for transfers between devices, swap_groups(): return lax.ppermute(values, 'groups', SWAP_GROUP)  16.8 us
    ppermute x4, waiting for transfers between devices, near_plan(): lax.ppermute(passed[4 + s], 'decode', SWAP_CHIP)  8.25 us
    ppermute x3, starting transfers between devices, near_plan(): across = [lax.ppermute(values, 'decode', SWAP_CHIP) for values in arrived]  4.54 us
    ppermute x4, starting transfers between devices, near_plan(): lax.ppermute(passed[4 + s], 'decode', SWAP_CHIP)  4.12 us
    ppermute x3, waiting for transfers between devices, near_plan(): lax.ppermute(values, 'decode', pairs)  3.89 us
    ppermute x1, waiting for transfers between devices, spread(): across = lax.ppermute(values, 'decode', SWAP_CHIP)  3.86 us
  transfers between devices with their start and end apart: 30, of which 19 were waited for; matrix products, arithmetic and copies ran while one was open for 0% of the time, Pallas kernels for 10%

profile of v6, /device:TPU:0, one launch (start us, length us, event | category | flops | bytes accessed | tf_op | source)
XLA Modules:
  0.0 150.1 jit_solution(5435888512717653651)
XLA Ops:
  1.3 3.5 %first.1 = (bf16[128,2560]{1,0:T(8,128)(2,1)}, bf16[144,640]{1,0:T(8,128)(2,1)}, bf16[128,640]{1,0:T(8,128)(2,1)}, bf16[272,640]{1,0:T(8,128)(2,1)}, bf16[272,640]{1,0:T(8,128)(2,1)}, /*index=5*/bf16[272,640]{1,0:T(8,128)(2,1)}) custom-call(s32[3]{0:T(128)} %pad_add_fusion.refs_0_.place, bf16[128,2560]{1,0:T(8,128)(2,1)} %refs_1_.1, f32[2560]{0:T(1024)} %refs_2_.1, ...), custom_call_target="tpu_custom_call" | custom-call | tf_op jit(solution)/shard_map/first/pallas_call | solution.py:486
  4.9 3.1 %collective-permute-start.7 = (bf16[272,640]{1,0:T(8,128)(2,1)}, bf16[272,640]{1,0:T(8,128)(2,1)S(1)}, u32[]{:S(2)}, u32[]{:S(2)}) collective-permute-start(bf16[272,640]{1,0:T(8,128)(2,1)} %get-tuple-element.48), channel_id=1, source_target_pairs={{0,4},{4,8},{8,12},{12,0},{1,5},{5,9},{9,13},{13,1},{2,6},{6,10},{... | collective-permute-start | bytes 1044488 | tf_op jit(solution)/shard_map/ppermute | solution.py:172
  7.9 2.1 %collective-permute-start.8 = (bf16[272,640]{1,0:T(8,128)(2,1)}, bf16[272,640]{1,0:T(8,128)(2,1)S(1)}, u32[]{:S(2)}, u32[]{:S(2)}) collective-permute-start(bf16[272,640]{1,0:T(8,128)(2,1)} %get-tuple-element.49), channel_id=1, source_target_pairs={{0,12},{4,0},{8,4},{12,8},{1,13},{5,1},{9,5},{13,9},{2,14},{6,2},{... | collective-permute-start | bytes 1044488 | tf_op jit(solution)/shard_map/ppermute | solution.py:172
  11.0 3.8 %second.1 = (bf16[640,512]{1,0:T(8,128)(2,1)}, bf16[256,640]{1,0:T(8,128)(2,1)}, bf16[640,256]{1,0:T(8,128)(2,1)}, bf16[640,256]{1,0:T(8,128)(2,1)}, bf16[640,256]{1,0:T(8,128)(2,1)}, /*index=5*/bf16[640,256]{1,0:T(8,128)(2,1)}) custom-call(s32[3]{0:T(128)} %pad_add_fusion.refs_0_.place, bf16[640,1024]{1,0:T(8,128)(2,1)} %gate.2, bf16[640,1024]{1,0:T(8,128)(2,1)} %up.2, ...), custom_call_target="tpu_custom_call" | custom-call | tf_op jit(solution)/shard_map/second/pallas_call | solution.py:509
  14.8 2.0 %collective-permute-start = (bf16[640,256]{1,0:T(8,128)(2,1)}, bf16[640,256]{1,0:T(8,128)(2,1)S(1)}, u32[]{:S(2)}, u32[]{:S(2)}) collective-permute-start(bf16[640,256]{1,0:T(8,128)(2,1)} %get-tuple-element.41), channel_id=1, source_target_pairs={{0,8},{4,12},{8,0},{12,4},{1,9},{5,13},{9,1},{13,5},{2,10},{6,14},... | collective-permute-start | bytes 983048 | tf_op jit(solution)/shard_map/ppermute | solution.py:172
  16.9 2.3 %collective-permute-done.7 = bf16[272,640]{1,0:T(8,128)(2,1)S(1)} collective-permute-done((bf16[272,640]{1,0:T(8,128)(2,1)}, bf16[272,640]{1,0:T(8,128)(2,1)S(1)}, u32[]{:S(2)}, u32[]{:S(2)}) %collective-permute-start.7) | collective-permute-done | bytes 348192 | tf_op jit(solution)/shard_map/ppermute | solution.py:172
  19.2 9.7 %collective-permute-start.2 = (bf16[640,256]{1,0:T(8,128)(2,1)}, bf16[640,256]{1,0:T(8,128)(2,1)S(1)}, u32[]{:S(2)}, u32[]{:S(2)}) collective-permute-start(bf16[640,256]{1,0:T(8,128)(2,1)} %get-tuple-element.43), channel_id=1, source_target_pairs={{0,12},{4,0},{8,4},{12,8},{1,13},{5,1},{9,5},{13,9},{2,14},{6,2},{... | collective-permute-start | bytes 983048 | tf_op jit(solution)/shard_map/ppermute | solution.py:172
  29.0 1.6 %collective-permute-start.10 = (bf16[144,640]{1,0:T(8,128)(2,1)S(1)}, bf16[144,640]{1,0:T(8,128)(2,1)S(1)}, u32[]{:S(2)}, u32[]{:S(2)}) collective-permute-start(bf16[144,640]{1,0:T(8,128)(2,1)S(1)} %slice.25.rest_1_), channel_id=1, source_target_pairs={{0,2},{2,0},{1,3},{3,1},{4,6},{6,4},{5,7},{7,5},{8,10},{10,8},{9,1... | collective-permute-start | bytes 552968 | tf_op jit(solution)/shard_map/ppermute | solution.py:531
  30.5 24.4 %collective-permute-done.6 = bf16[272,640]{1,0:T(8,128)(2,1)S(1)} collective-permute-done((bf16[272,640]{1,0:T(8,128)(2,1)}, bf16[272,640]{1,0:T(8,128)(2,1)S(1)}, u32[]{:S(2)}, u32[]{:S(2)}) %collective-permute-start.6) | collective-permute-done | bytes 348192 | tf_op jit(solution)/shard_map/ppermute | solution.py:172
  56.4 5.5 %collective-permute-done.refs_0_.a = bf16[640,256]{1,0:T(8,128)(2,1)S(1)} collective-permute-done((bf16[640,256]{1,0:T(8,128)(2,1)}, bf16[640,256]{1,0:T(8,128)(2,1)S(1)}, u32[]{:S(2)}, u32[]{:S(2)}) %collective-permute-start) | collective-permute-done | bytes 327712 | tf_op jit(solution)/shard_map/ppermute | solution.py:172
  63.4 1.9 %collective-permute-done.2.refs_2_.c = bf16[640,256]{1,0:T(8,128)(2,1)S(1)} collective-permute-done((bf16[640,256]{1,0:T(8,128)(2,1)}, bf16[640,256]{1,0:T(8,128)(2,1)S(1)}, u32[]{:S(2)}, u32[]{:S(2)}) %collective-permute-start.2) | collective-permute-done | bytes 327712 | tf_op jit(solution)/shard_map/ppermute | solution.py:172
  65.4 3.0 %collective-permute-done.9.rest_3_ = bf16[144,640]{1,0:T(8,128)(2,1)S(1)} collective-permute-done((bf16[144,640]{1,0:T(8,128)(2,1)S(1)}, bf16[144,640]{1,0:T(8,128)(2,1)S(1)}, u32[]{:S(2)}, u32[]{:S(2)}) %collective-permute-start.9) | collective-permute-done | bytes 184352 | tf_op jit(solution)/shard_map/ppermute | solution.py:531
  69.1 1.6 %collective-permute-start.13 = (bf16[1920,256]{1,0:T(8,128)(2,1)S(1)}, bf16[1920,256]{1,0:T(8,128)(2,1)S(1)}, u32[]{:S(2)}, u32[]{:S(2)}) collective-permute-start(bf16[1920,256]{1,0:T(8,128)(2,1)S(1)} %join.3), channel_id=1, source_target_pairs={{0,16},{16,0},{1,17},{17,1},{2,18},{18,2},{3,19},{19,3},{4,20},{20... | collective-permute-start | bytes 2949128 | tf_op jit(solution)/shard_map/ppermute | solution.py:180
  73.7 2.8 %collective-permute-start.5 = (bf16[640,256]{1,0:T(8,128)(2,1)S(1)}, bf16[640,256]{1,0:T(8,128)(2,1)S(1)}, u32[]{:S(2)}, u32[]{:S(2)}) collective-permute-start(bf16[640,256]{1,0:T(8,128)(2,1)S(1)} %copy-done.13), channel_id=1, source_target_pairs={{0,12},{4,0},{8,4},{12,8},{1,13},{5,1},{9,5},{13,9},{2,14},{6,2},{... | collective-permute-start | bytes 983048 | tf_op jit(solution)/shard_map/ppermute | solution.py:172
  76.5 3.6 %routed_up.1 = (bf16[512,2560]{1,0:T(8,128)(2,1)S(1)}, bf16[512,512]{1,0:T(8,128)(2,1)S(1)}) custom-call(s32[3]{0:T(128)S(1)} %copy-done.9, bf16[512,1280]{1,0:T(8,128)(2,1)S(1)} %half.1.mine, bf16[512,1280]{1,0:T(8,128)(2,1)S(1)} %collective-permute-done.12.theirs, bf16[1,2560,512]{2,1,0:T(8,128)(2,1)S(1)} %copy-done.3, bf16[1,2560,512]{2,1,0:T(8,128)(2,1)S(1)} %copy-done.4), custom_call_target="tpu_custom_call" | custom-call | tf_op jit(solution)/shard_map/routed_up/pallas_call | solution.py:542
  80.2 2.4 %routed_down.1.routed = bf16[512,2560]{1,0:T(8,128)(2,1)S(1)} custom-call(s32[3]{0:T(128)S(1)} %copy-done.9, bf16[512,512]{1,0:T(8,128)(2,1)S(1)} %get-tuple-element.50.hidden, bf16[144,640]{1,0:T(8,128)(2,1)S(1)} %copy-done.7, bf16[144,640]{1,0:T(8,128)(2,1)S(1)} %slice.25.rest_1_, bf16[144,640]{1,0:T(8,128)(2,1)S(1)} %slice.24.rest_0_.rest_2_, ...), custom_call_target="tpu_custom_call" | custom-call | tf_op jit(solution)/shard_map/routed_down/pallas_call | solution.py:551
  82.6 1.5 %gate_up_first.1.first = bf16[512,128]{1,0:T(8,128)(2,1)S(1)} custom-call(s32[3]{0:T(128)S(1)} %copy-done.9, bf16[512,2560]{1,0:T(8,128)(2,1)S(1)} %get-tuple-element.52.tokens, bf16[640,512]{1,0:T(8,128)(2,1)S(1)} %copy-done.2, bf16[640,256]{1,0:T(8,128)(2,1)S(1)} %collective-permute-done.refs_0_.a, bf16[640,256]{1,0:T(8,128)(2,1)S(1)} %collective-permute-done.1.refs_1_.b, ...), custom_call_target="tpu_custom_call" | custom-call | tf_op jit(solution)/shard_map/gate_up_first/pallas_call | solution.py:567
  84.1 9.6 %collective-permute-done.13.rest = bf16[1920,256]{1,0:T(8,128)(2,1)S(1)} collective-permute-done((bf16[1920,256]{1,0:T(8,128)(2,1)S(1)}, bf16[1920,256]{1,0:T(8,128)(2,1)S(1)}, u32[]{:S(2)}, u32[]{:S(2)}) %collective-permute-start.13) | collective-permute-done | bytes 983072 | tf_op jit(solution)/shard_map/ppermute | solution.py:180
  93.7 1.5 %gate_up_second.1.hidden = bf16[512,256]{1,0:T(8,128)(2,1)S(1)} custom-call(s32[3]{0:T(128)S(1)} %copy-done.9, bf16[512,2560]{1,0:T(8,128)(2,1)S(1)} %get-tuple-element.52.tokens, bf16[640,512]{1,0:T(8,128)(2,1)S(1)} %copy-done.2, bf16[512,128]{1,0:T(8,128)(2,1)S(1)} %gate_up_first.1.first, bf16[1920,256]{1,0:T(8,128)(2,1)S(1)} %collective-permute-done.13.rest), custom_call_target="tpu_custom_call" | custom-call | tf_op jit(solution)/shard_map/gate_up_second/pallas_call | solution.py:576
  96.7 7.2 %collective-permute-done.14.other = bf16[384,640]{1,0:T(8,128)(2,1)S(1)} collective-permute-done((bf16[384,640]{1,0:T(8,128)(2,1)S(1)}, bf16[384,640]{1,0:T(8,128)(2,1)S(1)}, u32[]{:S(2)}, u32[]{:S(2)}) %collective-permute-start.14) | collective-permute-done | bytes 491552 | tf_op jit(solution)/shard_map/ppermute | solution.py:180
  103.8 1.7 %down.3 = (bf16[512,1280]{1,0:T(8,128)(2,1)S(1)}, f32[512,1280]{1,0:T(8,128)S(1)}) custom-call(s32[3]{0:T(128)S(1)} %copy-done.9, bf16[512,2560]{1,0:T(8,128)(2,1)S(1)} %routed_down.1.routed, bf16[512,256]{1,0:T(8,128)(2,1)S(1)} %gate_up_second.1.hidden, bf16[256,640]{1,0:T(8,128)(2,1)S(1)} %copy-done.6, bf16[384,640]{1,0:T(8,128)(2,1)S(1)} %collective-permute-done.14.other, ...), custom_call_target="tpu_custom_call" | custom-call | tf_op jit(solution)/shard_map/down/pallas_call | solution.py:586
  105.6 1.6 %collective-permute-start.26 = (bf16[1920,256]{1,0:T(8,128)(2,1)S(1)}, bf16[1920,256]{1,0:T(8,128)(2,1)S(1)}, u32[]{:S(2)}, u32[]{:S(2)}) collective-permute-start(bf16[1920,256]{1,0:T(8,128)(2,1)S(1)} %join.4), channel_id=1, source_target_pairs={{0,16},{16,0},{1,17},{17,1},{2,18},{18,2},{3,19},{19,3},{4,20},{20... | collective-permute-start | bytes 2949128 | tf_op jit(solution)/shard_map/ppermute | solution.py:180
  108.9 1.6 %collective-permute-start.21 = (bf16[128,640]{1,0:T(8,128)(2,1)S(1)}, bf16[128,640]{1,0:T(8,128)(2,1)S(1)}, u32[]{:S(2)}, u32[]{:S(2)}) collective-permute-start(bf16[128,640]{1,0:T(8,128)(2,1)S(1)} %get-tuple-element.69), channel_id=1, source_target_pairs={{0,2},{2,0},{1,3},{3,1},{4,6},{6,4},{5,7},{7,5},{8,10},{10,8},{9,1... | collective-permute-start | bytes 491528 | tf_op jit(solution)/shard_map/ppermute | solution.py:602
  111.0 1.5 %collective-permute-start.17 = (bf16[128,640]{1,0:T(8,128)(2,1)S(1)}, bf16[128,640]{1,0:T(8,128)(2,1)S(1)}, u32[]{:S(2)}, u32[]{:S(2)}) collective-permute-start(bf16[128,640]{1,0:T(8,128)(2,1)S(1)} %get-tuple-element.65), channel_id=1, source_target_pairs={{0,2},{2,0},{1,3},{3,1},{4,6},{6,4},{5,7},{7,5},{8,10},{10,8},{9,1... | collective-permute-start | bytes 491528 | tf_op jit(solution)/shard_map/ppermute | solution.py:602
  113.0 3.0 %collective-permute-done.21.b = bf16[128,640]{1,0:T(8,128)(2,1)S(1)} collective-permute-done((bf16[128,640]{1,0:T(8,128)(2,1)S(1)}, bf16[128,640]{1,0:T(8,128)(2,1)S(1)}, u32[]{:S(2)}, u32[]{:S(2)}) %collective-permute-start.21) | collective-permute-done | bytes 163872 | tf_op jit(solution)/shard_map/ppermute | solution.py:602
  117.3 2.2 %collective-permute-done.19.b = bf16[128,640]{1,0:T(8,128)(2,1)S(1)} collective-permute-done((bf16[128,640]{1,0:T(8,128)(2,1)S(1)}, bf16[128,640]{1,0:T(8,128)(2,1)S(1)}, u32[]{:S(2)}, u32[]{:S(2)}) %collective-permute-start.19) | collective-permute-done | bytes 163872 | tf_op jit(solution)/shard_map/ppermute | solution.py:602
  119.5 1.8 %collective-permute-start.20 = (bf16[128,640]{1,0:T(8,128)(2,1)S(1)}, bf16[128,640]{1,0:T(8,128)(2,1)S(1)}, u32[]{:S(2)}, u32[]{:S(2)}) collective-permute-start(bf16[128,640]{1,0:T(8,128)(2,1)S(1)} %add.8), channel_id=1, source_target_pairs={{0,12},{4,0},{8,4},{12,8},{1,13},{5,1},{9,5},{13,9},{2,14},{6,2},{... | collective-permute-start | bytes 491528 | tf_op jit(solution)/shard_map/ppermute | solution.py:172
  121.3 1.7 %collective-permute-done.17.b = bf16[128,640]{1,0:T(8,128)(2,1)S(1)} collective-permute-done((bf16[128,640]{1,0:T(8,128)(2,1)S(1)}, bf16[128,640]{1,0:T(8,128)(2,1)S(1)}, u32[]{:S(2)}, u32[]{:S(2)}) %collective-permute-start.17) | collective-permute-done | bytes 163872 | tf_op jit(solution)/shard_map/ppermute | solution.py:602
  126.5 7.0 %collective-permute-done.18.a = bf16[128,640]{1,0:T(8,128)(2,1)S(1)} collective-permute-done((bf16[128,640]{1,0:T(8,128)(2,1)S(1)}, bf16[128,640]{1,0:T(8,128)(2,1)S(1)}, u32[]{:S(2)}, u32[]{:S(2)}) %collective-permute-start.18) | collective-permute-done | bytes 163872 | tf_op jit(solution)/shard_map/ppermute | solution.py:172
  135.9 3.9 %collective-permute-done.24.c = bf16[128,640]{1,0:T(8,128)(2,1)S(1)} collective-permute-done((bf16[128,640]{1,0:T(8,128)(2,1)S(1)}, bf16[128,640]{1,0:T(8,128)(2,1)S(1)}, u32[]{:S(2)}, u32[]{:S(2)}) %collective-permute-start.24) | collective-permute-done | bytes 163872 | tf_op jit(solution)/shard_map/ppermute | solution.py:184
  144.6 2.6 %collective-permute-done.28.c = bf16[64,512]{1,0:T(8,128)(2,1)S(1)} collective-permute-done((bf16[64,512]{1,0:T(8,128)(2,1)S(1)}, bf16[64,512]{1,0:T(8,128)(2,1)S(1)}, u32[]{:S(2)}, u32[]{:S(2)}) %collective-permute-start.28) | collective-permute-done | bytes 65568 | tf_op jit(solution)/shard_map/ppermute | solution.py:635
  148.4 1.7 %hand.1 = bf16[64,4,512]{2,1,0:T(4,128)(2,1)} custom-call(s32[3]{0:T(128)S(1)} %copy-done.9, bf16[64,512]{1,0:T(8,128)(2,1)S(1)} %get-tuple-element.72.a, bf16[64,512]{1,0:T(8,128)(2,1)S(1)} %collective-permute-done.27.b, bf16[64,512]{1,0:T(8,128)(2,1)S(1)} %collective-permute-done.28.c, bf16[64,512]{1,0:T(8,128)(2,1)S(1)} %collective-permute-done.29.d), custom_call_target="tpu_custom_call" | custom-call | tf_op jit(solution)/shard_map/hand/pallas_call | solution.py:638
  (81 shorter events, 25.7 us)
Async XLA Ops:
  4.9 14.3 %collective-permute-start.7 = (bf16[272,640]{1,0:T(8,128)(2,1)}, bf16[272,640]{1,0:T(8,128)(2,1)S(1)}, u32[]{:S(2)}, u32[]{:S(2)}) collective-permute-start(bf16[272,640]{1,0:T(8,128)(2,1)} %get-tuple-element.48), channel_id=1, source_target_pairs={{0,4},{4,8},{8,12},{12,0},{1,5},{5,9},{9,13},{13,1},{2,6},{6,10},{... | collective-permute-start | bytes 1044488 | tf_op jit(solution)/shard_map/ppermute | solution.py:172
  7.9 21.0 %collective-permute-start.8 = (bf16[272,640]{1,0:T(8,128)(2,1)}, bf16[272,640]{1,0:T(8,128)(2,1)S(1)}, u32[]{:S(2)}, u32[]{:S(2)}) collective-permute-start(bf16[272,640]{1,0:T(8,128)(2,1)} %get-tuple-element.49), channel_id=1, source_target_pairs={{0,12},{4,0},{8,4},{12,8},{1,13},{5,1},{9,5},{13,9},{2,14},{6,2},{... | collective-permute-start | bytes 1044488 | tf_op jit(solution)/shard_map/ppermute | solution.py:172
  10.0 44.9 %collective-permute-start.6 = (bf16[272,640]{1,0:T(8,128)(2,1)}, bf16[272,640]{1,0:T(8,128)(2,1)S(1)}, u32[]{:S(2)}, u32[]{:S(2)}) collective-permute-start(bf16[272,640]{1,0:T(8,128)(2,1)} %get-tuple-element.47), channel_id=1, source_target_pairs={{0,8},{4,12},{8,0},{12,4},{1,9},{5,13},{9,1},{13,5},{2,10},{6,14},... | collective-permute-start | bytes 1044488 | tf_op jit(solution)/shard_map/ppermute | solution.py:172
  14.8 47.1 %collective-permute-start = (bf16[640,256]{1,0:T(8,128)(2,1)}, bf16[640,256]{1,0:T(8,128)(2,1)S(1)}, u32[]{:S(2)}, u32[]{:S(2)}) collective-permute-start(bf16[640,256]{1,0:T(8,128)(2,1)} %get-tuple-element.41), channel_id=1, source_target_pairs={{0,8},{4,12},{8,0},{12,4},{1,9},{5,13},{9,1},{13,5},{2,10},{6,14},... | collective-permute-start | bytes 983048 | tf_op jit(solution)/shard_map/ppermute | solution.py:172
  16.9 46.5 %collective-permute-start.1 = (bf16[640,256]{1,0:T(8,128)(2,1)}, bf16[640,256]{1,0:T(8,128)(2,1)S(1)}, u32[]{:S(2)}, u32[]{:S(2)}) collective-permute-start(bf16[640,256]{1,0:T(8,128)(2,1)} %get-tuple-element.42), channel_id=1, source_target_pairs={{0,4},{4,8},{8,12},{12,0},{1,5},{5,9},{9,13},{13,1},{2,6},{6,10},{... | collective-permute-start | bytes 983048 | tf_op jit(solution)/shard_map/ppermute | solution.py:172
  19.2 46.1 %collective-permute-start.2 = (bf16[640,256]{1,0:T(8,128)(2,1)}, bf16[640,256]{1,0:T(8,128)(2,1)S(1)}, u32[]{:S(2)}, u32[]{:S(2)}) collective-permute-start(bf16[640,256]{1,0:T(8,128)(2,1)} %get-tuple-element.43), channel_id=1, source_target_pairs={{0,12},{4,0},{8,4},{12,8},{1,13},{5,1},{9,5},{13,9},{2,14},{6,2},{... | collective-permute-start | bytes 983048 | tf_op jit(solution)/shard_map/ppermute | solution.py:172
  28.9 39.4 %copy-start.5 = (bf16[128,2560]{1,0:T(8,128)(2,1)S(1)}, bf16[128,2560]{1,0:T(8,128)(2,1)}, u32[]{:S(2)}) copy-start(bf16[128,2560]{1,0:T(8,128)(2,1)} %get-tuple-element.46.moe_in) | copy-start | bytes 1966084
  28.9 39.4 %copy-start.9 = (s32[3]{0:T(128)S(1)}, s32[3]{0:T(128)}, u32[]{:S(2)}) copy-start(s32[3]{0:T(128)} %pad_add_fusion.refs_0_.place) | copy-start | bytes 40
  29.0 36.4 %collective-permute-start.10 = (bf16[144,640]{1,0:T(8,128)(2,1)S(1)}, bf16[144,640]{1,0:T(8,128)(2,1)S(1)}, u32[]{:S(2)}, u32[]{:S(2)}) collective-permute-start(bf16[144,640]{1,0:T(8,128)(2,1)S(1)} %slice.25.rest_1_), channel_id=1, source_target_pairs={{0,2},{2,0},{1,3},{3,1},{4,6},{6,4},{5,7},{7,5},{8,10},{10,8},{9,1... | collective-permute-start | bytes 552968 | tf_op jit(solution)/shard_map/ppermute | solution.py:531
  54.9 10.4 %collective-permute-start.11 = (bf16[144,640]{1,0:T(8,128)(2,1)S(1)}, bf16[144,640]{1,0:T(8,128)(2,1)S(1)}, u32[]{:S(2)}, u32[]{:S(2)}) collective-permute-start(bf16[144,640]{1,0:T(8,128)(2,1)S(1)} %slice.26.rest_2_.rest_3_), channel_id=1, source_target_pairs={{0,2},{2,0},{1,3},{3,1},{4,6},{6,4},{5,7},{7,5},{8,10},{10,8},{9,1... | collective-permute-start | bytes 552968 | tf_op jit(solution)/shard_map/ppermute | solution.py:531
  61.9 6.5 %collective-permute-start.9 = (bf16[144,640]{1,0:T(8,128)(2,1)S(1)}, bf16[144,640]{1,0:T(8,128)(2,1)S(1)}, u32[]{:S(2)}, u32[]{:S(2)}) collective-permute-start(bf16[144,640]{1,0:T(8,128)(2,1)S(1)} %slice.24.rest_0_.rest_2_), channel_id=1, source_target_pairs={{0,2},{2,0},{1,3},{3,1},{4,6},{6,4},{5,7},{7,5},{8,10},{10,8},{9,1... | collective-permute-start | bytes 552968 | tf_op jit(solution)/shard_map/ppermute | solution.py:531
  69.0 4.6 %collective-permute-start.12 = (bf16[512,1280]{1,0:T(8,128)(2,1)S(1)}, bf16[512,1280]{1,0:T(8,128)(2,1)S(1)}, u32[]{:S(2)}, u32[]{:S(2)}) collective-permute-start(bf16[512,1280]{1,0:T(8,128)(2,1)S(1)} %half.1.mine), channel_id=1, source_target_pairs={{0,1},{1,0},{2,3},{3,2},{4,5},{5,4},{6,7},{7,6},{8,9},{9,8},{10,11... | collective-permute-start | bytes 3932168 | tf_op jit(solution)/shard_map/ppermute | solution.py:538
  69.1 24.6 %collective-permute-start.13 = (bf16[1920,256]{1,0:T(8,128)(2,1)S(1)}, bf16[1920,256]{1,0:T(8,128)(2,1)S(1)}, u32[]{:S(2)}, u32[]{:S(2)}) collective-permute-start(bf16[1920,256]{1,0:T(8,128)(2,1)S(1)} %join.3), channel_id=1, source_target_pairs={{0,16},{16,0},{1,17},{17,1},{2,18},{18,2},{3,19},{19,3},{4,20},{20... | collective-permute-start | bytes 2949128 | tf_op jit(solution)/shard_map/ppermute | solution.py:180
  70.8 33.0 %collective-permute-start.14 = (bf16[384,640]{1,0:T(8,128)(2,1)S(1)}, bf16[384,640]{1,0:T(8,128)(2,1)S(1)}, u32[]{:S(2)}, u32[]{:S(2)}) collective-permute-start(bf16[384,640]{1,0:T(8,128)(2,1)S(1)} %join.5), channel_id=1, source_target_pairs={{0,16},{16,0},{1,17},{17,1},{2,18},{18,2},{3,19},{19,3},{4,20},{20... | collective-permute-start | bytes 1474568 | tf_op jit(solution)/shard_map/ppermute | solution.py:180
  71.4 25.2 %collective-permute-start.3 = (bf16[640,256]{1,0:T(8,128)(2,1)S(1)}, bf16[640,256]{1,0:T(8,128)(2,1)S(1)}, u32[]{:S(2)}, u32[]{:S(2)}) collective-permute-start(bf16[640,256]{1,0:T(8,128)(2,1)S(1)} %copy-done.13), channel_id=1, source_target_pairs={{0,8},{4,12},{8,0},{12,4},{1,9},{5,13},{9,1},{13,5},{2,10},{6,14},... | collective-permute-start | bytes 983048 | tf_op jit(solution)/shard_map/ppermute | solution.py:172
  72.7 23.9 %collective-permute-start.4 = (bf16[640,256]{1,0:T(8,128)(2,1)S(1)}, bf16[640,256]{1,0:T(8,128)(2,1)S(1)}, u32[]{:S(2)}, u32[]{:S(2)}) collective-permute-start(bf16[640,256]{1,0:T(8,128)(2,1)S(1)} %copy-done.13), channel_id=1, source_target_pairs={{0,4},{4,8},{8,12},{12,0},{1,5},{5,9},{9,13},{13,1},{2,6},{6,10},{... | collective-permute-start | bytes 983048 | tf_op jit(solution)/shard_map/ppermute | solution.py:172
  73.7 22.9 %collective-permute-start.5 = (bf16[640,256]{1,0:T(8,128)(2,1)S(1)}, bf16[640,256]{1,0:T(8,128)(2,1)S(1)}, u32[]{:S(2)}, u32[]{:S(2)}) collective-permute-start(bf16[640,256]{1,0:T(8,128)(2,1)S(1)} %copy-done.13), channel_id=1, source_target_pairs={{0,12},{4,0},{8,4},{12,8},{1,13},{5,1},{9,5},{13,9},{2,14},{6,2},{... | collective-permute-start | bytes 983048 | tf_op jit(solution)/shard_map/ppermute | solution.py:172
  105.5 3.1 %collective-permute-start.15 = (bf16[512,1280]{1,0:T(8,128)(2,1)S(1)}, bf16[512,1280]{1,0:T(8,128)(2,1)S(1)}, u32[]{:S(2)}, u32[]{:S(2)}) collective-permute-start(bf16[512,1280]{1,0:T(8,128)(2,1)S(1)} %get-tuple-element.61), channel_id=1, source_target_pairs={{0,1},{1,0},{2,3},{3,2},{4,5},{5,4},{6,7},{7,6},{8,9},{9,8},{10,11... | collective-permute-start | bytes 3932168 | tf_op jit(solution)/shard_map/ppermute | solution.py:594
  105.6 34.2 %collective-permute-start.26 = (bf16[1920,256]{1,0:T(8,128)(2,1)S(1)}, bf16[1920,256]{1,0:T(8,128)(2,1)S(1)}, u32[]{:S(2)}, u32[]{:S(2)}) collective-permute-start(bf16[1920,256]{1,0:T(8,128)(2,1)S(1)} %join.4), channel_id=1, source_target_pairs={{0,16},{16,0},{1,17},{17,1},{2,18},{18,2},{3,19},{19,3},{4,20},{20... | collective-permute-start | bytes 2949128 | tf_op jit(solution)/shard_map/ppermute | solution.py:180
  108.9 7.1 %collective-permute-start.21 = (bf16[128,640]{1,0:T(8,128)(2,1)S(1)}, bf16[128,640]{1,0:T(8,128)(2,1)S(1)}, u32[]{:S(2)}, u32[]{:S(2)}) collective-permute-start(bf16[128,640]{1,0:T(8,128)(2,1)S(1)} %get-tuple-element.69), channel_id=1, source_target_pairs={{0,2},{2,0},{1,3},{3,1},{4,6},{6,4},{5,7},{7,5},{8,10},{10,8},{9,1... | collective-permute-start | bytes 491528 | tf_op jit(solution)/shard_map/ppermute | solution.py:602
  110.5 9.0 %collective-permute-start.19 = (bf16[128,640]{1,0:T(8,128)(2,1)S(1)}, bf16[128,640]{1,0:T(8,128)(2,1)S(1)}, u32[]{:S(2)}, u32[]{:S(2)}) collective-permute-start(bf16[128,640]{1,0:T(8,128)(2,1)S(1)} %get-tuple-element.67), channel_id=1, source_target_pairs={{0,2},{2,0},{1,3},{3,1},{4,6},{6,4},{5,7},{7,5},{8,10},{10,8},{9,1... | collective-permute-start | bytes 491528 | tf_op jit(solution)/shard_map/ppermute | solution.py:602
  111.0 12.0 %collective-permute-start.17 = (bf16[128,640]{1,0:T(8,128)(2,1)S(1)}, bf16[128,640]{1,0:T(8,128)(2,1)S(1)}, u32[]{:S(2)}, u32[]{:S(2)}) collective-permute-start(bf16[128,640]{1,0:T(8,128)(2,1)S(1)} %get-tuple-element.65), channel_id=1, source_target_pairs={{0,2},{2,0},{1,3},{3,1},{4,6},{6,4},{5,7},{7,5},{8,10},{10,8},{9,1... | collective-permute-start | bytes 491528 | tf_op jit(solution)/shard_map/ppermute | solution.py:602
  112.5 13.2 %collective-permute-start.16 = (bf16[128,640]{1,0:T(8,128)(2,1)S(1)}, bf16[128,640]{1,0:T(8,128)(2,1)S(1)}, u32[]{:S(2)}, u32[]{:S(2)}) collective-permute-start(bf16[128,640]{1,0:T(8,128)(2,1)S(1)} %get-tuple-element.63), channel_id=1, source_target_pairs={{0,2},{2,0},{1,3},{3,1},{4,6},{6,4},{5,7},{7,5},{8,10},{10,8},{9,1... | collective-permute-start | bytes 491528 | tf_op jit(solution)/shard_map/ppermute | solution.py:602
  116.1 9.7 %collective-permute-start.22 = (bf16[128,640]{1,0:T(8,128)(2,1)S(1)}, bf16[128,640]{1,0:T(8,128)(2,1)S(1)}, u32[]{:S(2)}, u32[]{:S(2)}) collective-permute-start(bf16[128,640]{1,0:T(8,128)(2,1)S(1)} %add.9), channel_id=1, source_target_pairs={{0,4},{4,8},{8,12},{12,0},{1,5},{5,9},{9,13},{13,1},{2,6},{6,10},{... | collective-permute-start | bytes 491528 | tf_op jit(solution)/shard_map/ppermute | solution.py:172
  119.5 7.0 %collective-permute-start.20 = (bf16[128,640]{1,0:T(8,128)(2,1)S(1)}, bf16[128,640]{1,0:T(8,128)(2,1)S(1)}, u32[]{:S(2)}, u32[]{:S(2)}) collective-permute-start(bf16[128,640]{1,0:T(8,128)(2,1)S(1)} %add.8), channel_id=1, source_target_pairs={{0,12},{4,0},{8,4},{12,8},{1,13},{5,1},{9,5},{13,9},{2,14},{6,2},{... | collective-permute-start | bytes 491528 | tf_op jit(solution)/shard_map/ppermute | solution.py:172
  123.0 10.5 %collective-permute-start.18 = (bf16[128,640]{1,0:T(8,128)(2,1)S(1)}, bf16[128,640]{1,0:T(8,128)(2,1)S(1)}, u32[]{:S(2)}, u32[]{:S(2)}) collective-permute-start(bf16[128,640]{1,0:T(8,128)(2,1)S(1)} %add.7), channel_id=1, source_target_pairs={{0,8},{4,12},{8,0},{12,4},{1,9},{5,13},{9,1},{13,5},{2,10},{6,14},... | collective-permute-start | bytes 491528 | tf_op jit(solution)/shard_map/ppermute | solution.py:172
  134.4 5.3 %collective-permute-start.24 = (bf16[128,640]{1,0:T(8,128)(2,1)S(1)}, bf16[128,640]{1,0:T(8,128)(2,1)S(1)}, u32[]{:S(2)}, u32[]{:S(2)}) collective-permute-start(bf16[128,640]{1,0:T(8,128)(2,1)S(1)} %get-tuple-element.71.a), channel_id=1, source_target_pairs={{0,2},{2,0},{1,3},{3,1},{4,6},{6,4},{5,7},{7,5},{8,10},{10,8},{9,1... | collective-permute-start | bytes 491528 | tf_op jit(solution)/shard_map/ppermute | solution.py:184
  135.9 3.9 %collective-permute-start.23 = (bf16[128,640]{1,0:T(8,128)(2,1)S(1)}, bf16[128,640]{1,0:T(8,128)(2,1)S(1)}, u32[]{:S(2)}, u32[]{:S(2)}) collective-permute-start(bf16[128,640]{1,0:T(8,128)(2,1)S(1)} %get-tuple-element.71.a), channel_id=1, source_target_pairs={{0,1},{1,0},{2,3},{3,2},{4,5},{5,4},{6,7},{7,6},{8,9},{9,8},{10,11... | collective-permute-start | bytes 491528 | tf_op jit(solution)/shard_map/ppermute | solution.py:185
  139.7 1.4 collective-permute-start.25
  142.6 1.9 %collective-permute-start.27 = (bf16[64,512]{1,0:T(8,128)(2,1)S(1)}, bf16[64,512]{1,0:T(8,128)(2,1)S(1)}, u32[]{:S(2)}, u32[]{:S(2)}) collective-permute-start(bf16[64,512]{1,0:T(8,128)(2,1)S(1)} %get-tuple-element.73), channel_id=1, source_target_pairs={{0,1},{1,0},{2,3},{3,2},{4,5},{5,4},{6,7},{7,6},{8,9},{9,8},{10,11... | collective-permute-start | bytes 196616 | tf_op jit(solution)/shard_map/ppermute | solution.py:635
  142.8 4.4 %collective-permute-start.28 = (bf16[64,512]{1,0:T(8,128)(2,1)S(1)}, bf16[64,512]{1,0:T(8,128)(2,1)S(1)}, u32[]{:S(2)}, u32[]{:S(2)}) collective-permute-start(bf16[64,512]{1,0:T(8,128)(2,1)S(1)} %get-tuple-element.74), channel_id=1, source_target_pairs={{0,2},{2,0},{1,3},{3,1},{4,6},{6,4},{5,7},{7,5},{8,10},{10,8},{9,1... | collective-permute-start | bytes 196616 | tf_op jit(solution)/shard_map/ppermute | solution.py:635
  144.3 4.1 %collective-permute-start.29 = (bf16[64,512]{1,0:T(8,128)(2,1)S(1)}, bf16[64,512]{1,0:T(8,128)(2,1)S(1)}, u32[]{:S(2)}, u32[]{:S(2)}) collective-permute-start(bf16[64,512]{1,0:T(8,128)(2,1)S(1)} %get-tuple-element.75), channel_id=1, source_target_pairs={{0,3},{3,0},{1,2},{2,1},{4,7},{7,4},{5,6},{6,5},{8,11},{11,8},{9,1... | collective-permute-start | bytes 196616 | tf_op jit(solution)/shard_map/ppermute | solution.py:635
  (12 other events, 170.2 us)

commit v7 on v6

--- a/solution.py
+++ b/solution.py
@@ -294,16 +294,25 @@
     )(*parts)[0]
 
 
-def half_kernel(place, moe_in, *rest):
-    own, across, out = rest[:3], rest[3:6], rest[6]
+def part_kernel(a, b, c, tops, downs):
+    top = tops.shape[0] // 3
+    low = downs.shape[0] // 3
+    for i, part in enumerate((a, b, c)):
+        tops[i * top : (i + 1) * top, :] = part[:top, :]
+        downs[i * low : (i + 1) * low, :] = part[top:, :]
+
+
+def half_kernel(place, moe_in, a, b, c, across, out):
+    own = (a, b, c)
     rows = moe_in.shape[0]
+    top = across.shape[0] // 3
     piece = out.shape[1] // 2
     out[:rows, :piece] = moe_in[:, lanes(place[1], piece)]
     out[:rows, piece:] = moe_in[:, lanes(place[1] ^ 2, piece)]
     for i, shift in enumerate(SHIFTS):
         span = slice(shift * rows, (shift + 1) * rows)
         out[span, :piece] = own[i][:rows, :]
-        out[span, piece:] = across[i][:rows, :]
+        out[span, piece:] = across[i * top : i * top + rows, :]
 
 
 def routed_up_kernel(place, mine, theirs, gate, up, tokens, hidden):
@@ -373,7 +382,7 @@
     weights[:, lanes(zone, piece)] = own[...]
     for i, (shift, part) in enumerate(zip(SHIFTS, (a, b, c))):
         cols = lanes(lax.rem(zone - shift + 4, 4), piece)
-        weights[pl.ds(pl.multiple_of(group * half, 128), half), cols] = part[...]
+        weights[pl.ds(pl.multiple_of(group * half, 128), half), cols] = part[-half:, :]
         weights[pl.ds(pl.multiple_of((1 - group) * half, 128), half), cols] = other[
             i * half : (i + 1) * half, :
         ]
@@ -421,7 +430,7 @@
     for part, pieces in ((0, got), (1, other)):
         value = dot(ready[:, lanes(zone, near)], own[:, lanes(group ^ part, half)])
         for i, shift in enumerate(SHIFTS):
-            source = lax.rem(zone - shift + 4, 4)
+            source = zone ^ shift
             value = value + dot(ready[:, lanes(source, near)], pieces[i][...])
         key_value[:, lanes(group ^ part, half)] = value.astype(BF16)
     held = full.shape[0] // BLOCK
@@ -519,26 +528,27 @@
     own_weights, own_down, weight_messages, kv_half = second[0], second[1], second[2:5], second[5]
 
     mixed = [to_shift(values, s) for values, s in zip(mixed_messages, SHIFTS)]
-    top = rows + META
-    arrived = [values[:top] for values in mixed]
     got = [to_shift(values, s) for values, s in zip(weight_messages, SHIFTS)]
-    joined = join(*got)
+    tops, downs = call(
+        part_kernel,
+        [((3 * (rows + META), piece), BF16), ((3 * half, piece), BF16)],
+        [VMEM] * 3,
+        name="part",
+    )(*lax.optimization_barrier((*mixed, got[0]))[:3])
+    down_other = swap_groups(downs)
+    joined = join(*lax.optimization_barrier(tuple(got) + (down_other,))[:3])
     other = swap_groups(joined)
 
-    down_got = [values[top:] for values in mixed]
-    down_other = swap_groups(join(*down_got))
-
-    across = [lax.ppermute(values, "decode", SWAP_CHIP) for values in arrived]
+
+    across = lax.ppermute(tops, "decode", SWAP_CHIP)
     (token_half,) = call(
         half_kernel,
         [((total_rows, 2 * piece), BF16)],
-        [SMEM] + [VMEM] * 7,
+        [SMEM] + [VMEM] * 5,
         name="half",
-    )(after(place, joined), moe_in, *arrived, *across)
+    )(after(place, joined), moe_in, *mixed, across)
     token_rest = lax.ppermute(token_half, "decode", SWAP_CORE)
 
-    kv_half = after(kv_half, joined)
-    kv_got = [to_shift(kv_half, s) for s in SHIFTS]
     tokens, routed_hidden = call(
         routed_up_kernel,
         [((total_rows, width), BF16), ((total_rows, routed_width), BF16)],
@@ -560,7 +570,7 @@
         place,
         routed_hidden,
         message,
-        *[arrived[SHIFTS.index(s)] for s in range(1, zones)],
+        *[mixed[SHIFTS.index(s)] for s in range(1, zones)],
         w_down,
     )
 
@@ -573,6 +583,10 @@
         name="gate_up_first",
         vmem=12,
     )(after(place, routed), tokens, own_weights, *got)
+    kv_half = after(kv_half, joined)
+    kv_far = lax.ppermute(kv_half, "expert", SWAP_CHIP)
+    kv_near = lax.ppermute(kv_half, "expert", SWAP_CORE)
+    kv_got = [kv_far, kv_near, lax.ppermute(after(kv_far, first_half), "expert", SWAP_CORE)]
     (shared_hidden,) = call(
         gate_up_second_kernel,
         [((total_rows, hidden), BF16)],
@@ -590,7 +604,7 @@
         [pltpu.VMEM((hidden, width), BF16)],
         name="down",
         vmem=14,
-    )(after(place, kv_joined), routed, shared_hidden, own_down, down_other, *down_got)
+    )(after(place, kv_joined), routed, shared_hidden, own_down, down_other, *mixed)
     beside = lax.ppermute(send, "decode", SWAP_CORE)
     kv_other = swap_groups(kv_joined)
     passed = call(

time: 150 us -> 148 us (0.987)
  starting transfers between devices: 43.2 us -> 34.6 us
  waiting for transfers between devices: 81.8 us -> 88.3 us
    ppermute x12 -> x9, waiting for transfers between devices: 43.2 us -> 57.8 us  [to_shift(): lax.ppermute(values, 'expert', [(i, (i + shift) % count) for i in range(c...]
    ppermute x3, waiting for transfers between devices: 16.8 us -> 5.89 us  [swap_groups(): return lax.ppermute(values, 'groups', SWAP_GROUP)]
    ppermute x12 -> x9, starting transfers between devices: 27.3 us -> 18.9 us  [to_shift(): lax.ppermute(values, 'expert', [(i, (i + shift) % count) for i in range(c...]
    ppermute x3 -> x4, waiting for transfers between devices: 3.01 us -> 8.03 us  [the longest x1 6.52 us: near_plan(): kv_far = lax.ppermute(kv_half, 'expert', SWAP_CHIP)]
    ppermute x4, waiting for transfers between devices: 8.25 us -> 5.44 us  [near_plan(): lax.ppermute(passed[4 + s], 'decode', SWAP_CHIP)]
    ppermute x3 -> x4, starting transfers between devices: 4.54 us -> 5.17 us  [the longest x1 1.85 us: near_plan(): kv_far = lax.ppermute(kv_half, 'expert', SWAP_CHIP)]
  transfers between devices with their start and end apart: 30 -> 28, of which waited for: 19 -> 16; matrix products, arithmetic and copies ran while one was open for 0% -> 0% of each run, Pallas kernels for 10% -> 10%
where the time goes in v7:
time: 148 us
  waiting for transfers between devices  88.3 us (60%)
  starting transfers between devices  34.6 us (23%)
  Pallas kernels  23.4 us (16%)
    ppermute x9, waiting for transfers between devices, to_shift(): lax.ppermute(values, 'expert', [(i, (i + shift) % count) for i in range(c...  57.8 us
    ppermute x9, starting transfers between devices, to_shift(): lax.ppermute(values, 'expert', [(i, (i + shift) % count) for i in range(c...  18.9 us
    ppermute x1, waiting for transfers between devices, near_plan(): kv_far = lax.ppermute(kv_half, 'expert', SWAP_CHIP)  6.52 us
    ppermute x3, waiting for transfers between devices, swap_groups(): return lax.ppermute(values, 'groups', SWAP_GROUP)  5.89 us
    ppermute x4, waiting for transfers between devices, near_plan(): lax.ppermute(passed[4 + s], 'decode', SWAP_CHIP)  5.44 us
    ppermute x1, waiting for transfers between devices, spread(): across = lax.ppermute(values, 'decode', SWAP_CHIP)  4.74 us
    ppermute x4, starting transfers between devices, near_plan(): lax.ppermute(passed[4 + s], 'decode', SWAP_CHIP)  4.15 us
    pallas_call x1, Pallas kernels, near_plan(): call(second_kernel, [((near, 2 * hidden), BF16), ((hidden, piece), BF16)]...  3.84 us
  transfers between devices with their start and end apart: 28, of which 16 were waited for; matrix products, arithmetic and copies ran while one was open for 0% of the time, Pallas kernels for 10%

profile of v7, /device:TPU:0, one launch (start us, length us, event | category | flops | bytes accessed | tf_op | source)
XLA Modules:
  0.0 147.9 jit_solution(11357106424992182587)
XLA Ops:
  1.3 3.5 %first.1 = (bf16[128,2560]{1,0:T(8,128)(2,1)}, bf16[144,640]{1,0:T(8,128)(2,1)}, bf16[128,640]{1,0:T(8,128)(2,1)}, bf16[272,640]{1,0:T(8,128)(2,1)}, bf16[272,640]{1,0:T(8,128)(2,1)}, /*index=5*/bf16[272,640]{1,0:T(8,128)(2,1)}) custom-call(s32[3]{0:T(128)} %pad_add_fusion.refs_0_.place, bf16[128,2560]{1,0:T(8,128)(2,1)} %refs_1_.1, f32[2560]{0:T(1024)} %refs_2_.1, ...), custom_call_target="tpu_custom_call" | custom-call | tf_op jit(solution)/shard_map/first/pallas_call | solution.py:495
  4.8 4.1 %collective-permute-start.3 = (bf16[272,640]{1,0:T(8,128)(2,1)}, bf16[272,640]{1,0:T(8,128)(2,1)S(1)}, u32[]{:S(2)}, u32[]{:S(2)}) collective-permute-start(bf16[272,640]{1,0:T(8,128)(2,1)} %get-tuple-element.53), channel_id=1, source_target_pairs={{0,8},{4,12},{8,0},{12,4},{1,9},{5,13},{9,1},{13,5},{2,10},{6,14},... | collective-permute-start | bytes 1044488 | tf_op jit(solution)/shard_map/ppermute | solution.py:172
  8.9 1.6 %collective-permute-start.4 = (bf16[272,640]{1,0:T(8,128)(2,1)}, bf16[272,640]{1,0:T(8,128)(2,1)S(1)}, u32[]{:S(2)}, u32[]{:S(2)}) collective-permute-start(bf16[272,640]{1,0:T(8,128)(2,1)} %get-tuple-element.54), channel_id=1, source_target_pairs={{0,4},{4,8},{8,12},{12,0},{1,5},{5,9},{9,13},{13,1},{2,6},{6,10},{... | collective-permute-start | bytes 1044488 | tf_op jit(solution)/shard_map/ppermute | solution.py:172
  10.5 2.2 %collective-permute-start.5 = (bf16[272,640]{1,0:T(8,128)(2,1)}, bf16[272,640]{1,0:T(8,128)(2,1)S(1)}, u32[]{:S(2)}, u32[]{:S(2)}) collective-permute-start(bf16[272,640]{1,0:T(8,128)(2,1)} %get-tuple-element.55), channel_id=1, source_target_pairs={{0,12},{4,0},{8,4},{12,8},{1,13},{5,1},{9,5},{13,9},{2,14},{6,2},{... | collective-permute-start | bytes 1044488 | tf_op jit(solution)/shard_map/ppermute | solution.py:172
  12.8 3.8 %second.1 = (bf16[640,512]{1,0:T(8,128)(2,1)}, bf16[256,640]{1,0:T(8,128)(2,1)}, bf16[640,256]{1,0:T(8,128)(2,1)}, bf16[640,256]{1,0:T(8,128)(2,1)}, bf16[640,256]{1,0:T(8,128)(2,1)}, /*index=5*/bf16[640,256]{1,0:T(8,128)(2,1)}) custom-call(s32[3]{0:T(128)} %pad_add_fusion.refs_0_.place, bf16[640,1024]{1,0:T(8,128)(2,1)} %gate.2, bf16[640,1024]{1,0:T(8,128)(2,1)} %up.2, ...), custom_call_target="tpu_custom_call" | custom-call | tf_op jit(solution)/shard_map/second/pallas_call | solution.py:518
  16.7 37.1 %collective-permute-done.refs_0_.a = bf16[640,256]{1,0:T(8,128)(2,1)S(1)} collective-permute-done((bf16[640,256]{1,0:T(8,128)(2,1)}, bf16[640,256]{1,0:T(8,128)(2,1)S(1)}, u32[]{:S(2)}, u32[]{:S(2)}) %collective-permute-start) | collective-permute-done | bytes 327712 | tf_op jit(solution)/shard_map/ppermute | solution.py:172
  53.9 1.6 %collective-permute-start.9 = (bf16[432,640]{1,0:T(8,128)(2,1)S(1)}, bf16[432,640]{1,0:T(8,128)(2,1)S(1)}, u32[]{:S(2)}, u32[]{:S(2)}) collective-permute-start(bf16[432,640]{1,0:T(8,128)(2,1)S(1)} %get-tuple-element.66), channel_id=1, source_target_pairs={{0,2},{2,0},{1,3},{3,1},{4,6},{6,4},{5,7},{7,5},{8,10},{10,8},{9,1... | collective-permute-start | bytes 1658888 | tf_op jit(solution)/shard_map/ppermute | solution.py:543
  57.7 3.1 %collective-permute-start.2 = (bf16[640,256]{1,0:T(8,128)(2,1)}, bf16[640,256]{1,0:T(8,128)(2,1)S(1)}, u32[]{:S(2)}, u32[]{:S(2)}) collective-permute-start(bf16[640,256]{1,0:T(8,128)(2,1)} %get-tuple-element.52), channel_id=1, source_target_pairs={{0,12},{4,0},{8,4},{12,8},{1,13},{5,1},{9,5},{13,9},{2,14},{6,2},{... | collective-permute-start | bytes 983048 | tf_op jit(solution)/shard_map/ppermute | solution.py:172
  60.8 8.9 %collective-permute-done.1.refs_1_.b = bf16[640,256]{1,0:T(8,128)(2,1)S(1)} collective-permute-done((bf16[640,256]{1,0:T(8,128)(2,1)}, bf16[640,256]{1,0:T(8,128)(2,1)S(1)}, u32[]{:S(2)}, u32[]{:S(2)}) %collective-permute-start.1) | collective-permute-done | bytes 327712 | tf_op jit(solution)/shard_map/ppermute | solution.py:172
  69.7 4.1 %collective-permute-done.2.refs_2_.c = bf16[640,256]{1,0:T(8,128)(2,1)S(1)} collective-permute-done((bf16[640,256]{1,0:T(8,128)(2,1)}, bf16[640,256]{1,0:T(8,128)(2,1)S(1)}, u32[]{:S(2)}, u32[]{:S(2)}) %collective-permute-start.2) | collective-permute-done | bytes 327712 | tf_op jit(solution)/shard_map/ppermute | solution.py:172
  75.2 1.9 %collective-permute-start.7 = (bf16[640,256]{1,0:T(8,128)(2,1)S(1)}, bf16[640,256]{1,0:T(8,128)(2,1)S(1)}, u32[]{:S(2)}, u32[]{:S(2)}) collective-permute-start(bf16[640,256]{1,0:T(8,128)(2,1)S(1)} %copy-done.13), channel_id=1, source_target_pairs={{0,8},{8,0},{4,12},{12,4},{1,9},{9,1},{5,13},{13,5},{2,10},{10,2},... | collective-permute-start | bytes 983048 | tf_op jit(solution)/shard_map/ppermute | solution.py:587
  77.0 1.7 %collective-permute-start.8 = (bf16[640,256]{1,0:T(8,128)(2,1)S(1)}, bf16[640,256]{1,0:T(8,128)(2,1)S(1)}, u32[]{:S(2)}, u32[]{:S(2)}) collective-permute-start(bf16[640,256]{1,0:T(8,128)(2,1)S(1)} %copy-done.13), channel_id=1, source_target_pairs={{0,4},{4,0},{8,12},{12,8},{1,5},{5,1},{9,13},{13,9},{2,6},{6,2},{1... | collective-permute-start | bytes 983048 | tf_op jit(solution)/shard_map/ppermute | solution.py:588
  78.8 3.6 %routed_up.1 = (bf16[512,2560]{1,0:T(8,128)(2,1)S(1)}, bf16[512,512]{1,0:T(8,128)(2,1)S(1)}) custom-call(s32[3]{0:T(128)S(1)} %copy-done.9, bf16[512,1280]{1,0:T(8,128)(2,1)S(1)} %half.1.mine, bf16[512,1280]{1,0:T(8,128)(2,1)S(1)} %collective-permute-done.10.theirs, bf16[1,2560,512]{2,1,0:T(8,128)(2,1)S(1)} %copy-done.2, bf16[1,2560,512]{2,1,0:T(8,128)(2,1)S(1)} %copy-done.3), custom_call_target="tpu_custom_call" | custom-call | tf_op jit(solution)/shard_map/routed_up/pallas_call | solution.py:552
  82.4 2.4 %routed_down.1.routed = bf16[512,2560]{1,0:T(8,128)(2,1)S(1)} custom-call(s32[3]{0:T(128)S(1)} %copy-done.9, bf16[512,512]{1,0:T(8,128)(2,1)S(1)} %get-tuple-element.67.hidden, bf16[144,640]{1,0:T(8,128)(2,1)S(1)} %copy-done.7, bf16[272,640]{1,0:T(8,128)(2,1)S(1)} %collective-permute-done.4.b.rest_1_, bf16[272,640]{1,0:T(8,128)(2,1)S(1)} %collective-permute-done.3.a.rest_2_, ...), custom_call_target="tpu_custom_call" | custom-call | tf_op jit(solution)/shard_map/routed_down/pallas_call | solution.py:561
  84.8 1.5 %gate_up_first.1.first = bf16[512,128]{1,0:T(8,128)(2,1)S(1)} custom-call(s32[3]{0:T(128)S(1)} %copy-done.9, bf16[512,2560]{1,0:T(8,128)(2,1)S(1)} %get-tuple-element.70.tokens, bf16[640,512]{1,0:T(8,128)(2,1)S(1)} %copy-done.1, bf16[640,256]{1,0:T(8,128)(2,1)S(1)} %collective-permute-done.refs_0_.a, bf16[640,256]{1,0:T(8,128)(2,1)S(1)} %collective-permute-done.1.refs_1_.b, ...), custom_call_target="tpu_custom_call" | custom-call | tf_op jit(solution)/shard_map/gate_up_first/pallas_call | solution.py:577
  86.4 6.5 %collective-permute-done.7.refs_0_.rest_0_ = bf16[640,256]{1,0:T(8,128)(2,1)S(1)} collective-permute-done((bf16[640,256]{1,0:T(8,128)(2,1)S(1)}, bf16[640,256]{1,0:T(8,128)(2,1)S(1)}, u32[]{:S(2)}, u32[]{:S(2)}) %collective-permute-start.7) | collective-permute-done | bytes 327712 | tf_op jit(solution)/shard_map/ppermute | solution.py:587
  92.9 5.9 %collective-permute-done.12.rest = bf16[1920,256]{1,0:T(8,128)(2,1)S(1)} collective-permute-done((bf16[1920,256]{1,0:T(8,128)(2,1)S(1)}, bf16[1920,256]{1,0:T(8,128)(2,1)S(1)}, u32[]{:S(2)}, u32[]{:S(2)}) %collective-permute-start.12) | collective-permute-done | bytes 983072 | tf_op jit(solution)/shard_map/ppermute | solution.py:180
  98.8 1.5 %gate_up_second.1.hidden = bf16[512,256]{1,0:T(8,128)(2,1)S(1)} custom-call(s32[3]{0:T(128)S(1)} %copy-done.9, bf16[512,2560]{1,0:T(8,128)(2,1)S(1)} %get-tuple-element.70.tokens, bf16[640,512]{1,0:T(8,128)(2,1)S(1)} %copy-done.1, bf16[512,128]{1,0:T(8,128)(2,1)S(1)} %gate_up_first.1.first, bf16[1920,256]{1,0:T(8,128)(2,1)S(1)} %collective-permute-done.12.rest), custom_call_target="tpu_custom_call" | custom-call | tf_op jit(solution)/shard_map/gate_up_second/pallas_call | solution.py:590
  101.9 1.7 %down.3 = (bf16[512,1280]{1,0:T(8,128)(2,1)S(1)}, f32[512,1280]{1,0:T(8,128)S(1)}) custom-call(s32[3]{0:T(128)S(1)} %copy-done.9, bf16[512,2560]{1,0:T(8,128)(2,1)S(1)} %routed_down.1.routed, bf16[512,256]{1,0:T(8,128)(2,1)S(1)} %gate_up_second.1.hidden, bf16[256,640]{1,0:T(8,128)(2,1)S(1)} %copy-done.6, bf16[384,640]{1,0:T(8,128)(2,1)S(1)} %collective-permute-done.6.other, ...), custom_call_target="tpu_custom_call" | custom-call | tf_op jit(solution)/shard_map/down/pallas_call | solution.py:600
  103.7 1.6 %collective-permute-start.24 = (bf16[1920,256]{1,0:T(8,128)(2,1)S(1)}, bf16[1920,256]{1,0:T(8,128)(2,1)S(1)}, u32[]{:S(2)}, u32[]{:S(2)}) collective-permute-start(bf16[1920,256]{1,0:T(8,128)(2,1)S(1)} %join.3), channel_id=1, source_target_pairs={{0,16},{16,0},{1,17},{17,1},{2,18},{18,2},{3,19},{19,3},{4,20},{20... | collective-permute-start | bytes 2949128 | tf_op jit(solution)/shard_map/ppermute | solution.py:180
  107.5 1.5 %collective-permute-start.17 = (bf16[128,640]{1,0:T(8,128)(2,1)S(1)}, bf16[128,640]{1,0:T(8,128)(2,1)S(1)}, u32[]{:S(2)}, u32[]{:S(2)}) collective-permute-start(bf16[128,640]{1,0:T(8,128)(2,1)S(1)} %get-tuple-element.85), channel_id=1, source_target_pairs={{0,2},{2,0},{1,3},{3,1},{4,6},{6,4},{5,7},{7,5},{8,10},{10,8},{9,1... | collective-permute-start | bytes 491528 | tf_op jit(solution)/shard_map/ppermute | solution.py:616
  109.5 1.5 %collective-permute-start.14 = (bf16[128,640]{1,0:T(8,128)(2,1)S(1)}, bf16[128,640]{1,0:T(8,128)(2,1)S(1)}, u32[]{:S(2)}, u32[]{:S(2)}) collective-permute-start(bf16[128,640]{1,0:T(8,128)(2,1)S(1)} %get-tuple-element.81), channel_id=1, source_target_pairs={{0,2},{2,0},{1,3},{3,1},{4,6},{6,4},{5,7},{7,5},{8,10},{10,8},{9,1... | collective-permute-start | bytes 491528 | tf_op jit(solution)/shard_map/ppermute | solution.py:616
  111.1 3.0 %collective-permute-done.19.b = bf16[128,640]{1,0:T(8,128)(2,1)S(1)} collective-permute-done((bf16[128,640]{1,0:T(8,128)(2,1)S(1)}, bf16[128,640]{1,0:T(8,128)(2,1)S(1)}, u32[]{:S(2)}, u32[]{:S(2)}) %collective-permute-start.19) | collective-permute-done | bytes 163872 | tf_op jit(solution)/shard_map/ppermute | solution.py:616
  115.4 2.2 %collective-permute-done.17.b = bf16[128,640]{1,0:T(8,128)(2,1)S(1)} collective-permute-done((bf16[128,640]{1,0:T(8,128)(2,1)S(1)}, bf16[128,640]{1,0:T(8,128)(2,1)S(1)}, u32[]{:S(2)}, u32[]{:S(2)}) %collective-permute-start.17) | collective-permute-done | bytes 163872 | tf_op jit(solution)/shard_map/ppermute | solution.py:616
  117.6 3.6 %collective-permute-start.18 = (bf16[128,640]{1,0:T(8,128)(2,1)S(1)}, bf16[128,640]{1,0:T(8,128)(2,1)S(1)}, u32[]{:S(2)}, u32[]{:S(2)}) collective-permute-start(bf16[128,640]{1,0:T(8,128)(2,1)S(1)} %add.8), channel_id=1, source_target_pairs={{0,12},{4,0},{8,4},{12,8},{1,13},{5,1},{9,5},{13,9},{2,14},{6,2},{... | collective-permute-start | bytes 491528 | tf_op jit(solution)/shard_map/ppermute | solution.py:172
  121.2 2.3 %collective-permute-start.16 = (bf16[128,640]{1,0:T(8,128)(2,1)S(1)}, bf16[128,640]{1,0:T(8,128)(2,1)S(1)}, u32[]{:S(2)}, u32[]{:S(2)}) collective-permute-start(bf16[128,640]{1,0:T(8,128)(2,1)S(1)} %add.7), channel_id=1, source_target_pairs={{0,8},{4,12},{8,0},{12,4},{1,9},{5,13},{9,1},{13,5},{2,10},{6,14},... | collective-permute-start | bytes 491528 | tf_op jit(solution)/shard_map/ppermute | solution.py:172
  123.8 1.8 %collective-permute-done.18.b = bf16[128,640]{1,0:T(8,128)(2,1)S(1)} collective-permute-done((bf16[128,640]{1,0:T(8,128)(2,1)S(1)}, bf16[128,640]{1,0:T(8,128)(2,1)S(1)}, u32[]{:S(2)}, u32[]{:S(2)}) %collective-permute-start.18) | collective-permute-done | bytes 163872 | tf_op jit(solution)/shard_map/ppermute | solution.py:172
  125.6 6.0 %collective-permute-done.16.a = bf16[128,640]{1,0:T(8,128)(2,1)S(1)} collective-permute-done((bf16[128,640]{1,0:T(8,128)(2,1)S(1)}, bf16[128,640]{1,0:T(8,128)(2,1)S(1)}, u32[]{:S(2)}, u32[]{:S(2)}) %collective-permute-start.16) | collective-permute-done | bytes 163872 | tf_op jit(solution)/shard_map/ppermute | solution.py:172
  133.0 4.7 %collective-permute-done.22.c = bf16[128,640]{1,0:T(8,128)(2,1)S(1)} collective-permute-done((bf16[128,640]{1,0:T(8,128)(2,1)S(1)}, bf16[128,640]{1,0:T(8,128)(2,1)S(1)}, u32[]{:S(2)}, u32[]{:S(2)}) %collective-permute-start.22) | collective-permute-done | bytes 163872 | tf_op jit(solution)/shard_map/ppermute | solution.py:184
  139.2 1.6 %kv.3 = (bf16[64,512]{1,0:T(8,128)(2,1)S(1)}, bf16[64,512]{1,0:T(8,128)(2,1)S(1)}, bf16[64,512]{1,0:T(8,128)(2,1)S(1)}, bf16[64,512]{1,0:T(8,128)(2,1)S(1)}) custom-call(s32[3]{0:T(128)S(1)} %copy-done.9, s32[1,4]{1,0:T(1,128)S(1)} %copy-done.11, s32[1,4]{1,0:T(1,128)S(1)} %copy-done.12, f32[2560]{0:T(1024)S(1)} %copy-done.10, ...), custom_call_target="tpu_custom_call" | custom-call | tf_op jit(solution)/shard_map/kv/pallas_call | solution.py:627
  142.7 3.2 %collective-permute-done.26.c = bf16[64,512]{1,0:T(8,128)(2,1)S(1)} collective-permute-done((bf16[64,512]{1,0:T(8,128)(2,1)S(1)}, bf16[64,512]{1,0:T(8,128)(2,1)S(1)}, u32[]{:S(2)}, u32[]{:S(2)}) %collective-permute-start.26) | collective-permute-done | bytes 65568 | tf_op jit(solution)/shard_map/ppermute | solution.py:649
  146.2 1.7 %hand.1 = bf16[64,4,512]{2,1,0:T(4,128)(2,1)} custom-call(s32[3]{0:T(128)S(1)} %copy-done.9, bf16[64,512]{1,0:T(8,128)(2,1)S(1)} %get-tuple-element.90.a, bf16[64,512]{1,0:T(8,128)(2,1)S(1)} %collective-permute-done.25.b, bf16[64,512]{1,0:T(8,128)(2,1)S(1)} %collective-permute-done.26.c, bf16[64,512]{1,0:T(8,128)(2,1)S(1)} %collective-permute-done.27.d), custom_call_target="tpu_custom_call" | custom-call | tf_op jit(solution)/shard_map/hand/pallas_call | solution.py:652
  (71 shorter events, 15.5 us)
Async XLA Ops:
  4.8 48.9 %collective-permute-start.3 = (bf16[272,640]{1,0:T(8,128)(2,1)}, bf16[272,640]{1,0:T(8,128)(2,1)S(1)}, u32[]{:S(2)}, u32[]{:S(2)}) collective-permute-start(bf16[272,640]{1,0:T(8,128)(2,1)} %get-tuple-element.53), channel_id=1, source_target_pairs={{0,8},{4,12},{8,0},{12,4},{1,9},{5,13},{9,1},{13,5},{2,10},{6,14},... | collective-permute-start | bytes 1044488 | tf_op jit(solution)/shard_map/ppermute | solution.py:172
  8.9 44.8 %collective-permute-start.4 = (bf16[272,640]{1,0:T(8,128)(2,1)}, bf16[272,640]{1,0:T(8,128)(2,1)S(1)}, u32[]{:S(2)}, u32[]{:S(2)}) collective-permute-start(bf16[272,640]{1,0:T(8,128)(2,1)} %get-tuple-element.54), channel_id=1, source_target_pairs={{0,4},{4,8},{8,12},{12,0},{1,5},{5,9},{9,13},{13,1},{2,6},{6,10},{... | collective-permute-start | bytes 1044488 | tf_op jit(solution)/shard_map/ppermute | solution.py:172
  10.5 43.3 %collective-permute-start.5 = (bf16[272,640]{1,0:T(8,128)(2,1)}, bf16[272,640]{1,0:T(8,128)(2,1)S(1)}, u32[]{:S(2)}, u32[]{:S(2)}) collective-permute-start(bf16[272,640]{1,0:T(8,128)(2,1)} %get-tuple-element.55), channel_id=1, source_target_pairs={{0,12},{4,0},{8,4},{12,8},{1,13},{5,1},{9,5},{13,9},{2,14},{6,2},{... | collective-permute-start | bytes 1044488 | tf_op jit(solution)/shard_map/ppermute | solution.py:172
  16.6 57.2 %copy-start.5 = (bf16[128,2560]{1,0:T(8,128)(2,1)S(1)}, bf16[128,2560]{1,0:T(8,128)(2,1)}, u32[]{:S(2)}) copy-start(bf16[128,2560]{1,0:T(8,128)(2,1)} %get-tuple-element.65.moe_in) | copy-start | bytes 1966084
  16.6 57.2 %copy-start.9 = (s32[3]{0:T(128)S(1)}, s32[3]{0:T(128)}, u32[]{:S(2)}) copy-start(s32[3]{0:T(128)} %pad_add_fusion.refs_0_.place) | copy-start | bytes 40
  16.6 37.1 %collective-permute-start = (bf16[640,256]{1,0:T(8,128)(2,1)}, bf16[640,256]{1,0:T(8,128)(2,1)S(1)}, u32[]{:S(2)}, u32[]{:S(2)}) collective-permute-start(bf16[640,256]{1,0:T(8,128)(2,1)} %get-tuple-element.50), channel_id=1, source_target_pairs={{0,8},{4,12},{8,0},{12,4},{1,9},{5,13},{9,1},{13,5},{2,10},{6,14},... | collective-permute-start | bytes 983048 | tf_op jit(solution)/shard_map/ppermute | solution.py:172
  53.9 20.0 %collective-permute-start.9 = (bf16[432,640]{1,0:T(8,128)(2,1)S(1)}, bf16[432,640]{1,0:T(8,128)(2,1)S(1)}, u32[]{:S(2)}, u32[]{:S(2)}) collective-permute-start(bf16[432,640]{1,0:T(8,128)(2,1)S(1)} %get-tuple-element.66), channel_id=1, source_target_pairs={{0,2},{2,0},{1,3},{3,1},{4,6},{6,4},{5,7},{7,5},{8,10},{10,8},{9,1... | collective-permute-start | bytes 1658888 | tf_op jit(solution)/shard_map/ppermute | solution.py:543
  55.5 18.3 %collective-permute-start.6 = (bf16[384,640]{1,0:T(8,128)(2,1)S(1)}, bf16[384,640]{1,0:T(8,128)(2,1)S(1)}, u32[]{:S(2)}, u32[]{:S(2)}) collective-permute-start(bf16[384,640]{1,0:T(8,128)(2,1)S(1)} %get-tuple-element.59), channel_id=1, source_target_pairs={{0,16},{16,0},{1,17},{17,1},{2,18},{18,2},{3,19},{19,3},{4,20},{20... | collective-permute-start | bytes 1474568 | tf_op jit(solution)/shard_map/ppermute | solution.py:180
  57.0 12.7 %collective-permute-start.1 = (bf16[640,256]{1,0:T(8,128)(2,1)}, bf16[640,256]{1,0:T(8,128)(2,1)S(1)}, u32[]{:S(2)}, u32[]{:S(2)}) collective-permute-start(bf16[640,256]{1,0:T(8,128)(2,1)} %get-tuple-element.51), channel_id=1, source_target_pairs={{0,4},{4,8},{8,12},{12,0},{1,5},{5,9},{9,13},{13,1},{2,6},{6,10},{... | collective-permute-start | bytes 983048 | tf_op jit(solution)/shard_map/ppermute | solution.py:172
  57.7 16.0 %collective-permute-start.2 = (bf16[640,256]{1,0:T(8,128)(2,1)}, bf16[640,256]{1,0:T(8,128)(2,1)S(1)}, u32[]{:S(2)}, u32[]{:S(2)}) collective-permute-start(bf16[640,256]{1,0:T(8,128)(2,1)} %get-tuple-element.52), channel_id=1, source_target_pairs={{0,12},{4,0},{8,4},{12,8},{1,13},{5,1},{9,5},{13,9},{2,14},{6,2},{... | collective-permute-start | bytes 983048 | tf_op jit(solution)/shard_map/ppermute | solution.py:172
  74.5 4.2 %collective-permute-start.10 = (bf16[512,1280]{1,0:T(8,128)(2,1)S(1)}, bf16[512,1280]{1,0:T(8,128)(2,1)S(1)}, u32[]{:S(2)}, u32[]{:S(2)}) collective-permute-start(bf16[512,1280]{1,0:T(8,128)(2,1)S(1)} %half.1.mine), channel_id=1, source_target_pairs={{0,1},{1,0},{2,3},{3,2},{4,5},{5,4},{6,7},{7,6},{8,9},{9,8},{10,11... | collective-permute-start | bytes 3932168 | tf_op jit(solution)/shard_map/ppermute | solution.py:550
  74.6 24.2 %collective-permute-start.12 = (bf16[1920,256]{1,0:T(8,128)(2,1)S(1)}, bf16[1920,256]{1,0:T(8,128)(2,1)S(1)}, u32[]{:S(2)}, u32[]{:S(2)}) collective-permute-start(bf16[1920,256]{1,0:T(8,128)(2,1)S(1)} %join.2), channel_id=1, source_target_pairs={{0,16},{16,0},{1,17},{17,1},{2,18},{18,2},{3,19},{19,3},{4,20},{20... | collective-permute-start | bytes 2949128 | tf_op jit(solution)/shard_map/ppermute | solution.py:180
  75.2 17.7 %collective-permute-start.7 = (bf16[640,256]{1,0:T(8,128)(2,1)S(1)}, bf16[640,256]{1,0:T(8,128)(2,1)S(1)}, u32[]{:S(2)}, u32[]{:S(2)}) collective-permute-start(bf16[640,256]{1,0:T(8,128)(2,1)S(1)} %copy-done.13), channel_id=1, source_target_pairs={{0,8},{8,0},{4,12},{12,4},{1,9},{9,1},{5,13},{13,5},{2,10},{10,2},... | collective-permute-start | bytes 983048 | tf_op jit(solution)/shard_map/ppermute | solution.py:587
  77.0 23.3 %collective-permute-start.8 = (bf16[640,256]{1,0:T(8,128)(2,1)S(1)}, bf16[640,256]{1,0:T(8,128)(2,1)S(1)}, u32[]{:S(2)}, u32[]{:S(2)}) collective-permute-start(bf16[640,256]{1,0:T(8,128)(2,1)S(1)} %copy-done.13), channel_id=1, source_target_pairs={{0,4},{4,0},{8,12},{12,8},{1,5},{5,1},{9,13},{13,9},{2,6},{6,2},{1... | collective-permute-start | bytes 983048 | tf_op jit(solution)/shard_map/ppermute | solution.py:588
  92.9 9.0 %collective-permute-start.11 = (bf16[640,256]{1,0:T(8,128)(2,1)S(1)}, bf16[640,256]{1,0:T(8,128)(2,1)S(1)}, u32[]{:S(2)}, u32[]{:S(2)}) collective-permute-start(bf16[640,256]{1,0:T(8,128)(2,1)S(1)} %collective-permute-done.7.refs_0_.rest_0_), channel_id=1, source_target_pairs={{0,4},{4,0},{8,12},{12,8},{1,5},{5,1},{9,13},{13,9},{2,6},{6,2},{1... | collective-permute-start | bytes 983048 | tf_op jit(solution)/shard_map/ppermute | solution.py:589
  103.6 3.1 %collective-permute-start.13 = (bf16[512,1280]{1,0:T(8,128)(2,1)S(1)}, bf16[512,1280]{1,0:T(8,128)(2,1)S(1)}, u32[]{:S(2)}, u32[]{:S(2)}) collective-permute-start(bf16[512,1280]{1,0:T(8,128)(2,1)S(1)} %get-tuple-element.79), channel_id=1, source_target_pairs={{0,1},{1,0},{2,3},{3,2},{4,5},{5,4},{6,7},{7,6},{8,9},{9,8},{10,11... | collective-permute-start | bytes 3932168 | tf_op jit(solution)/shard_map/ppermute | solution.py:608
  103.7 34.1 %collective-permute-start.24 = (bf16[1920,256]{1,0:T(8,128)(2,1)S(1)}, bf16[1920,256]{1,0:T(8,128)(2,1)S(1)}, u32[]{:S(2)}, u32[]{:S(2)}) collective-permute-start(bf16[1920,256]{1,0:T(8,128)(2,1)S(1)} %join.3), channel_id=1, source_target_pairs={{0,16},{16,0},{1,17},{17,1},{2,18},{18,2},{3,19},{19,3},{4,20},{20... | collective-permute-start | bytes 2949128 | tf_op jit(solution)/shard_map/ppermute | solution.py:180
  106.9 7.1 %collective-permute-start.19 = (bf16[128,640]{1,0:T(8,128)(2,1)S(1)}, bf16[128,640]{1,0:T(8,128)(2,1)S(1)}, u32[]{:S(2)}, u32[]{:S(2)}) collective-permute-start(bf16[128,640]{1,0:T(8,128)(2,1)S(1)} %get-tuple-element.87), channel_id=1, source_target_pairs={{0,2},{2,0},{1,3},{3,1},{4,6},{6,4},{5,7},{7,5},{8,10},{10,8},{9,1... | collective-permute-start | bytes 491528 | tf_op jit(solution)/shard_map/ppermute | solution.py:616
  107.5 10.1 %collective-permute-start.17 = (bf16[128,640]{1,0:T(8,128)(2,1)S(1)}, bf16[128,640]{1,0:T(8,128)(2,1)S(1)}, u32[]{:S(2)}, u32[]{:S(2)}) collective-permute-start(bf16[128,640]{1,0:T(8,128)(2,1)S(1)} %get-tuple-element.85), channel_id=1, source_target_pairs={{0,2},{2,0},{1,3},{3,1},{4,6},{6,4},{5,7},{7,5},{8,10},{10,8},{9,1... | collective-permute-start | bytes 491528 | tf_op jit(solution)/shard_map/ppermute | solution.py:616
  109.0 12.1 %collective-permute-start.15 = (bf16[128,640]{1,0:T(8,128)(2,1)S(1)}, bf16[128,640]{1,0:T(8,128)(2,1)S(1)}, u32[]{:S(2)}, u32[]{:S(2)}) collective-permute-start(bf16[128,640]{1,0:T(8,128)(2,1)S(1)} %get-tuple-element.83), channel_id=1, source_target_pairs={{0,2},{2,0},{1,3},{3,1},{4,6},{6,4},{5,7},{7,5},{8,10},{10,8},{9,1... | collective-permute-start | bytes 491528 | tf_op jit(solution)/shard_map/ppermute | solution.py:616
  109.5 14.2 %collective-permute-start.14 = (bf16[128,640]{1,0:T(8,128)(2,1)S(1)}, bf16[128,640]{1,0:T(8,128)(2,1)S(1)}, u32[]{:S(2)}, u32[]{:S(2)}) collective-permute-start(bf16[128,640]{1,0:T(8,128)(2,1)S(1)} %get-tuple-element.81), channel_id=1, source_target_pairs={{0,2},{2,0},{1,3},{3,1},{4,6},{6,4},{5,7},{7,5},{8,10},{10,8},{9,1... | collective-permute-start | bytes 491528 | tf_op jit(solution)/shard_map/ppermute | solution.py:616
  114.1 25.1 %copy-start = (bf16[640,512]{1,0:T(8,128)(2,1)S(1)}, bf16[640,512]{1,0:T(8,128)(2,1)}, u32[]{:S(2)}) copy-start(bf16[640,512]{1,0:T(8,128)(2,1)} %own.1) | copy-start | bytes 1966084
  114.1 25.1 %copy-start.10 = (f32[2560]{0:T(1024)S(1)}, f32[2560]{0:T(1024)}, u32[]{:S(2)}) copy-start(f32[2560]{0:T(1024)} %gain.1) | copy-start | bytes 30724
  114.2 9.6 %collective-permute-start.20 = (bf16[128,640]{1,0:T(8,128)(2,1)S(1)}, bf16[128,640]{1,0:T(8,128)(2,1)S(1)}, u32[]{:S(2)}, u32[]{:S(2)}) collective-permute-start(bf16[128,640]{1,0:T(8,128)(2,1)S(1)} %add.9), channel_id=1, source_target_pairs={{0,4},{4,8},{8,12},{12,0},{1,5},{5,9},{9,13},{13,1},{2,6},{6,10},{... | collective-permute-start | bytes 491528 | tf_op jit(solution)/shard_map/ppermute | solution.py:172
  117.6 8.0 %collective-permute-start.18 = (bf16[128,640]{1,0:T(8,128)(2,1)S(1)}, bf16[128,640]{1,0:T(8,128)(2,1)S(1)}, u32[]{:S(2)}, u32[]{:S(2)}) collective-permute-start(bf16[128,640]{1,0:T(8,128)(2,1)S(1)} %add.8), channel_id=1, source_target_pairs={{0,12},{4,0},{8,4},{12,8},{1,13},{5,1},{9,5},{13,9},{2,14},{6,2},{... | collective-permute-start | bytes 491528 | tf_op jit(solution)/shard_map/ppermute | solution.py:172
  121.2 10.4 %collective-permute-start.16 = (bf16[128,640]{1,0:T(8,128)(2,1)S(1)}, bf16[128,640]{1,0:T(8,128)(2,1)S(1)}, u32[]{:S(2)}, u32[]{:S(2)}) collective-permute-start(bf16[128,640]{1,0:T(8,128)(2,1)S(1)} %add.7), channel_id=1, source_target_pairs={{0,8},{4,12},{8,0},{12,4},{1,9},{5,13},{9,1},{13,5},{2,10},{6,14},... | collective-permute-start | bytes 491528 | tf_op jit(solution)/shard_map/ppermute | solution.py:172
  132.5 5.3 %collective-permute-start.22 = (bf16[128,640]{1,0:T(8,128)(2,1)S(1)}, bf16[128,640]{1,0:T(8,128)(2,1)S(1)}, u32[]{:S(2)}, u32[]{:S(2)}) collective-permute-start(bf16[128,640]{1,0:T(8,128)(2,1)S(1)} %get-tuple-element.89.a), channel_id=1, source_target_pairs={{0,2},{2,0},{1,3},{3,1},{4,6},{6,4},{5,7},{7,5},{8,10},{10,8},{9,1... | collective-permute-start | bytes 491528 | tf_op jit(solution)/shard_map/ppermute | solution.py:184
  133.0 4.8 %collective-permute-start.21 = (bf16[128,640]{1,0:T(8,128)(2,1)S(1)}, bf16[128,640]{1,0:T(8,128)(2,1)S(1)}, u32[]{:S(2)}, u32[]{:S(2)}) collective-permute-start(bf16[128,640]{1,0:T(8,128)(2,1)S(1)} %get-tuple-element.89.a), channel_id=1, source_target_pairs={{0,1},{1,0},{2,3},{3,2},{4,5},{5,4},{6,7},{7,6},{8,9},{9,8},{10,11... | collective-permute-start | bytes 491528 | tf_op jit(solution)/shard_map/ppermute | solution.py:185
  137.8 1.4 collective-permute-start.23
  140.8 1.9 %collective-permute-start.25 = (bf16[64,512]{1,0:T(8,128)(2,1)S(1)}, bf16[64,512]{1,0:T(8,128)(2,1)S(1)}, u32[]{:S(2)}, u32[]{:S(2)}) collective-permute-start(bf16[64,512]{1,0:T(8,128)(2,1)S(1)} %get-tuple-element.91), channel_id=1, source_target_pairs={{0,1},{1,0},{2,3},{3,2},{4,5},{5,4},{6,7},{7,6},{8,9},{9,8},{10,11... | collective-permute-start | bytes 196616 | tf_op jit(solution)/shard_map/ppermute | solution.py:649
  141.0 4.9 %collective-permute-start.26 = (bf16[64,512]{1,0:T(8,128)(2,1)S(1)}, bf16[64,512]{1,0:T(8,128)(2,1)S(1)}, u32[]{:S(2)}, u32[]{:S(2)}) collective-permute-start(bf16[64,512]{1,0:T(8,128)(2,1)S(1)} %get-tuple-element.92), channel_id=1, source_target_pairs={{0,2},{2,0},{1,3},{3,1},{4,6},{6,4},{5,7},{7,5},{8,10},{10,8},{9,1... | collective-permute-start | bytes 196616 | tf_op jit(solution)/shard_map/ppermute | solution.py:649
  141.6 4.6 %collective-permute-start.27 = (bf16[64,512]{1,0:T(8,128)(2,1)S(1)}, bf16[64,512]{1,0:T(8,128)(2,1)S(1)}, u32[]{:S(2)}, u32[]{:S(2)}) collective-permute-start(bf16[64,512]{1,0:T(8,128)(2,1)S(1)} %get-tuple-element.93), channel_id=1, source_target_pairs={{0,3},{3,0},{1,2},{2,1},{4,7},{7,4},{5,6},{6,5},{8,11},{11,8},{9,1... | collective-permute-start | bytes 196616 | tf_op jit(solution)/shard_map/ppermute | solution.py:649
  (10 other events, 121.0 us)

commit v8 on v7

--- a/solution.py
+++ b/solution.py
@@ -367,10 +367,10 @@
     hidden[...] = gate_up_half(place, tokens, own, (a, b, c), 0)
 
 
-def gate_up_second_kernel(place, tokens, own, first, rest, hidden):
+def gate_up_second_kernel(place, tokens, own, first, a, rest, hidden):
     half = first.shape[1]
     near = own.shape[0]
-    a, b, c = [rest.at[i * near : (i + 1) * near, :] for i in range(3)]
+    b, c = rest.at[:near, :], rest.at[near:, :]
     hidden[:, lanes(place[2], half)] = first[...]
     hidden[:, lanes(1 - place[2], half)] = gate_up_half(place, tokens, own, (a, b, c), 1)
 
@@ -414,10 +414,10 @@
 
 
 def kv_kernel(place, owner, blocks, gain, a, b, c, d, own, *rest):
-    got, outs = rest[:3], rest[4:8]
-    full, key_value, ready = rest[8:]
+    got, outs = rest[:3], rest[5:9]
+    full, key_value, ready = rest[9:]
     rows = own.shape[0]
-    other = [rest[3].at[i * rows : (i + 1) * rows, :] for i in range(3)]
+    other = [rest[3].at[:rows, :], rest[3].at[rows:, :], rest[4]]
     zone, slot, group = place[0], place[1], place[2]
     piece = a.shape[1]
     for j, part in enumerate((a, b, c, d)):
@@ -536,8 +536,9 @@
         name="part",
     )(*lax.optimization_barrier((*mixed, got[0]))[:3])
     down_other = swap_groups(downs)
-    joined = join(*lax.optimization_barrier(tuple(got) + (down_other,))[:3])
-    other = swap_groups(joined)
+    other_far = swap_groups(got[0])
+    joined = join(*lax.optimization_barrier((got[1], got[2], down_other))[:2])
+    other_rest = swap_groups(joined)
 
 
     across = lax.ppermute(tops, "decode", SWAP_CHIP)
@@ -546,7 +547,7 @@
         [((total_rows, 2 * piece), BF16)],
         [SMEM] + [VMEM] * 5,
         name="half",
-    )(after(place, joined), moe_in, *mixed, across)
+    )(after(place, joined, other_far), moe_in, *mixed, across)
     token_rest = lax.ppermute(token_half, "decode", SWAP_CORE)
 
     tokens, routed_hidden = call(
@@ -586,17 +587,17 @@
     kv_half = after(kv_half, joined)
     kv_far = lax.ppermute(kv_half, "expert", SWAP_CHIP)
     kv_near = lax.ppermute(kv_half, "expert", SWAP_CORE)
-    kv_got = [kv_far, kv_near, lax.ppermute(after(kv_far, first_half), "expert", SWAP_CORE)]
+    kv_passed = lax.ppermute(kv_far, "expert", SWAP_CORE)
     (shared_hidden,) = call(
         gate_up_second_kernel,
         [((total_rows, hidden), BF16)],
-        [SMEM] + [VMEM] * 4,
+        [SMEM] + [VMEM] * 5,
         flops=2 * total_rows * width * hidden,
         moved=4 << 20,
         name="gate_up_second",
         vmem=12,
-    )(place, tokens, own_weights, first_half, other)
-    kv_joined = join(*lax.optimization_barrier(tuple(kv_got) + (routed, shared_hidden))[:3])
+    )(place, tokens, own_weights, first_half, other_far, other_rest)
+    kv_joined = join(*lax.optimization_barrier((kv_far, kv_near, routed, shared_hidden))[:2])
     send, keep = call(
         down_kernel,
         [((total_rows, 2 * piece), BF16), ((total_rows, 2 * piece), F32)],
@@ -614,6 +615,8 @@
         name="pass",
     )(keep, beside)
     crossed = {s: lax.ppermute(passed[4 + s], "decode", SWAP_CHIP) for s in SHIFTS + (0,)}
+    kv_passed = after(kv_passed, crossed[SHIFTS[0]])
+    kv_other_passed = swap_groups(kv_passed)
     returned = []
     for s in SHIFTS:
         (summed,) = call(add_kernel, [((rows, piece), BF16)], [VMEM] * 2, name="add")(
@@ -627,7 +630,7 @@
     handed = call(
         kv_kernel,
         [((QCAP * BLOCK, kv_width), BF16)] * 4,
-        [SMEM] * 3 + [VMEM] * 10,
+        [SMEM] * 3 + [VMEM] * 11,
         [
             pltpu.VMEM((rows, width), F32),
             pltpu.VMEM((rows, kv_width), BF16),
@@ -642,8 +645,11 @@
         attn_gain,
         *spread(layer_rows),
         w_kv,
-        *kv_got,
+        kv_far,
+        kv_near,
+        kv_passed,
         kv_other,
+        kv_other_passed,
     )
     received = [handed[0]] + [
         lax.ppermute(values, "decode", pairs)

time: 148 us -> 145 us (0.980)
  waiting for transfers between devices: 88.3 us -> 80.9 us
  starting transfers between devices: 34.6 us -> 38.8 us
    ppermute x1, waiting for transfers between devices: 6.52 us -> 0.92 us  [near_plan(): kv_far = lax.ppermute(kv_half, 'expert', SWAP_CHIP)]
    ppermute x1, starting transfers between devices: 1.71 us -> 4.69 us  [near_plan(): kv_near = lax.ppermute(kv_half, 'expert', SWAP_CORE)]
    ppermute x3 -> x5, starting transfers between devices: 3.68 us -> 6.47 us  [swap_groups(): return lax.ppermute(values, 'groups', SWAP_GROUP)]
    ppermute x3 -> x5, waiting for transfers between devices: 5.89 us -> 3.44 us  [swap_groups(): return lax.ppermute(values, 'groups', SWAP_GROUP)]
    ppermute x4, waiting for transfers between devices: 5.44 us -> 7.65 us  [near_plan(): lax.ppermute(passed[4 + s], 'decode', SWAP_CHIP)]
    ppermute x1, starting transfers between devices: 0.01 us -> 1.71 us  [near_plan(): kv_passed = lax.ppermute(kv_far, 'expert', SWAP_CORE)]
    ppermute x1, starting transfers between devices: 1.85 us -> 0.34 us  [near_plan(): kv_far = lax.ppermute(kv_half, 'expert', SWAP_CHIP)]
    ppermute x1, waiting for transfers between devices: 1.51 us -> 0.01 us  [near_plan(): kv_passed = lax.ppermute(kv_far, 'expert', SWAP_CORE)]
  transfers between devices with their start and end apart: 28 -> 30, of which waited for: 16 -> 17; matrix products, arithmetic and copies ran while one was open for 0% -> 0% of each run, Pallas kernels for 10% -> 10%
where the time goes in v8:
time: 145 us
  waiting for transfers between devices  80.9 us (56%)
  starting transfers between devices  38.8 us (27%)
  Pallas kernels  23.4 us (16%)
    ppermute x9, waiting for transfers between devices, to_shift(): lax.ppermute(values, 'expert', [(i, (i + shift) % count) for i in range(c...  57.8 us
    ppermute x9, starting transfers between devices, to_shift(): lax.ppermute(values, 'expert', [(i, (i + shift) % count) for i in range(c...  18 us
    ppermute x4, waiting for transfers between devices, near_plan(): lax.ppermute(passed[4 + s], 'decode', SWAP_CHIP)  7.65 us
    ppermute x5, starting transfers between devices, swap_groups(): return lax.ppermute(values, 'groups', SWAP_GROUP)  6.47 us
    ppermute x1, waiting for transfers between devices, spread(): across = lax.ppermute(values, 'decode', SWAP_CHIP)  4.79 us
    ppermute x1, starting transfers between devices, near_plan(): kv_near = lax.ppermute(kv_half, 'expert', SWAP_CORE)  4.69 us
    pallas_call x1, Pallas kernels, near_plan(): call(second_kernel, [((near, 2 * hidden), BF16), ((hidden, piece), BF16)]...  3.85 us
    pallas_call x1, Pallas kernels, near_plan(): call(routed_up_kernel, [((total_rows, width), BF16), ((total_rows, routed...  3.61 us
  transfers between devices with their start and end apart: 30, of which 17 were waited for; matrix products, arithmetic and copies ran while one was open for 0% of the time, Pallas kernels for 10%

profile of v8, /device:TPU:0, one launch (start us, length us, event | category | flops | bytes accessed | tf_op | source)
XLA Modules:
  0.0 144.8 jit_solution(9094852386385990077)
XLA Ops:
  1.3 3.5 %first.1 = (bf16[128,2560]{1,0:T(8,128)(2,1)}, bf16[144,640]{1,0:T(8,128)(2,1)}, bf16[128,640]{1,0:T(8,128)(2,1)}, bf16[272,640]{1,0:T(8,128)(2,1)}, bf16[272,640]{1,0:T(8,128)(2,1)}, /*index=5*/bf16[272,640]{1,0:T(8,128)(2,1)}) custom-call(s32[3]{0:T(128)} %pad_add_fusion.refs_0_.place, bf16[128,2560]{1,0:T(8,128)(2,1)} %refs_1_.1, f32[2560]{0:T(1024)} %refs_2_.1, ...), custom_call_target="tpu_custom_call" | custom-call | tf_op jit(solution)/shard_map/first/pallas_call | solution.py:495
  4.9 4.1 %collective-permute-start.2 = (bf16[272,640]{1,0:T(8,128)(2,1)}, bf16[272,640]{1,0:T(8,128)(2,1)S(1)}, u32[]{:S(2)}, u32[]{:S(2)}) collective-permute-start(bf16[272,640]{1,0:T(8,128)(2,1)} %get-tuple-element.50), channel_id=1, source_target_pairs={{0,8},{4,12},{8,0},{12,4},{1,9},{5,13},{9,1},{13,5},{2,10},{6,14},... | collective-permute-start | bytes 1044488 | tf_op jit(solution)/shard_map/ppermute | solution.py:172
  9.0 1.6 %collective-permute-start.3 = (bf16[272,640]{1,0:T(8,128)(2,1)}, bf16[272,640]{1,0:T(8,128)(2,1)S(1)}, u32[]{:S(2)}, u32[]{:S(2)}) collective-permute-start(bf16[272,640]{1,0:T(8,128)(2,1)} %get-tuple-element.51), channel_id=1, source_target_pairs={{0,4},{4,8},{8,12},{12,0},{1,5},{5,9},{9,13},{13,1},{2,6},{6,10},{... | collective-permute-start | bytes 1044488 | tf_op jit(solution)/shard_map/ppermute | solution.py:172
  10.5 2.2 %collective-permute-start.4 = (bf16[272,640]{1,0:T(8,128)(2,1)}, bf16[272,640]{1,0:T(8,128)(2,1)S(1)}, u32[]{:S(2)}, u32[]{:S(2)}) collective-permute-start(bf16[272,640]{1,0:T(8,128)(2,1)} %get-tuple-element.52), channel_id=1, source_target_pairs={{0,12},{4,0},{8,4},{12,8},{1,13},{5,1},{9,5},{13,9},{2,14},{6,2},{... | collective-permute-start | bytes 1044488 | tf_op jit(solution)/shard_map/ppermute | solution.py:172
  12.8 3.9 %second.1 = (bf16[640,512]{1,0:T(8,128)(2,1)}, bf16[256,640]{1,0:T(8,128)(2,1)}, bf16[640,256]{1,0:T(8,128)(2,1)}, bf16[640,256]{1,0:T(8,128)(2,1)}, bf16[640,256]{1,0:T(8,128)(2,1)}, /*index=5*/bf16[640,256]{1,0:T(8,128)(2,1)}) custom-call(s32[3]{0:T(128)} %pad_add_fusion.refs_0_.place, bf16[640,1024]{1,0:T(8,128)(2,1)} %gate.2, bf16[640,1024]{1,0:T(8,128)(2,1)} %up.2, ...), custom_call_target="tpu_custom_call" | custom-call | tf_op jit(solution)/shard_map/second/pallas_call | solution.py:518
  16.7 37.0 %collective-permute-done.5.a = bf16[640,256]{1,0:T(8,128)(2,1)S(1)} collective-permute-done((bf16[640,256]{1,0:T(8,128)(2,1)}, bf16[640,256]{1,0:T(8,128)(2,1)S(1)}, u32[]{:S(2)}, u32[]{:S(2)}) %collective-permute-start.5) | collective-permute-done | bytes 327712 | tf_op jit(solution)/shard_map/ppermute | solution.py:172
  53.9 1.6 %collective-permute-start.10 = (bf16[432,640]{1,0:T(8,128)(2,1)S(1)}, bf16[432,640]{1,0:T(8,128)(2,1)S(1)}, u32[]{:S(2)}, u32[]{:S(2)}) collective-permute-start(bf16[432,640]{1,0:T(8,128)(2,1)S(1)} %get-tuple-element.63), channel_id=1, source_target_pairs={{0,2},{2,0},{1,3},{3,1},{4,6},{6,4},{5,7},{7,5},{8,10},{10,8},{9,1... | collective-permute-start | bytes 1658888 | tf_op jit(solution)/shard_map/ppermute | solution.py:544
  55.5 1.5 %collective-permute-start.6 = (bf16[384,640]{1,0:T(8,128)(2,1)S(1)}, bf16[384,640]{1,0:T(8,128)(2,1)S(1)}, u32[]{:S(2)}, u32[]{:S(2)}) collective-permute-start(bf16[384,640]{1,0:T(8,128)(2,1)S(1)} %get-tuple-element.57), channel_id=1, source_target_pairs={{0,16},{16,0},{1,17},{17,1},{2,18},{18,2},{3,19},{19,3},{4,20},{20... | collective-permute-start | bytes 1474568 | tf_op jit(solution)/shard_map/ppermute | solution.py:180
  57.8 3.1 %collective-permute-start.1 = (bf16[640,256]{1,0:T(8,128)(2,1)}, bf16[640,256]{1,0:T(8,128)(2,1)S(1)}, u32[]{:S(2)}, u32[]{:S(2)}) collective-permute-start(bf16[640,256]{1,0:T(8,128)(2,1)} %get-tuple-element.49), channel_id=1, source_target_pairs={{0,12},{4,0},{8,4},{12,8},{1,13},{5,1},{9,5},{13,9},{2,14},{6,2},{... | collective-permute-start | bytes 983048 | tf_op jit(solution)/shard_map/ppermute | solution.py:172
  61.4 8.4 %collective-permute-done.refs_0_.b = bf16[640,256]{1,0:T(8,128)(2,1)S(1)} collective-permute-done((bf16[640,256]{1,0:T(8,128)(2,1)}, bf16[640,256]{1,0:T(8,128)(2,1)S(1)}, u32[]{:S(2)}, u32[]{:S(2)}) %collective-permute-start) | collective-permute-done | bytes 327712 | tf_op jit(solution)/shard_map/ppermute | solution.py:172
  69.7 4.1 %collective-permute-done.1.refs_1_.c = bf16[640,256]{1,0:T(8,128)(2,1)S(1)} collective-permute-done((bf16[640,256]{1,0:T(8,128)(2,1)}, bf16[640,256]{1,0:T(8,128)(2,1)S(1)}, u32[]{:S(2)}, u32[]{:S(2)}) %collective-permute-start.1) | collective-permute-done | bytes 327712 | tf_op jit(solution)/shard_map/ppermute | solution.py:172
  75.1 1.6 %collective-permute-start.12 = (bf16[1280,256]{1,0:T(8,128)(2,1)S(1)}, bf16[1280,256]{1,0:T(8,128)(2,1)S(1)}, u32[]{:S(2)}, u32[]{:S(2)}) collective-permute-start(bf16[1280,256]{1,0:T(8,128)(2,1)S(1)} %join.2), channel_id=1, source_target_pairs={{0,16},{16,0},{1,17},{17,1},{2,18},{18,2},{3,19},{19,3},{4,20},{20... | collective-permute-start | bytes 1966088 | tf_op jit(solution)/shard_map/ppermute | solution.py:180
  77.1 4.7 %collective-permute-start.8 = (bf16[640,256]{1,0:T(8,128)(2,1)}, bf16[640,256]{1,0:T(8,128)(2,1)S(1)}, u32[]{:S(2)}, u32[]{:S(2)}) collective-permute-start(bf16[640,256]{1,0:T(8,128)(2,1)} %get-tuple-element.60), channel_id=1, source_target_pairs={{0,4},{4,0},{8,12},{12,8},{1,5},{5,1},{9,13},{13,9},{2,6},{6,2},{1... | collective-permute-start | bytes 983048 | tf_op jit(solution)/shard_map/ppermute | solution.py:589
  81.8 3.6 %routed_up.1 = (bf16[512,2560]{1,0:T(8,128)(2,1)S(1)}, bf16[512,512]{1,0:T(8,128)(2,1)S(1)}) custom-call(s32[3]{0:T(128)S(1)} %copy-done.9, bf16[512,1280]{1,0:T(8,128)(2,1)S(1)} %half.1.mine, bf16[512,1280]{1,0:T(8,128)(2,1)S(1)} %collective-permute-done.11.theirs, bf16[1,2560,512]{2,1,0:T(8,128)(2,1)S(1)} %copy-done.2, bf16[1,2560,512]{2,1,0:T(8,128)(2,1)S(1)} %copy-done.3), custom_call_target="tpu_custom_call" | custom-call | tf_op jit(solution)/shard_map/routed_up/pallas_call | solution.py:553
  85.4 2.4 %routed_down.1.routed = bf16[512,2560]{1,0:T(8,128)(2,1)S(1)} custom-call(s32[3]{0:T(128)S(1)} %copy-done.9, bf16[512,512]{1,0:T(8,128)(2,1)S(1)} %get-tuple-element.64.hidden, bf16[144,640]{1,0:T(8,128)(2,1)S(1)} %copy-done.7, bf16[272,640]{1,0:T(8,128)(2,1)S(1)} %collective-permute-done.3.b.rest_1_, bf16[272,640]{1,0:T(8,128)(2,1)S(1)} %collective-permute-done.2.a.rest_2_, ...), custom_call_target="tpu_custom_call" | custom-call | tf_op jit(solution)/shard_map/routed_down/pallas_call | solution.py:562
  87.8 1.5 %gate_up_first.1.first = bf16[512,128]{1,0:T(8,128)(2,1)S(1)} custom-call(s32[3]{0:T(128)S(1)} %copy-done.9, bf16[512,2560]{1,0:T(8,128)(2,1)S(1)} %get-tuple-element.66.tokens, bf16[640,512]{1,0:T(8,128)(2,1)S(1)} %copy-done.1, bf16[640,256]{1,0:T(8,128)(2,1)S(1)} %collective-permute-done.5.a, bf16[640,256]{1,0:T(8,128)(2,1)S(1)} %collective-permute-done.refs_0_.b, ...), custom_call_target="tpu_custom_call" | custom-call | tf_op jit(solution)/shard_map/gate_up_first/pallas_call | solution.py:578
  89.4 2.9 %collective-permute-done.12.rest = bf16[1280,256]{1,0:T(8,128)(2,1)S(1)} collective-permute-done((bf16[1280,256]{1,0:T(8,128)(2,1)S(1)}, bf16[1280,256]{1,0:T(8,128)(2,1)S(1)}, u32[]{:S(2)}, u32[]{:S(2)}) %collective-permute-start.12) | collective-permute-done | bytes 655392 | tf_op jit(solution)/shard_map/ppermute | solution.py:180
  92.3 1.5 %gate_up_second.1.hidden = bf16[512,256]{1,0:T(8,128)(2,1)S(1)} custom-call(s32[3]{0:T(128)S(1)} %copy-done.9, bf16[512,2560]{1,0:T(8,128)(2,1)S(1)} %get-tuple-element.66.tokens, bf16[640,512]{1,0:T(8,128)(2,1)S(1)} %copy-done.1, bf16[512,128]{1,0:T(8,128)(2,1)S(1)} %gate_up_first.1.first, bf16[640,256]{1,0:T(8,128)(2,1)S(1)} %collective-permute-done.9.a, ...), custom_call_target="tpu_custom_call" | custom-call | tf_op jit(solution)/shard_map/gate_up_second/pallas_call | solution.py:591
  94.9 1.7 %down.3 = (bf16[512,1280]{1,0:T(8,128)(2,1)S(1)}, f32[512,1280]{1,0:T(8,128)S(1)}) custom-call(s32[3]{0:T(128)S(1)} %copy-done.9, bf16[512,2560]{1,0:T(8,128)(2,1)S(1)} %routed_down.1.routed, bf16[512,256]{1,0:T(8,128)(2,1)S(1)} %gate_up_second.1.hidden, bf16[256,640]{1,0:T(8,128)(2,1)S(1)} %copy-done.6, bf16[384,640]{1,0:T(8,128)(2,1)S(1)} %collective-permute-done.6.other, ...), custom_call_target="tpu_custom_call" | custom-call | tf_op jit(solution)/shard_map/down/pallas_call | solution.py:601
  96.6 1.7 %collective-permute-start.24 = (bf16[640,256]{1,0:T(8,128)(2,1)S(1)}, bf16[640,256]{1,0:T(8,128)(2,1)S(1)}, u32[]{:S(2)}, u32[]{:S(2)}) collective-permute-start(bf16[640,256]{1,0:T(8,128)(2,1)S(1)} %collective-permute-done.7.refs_0_.rest_0_), channel_id=1, source_target_pairs={{0,4},{4,0},{8,12},{12,8},{1,5},{5,1},{9,13},{13,9},{2,6},{6,2},{1... | collective-permute-start | bytes 983048 | tf_op jit(solution)/shard_map/ppermute | solution.py:590
  103.9 3.1 %collective-permute-done.19.b = bf16[128,640]{1,0:T(8,128)(2,1)S(1)} collective-permute-done((bf16[128,640]{1,0:T(8,128)(2,1)S(1)}, bf16[128,640]{1,0:T(8,128)(2,1)S(1)}, u32[]{:S(2)}, u32[]{:S(2)}) %collective-permute-start.19) | collective-permute-done | bytes 163872 | tf_op jit(solution)/shard_map/ppermute | solution.py:617
  107.7 2.8 %collective-permute-done.17.b = bf16[128,640]{1,0:T(8,128)(2,1)S(1)} collective-permute-done((bf16[128,640]{1,0:T(8,128)(2,1)S(1)}, bf16[128,640]{1,0:T(8,128)(2,1)S(1)}, u32[]{:S(2)}, u32[]{:S(2)}) %collective-permute-start.17) | collective-permute-done | bytes 163872 | tf_op jit(solution)/shard_map/ppermute | solution.py:617
  110.5 1.7 %collective-permute-start.20 = (bf16[128,640]{1,0:T(8,128)(2,1)S(1)}, bf16[128,640]{1,0:T(8,128)(2,1)S(1)}, u32[]{:S(2)}, u32[]{:S(2)}) collective-permute-start(bf16[128,640]{1,0:T(8,128)(2,1)S(1)} %add.9), channel_id=1, source_target_pairs={{0,4},{4,8},{8,12},{12,0},{1,5},{5,9},{9,13},{13,1},{2,6},{6,10},{... | collective-permute-start | bytes 491528 | tf_op jit(solution)/shard_map/ppermute | solution.py:172
  112.2 1.8 %collective-permute-done.15.b = bf16[128,640]{1,0:T(8,128)(2,1)S(1)} collective-permute-done((bf16[128,640]{1,0:T(8,128)(2,1)S(1)}, bf16[128,640]{1,0:T(8,128)(2,1)S(1)}, u32[]{:S(2)}, u32[]{:S(2)}) %collective-permute-start.15) | collective-permute-done | bytes 163872 | tf_op jit(solution)/shard_map/ppermute | solution.py:617
  114.0 4.4 %collective-permute-start.18 = (bf16[128,640]{1,0:T(8,128)(2,1)S(1)}, bf16[128,640]{1,0:T(8,128)(2,1)S(1)}, u32[]{:S(2)}, u32[]{:S(2)}) collective-permute-start(bf16[128,640]{1,0:T(8,128)(2,1)S(1)} %add.8), channel_id=1, source_target_pairs={{0,12},{4,0},{8,4},{12,8},{1,13},{5,1},{9,5},{13,9},{2,14},{6,2},{... | collective-permute-start | bytes 491528 | tf_op jit(solution)/shard_map/ppermute | solution.py:172
  118.6 1.6 %collective-permute-start.26 = (bf16[640,256]{1,0:T(8,128)(2,1)S(1)}, bf16[640,256]{1,0:T(8,128)(2,1)S(1)}, u32[]{:S(2)}, u32[]{:S(2)}) collective-permute-start(bf16[640,256]{1,0:T(8,128)(2,1)S(1)} %collective-permute-done.24.rest_2_), channel_id=1, source_target_pairs={{0,16},{16,0},{1,17},{17,1},{2,18},{18,2},{3,19},{19,3},{4,20},{20... | collective-permute-start | bytes 983048 | tf_op jit(solution)/shard_map/ppermute | solution.py:180
  120.2 2.1 %collective-permute-done.18.b = bf16[128,640]{1,0:T(8,128)(2,1)S(1)} collective-permute-done((bf16[128,640]{1,0:T(8,128)(2,1)S(1)}, bf16[128,640]{1,0:T(8,128)(2,1)S(1)}, u32[]{:S(2)}, u32[]{:S(2)}) %collective-permute-start.18) | collective-permute-done | bytes 163872 | tf_op jit(solution)/shard_map/ppermute | solution.py:172
  122.3 6.2 %collective-permute-done.16.a = bf16[128,640]{1,0:T(8,128)(2,1)S(1)} collective-permute-done((bf16[128,640]{1,0:T(8,128)(2,1)S(1)}, bf16[128,640]{1,0:T(8,128)(2,1)S(1)}, u32[]{:S(2)}, u32[]{:S(2)}) %collective-permute-start.16) | collective-permute-done | bytes 163872 | tf_op jit(solution)/shard_map/ppermute | solution.py:172
  129.9 4.8 %collective-permute-done.22.c = bf16[128,640]{1,0:T(8,128)(2,1)S(1)} collective-permute-done((bf16[128,640]{1,0:T(8,128)(2,1)S(1)}, bf16[128,640]{1,0:T(8,128)(2,1)S(1)}, u32[]{:S(2)}, u32[]{:S(2)}) %collective-permute-start.22) | collective-permute-done | bytes 163872 | tf_op jit(solution)/shard_map/ppermute | solution.py:184
  136.1 1.6 %kv.3 = (bf16[64,512]{1,0:T(8,128)(2,1)S(1)}, bf16[64,512]{1,0:T(8,128)(2,1)S(1)}, bf16[64,512]{1,0:T(8,128)(2,1)S(1)}, bf16[64,512]{1,0:T(8,128)(2,1)S(1)}) custom-call(s32[3]{0:T(128)S(1)} %copy-done.9, s32[1,4]{1,0:T(1,128)S(1)} %copy-done.11, s32[1,4]{1,0:T(1,128)S(1)} %copy-done.12, f32[2560]{0:T(1024)S(1)} %copy-done.10, ...), custom_call_target="tpu_custom_call" | custom-call | tf_op jit(solution)/shard_map/kv/pallas_call | solution.py:630
  139.6 3.2 %collective-permute-done.28.c = bf16[64,512]{1,0:T(8,128)(2,1)S(1)} collective-permute-done((bf16[64,512]{1,0:T(8,128)(2,1)S(1)}, bf16[64,512]{1,0:T(8,128)(2,1)S(1)}, u32[]{:S(2)}, u32[]{:S(2)}) %collective-permute-start.28) | collective-permute-done | bytes 65568 | tf_op jit(solution)/shard_map/ppermute | solution.py:655
  143.1 1.7 %hand.1 = bf16[64,4,512]{2,1,0:T(4,128)(2,1)} custom-call(s32[3]{0:T(128)S(1)} %copy-done.9, bf16[64,512]{1,0:T(8,128)(2,1)S(1)} %get-tuple-element.86.a, bf16[64,512]{1,0:T(8,128)(2,1)S(1)} %collective-permute-done.27.b, bf16[64,512]{1,0:T(8,128)(2,1)S(1)} %collective-permute-done.28.c, bf16[64,512]{1,0:T(8,128)(2,1)S(1)} %collective-permute-done.29.d), custom_call_target="tpu_custom_call" | custom-call | tf_op jit(solution)/shard_map/hand/pallas_call | solution.py:658
  (73 shorter events, 16.3 us)
Async XLA Ops:
  4.9 48.9 %collective-permute-start.2 = (bf16[272,640]{1,0:T(8,128)(2,1)}, bf16[272,640]{1,0:T(8,128)(2,1)S(1)}, u32[]{:S(2)}, u32[]{:S(2)}) collective-permute-start(bf16[272,640]{1,0:T(8,128)(2,1)} %get-tuple-element.50), channel_id=1, source_target_pairs={{0,8},{4,12},{8,0},{12,4},{1,9},{5,13},{9,1},{13,5},{2,10},{6,14},... | collective-permute-start | bytes 1044488 | tf_op jit(solution)/shard_map/ppermute | solution.py:172
  9.0 44.8 %collective-permute-start.3 = (bf16[272,640]{1,0:T(8,128)(2,1)}, bf16[272,640]{1,0:T(8,128)(2,1)S(1)}, u32[]{:S(2)}, u32[]{:S(2)}) collective-permute-start(bf16[272,640]{1,0:T(8,128)(2,1)} %get-tuple-element.51), channel_id=1, source_target_pairs={{0,4},{4,8},{8,12},{12,0},{1,5},{5,9},{9,13},{13,1},{2,6},{6,10},{... | collective-permute-start | bytes 1044488 | tf_op jit(solution)/shard_map/ppermute | solution.py:172
  10.5 43.3 %collective-permute-start.4 = (bf16[272,640]{1,0:T(8,128)(2,1)}, bf16[272,640]{1,0:T(8,128)(2,1)S(1)}, u32[]{:S(2)}, u32[]{:S(2)}) collective-permute-start(bf16[272,640]{1,0:T(8,128)(2,1)} %get-tuple-element.52), channel_id=1, source_target_pairs={{0,12},{4,0},{8,4},{12,8},{1,13},{5,1},{9,5},{13,9},{2,14},{6,2},{... | collective-permute-start | bytes 1044488 | tf_op jit(solution)/shard_map/ppermute | solution.py:172
  16.6 57.7 %copy-start.5 = (bf16[128,2560]{1,0:T(8,128)(2,1)S(1)}, bf16[128,2560]{1,0:T(8,128)(2,1)}, u32[]{:S(2)}) copy-start(bf16[128,2560]{1,0:T(8,128)(2,1)} %get-tuple-element.62.moe_in) | copy-start | bytes 1966084
  16.7 57.7 %copy-start.9 = (s32[3]{0:T(128)S(1)}, s32[3]{0:T(128)}, u32[]{:S(2)}) copy-start(s32[3]{0:T(128)} %pad_add_fusion.refs_0_.place) | copy-start | bytes 40
  16.7 37.1 %collective-permute-start.5 = (bf16[640,256]{1,0:T(8,128)(2,1)}, bf16[640,256]{1,0:T(8,128)(2,1)S(1)}, u32[]{:S(2)}, u32[]{:S(2)}) collective-permute-start(bf16[640,256]{1,0:T(8,128)(2,1)} %get-tuple-element.53), channel_id=1, source_target_pairs={{0,8},{4,12},{8,0},{12,4},{1,9},{5,13},{9,1},{13,5},{2,10},{6,14},... | collective-permute-start | bytes 983048 | tf_op jit(solution)/shard_map/ppermute | solution.py:172
  53.9 20.5 %collective-permute-start.10 = (bf16[432,640]{1,0:T(8,128)(2,1)S(1)}, bf16[432,640]{1,0:T(8,128)(2,1)S(1)}, u32[]{:S(2)}, u32[]{:S(2)}) collective-permute-start(bf16[432,640]{1,0:T(8,128)(2,1)S(1)} %get-tuple-element.63), channel_id=1, source_target_pairs={{0,2},{2,0},{1,3},{3,1},{4,6},{6,4},{5,7},{7,5},{8,10},{10,8},{9,1... | collective-permute-start | bytes 1658888 | tf_op jit(solution)/shard_map/ppermute | solution.py:544
  55.5 18.3 %collective-permute-start.6 = (bf16[384,640]{1,0:T(8,128)(2,1)S(1)}, bf16[384,640]{1,0:T(8,128)(2,1)S(1)}, u32[]{:S(2)}, u32[]{:S(2)}) collective-permute-start(bf16[384,640]{1,0:T(8,128)(2,1)S(1)} %get-tuple-element.57), channel_id=1, source_target_pairs={{0,16},{16,0},{1,17},{17,1},{2,18},{18,2},{3,19},{19,3},{4,20},{20... | collective-permute-start | bytes 1474568 | tf_op jit(solution)/shard_map/ppermute | solution.py:180
  57.0 12.7 %collective-permute-start = (bf16[640,256]{1,0:T(8,128)(2,1)}, bf16[640,256]{1,0:T(8,128)(2,1)S(1)}, u32[]{:S(2)}, u32[]{:S(2)}) collective-permute-start(bf16[640,256]{1,0:T(8,128)(2,1)} %get-tuple-element.48), channel_id=1, source_target_pairs={{0,4},{4,8},{8,12},{12,0},{1,5},{5,9},{9,13},{13,1},{2,6},{6,10},{... | collective-permute-start | bytes 983048 | tf_op jit(solution)/shard_map/ppermute | solution.py:172
  57.8 16.0 %collective-permute-start.1 = (bf16[640,256]{1,0:T(8,128)(2,1)}, bf16[640,256]{1,0:T(8,128)(2,1)S(1)}, u32[]{:S(2)}, u32[]{:S(2)}) collective-permute-start(bf16[640,256]{1,0:T(8,128)(2,1)} %get-tuple-element.49), channel_id=1, source_target_pairs={{0,12},{4,0},{8,4},{12,8},{1,13},{5,1},{9,5},{13,9},{2,14},{6,2},{... | collective-permute-start | bytes 983048 | tf_op jit(solution)/shard_map/ppermute | solution.py:172
  60.9 13.5 %collective-permute-start.9 = (bf16[640,256]{1,0:T(8,128)(2,1)S(1)}, bf16[640,256]{1,0:T(8,128)(2,1)S(1)}, u32[]{:S(2)}, u32[]{:S(2)}) collective-permute-start(bf16[640,256]{1,0:T(8,128)(2,1)S(1)} %collective-permute-done.5.a), channel_id=1, source_target_pairs={{0,16},{16,0},{1,17},{17,1},{2,18},{18,2},{3,19},{19,3},{4,20},{20... | collective-permute-start | bytes 983048 | tf_op jit(solution)/shard_map/ppermute | solution.py:180
  75.0 6.7 %collective-permute-start.11 = (bf16[512,1280]{1,0:T(8,128)(2,1)S(1)}, bf16[512,1280]{1,0:T(8,128)(2,1)S(1)}, u32[]{:S(2)}, u32[]{:S(2)}) collective-permute-start(bf16[512,1280]{1,0:T(8,128)(2,1)S(1)} %half.1.mine), channel_id=1, source_target_pairs={{0,1},{1,0},{2,3},{3,2},{4,5},{5,4},{6,7},{7,6},{8,9},{9,8},{10,11... | collective-permute-start | bytes 3932168 | tf_op jit(solution)/shard_map/ppermute | solution.py:551
  75.1 17.1 %collective-permute-start.12 = (bf16[1280,256]{1,0:T(8,128)(2,1)S(1)}, bf16[1280,256]{1,0:T(8,128)(2,1)S(1)}, u32[]{:S(2)}, u32[]{:S(2)}) collective-permute-start(bf16[1280,256]{1,0:T(8,128)(2,1)S(1)} %join.2), channel_id=1, source_target_pairs={{0,16},{16,0},{1,17},{17,1},{2,18},{18,2},{3,19},{19,3},{4,20},{20... | collective-permute-start | bytes 1966088 | tf_op jit(solution)/shard_map/ppermute | solution.py:180
  76.7 18.0 %collective-permute-start.7 = (bf16[640,256]{1,0:T(8,128)(2,1)}, bf16[640,256]{1,0:T(8,128)(2,1)S(1)}, u32[]{:S(2)}, u32[]{:S(2)}) collective-permute-start(bf16[640,256]{1,0:T(8,128)(2,1)} %get-tuple-element.60), channel_id=1, source_target_pairs={{0,8},{8,0},{4,12},{12,4},{1,9},{9,1},{5,13},{13,5},{2,10},{10,2},... | collective-permute-start | bytes 983048 | tf_op jit(solution)/shard_map/ppermute | solution.py:588
  77.1 17.8 %collective-permute-start.8 = (bf16[640,256]{1,0:T(8,128)(2,1)}, bf16[640,256]{1,0:T(8,128)(2,1)S(1)}, u32[]{:S(2)}, u32[]{:S(2)}) collective-permute-start(bf16[640,256]{1,0:T(8,128)(2,1)} %get-tuple-element.60), channel_id=1, source_target_pairs={{0,4},{4,0},{8,12},{12,8},{1,5},{5,1},{9,13},{13,9},{2,6},{6,2},{1... | collective-permute-start | bytes 983048 | tf_op jit(solution)/shard_map/ppermute | solution.py:589
  96.6 3.1 %collective-permute-start.13 = (bf16[512,1280]{1,0:T(8,128)(2,1)S(1)}, bf16[512,1280]{1,0:T(8,128)(2,1)S(1)}, u32[]{:S(2)}, u32[]{:S(2)}) collective-permute-start(bf16[512,1280]{1,0:T(8,128)(2,1)S(1)} %get-tuple-element.74), channel_id=1, source_target_pairs={{0,1},{1,0},{2,3},{3,2},{4,5},{5,4},{6,7},{7,6},{8,9},{9,8},{10,11... | collective-permute-start | bytes 3932168 | tf_op jit(solution)/shard_map/ppermute | solution.py:609
  96.6 21.8 %collective-permute-start.24 = (bf16[640,256]{1,0:T(8,128)(2,1)S(1)}, bf16[640,256]{1,0:T(8,128)(2,1)S(1)}, u32[]{:S(2)}, u32[]{:S(2)}) collective-permute-start(bf16[640,256]{1,0:T(8,128)(2,1)S(1)} %collective-permute-done.7.refs_0_.rest_0_), channel_id=1, source_target_pairs={{0,4},{4,0},{8,12},{12,8},{1,5},{5,1},{9,13},{13,9},{2,6},{6,2},{1... | collective-permute-start | bytes 983048 | tf_op jit(solution)/shard_map/ppermute | solution.py:590
  99.9 7.1 %collective-permute-start.19 = (bf16[128,640]{1,0:T(8,128)(2,1)S(1)}, bf16[128,640]{1,0:T(8,128)(2,1)S(1)}, u32[]{:S(2)}, u32[]{:S(2)}) collective-permute-start(bf16[128,640]{1,0:T(8,128)(2,1)S(1)} %get-tuple-element.82), channel_id=1, source_target_pairs={{0,2},{2,0},{1,3},{3,1},{4,6},{6,4},{5,7},{7,5},{8,10},{10,8},{9,1... | collective-permute-start | bytes 491528 | tf_op jit(solution)/shard_map/ppermute | solution.py:617
  100.6 9.9 %collective-permute-start.17 = (bf16[128,640]{1,0:T(8,128)(2,1)S(1)}, bf16[128,640]{1,0:T(8,128)(2,1)S(1)}, u32[]{:S(2)}, u32[]{:S(2)}) collective-permute-start(bf16[128,640]{1,0:T(8,128)(2,1)S(1)} %get-tuple-element.80), channel_id=1, source_target_pairs={{0,2},{2,0},{1,3},{3,1},{4,6},{6,4},{5,7},{7,5},{8,10},{10,8},{9,1... | collective-permute-start | bytes 491528 | tf_op jit(solution)/shard_map/ppermute | solution.py:617
  102.0 12.0 %collective-permute-start.15 = (bf16[128,640]{1,0:T(8,128)(2,1)S(1)}, bf16[128,640]{1,0:T(8,128)(2,1)S(1)}, u32[]{:S(2)}, u32[]{:S(2)}) collective-permute-start(bf16[128,640]{1,0:T(8,128)(2,1)S(1)} %get-tuple-element.78), channel_id=1, source_target_pairs={{0,2},{2,0},{1,3},{3,1},{4,6},{6,4},{5,7},{7,5},{8,10},{10,8},{9,1... | collective-permute-start | bytes 491528 | tf_op jit(solution)/shard_map/ppermute | solution.py:617
  102.6 32.0 %collective-permute-start.25 = (bf16[1280,256]{1,0:T(8,128)(2,1)S(1)}, bf16[1280,256]{1,0:T(8,128)(2,1)S(1)}, u32[]{:S(2)}, u32[]{:S(2)}) collective-permute-start(bf16[1280,256]{1,0:T(8,128)(2,1)S(1)} %join.3), channel_id=1, source_target_pairs={{0,16},{16,0},{1,17},{17,1},{2,18},{18,2},{3,19},{19,3},{4,20},{20... | collective-permute-start | bytes 1966088 | tf_op jit(solution)/shard_map/ppermute | solution.py:180
  107.0 11.6 %collective-permute-start.14 = (bf16[128,640]{1,0:T(8,128)(2,1)S(1)}, bf16[128,640]{1,0:T(8,128)(2,1)S(1)}, u32[]{:S(2)}, u32[]{:S(2)}) collective-permute-start(bf16[128,640]{1,0:T(8,128)(2,1)S(1)} %get-tuple-element.76), channel_id=1, source_target_pairs={{0,2},{2,0},{1,3},{3,1},{4,6},{6,4},{5,7},{7,5},{8,10},{10,8},{9,1... | collective-permute-start | bytes 491528 | tf_op jit(solution)/shard_map/ppermute | solution.py:617
  110.5 9.6 %collective-permute-start.20 = (bf16[128,640]{1,0:T(8,128)(2,1)S(1)}, bf16[128,640]{1,0:T(8,128)(2,1)S(1)}, u32[]{:S(2)}, u32[]{:S(2)}) collective-permute-start(bf16[128,640]{1,0:T(8,128)(2,1)S(1)} %add.9), channel_id=1, source_target_pairs={{0,4},{4,8},{8,12},{12,0},{1,5},{5,9},{9,13},{13,1},{2,6},{6,10},{... | collective-permute-start | bytes 491528 | tf_op jit(solution)/shard_map/ppermute | solution.py:172
  114.0 8.2 %collective-permute-start.18 = (bf16[128,640]{1,0:T(8,128)(2,1)S(1)}, bf16[128,640]{1,0:T(8,128)(2,1)S(1)}, u32[]{:S(2)}, u32[]{:S(2)}) collective-permute-start(bf16[128,640]{1,0:T(8,128)(2,1)S(1)} %add.8), channel_id=1, source_target_pairs={{0,12},{4,0},{8,4},{12,8},{1,13},{5,1},{9,5},{13,9},{2,14},{6,2},{... | collective-permute-start | bytes 491528 | tf_op jit(solution)/shard_map/ppermute | solution.py:172
  118.5 10.0 %collective-permute-start.16 = (bf16[128,640]{1,0:T(8,128)(2,1)S(1)}, bf16[128,640]{1,0:T(8,128)(2,1)S(1)}, u32[]{:S(2)}, u32[]{:S(2)}) collective-permute-start(bf16[128,640]{1,0:T(8,128)(2,1)S(1)} %add.7), channel_id=1, source_target_pairs={{0,8},{4,12},{8,0},{12,4},{1,9},{5,13},{9,1},{13,5},{2,10},{6,14},... | collective-permute-start | bytes 491528 | tf_op jit(solution)/shard_map/ppermute | solution.py:172
  118.6 16.1 %collective-permute-start.26 = (bf16[640,256]{1,0:T(8,128)(2,1)S(1)}, bf16[640,256]{1,0:T(8,128)(2,1)S(1)}, u32[]{:S(2)}, u32[]{:S(2)}) collective-permute-start(bf16[640,256]{1,0:T(8,128)(2,1)S(1)} %collective-permute-done.24.rest_2_), channel_id=1, source_target_pairs={{0,16},{16,0},{1,17},{17,1},{2,18},{18,2},{3,19},{19,3},{4,20},{20... | collective-permute-start | bytes 983048 | tf_op jit(solution)/shard_map/ppermute | solution.py:180
  129.3 5.4 %collective-permute-start.22 = (bf16[128,640]{1,0:T(8,128)(2,1)S(1)}, bf16[128,640]{1,0:T(8,128)(2,1)S(1)}, u32[]{:S(2)}, u32[]{:S(2)}) collective-permute-start(bf16[128,640]{1,0:T(8,128)(2,1)S(1)} %get-tuple-element.84.a), channel_id=1, source_target_pairs={{0,2},{2,0},{1,3},{3,1},{4,6},{6,4},{5,7},{7,5},{8,10},{10,8},{9,1... | collective-permute-start | bytes 491528 | tf_op jit(solution)/shard_map/ppermute | solution.py:184
  129.9 4.8 %collective-permute-start.21 = (bf16[128,640]{1,0:T(8,128)(2,1)S(1)}, bf16[128,640]{1,0:T(8,128)(2,1)S(1)}, u32[]{:S(2)}, u32[]{:S(2)}) collective-permute-start(bf16[128,640]{1,0:T(8,128)(2,1)S(1)} %get-tuple-element.84.a), channel_id=1, source_target_pairs={{0,1},{1,0},{2,3},{3,2},{4,5},{5,4},{6,7},{7,6},{8,9},{9,8},{10,11... | collective-permute-start | bytes 491528 | tf_op jit(solution)/shard_map/ppermute | solution.py:185
  134.7 1.4 collective-permute-start.23
  137.7 1.9 %collective-permute-start.27 = (bf16[64,512]{1,0:T(8,128)(2,1)S(1)}, bf16[64,512]{1,0:T(8,128)(2,1)S(1)}, u32[]{:S(2)}, u32[]{:S(2)}) collective-permute-start(bf16[64,512]{1,0:T(8,128)(2,1)S(1)} %get-tuple-element.87), channel_id=1, source_target_pairs={{0,1},{1,0},{2,3},{3,2},{4,5},{5,4},{6,7},{7,6},{8,9},{9,8},{10,11... | collective-permute-start | bytes 196616 | tf_op jit(solution)/shard_map/ppermute | solution.py:655
  137.9 4.9 %collective-permute-start.28 = (bf16[64,512]{1,0:T(8,128)(2,1)S(1)}, bf16[64,512]{1,0:T(8,128)(2,1)S(1)}, u32[]{:S(2)}, u32[]{:S(2)}) collective-permute-start(bf16[64,512]{1,0:T(8,128)(2,1)S(1)} %get-tuple-element.88), channel_id=1, source_target_pairs={{0,2},{2,0},{1,3},{3,1},{4,6},{6,4},{5,7},{7,5},{8,10},{10,8},{9,1... | collective-permute-start | bytes 196616 | tf_op jit(solution)/shard_map/ppermute | solution.py:655
  138.5 4.5 %collective-permute-start.29 = (bf16[64,512]{1,0:T(8,128)(2,1)S(1)}, bf16[64,512]{1,0:T(8,128)(2,1)S(1)}, u32[]{:S(2)}, u32[]{:S(2)}) collective-permute-start(bf16[64,512]{1,0:T(8,128)(2,1)S(1)} %get-tuple-element.89), channel_id=1, source_target_pairs={{0,3},{3,0},{1,2},{2,1},{4,7},{7,4},{5,6},{6,5},{8,11},{11,8},{9,1... | collective-permute-start | bytes 196616 | tf_op jit(solution)/shard_map/ppermute | solution.py:655
  (11 other events, 193.2 us)

commit v9 on v8

--- a/solution.py
+++ b/solution.py
@@ -614,7 +614,8 @@
         [VMEM] * 2,
         name="pass",
     )(keep, beside)
-    crossed = {s: lax.ppermute(passed[4 + s], "decode", SWAP_CHIP) for s in SHIFTS + (0,)}
+    crossed = {s: lax.ppermute(passed[4 + s], "decode", SWAP_CHIP) for s in SHIFTS}
+    crossed[0] = lax.ppermute(after(passed[4], crossed[SHIFTS[1]]), "decode", SWAP_CHIP)
     kv_passed = after(kv_passed, crossed[SHIFTS[0]])
     kv_other_passed = swap_groups(kv_passed)
     returned = []

time: 145 us -> 142 us (0.979)
  waiting for transfers between devices: 80.9 us -> 77.3 us
    ppermute x4 -> x3, waiting for transfers between devices: 7.65 us -> 4.77 us  [near_plan(): lax.ppermute(passed[4 + s], 'decode', SWAP_CHIP)]
    ppermute x4 -> x3, starting transfers between devices: 3.41 us -> 2.75 us  [near_plan(): lax.ppermute(passed[4 + s], 'decode', SWAP_CHIP)]
  transfers between devices with their start and end apart: 30 -> 30, of which waited for: 17 -> 16; matrix products, arithmetic and copies ran while one was open for 0% -> 0% of each run, Pallas kernels for 10% -> 10%
where the time goes in v9:
time: 142 us; the launch traced here: 141 us
  waiting for transfers between devices  77.3 us (54%)
  starting transfers between devices  39 us (27%)
  Pallas kernels  23.4 us (16%)
    ppermute x9, waiting for transfers between devices, to_shift(): lax.ppermute(values, 'expert', [(i, (i + shift) % count) for i in range(c...  57.1 us
    ppermute x9, starting transfers between devices, to_shift(): lax.ppermute(values, 'expert', [(i, (i + shift) % count) for i in range(c...  18.5 us
    ppermute x5, starting transfers between devices, swap_groups(): return lax.ppermute(values, 'groups', SWAP_GROUP)  6.18 us
    ppermute x3, waiting for transfers between devices, near_plan(): lax.ppermute(passed[4 + s], 'decode', SWAP_CHIP)  4.77 us
    ppermute x1, waiting for transfers between devices, spread(): across = lax.ppermute(values, 'decode', SWAP_CHIP)  4.75 us
    ppermute x1, starting transfers between devices, near_plan(): kv_near = lax.ppermute(kv_half, 'expert', SWAP_CORE)  4.69 us
    pallas_call x1, Pallas kernels, near_plan(): call(second_kernel, [((near, 2 * hidden), BF16), ((hidden, piece), BF16)]...  3.85 us
    pallas_call x1, Pallas kernels, near_plan(): call(routed_up_kernel, [((total_rows, width), BF16), ((total_rows, routed...  3.61 us
  transfers between devices with their start and end apart: 30, of which 16 were waited for; matrix products, arithmetic and copies ran while one was open for 0% of the time, Pallas kernels for 10%

profile of v9, /device:TPU:0, one launch (start us, length us, event | category | flops | bytes accessed | tf_op | source)
XLA Modules:
  0.0 141.3 jit_solution(4084519693505868278)
XLA Ops:
  1.3 3.5 %first.1 = (bf16[128,2560]{1,0:T(8,128)(2,1)}, bf16[144,640]{1,0:T(8,128)(2,1)}, bf16[128,640]{1,0:T(8,128)(2,1)}, bf16[272,640]{1,0:T(8,128)(2,1)}, bf16[272,640]{1,0:T(8,128)(2,1)}, /*index=5*/bf16[272,640]{1,0:T(8,128)(2,1)}) custom-call(s32[3]{0:T(128)} %pad_add_fusion.refs_0_.place, bf16[128,2560]{1,0:T(8,128)(2,1)} %refs_1_.1, f32[2560]{0:T(1024)} %refs_2_.1, ...), custom_call_target="tpu_custom_call" | custom-call | tf_op jit(solution)/shard_map/first/pallas_call | solution.py:495
  4.9 4.1 %collective-permute-start.2 = (bf16[272,640]{1,0:T(8,128)(2,1)}, bf16[272,640]{1,0:T(8,128)(2,1)S(1)}, u32[]{:S(2)}, u32[]{:S(2)}) collective-permute-start(bf16[272,640]{1,0:T(8,128)(2,1)} %get-tuple-element.51), channel_id=1, source_target_pairs={{0,8},{4,12},{8,0},{12,4},{1,9},{5,13},{9,1},{13,5},{2,10},{6,14},... | collective-permute-start | bytes 1044488 | tf_op jit(solution)/shard_map/ppermute | solution.py:172
  9.0 1.6 %collective-permute-start.3 = (bf16[272,640]{1,0:T(8,128)(2,1)}, bf16[272,640]{1,0:T(8,128)(2,1)S(1)}, u32[]{:S(2)}, u32[]{:S(2)}) collective-permute-start(bf16[272,640]{1,0:T(8,128)(2,1)} %get-tuple-element.52), channel_id=1, source_target_pairs={{0,4},{4,8},{8,12},{12,0},{1,5},{5,9},{9,13},{13,1},{2,6},{6,10},{... | collective-permute-start | bytes 1044488 | tf_op jit(solution)/shard_map/ppermute | solution.py:172
  10.5 2.2 %collective-permute-start.4 = (bf16[272,640]{1,0:T(8,128)(2,1)}, bf16[272,640]{1,0:T(8,128)(2,1)S(1)}, u32[]{:S(2)}, u32[]{:S(2)}) collective-permute-start(bf16[272,640]{1,0:T(8,128)(2,1)} %get-tuple-element.53), channel_id=1, source_target_pairs={{0,12},{4,0},{8,4},{12,8},{1,13},{5,1},{9,5},{13,9},{2,14},{6,2},{... | collective-permute-start | bytes 1044488 | tf_op jit(solution)/shard_map/ppermute | solution.py:172
  12.8 3.9 %second.1 = (bf16[640,512]{1,0:T(8,128)(2,1)}, bf16[256,640]{1,0:T(8,128)(2,1)}, bf16[640,256]{1,0:T(8,128)(2,1)}, bf16[640,256]{1,0:T(8,128)(2,1)}, bf16[640,256]{1,0:T(8,128)(2,1)}, /*index=5*/bf16[640,256]{1,0:T(8,128)(2,1)}) custom-call(s32[3]{0:T(128)} %pad_add_fusion.refs_0_.place, bf16[640,1024]{1,0:T(8,128)(2,1)} %gate.2, bf16[640,1024]{1,0:T(8,128)(2,1)} %up.2, ...), custom_call_target="tpu_custom_call" | custom-call | tf_op jit(solution)/shard_map/second/pallas_call | solution.py:518
  16.7 37.0 %collective-permute-done.5.a = bf16[640,256]{1,0:T(8,128)(2,1)S(1)} collective-permute-done((bf16[640,256]{1,0:T(8,128)(2,1)}, bf16[640,256]{1,0:T(8,128)(2,1)S(1)}, u32[]{:S(2)}, u32[]{:S(2)}) %collective-permute-start.5) | collective-permute-done | bytes 327712 | tf_op jit(solution)/shard_map/ppermute | solution.py:172
  53.9 1.6 %collective-permute-start.10 = (bf16[432,640]{1,0:T(8,128)(2,1)S(1)}, bf16[432,640]{1,0:T(8,128)(2,1)S(1)}, u32[]{:S(2)}, u32[]{:S(2)}) collective-permute-start(bf16[432,640]{1,0:T(8,128)(2,1)S(1)} %get-tuple-element.64), channel_id=1, source_target_pairs={{0,2},{2,0},{1,3},{3,1},{4,6},{6,4},{5,7},{7,5},{8,10},{10,8},{9,1... | collective-permute-start | bytes 1658888 | tf_op jit(solution)/shard_map/ppermute | solution.py:544
  55.5 1.5 %collective-permute-start.6 = (bf16[384,640]{1,0:T(8,128)(2,1)S(1)}, bf16[384,640]{1,0:T(8,128)(2,1)S(1)}, u32[]{:S(2)}, u32[]{:S(2)}) collective-permute-start(bf16[384,640]{1,0:T(8,128)(2,1)S(1)} %get-tuple-element.58), channel_id=1, source_target_pairs={{0,16},{16,0},{1,17},{17,1},{2,18},{18,2},{3,19},{19,3},{4,20},{20... | collective-permute-start | bytes 1474568 | tf_op jit(solution)/shard_map/ppermute | solution.py:180
  57.8 3.1 %collective-permute-start.1 = (bf16[640,256]{1,0:T(8,128)(2,1)}, bf16[640,256]{1,0:T(8,128)(2,1)S(1)}, u32[]{:S(2)}, u32[]{:S(2)}) collective-permute-start(bf16[640,256]{1,0:T(8,128)(2,1)} %get-tuple-element.50), channel_id=1, source_target_pairs={{0,12},{4,0},{8,4},{12,8},{1,13},{5,1},{9,5},{13,9},{2,14},{6,2},{... | collective-permute-start | bytes 983048 | tf_op jit(solution)/shard_map/ppermute | solution.py:172
  61.4 8.4 %collective-permute-done.refs_0_.b = bf16[640,256]{1,0:T(8,128)(2,1)S(1)} collective-permute-done((bf16[640,256]{1,0:T(8,128)(2,1)}, bf16[640,256]{1,0:T(8,128)(2,1)S(1)}, u32[]{:S(2)}, u32[]{:S(2)}) %collective-permute-start) | collective-permute-done | bytes 327712 | tf_op jit(solution)/shard_map/ppermute | solution.py:172
  69.7 4.1 %collective-permute-done.1.refs_1_.c = bf16[640,256]{1,0:T(8,128)(2,1)S(1)} collective-permute-done((bf16[640,256]{1,0:T(8,128)(2,1)}, bf16[640,256]{1,0:T(8,128)(2,1)S(1)}, u32[]{:S(2)}, u32[]{:S(2)}) %collective-permute-start.1) | collective-permute-done | bytes 327712 | tf_op jit(solution)/shard_map/ppermute | solution.py:172
  75.1 1.6 %collective-permute-start.12 = (bf16[1280,256]{1,0:T(8,128)(2,1)S(1)}, bf16[1280,256]{1,0:T(8,128)(2,1)S(1)}, u32[]{:S(2)}, u32[]{:S(2)}) collective-permute-start(bf16[1280,256]{1,0:T(8,128)(2,1)S(1)} %join.2), channel_id=1, source_target_pairs={{0,16},{16,0},{1,17},{17,1},{2,18},{18,2},{3,19},{19,3},{4,20},{20... | collective-permute-start | bytes 1966088 | tf_op jit(solution)/shard_map/ppermute | solution.py:180
  77.1 4.7 %collective-permute-start.8 = (bf16[640,256]{1,0:T(8,128)(2,1)}, bf16[640,256]{1,0:T(8,128)(2,1)S(1)}, u32[]{:S(2)}, u32[]{:S(2)}) collective-permute-start(bf16[640,256]{1,0:T(8,128)(2,1)} %get-tuple-element.61), channel_id=1, source_target_pairs={{0,4},{4,0},{8,12},{12,8},{1,5},{5,1},{9,13},{13,9},{2,6},{6,2},{1... | collective-permute-start | bytes 983048 | tf_op jit(solution)/shard_map/ppermute | solution.py:589
  81.8 3.6 %routed_up.1 = (bf16[512,2560]{1,0:T(8,128)(2,1)S(1)}, bf16[512,512]{1,0:T(8,128)(2,1)S(1)}) custom-call(s32[3]{0:T(128)S(1)} %copy-done.9, bf16[512,1280]{1,0:T(8,128)(2,1)S(1)} %half.1.mine, bf16[512,1280]{1,0:T(8,128)(2,1)S(1)} %collective-permute-done.11.theirs, bf16[1,2560,512]{2,1,0:T(8,128)(2,1)S(1)} %copy-done.2, bf16[1,2560,512]{2,1,0:T(8,128)(2,1)S(1)} %copy-done.3), custom_call_target="tpu_custom_call" | custom-call | tf_op jit(solution)/shard_map/routed_up/pallas_call | solution.py:553
  85.4 2.4 %routed_down.1.routed = bf16[512,2560]{1,0:T(8,128)(2,1)S(1)} custom-call(s32[3]{0:T(128)S(1)} %copy-done.9, bf16[512,512]{1,0:T(8,128)(2,1)S(1)} %get-tuple-element.65.hidden, bf16[144,640]{1,0:T(8,128)(2,1)S(1)} %copy-done.7, bf16[272,640]{1,0:T(8,128)(2,1)S(1)} %collective-permute-done.3.b.rest_1_, bf16[272,640]{1,0:T(8,128)(2,1)S(1)} %collective-permute-done.2.a.rest_2_, ...), custom_call_target="tpu_custom_call" | custom-call | tf_op jit(solution)/shard_map/routed_down/pallas_call | solution.py:562
  87.8 1.5 %gate_up_first.1.first = bf16[512,128]{1,0:T(8,128)(2,1)S(1)} custom-call(s32[3]{0:T(128)S(1)} %copy-done.9, bf16[512,2560]{1,0:T(8,128)(2,1)S(1)} %get-tuple-element.67.tokens, bf16[640,512]{1,0:T(8,128)(2,1)S(1)} %copy-done.1, bf16[640,256]{1,0:T(8,128)(2,1)S(1)} %collective-permute-done.5.a, bf16[640,256]{1,0:T(8,128)(2,1)S(1)} %collective-permute-done.refs_0_.b, ...), custom_call_target="tpu_custom_call" | custom-call | tf_op jit(solution)/shard_map/gate_up_first/pallas_call | solution.py:578
  89.4 2.9 %collective-permute-done.12.rest = bf16[1280,256]{1,0:T(8,128)(2,1)S(1)} collective-permute-done((bf16[1280,256]{1,0:T(8,128)(2,1)S(1)}, bf16[1280,256]{1,0:T(8,128)(2,1)S(1)}, u32[]{:S(2)}, u32[]{:S(2)}) %collective-permute-start.12) | collective-permute-done | bytes 655392 | tf_op jit(solution)/shard_map/ppermute | solution.py:180
  92.3 1.5 %gate_up_second.1.hidden = bf16[512,256]{1,0:T(8,128)(2,1)S(1)} custom-call(s32[3]{0:T(128)S(1)} %copy-done.9, bf16[512,2560]{1,0:T(8,128)(2,1)S(1)} %get-tuple-element.67.tokens, bf16[640,512]{1,0:T(8,128)(2,1)S(1)} %copy-done.1, bf16[512,128]{1,0:T(8,128)(2,1)S(1)} %gate_up_first.1.first, bf16[640,256]{1,0:T(8,128)(2,1)S(1)} %collective-permute-done.9.a, ...), custom_call_target="tpu_custom_call" | custom-call | tf_op jit(solution)/shard_map/gate_up_second/pallas_call | solution.py:591
  94.9 1.7 %down.3 = (bf16[512,1280]{1,0:T(8,128)(2,1)S(1)}, f32[512,1280]{1,0:T(8,128)S(1)}) custom-call(s32[3]{0:T(128)S(1)} %copy-done.9, bf16[512,2560]{1,0:T(8,128)(2,1)S(1)} %routed_down.1.routed, bf16[512,256]{1,0:T(8,128)(2,1)S(1)} %gate_up_second.1.hidden, bf16[256,640]{1,0:T(8,128)(2,1)S(1)} %copy-done.6, bf16[384,640]{1,0:T(8,128)(2,1)S(1)} %collective-permute-done.6.other, ...), custom_call_target="tpu_custom_call" | custom-call | tf_op jit(solution)/shard_map/down/pallas_call | solution.py:601
  96.6 1.7 %collective-permute-start.24 = (bf16[640,256]{1,0:T(8,128)(2,1)S(1)}, bf16[640,256]{1,0:T(8,128)(2,1)S(1)}, u32[]{:S(2)}, u32[]{:S(2)}) collective-permute-start(bf16[640,256]{1,0:T(8,128)(2,1)S(1)} %collective-permute-done.7.refs_0_.rest_0_), channel_id=1, source_target_pairs={{0,4},{4,0},{8,12},{12,8},{1,5},{5,1},{9,13},{13,9},{2,6},{6,2},{1... | collective-permute-start | bytes 983048 | tf_op jit(solution)/shard_map/ppermute | solution.py:590
  100.6 1.4 collective-permute-start.14
  103.9 3.1 %collective-permute-done.19.b = bf16[128,640]{1,0:T(8,128)(2,1)S(1)} collective-permute-done((bf16[128,640]{1,0:T(8,128)(2,1)S(1)}, bf16[128,640]{1,0:T(8,128)(2,1)S(1)}, u32[]{:S(2)}, u32[]{:S(2)}) %collective-permute-start.19) | collective-permute-done | bytes 163872 | tf_op jit(solution)/shard_map/ppermute | solution.py:617
  107.1 1.7 %collective-permute-start.20 = (bf16[128,640]{1,0:T(8,128)(2,1)S(1)}, bf16[128,640]{1,0:T(8,128)(2,1)S(1)}, u32[]{:S(2)}, u32[]{:S(2)}) collective-permute-start(bf16[128,640]{1,0:T(8,128)(2,1)S(1)} %add.9), channel_id=1, source_target_pairs={{0,4},{4,8},{8,12},{12,0},{1,5},{5,9},{9,13},{13,1},{2,6},{6,10},{... | collective-permute-start | bytes 491528 | tf_op jit(solution)/shard_map/ppermute | solution.py:172
  108.8 1.7 %collective-permute-done.14.b = bf16[128,640]{1,0:T(8,128)(2,1)S(1)} collective-permute-done((bf16[128,640]{1,0:T(8,128)(2,1)S(1)}, bf16[128,640]{1,0:T(8,128)(2,1)S(1)}, u32[]{:S(2)}, u32[]{:S(2)}) %collective-permute-start.14) | collective-permute-done | bytes 163872 | tf_op jit(solution)/shard_map/ppermute | solution.py:617
  110.5 4.4 %collective-permute-start.18 = (bf16[128,640]{1,0:T(8,128)(2,1)S(1)}, bf16[128,640]{1,0:T(8,128)(2,1)S(1)}, u32[]{:S(2)}, u32[]{:S(2)}) collective-permute-start(bf16[128,640]{1,0:T(8,128)(2,1)S(1)} %add.8), channel_id=1, source_target_pairs={{0,12},{4,0},{8,4},{12,8},{1,13},{5,1},{9,5},{13,9},{2,14},{6,2},{... | collective-permute-start | bytes 491528 | tf_op jit(solution)/shard_map/ppermute | solution.py:172
  117.4 1.5 %collective-permute-done.18.b = bf16[128,640]{1,0:T(8,128)(2,1)S(1)} collective-permute-done((bf16[128,640]{1,0:T(8,128)(2,1)S(1)}, bf16[128,640]{1,0:T(8,128)(2,1)S(1)}, u32[]{:S(2)}, u32[]{:S(2)}) %collective-permute-start.18) | collective-permute-done | bytes 163872 | tf_op jit(solution)/shard_map/ppermute | solution.py:172
  118.8 6.2 %collective-permute-done.17.a = bf16[128,640]{1,0:T(8,128)(2,1)S(1)} collective-permute-done((bf16[128,640]{1,0:T(8,128)(2,1)S(1)}, bf16[128,640]{1,0:T(8,128)(2,1)S(1)}, u32[]{:S(2)}, u32[]{:S(2)}) %collective-permute-start.17) | collective-permute-done | bytes 163872 | tf_op jit(solution)/shard_map/ppermute | solution.py:172
  126.5 4.8 %collective-permute-done.22.c = bf16[128,640]{1,0:T(8,128)(2,1)S(1)} collective-permute-done((bf16[128,640]{1,0:T(8,128)(2,1)S(1)}, bf16[128,640]{1,0:T(8,128)(2,1)S(1)}, u32[]{:S(2)}, u32[]{:S(2)}) %collective-permute-start.22) | collective-permute-done | bytes 163872 | tf_op jit(solution)/shard_map/ppermute | solution.py:184
  131.3 1.4 collective-permute-done.23.d
  132.7 1.6 %kv.3 = (bf16[64,512]{1,0:T(8,128)(2,1)S(1)}, bf16[64,512]{1,0:T(8,128)(2,1)S(1)}, bf16[64,512]{1,0:T(8,128)(2,1)S(1)}, bf16[64,512]{1,0:T(8,128)(2,1)S(1)}) custom-call(s32[3]{0:T(128)S(1)} %copy-done.9, s32[1,4]{1,0:T(1,128)S(1)} %copy-done.11, s32[1,4]{1,0:T(1,128)S(1)} %copy-done.12, f32[2560]{0:T(1024)S(1)} %copy-done.10, ...), custom_call_target="tpu_custom_call" | custom-call | tf_op jit(solution)/shard_map/kv/pallas_call | solution.py:631
  136.1 3.2 %collective-permute-done.28.c = bf16[64,512]{1,0:T(8,128)(2,1)S(1)} collective-permute-done((bf16[64,512]{1,0:T(8,128)(2,1)S(1)}, bf16[64,512]{1,0:T(8,128)(2,1)S(1)}, u32[]{:S(2)}, u32[]{:S(2)}) %collective-permute-start.28) | collective-permute-done | bytes 65568 | tf_op jit(solution)/shard_map/ppermute | solution.py:656
  139.6 1.7 %hand.1 = bf16[64,4,512]{2,1,0:T(4,128)(2,1)} custom-call(s32[3]{0:T(128)S(1)} %copy-done.9, bf16[64,512]{1,0:T(8,128)(2,1)S(1)} %get-tuple-element.88.a, bf16[64,512]{1,0:T(8,128)(2,1)S(1)} %collective-permute-done.27.b, bf16[64,512]{1,0:T(8,128)(2,1)S(1)} %collective-permute-done.28.c, bf16[64,512]{1,0:T(8,128)(2,1)S(1)} %collective-permute-done.29.d), custom_call_target="tpu_custom_call" | custom-call | tf_op jit(solution)/shard_map/hand/pallas_call | solution.py:659
  (73 shorter events, 15.2 us)
Async XLA Ops:
  4.9 48.9 %collective-permute-start.2 = (bf16[272,640]{1,0:T(8,128)(2,1)}, bf16[272,640]{1,0:T(8,128)(2,1)S(1)}, u32[]{:S(2)}, u32[]{:S(2)}) collective-permute-start(bf16[272,640]{1,0:T(8,128)(2,1)} %get-tuple-element.51), channel_id=1, source_target_pairs={{0,8},{4,12},{8,0},{12,4},{1,9},{5,13},{9,1},{13,5},{2,10},{6,14},... | collective-permute-start | bytes 1044488 | tf_op jit(solution)/shard_map/ppermute | solution.py:172
  9.0 44.8 %collective-permute-start.3 = (bf16[272,640]{1,0:T(8,128)(2,1)}, bf16[272,640]{1,0:T(8,128)(2,1)S(1)}, u32[]{:S(2)}, u32[]{:S(2)}) collective-permute-start(bf16[272,640]{1,0:T(8,128)(2,1)} %get-tuple-element.52), channel_id=1, source_target_pairs={{0,4},{4,8},{8,12},{12,0},{1,5},{5,9},{9,13},{13,1},{2,6},{6,10},{... | collective-permute-start | bytes 1044488 | tf_op jit(solution)/shard_map/ppermute | solution.py:172
  10.5 43.3 %collective-permute-start.4 = (bf16[272,640]{1,0:T(8,128)(2,1)}, bf16[272,640]{1,0:T(8,128)(2,1)S(1)}, u32[]{:S(2)}, u32[]{:S(2)}) collective-permute-start(bf16[272,640]{1,0:T(8,128)(2,1)} %get-tuple-element.53), channel_id=1, source_target_pairs={{0,12},{4,0},{8,4},{12,8},{1,13},{5,1},{9,5},{13,9},{2,14},{6,2},{... | collective-permute-start | bytes 1044488 | tf_op jit(solution)/shard_map/ppermute | solution.py:172
  16.6 57.7 %copy-start.5 = (bf16[128,2560]{1,0:T(8,128)(2,1)S(1)}, bf16[128,2560]{1,0:T(8,128)(2,1)}, u32[]{:S(2)}) copy-start(bf16[128,2560]{1,0:T(8,128)(2,1)} %get-tuple-element.63.moe_in) | copy-start | bytes 1966084
  16.7 57.7 %copy-start.9 = (s32[3]{0:T(128)S(1)}, s32[3]{0:T(128)}, u32[]{:S(2)}) copy-start(s32[3]{0:T(128)} %pad_add_fusion.refs_0_.place) | copy-start | bytes 40
  16.7 37.1 %collective-permute-start.5 = (bf16[640,256]{1,0:T(8,128)(2,1)}, bf16[640,256]{1,0:T(8,128)(2,1)S(1)}, u32[]{:S(2)}, u32[]{:S(2)}) collective-permute-start(bf16[640,256]{1,0:T(8,128)(2,1)} %get-tuple-element.54), channel_id=1, source_target_pairs={{0,8},{4,12},{8,0},{12,4},{1,9},{5,13},{9,1},{13,5},{2,10},{6,14},... | collective-permute-start | bytes 983048 | tf_op jit(solution)/shard_map/ppermute | solution.py:172
  53.9 20.5 %collective-permute-start.10 = (bf16[432,640]{1,0:T(8,128)(2,1)S(1)}, bf16[432,640]{1,0:T(8,128)(2,1)S(1)}, u32[]{:S(2)}, u32[]{:S(2)}) collective-permute-start(bf16[432,640]{1,0:T(8,128)(2,1)S(1)} %get-tuple-element.64), channel_id=1, source_target_pairs={{0,2},{2,0},{1,3},{3,1},{4,6},{6,4},{5,7},{7,5},{8,10},{10,8},{9,1... | collective-permute-start | bytes 1658888 | tf_op jit(solution)/shard_map/ppermute | solution.py:544
  55.5 18.3 %collective-permute-start.6 = (bf16[384,640]{1,0:T(8,128)(2,1)S(1)}, bf16[384,640]{1,0:T(8,128)(2,1)S(1)}, u32[]{:S(2)}, u32[]{:S(2)}) collective-permute-start(bf16[384,640]{1,0:T(8,128)(2,1)S(1)} %get-tuple-element.58), channel_id=1, source_target_pairs={{0,16},{16,0},{1,17},{17,1},{2,18},{18,2},{3,19},{19,3},{4,20},{20... | collective-permute-start | bytes 1474568 | tf_op jit(solution)/shard_map/ppermute | solution.py:180
  57.0 12.7 %collective-permute-start = (bf16[640,256]{1,0:T(8,128)(2,1)}, bf16[640,256]{1,0:T(8,128)(2,1)S(1)}, u32[]{:S(2)}, u32[]{:S(2)}) collective-permute-start(bf16[640,256]{1,0:T(8,128)(2,1)} %get-tuple-element.49), channel_id=1, source_target_pairs={{0,4},{4,8},{8,12},{12,0},{1,5},{5,9},{9,13},{13,1},{2,6},{6,10},{... | collective-permute-start | bytes 983048 | tf_op jit(solution)/shard_map/ppermute | solution.py:172
  57.8 16.0 %collective-permute-start.1 = (bf16[640,256]{1,0:T(8,128)(2,1)}, bf16[640,256]{1,0:T(8,128)(2,1)S(1)}, u32[]{:S(2)}, u32[]{:S(2)}) collective-permute-start(bf16[640,256]{1,0:T(8,128)(2,1)} %get-tuple-element.50), channel_id=1, source_target_pairs={{0,12},{4,0},{8,4},{12,8},{1,13},{5,1},{9,5},{13,9},{2,14},{6,2},{... | collective-permute-start | bytes 983048 | tf_op jit(solution)/shard_map/ppermute | solution.py:172
  60.9 13.5 %collective-permute-start.9 = (bf16[640,256]{1,0:T(8,128)(2,1)S(1)}, bf16[640,256]{1,0:T(8,128)(2,1)S(1)}, u32[]{:S(2)}, u32[]{:S(2)}) collective-permute-start(bf16[640,256]{1,0:T(8,128)(2,1)S(1)} %collective-permute-done.5.a), channel_id=1, source_target_pairs={{0,16},{16,0},{1,17},{17,1},{2,18},{18,2},{3,19},{19,3},{4,20},{20... | collective-permute-start | bytes 983048 | tf_op jit(solution)/shard_map/ppermute | solution.py:180
  75.0 6.7 %collective-permute-start.11 = (bf16[512,1280]{1,0:T(8,128)(2,1)S(1)}, bf16[512,1280]{1,0:T(8,128)(2,1)S(1)}, u32[]{:S(2)}, u32[]{:S(2)}) collective-permute-start(bf16[512,1280]{1,0:T(8,128)(2,1)S(1)} %half.1.mine), channel_id=1, source_target_pairs={{0,1},{1,0},{2,3},{3,2},{4,5},{5,4},{6,7},{7,6},{8,9},{9,8},{10,11... | collective-permute-start | bytes 3932168 | tf_op jit(solution)/shard_map/ppermute | solution.py:551
  75.1 17.1 %collective-permute-start.12 = (bf16[1280,256]{1,0:T(8,128)(2,1)S(1)}, bf16[1280,256]{1,0:T(8,128)(2,1)S(1)}, u32[]{:S(2)}, u32[]{:S(2)}) collective-permute-start(bf16[1280,256]{1,0:T(8,128)(2,1)S(1)} %join.2), channel_id=1, source_target_pairs={{0,16},{16,0},{1,17},{17,1},{2,18},{18,2},{3,19},{19,3},{4,20},{20... | collective-permute-start | bytes 1966088 | tf_op jit(solution)/shard_map/ppermute | solution.py:180
  76.7 18.0 %collective-permute-start.7 = (bf16[640,256]{1,0:T(8,128)(2,1)}, bf16[640,256]{1,0:T(8,128)(2,1)S(1)}, u32[]{:S(2)}, u32[]{:S(2)}) collective-permute-start(bf16[640,256]{1,0:T(8,128)(2,1)} %get-tuple-element.61), channel_id=1, source_target_pairs={{0,8},{8,0},{4,12},{12,4},{1,9},{9,1},{5,13},{13,5},{2,10},{10,2},... | collective-permute-start | bytes 983048 | tf_op jit(solution)/shard_map/ppermute | solution.py:588
  77.1 17.8 %collective-permute-start.8 = (bf16[640,256]{1,0:T(8,128)(2,1)}, bf16[640,256]{1,0:T(8,128)(2,1)S(1)}, u32[]{:S(2)}, u32[]{:S(2)}) collective-permute-start(bf16[640,256]{1,0:T(8,128)(2,1)} %get-tuple-element.61), channel_id=1, source_target_pairs={{0,4},{4,0},{8,12},{12,8},{1,5},{5,1},{9,13},{13,9},{2,6},{6,2},{1... | collective-permute-start | bytes 983048 | tf_op jit(solution)/shard_map/ppermute | solution.py:589
  96.6 3.1 %collective-permute-start.13 = (bf16[512,1280]{1,0:T(8,128)(2,1)S(1)}, bf16[512,1280]{1,0:T(8,128)(2,1)S(1)}, u32[]{:S(2)}, u32[]{:S(2)}) collective-permute-start(bf16[512,1280]{1,0:T(8,128)(2,1)S(1)} %get-tuple-element.75), channel_id=1, source_target_pairs={{0,1},{1,0},{2,3},{3,2},{4,5},{5,4},{6,7},{7,6},{8,9},{9,8},{10,11... | collective-permute-start | bytes 3932168 | tf_op jit(solution)/shard_map/ppermute | solution.py:609
  96.6 18.9 %collective-permute-start.24 = (bf16[640,256]{1,0:T(8,128)(2,1)S(1)}, bf16[640,256]{1,0:T(8,128)(2,1)S(1)}, u32[]{:S(2)}, u32[]{:S(2)}) collective-permute-start(bf16[640,256]{1,0:T(8,128)(2,1)S(1)} %collective-permute-done.7.refs_0_.rest_0_), channel_id=1, source_target_pairs={{0,4},{4,0},{8,12},{12,8},{1,5},{5,1},{9,13},{13,9},{2,6},{6,2},{1... | collective-permute-start | bytes 983048 | tf_op jit(solution)/shard_map/ppermute | solution.py:590
  99.9 7.1 %collective-permute-start.19 = (bf16[128,640]{1,0:T(8,128)(2,1)S(1)}, bf16[128,640]{1,0:T(8,128)(2,1)S(1)}, u32[]{:S(2)}, u32[]{:S(2)}) collective-permute-start(bf16[128,640]{1,0:T(8,128)(2,1)S(1)} %get-tuple-element.84), channel_id=1, source_target_pairs={{0,2},{2,0},{1,3},{3,1},{4,6},{6,4},{5,7},{7,5},{8,10},{10,8},{9,1... | collective-permute-start | bytes 491528 | tf_op jit(solution)/shard_map/ppermute | solution.py:617
  100.6 9.9 %collective-permute-start.14 = (bf16[128,640]{1,0:T(8,128)(2,1)S(1)}, bf16[128,640]{1,0:T(8,128)(2,1)S(1)}, u32[]{:S(2)}, u32[]{:S(2)}) collective-permute-start(bf16[128,640]{1,0:T(8,128)(2,1)S(1)} %get-tuple-element.78), channel_id=1, source_target_pairs={{0,2},{2,0},{1,3},{3,1},{4,6},{6,4},{5,7},{7,5},{8,10},{10,8},{9,1... | collective-permute-start | bytes 491528 | tf_op jit(solution)/shard_map/ppermute | solution.py:617
  102.0 13.0 %collective-permute-start.16 = (bf16[128,640]{1,0:T(8,128)(2,1)S(1)}, bf16[128,640]{1,0:T(8,128)(2,1)S(1)}, u32[]{:S(2)}, u32[]{:S(2)}) collective-permute-start(bf16[128,640]{1,0:T(8,128)(2,1)S(1)} %get-tuple-element.81), channel_id=1, source_target_pairs={{0,2},{2,0},{1,3},{3,1},{4,6},{6,4},{5,7},{7,5},{8,10},{10,8},{9,1... | collective-permute-start | bytes 491528 | tf_op jit(solution)/shard_map/ppermute | solution.py:617
  102.6 28.6 %collective-permute-start.25 = (bf16[1280,256]{1,0:T(8,128)(2,1)S(1)}, bf16[1280,256]{1,0:T(8,128)(2,1)S(1)}, u32[]{:S(2)}, u32[]{:S(2)}) collective-permute-start(bf16[1280,256]{1,0:T(8,128)(2,1)S(1)} %join.3), channel_id=1, source_target_pairs={{0,16},{16,0},{1,17},{17,1},{2,18},{18,2},{3,19},{19,3},{4,20},{20... | collective-permute-start | bytes 1966088 | tf_op jit(solution)/shard_map/ppermute | solution.py:180
  107.1 9.0 %collective-permute-start.20 = (bf16[128,640]{1,0:T(8,128)(2,1)S(1)}, bf16[128,640]{1,0:T(8,128)(2,1)S(1)}, u32[]{:S(2)}, u32[]{:S(2)}) collective-permute-start(bf16[128,640]{1,0:T(8,128)(2,1)S(1)} %add.9), channel_id=1, source_target_pairs={{0,4},{4,8},{8,12},{12,0},{1,5},{5,9},{9,13},{13,1},{2,6},{6,10},{... | collective-permute-start | bytes 491528 | tf_op jit(solution)/shard_map/ppermute | solution.py:172
  110.5 8.3 %collective-permute-start.18 = (bf16[128,640]{1,0:T(8,128)(2,1)S(1)}, bf16[128,640]{1,0:T(8,128)(2,1)S(1)}, u32[]{:S(2)}, u32[]{:S(2)}) collective-permute-start(bf16[128,640]{1,0:T(8,128)(2,1)S(1)} %add.8), channel_id=1, source_target_pairs={{0,12},{4,0},{8,4},{12,8},{1,13},{5,1},{9,5},{13,9},{2,14},{6,2},{... | collective-permute-start | bytes 491528 | tf_op jit(solution)/shard_map/ppermute | solution.py:172
  115.0 10.0 %collective-permute-start.17 = (bf16[128,640]{1,0:T(8,128)(2,1)S(1)}, bf16[128,640]{1,0:T(8,128)(2,1)S(1)}, u32[]{:S(2)}, u32[]{:S(2)}) collective-permute-start(bf16[128,640]{1,0:T(8,128)(2,1)S(1)} %add.7), channel_id=1, source_target_pairs={{0,8},{4,12},{8,0},{12,4},{1,9},{5,13},{9,1},{13,5},{2,10},{6,14},... | collective-permute-start | bytes 491528 | tf_op jit(solution)/shard_map/ppermute | solution.py:172
  115.6 9.5 %collective-permute-start.15 = (bf16[128,640]{1,0:T(8,128)(2,1)S(1)}, bf16[128,640]{1,0:T(8,128)(2,1)S(1)}, u32[]{:S(2)}, u32[]{:S(2)}) collective-permute-start(bf16[128,640]{1,0:T(8,128)(2,1)S(1)} %get-tuple-element.79), channel_id=1, source_target_pairs={{0,2},{2,0},{1,3},{3,1},{4,6},{6,4},{5,7},{7,5},{8,10},{10,8},{9,1... | collective-permute-start | bytes 491528 | tf_op jit(solution)/shard_map/ppermute | solution.py:618
  116.1 15.2 %collective-permute-start.26 = (bf16[640,256]{1,0:T(8,128)(2,1)S(1)}, bf16[640,256]{1,0:T(8,128)(2,1)S(1)}, u32[]{:S(2)}, u32[]{:S(2)}) collective-permute-start(bf16[640,256]{1,0:T(8,128)(2,1)S(1)} %collective-permute-done.24.rest_2_), channel_id=1, source_target_pairs={{0,16},{16,0},{1,17},{17,1},{2,18},{18,2},{3,19},{19,3},{4,20},{20... | collective-permute-start | bytes 983048 | tf_op jit(solution)/shard_map/ppermute | solution.py:180
  125.9 5.3 %collective-permute-start.22 = (bf16[128,640]{1,0:T(8,128)(2,1)S(1)}, bf16[128,640]{1,0:T(8,128)(2,1)S(1)}, u32[]{:S(2)}, u32[]{:S(2)}) collective-permute-start(bf16[128,640]{1,0:T(8,128)(2,1)S(1)} %get-tuple-element.86.a), channel_id=1, source_target_pairs={{0,2},{2,0},{1,3},{3,1},{4,6},{6,4},{5,7},{7,5},{8,10},{10,8},{9,1... | collective-permute-start | bytes 491528 | tf_op jit(solution)/shard_map/ppermute | solution.py:184
  126.5 4.8 %collective-permute-start.21 = (bf16[128,640]{1,0:T(8,128)(2,1)S(1)}, bf16[128,640]{1,0:T(8,128)(2,1)S(1)}, u32[]{:S(2)}, u32[]{:S(2)}) collective-permute-start(bf16[128,640]{1,0:T(8,128)(2,1)S(1)} %get-tuple-element.86.a), channel_id=1, source_target_pairs={{0,1},{1,0},{2,3},{3,2},{4,5},{5,4},{6,7},{7,6},{8,9},{9,8},{10,11... | collective-permute-start | bytes 491528 | tf_op jit(solution)/shard_map/ppermute | solution.py:185
  131.2 1.4 collective-permute-start.23
  134.2 1.9 %collective-permute-start.27 = (bf16[64,512]{1,0:T(8,128)(2,1)S(1)}, bf16[64,512]{1,0:T(8,128)(2,1)S(1)}, u32[]{:S(2)}, u32[]{:S(2)}) collective-permute-start(bf16[64,512]{1,0:T(8,128)(2,1)S(1)} %get-tuple-element.89), channel_id=1, source_target_pairs={{0,1},{1,0},{2,3},{3,2},{4,5},{5,4},{6,7},{7,6},{8,9},{9,8},{10,11... | collective-permute-start | bytes 196616 | tf_op jit(solution)/shard_map/ppermute | solution.py:656
  134.4 4.9 %collective-permute-start.28 = (bf16[64,512]{1,0:T(8,128)(2,1)S(1)}, bf16[64,512]{1,0:T(8,128)(2,1)S(1)}, u32[]{:S(2)}, u32[]{:S(2)}) collective-permute-start(bf16[64,512]{1,0:T(8,128)(2,1)S(1)} %get-tuple-element.90), channel_id=1, source_target_pairs={{0,2},{2,0},{1,3},{3,1},{4,6},{6,4},{5,7},{7,5},{8,10},{10,8},{9,1... | collective-permute-start | bytes 196616 | tf_op jit(solution)/shard_map/ppermute | solution.py:656
  135.1 4.6 %collective-permute-start.29 = (bf16[64,512]{1,0:T(8,128)(2,1)S(1)}, bf16[64,512]{1,0:T(8,128)(2,1)S(1)}, u32[]{:S(2)}, u32[]{:S(2)}) collective-permute-start(bf16[64,512]{1,0:T(8,128)(2,1)S(1)} %get-tuple-element.91), channel_id=1, source_target_pairs={{0,3},{3,0},{1,2},{2,1},{4,7},{7,4},{5,6},{6,5},{8,11},{11,8},{9,1... | collective-permute-start | bytes 196616 | tf_op jit(solution)/shard_map/ppermute | solution.py:656
  (11 other events, 178.6 us)

commit v10 on v9

--- a/solution.py
+++ b/solution.py
@@ -196,11 +196,11 @@
 
 
 def first_kernel(
-    capacity, place, resid, gain, score, ids, down, moe_in, message, share, *rest
+    capacity, resid, gain, score, ids, down, moe_in, message, share, *rest
 ):
     both, sem = rest[:3], rest[3]
     top = message.shape[0]
-    zone, slot, group = place[0], place[1], place[2]
+    zone, slot, group = [lax.axis_index(name) for name in ("expert", "decode", "groups")]
     count = 4
     hidden = down.shape[0] // count
     half = hidden // 2
@@ -500,13 +500,12 @@
             ((rows, piece), BF16),
         ]
         + [((rows + META + half, piece), BF16)] * 3,
-        [SMEM] + [VMEM] * 4 + [ANY],
+        [VMEM] * 4 + [ANY],
         [pltpu.SemaphoreType.DMA((3,))],
         moved=6 << 20,
         name="first",
         vmem=58,
     )(
-        place,
         resid,
         moe_gain,
         gate_score.reshape(1, rows),

time: 142 us -> 141 us (level)
  no operation moved by 1% of the time
where the time goes in v10:
time: 141 us
  waiting for transfers between devices  76.6 us (54%)
  starting transfers between devices  39 us (28%)
  Pallas kernels  23.4 us (17%)
    ppermute x9, waiting for transfers between devices, to_shift(): lax.ppermute(values, 'expert', [(i, (i + shift) % count) for i in range(c...  56.5 us
    ppermute x9, starting transfers between devices, to_shift(): lax.ppermute(values, 'expert', [(i, (i + shift) % count) for i in range(c...  18.5 us
    ppermute x5, starting transfers between devices, swap_groups(): return lax.ppermute(values, 'groups', SWAP_GROUP)  6.18 us
    ppermute x3, waiting for transfers between devices, near_plan(): lax.ppermute(passed[4 + s], 'decode', SWAP_CHIP)  4.76 us
    ppermute x1, waiting for transfers between devices, spread(): across = lax.ppermute(values, 'decode', SWAP_CHIP)  4.74 us
    ppermute x1, starting transfers between devices, near_plan(): kv_near = lax.ppermute(kv_half, 'expert', SWAP_CORE)  4.69 us
    pallas_call x1, Pallas kernels, near_plan(): call(second_kernel, [((near, 2 * hidden), BF16), ((hidden, piece), BF16)]...  3.85 us
    pallas_call x1, Pallas kernels, near_plan(): call(routed_up_kernel, [((total_rows, width), BF16), ((total_rows, routed...  3.61 us
  transfers between devices with their start and end apart: 30, of which 16 were waited for; matrix products, arithmetic and copies ran while one was open for 0% of the time, Pallas kernels for 10%

profile of v10, /device:TPU:0, one launch (start us, length us, event | category | flops | bytes accessed | tf_op | source)
XLA Modules:
  0.0 140.6 jit_solution(3792978794682401660)
XLA Ops:
  0.6 3.5 %first.1 = (bf16[128,2560]{1,0:T(8,128)(2,1)}, bf16[144,640]{1,0:T(8,128)(2,1)}, bf16[128,640]{1,0:T(8,128)(2,1)}, bf16[272,640]{1,0:T(8,128)(2,1)}, bf16[272,640]{1,0:T(8,128)(2,1)}, /*index=5*/bf16[272,640]{1,0:T(8,128)(2,1)}) custom-call(bf16[128,2560]{1,0:T(8,128)(2,1)} %refs_0_.1, f32[2560]{0:T(1024)} %refs_1_.1, f32[1,128]{1,0:T(1,128)} %bitcast.7, ...), custom_call_target="tpu_custom_call" | custom-call | tf_op jit(solution)/shard_map/first/pallas_call | solution.py:495
  4.2 4.1 %collective-permute-start.2 = (bf16[272,640]{1,0:T(8,128)(2,1)}, bf16[272,640]{1,0:T(8,128)(2,1)S(1)}, u32[]{:S(2)}, u32[]{:S(2)}) collective-permute-start(bf16[272,640]{1,0:T(8,128)(2,1)} %get-tuple-element.51), channel_id=1, source_target_pairs={{0,8},{4,12},{8,0},{12,4},{1,9},{5,13},{9,1},{13,5},{2,10},{6,14},... | collective-permute-start | bytes 1044488 | tf_op jit(solution)/shard_map/ppermute | solution.py:172
  8.3 1.6 %collective-permute-start.3 = (bf16[272,640]{1,0:T(8,128)(2,1)}, bf16[272,640]{1,0:T(8,128)(2,1)S(1)}, u32[]{:S(2)}, u32[]{:S(2)}) collective-permute-start(bf16[272,640]{1,0:T(8,128)(2,1)} %get-tuple-element.52), channel_id=1, source_target_pairs={{0,4},{4,8},{8,12},{12,0},{1,5},{5,9},{9,13},{13,1},{2,6},{6,10},{... | collective-permute-start | bytes 1044488 | tf_op jit(solution)/shard_map/ppermute | solution.py:172
  9.9 2.2 %collective-permute-start.4 = (bf16[272,640]{1,0:T(8,128)(2,1)}, bf16[272,640]{1,0:T(8,128)(2,1)S(1)}, u32[]{:S(2)}, u32[]{:S(2)}) collective-permute-start(bf16[272,640]{1,0:T(8,128)(2,1)} %get-tuple-element.53), channel_id=1, source_target_pairs={{0,12},{4,0},{8,4},{12,8},{1,13},{5,1},{9,5},{13,9},{2,14},{6,2},{... | collective-permute-start | bytes 1044488 | tf_op jit(solution)/shard_map/ppermute | solution.py:172
  12.8 3.9 %second.1 = (bf16[640,512]{1,0:T(8,128)(2,1)}, bf16[256,640]{1,0:T(8,128)(2,1)}, bf16[640,256]{1,0:T(8,128)(2,1)}, bf16[640,256]{1,0:T(8,128)(2,1)}, bf16[640,256]{1,0:T(8,128)(2,1)}, /*index=5*/bf16[640,256]{1,0:T(8,128)(2,1)}) custom-call(s32[3]{0:T(128)} %pad_add_fusion.place, bf16[640,1024]{1,0:T(8,128)(2,1)} %gate.2, bf16[640,1024]{1,0:T(8,128)(2,1)} %up.2, ...), custom_call_target="tpu_custom_call" | custom-call | tf_op jit(solution)/shard_map/second/pallas_call | solution.py:517
  16.7 36.4 %collective-permute-done.5.a = bf16[640,256]{1,0:T(8,128)(2,1)S(1)} collective-permute-done((bf16[640,256]{1,0:T(8,128)(2,1)}, bf16[640,256]{1,0:T(8,128)(2,1)S(1)}, u32[]{:S(2)}, u32[]{:S(2)}) %collective-permute-start.5) | collective-permute-done | bytes 327712 | tf_op jit(solution)/shard_map/ppermute | solution.py:172
  53.2 1.6 %collective-permute-start.10 = (bf16[432,640]{1,0:T(8,128)(2,1)S(1)}, bf16[432,640]{1,0:T(8,128)(2,1)S(1)}, u32[]{:S(2)}, u32[]{:S(2)}) collective-permute-start(bf16[432,640]{1,0:T(8,128)(2,1)S(1)} %get-tuple-element.64), channel_id=1, source_target_pairs={{0,2},{2,0},{1,3},{3,1},{4,6},{6,4},{5,7},{7,5},{8,10},{10,8},{9,1... | collective-permute-start | bytes 1658888 | tf_op jit(solution)/shard_map/ppermute | solution.py:543
  54.8 1.5 %collective-permute-start.6 = (bf16[384,640]{1,0:T(8,128)(2,1)S(1)}, bf16[384,640]{1,0:T(8,128)(2,1)S(1)}, u32[]{:S(2)}, u32[]{:S(2)}) collective-permute-start(bf16[384,640]{1,0:T(8,128)(2,1)S(1)} %get-tuple-element.58), channel_id=1, source_target_pairs={{0,16},{16,0},{1,17},{17,1},{2,18},{18,2},{3,19},{19,3},{4,20},{20... | collective-permute-start | bytes 1474568 | tf_op jit(solution)/shard_map/ppermute | solution.py:180
  57.1 3.1 %collective-permute-start.1 = (bf16[640,256]{1,0:T(8,128)(2,1)}, bf16[640,256]{1,0:T(8,128)(2,1)S(1)}, u32[]{:S(2)}, u32[]{:S(2)}) collective-permute-start(bf16[640,256]{1,0:T(8,128)(2,1)} %get-tuple-element.50), channel_id=1, source_target_pairs={{0,12},{4,0},{8,4},{12,8},{1,13},{5,1},{9,5},{13,9},{2,14},{6,2},{... | collective-permute-start | bytes 983048 | tf_op jit(solution)/shard_map/ppermute | solution.py:172
  60.7 8.4 %collective-permute-done.refs_0_.b = bf16[640,256]{1,0:T(8,128)(2,1)S(1)} collective-permute-done((bf16[640,256]{1,0:T(8,128)(2,1)}, bf16[640,256]{1,0:T(8,128)(2,1)S(1)}, u32[]{:S(2)}, u32[]{:S(2)}) %collective-permute-start) | collective-permute-done | bytes 327712 | tf_op jit(solution)/shard_map/ppermute | solution.py:172
  69.1 4.1 %collective-permute-done.1.refs_1_.c = bf16[640,256]{1,0:T(8,128)(2,1)S(1)} collective-permute-done((bf16[640,256]{1,0:T(8,128)(2,1)}, bf16[640,256]{1,0:T(8,128)(2,1)S(1)}, u32[]{:S(2)}, u32[]{:S(2)}) %collective-permute-start.1) | collective-permute-done | bytes 327712 | tf_op jit(solution)/shard_map/ppermute | solution.py:172
  74.4 1.6 %collective-permute-start.12 = (bf16[1280,256]{1,0:T(8,128)(2,1)S(1)}, bf16[1280,256]{1,0:T(8,128)(2,1)S(1)}, u32[]{:S(2)}, u32[]{:S(2)}) collective-permute-start(bf16[1280,256]{1,0:T(8,128)(2,1)S(1)} %join.2), channel_id=1, source_target_pairs={{0,16},{16,0},{1,17},{17,1},{2,18},{18,2},{3,19},{19,3},{4,20},{20... | collective-permute-start | bytes 1966088 | tf_op jit(solution)/shard_map/ppermute | solution.py:180
  76.4 4.7 %collective-permute-start.8 = (bf16[640,256]{1,0:T(8,128)(2,1)}, bf16[640,256]{1,0:T(8,128)(2,1)S(1)}, u32[]{:S(2)}, u32[]{:S(2)}) collective-permute-start(bf16[640,256]{1,0:T(8,128)(2,1)} %get-tuple-element.61), channel_id=1, source_target_pairs={{0,4},{4,0},{8,12},{12,8},{1,5},{5,1},{9,13},{13,9},{2,6},{6,2},{1... | collective-permute-start | bytes 983048 | tf_op jit(solution)/shard_map/ppermute | solution.py:588
  81.1 3.6 %routed_up.1 = (bf16[512,2560]{1,0:T(8,128)(2,1)S(1)}, bf16[512,512]{1,0:T(8,128)(2,1)S(1)}) custom-call(s32[3]{0:T(128)S(1)} %copy-done.9, bf16[512,1280]{1,0:T(8,128)(2,1)S(1)} %half.1.mine, bf16[512,1280]{1,0:T(8,128)(2,1)S(1)} %collective-permute-done.11.theirs, bf16[1,2560,512]{2,1,0:T(8,128)(2,1)S(1)} %copy-done.2, bf16[1,2560,512]{2,1,0:T(8,128)(2,1)S(1)} %copy-done.3), custom_call_target="tpu_custom_call" | custom-call | tf_op jit(solution)/shard_map/routed_up/pallas_call | solution.py:552
  84.7 2.4 %routed_down.1.routed = bf16[512,2560]{1,0:T(8,128)(2,1)S(1)} custom-call(s32[3]{0:T(128)S(1)} %copy-done.9, bf16[512,512]{1,0:T(8,128)(2,1)S(1)} %get-tuple-element.65.hidden, bf16[144,640]{1,0:T(8,128)(2,1)S(1)} %copy-done.7, bf16[272,640]{1,0:T(8,128)(2,1)S(1)} %collective-permute-done.3.b.rest_1_, bf16[272,640]{1,0:T(8,128)(2,1)S(1)} %collective-permute-done.2.a.rest_2_, ...), custom_call_target="tpu_custom_call" | custom-call | tf_op jit(solution)/shard_map/routed_down/pallas_call | solution.py:561
  87.2 1.5 %gate_up_first.1.first = bf16[512,128]{1,0:T(8,128)(2,1)S(1)} custom-call(s32[3]{0:T(128)S(1)} %copy-done.9, bf16[512,2560]{1,0:T(8,128)(2,1)S(1)} %get-tuple-element.67.tokens, bf16[640,512]{1,0:T(8,128)(2,1)S(1)} %copy-done.1, bf16[640,256]{1,0:T(8,128)(2,1)S(1)} %collective-permute-done.5.a, bf16[640,256]{1,0:T(8,128)(2,1)S(1)} %collective-permute-done.refs_0_.b, ...), custom_call_target="tpu_custom_call" | custom-call | tf_op jit(solution)/shard_map/gate_up_first/pallas_call | solution.py:577
  88.7 2.9 %collective-permute-done.12.rest = bf16[1280,256]{1,0:T(8,128)(2,1)S(1)} collective-permute-done((bf16[1280,256]{1,0:T(8,128)(2,1)S(1)}, bf16[1280,256]{1,0:T(8,128)(2,1)S(1)}, u32[]{:S(2)}, u32[]{:S(2)}) %collective-permute-start.12) | collective-permute-done | bytes 655392 | tf_op jit(solution)/shard_map/ppermute | solution.py:180
  91.6 1.5 %gate_up_second.1.hidden = bf16[512,256]{1,0:T(8,128)(2,1)S(1)} custom-call(s32[3]{0:T(128)S(1)} %copy-done.9, bf16[512,2560]{1,0:T(8,128)(2,1)S(1)} %get-tuple-element.67.tokens, bf16[640,512]{1,0:T(8,128)(2,1)S(1)} %copy-done.1, bf16[512,128]{1,0:T(8,128)(2,1)S(1)} %gate_up_first.1.first, bf16[640,256]{1,0:T(8,128)(2,1)S(1)} %collective-permute-done.9.a, ...), custom_call_target="tpu_custom_call" | custom-call | tf_op jit(solution)/shard_map/gate_up_second/pallas_call | solution.py:590
  94.2 1.7 %down.3 = (bf16[512,1280]{1,0:T(8,128)(2,1)S(1)}, f32[512,1280]{1,0:T(8,128)S(1)}) custom-call(s32[3]{0:T(128)S(1)} %copy-done.9, bf16[512,2560]{1,0:T(8,128)(2,1)S(1)} %routed_down.1.routed, bf16[512,256]{1,0:T(8,128)(2,1)S(1)} %gate_up_second.1.hidden, bf16[256,640]{1,0:T(8,128)(2,1)S(1)} %copy-done.6, bf16[384,640]{1,0:T(8,128)(2,1)S(1)} %collective-permute-done.6.other, ...), custom_call_target="tpu_custom_call" | custom-call | tf_op jit(solution)/shard_map/down/pallas_call | solution.py:600
  96.0 1.7 %collective-permute-start.24 = (bf16[640,256]{1,0:T(8,128)(2,1)S(1)}, bf16[640,256]{1,0:T(8,128)(2,1)S(1)}, u32[]{:S(2)}, u32[]{:S(2)}) collective-permute-start(bf16[640,256]{1,0:T(8,128)(2,1)S(1)} %collective-permute-done.7.refs_0_.rest_0_), channel_id=1, source_target_pairs={{0,4},{4,0},{8,12},{12,8},{1,5},{5,1},{9,13},{13,9},{2,6},{6,2},{1... | collective-permute-start | bytes 983048 | tf_op jit(solution)/shard_map/ppermute | solution.py:589
  99.9 1.4 collective-permute-start.14
  103.2 3.1 %collective-permute-done.19.b = bf16[128,640]{1,0:T(8,128)(2,1)S(1)} collective-permute-done((bf16[128,640]{1,0:T(8,128)(2,1)S(1)}, bf16[128,640]{1,0:T(8,128)(2,1)S(1)}, u32[]{:S(2)}, u32[]{:S(2)}) %collective-permute-start.19) | collective-permute-done | bytes 163872 | tf_op jit(solution)/shard_map/ppermute | solution.py:616
  106.4 1.7 %collective-permute-start.20 = (bf16[128,640]{1,0:T(8,128)(2,1)S(1)}, bf16[128,640]{1,0:T(8,128)(2,1)S(1)}, u32[]{:S(2)}, u32[]{:S(2)}) collective-permute-start(bf16[128,640]{1,0:T(8,128)(2,1)S(1)} %add.9), channel_id=1, source_target_pairs={{0,4},{4,8},{8,12},{12,0},{1,5},{5,9},{9,13},{13,1},{2,6},{6,10},{... | collective-permute-start | bytes 491528 | tf_op jit(solution)/shard_map/ppermute | solution.py:172
  108.2 1.7 %collective-permute-done.14.b = bf16[128,640]{1,0:T(8,128)(2,1)S(1)} collective-permute-done((bf16[128,640]{1,0:T(8,128)(2,1)S(1)}, bf16[128,640]{1,0:T(8,128)(2,1)S(1)}, u32[]{:S(2)}, u32[]{:S(2)}) %collective-permute-start.14) | collective-permute-done | bytes 163872 | tf_op jit(solution)/shard_map/ppermute | solution.py:616
  109.9 4.4 %collective-permute-start.18 = (bf16[128,640]{1,0:T(8,128)(2,1)S(1)}, bf16[128,640]{1,0:T(8,128)(2,1)S(1)}, u32[]{:S(2)}, u32[]{:S(2)}) collective-permute-start(bf16[128,640]{1,0:T(8,128)(2,1)S(1)} %add.8), channel_id=1, source_target_pairs={{0,12},{4,0},{8,4},{12,8},{1,13},{5,1},{9,5},{13,9},{2,14},{6,2},{... | collective-permute-start | bytes 491528 | tf_op jit(solution)/shard_map/ppermute | solution.py:172
  116.7 1.5 %collective-permute-done.18.b = bf16[128,640]{1,0:T(8,128)(2,1)S(1)} collective-permute-done((bf16[128,640]{1,0:T(8,128)(2,1)S(1)}, bf16[128,640]{1,0:T(8,128)(2,1)S(1)}, u32[]{:S(2)}, u32[]{:S(2)}) %collective-permute-start.18) | collective-permute-done | bytes 163872 | tf_op jit(solution)/shard_map/ppermute | solution.py:172
  118.2 6.2 %collective-permute-done.17.a = bf16[128,640]{1,0:T(8,128)(2,1)S(1)} collective-permute-done((bf16[128,640]{1,0:T(8,128)(2,1)S(1)}, bf16[128,640]{1,0:T(8,128)(2,1)S(1)}, u32[]{:S(2)}, u32[]{:S(2)}) %collective-permute-start.17) | collective-permute-done | bytes 163872 | tf_op jit(solution)/shard_map/ppermute | solution.py:172
  125.8 4.7 %collective-permute-done.22.c = bf16[128,640]{1,0:T(8,128)(2,1)S(1)} collective-permute-done((bf16[128,640]{1,0:T(8,128)(2,1)S(1)}, bf16[128,640]{1,0:T(8,128)(2,1)S(1)}, u32[]{:S(2)}, u32[]{:S(2)}) %collective-permute-start.22) | collective-permute-done | bytes 163872 | tf_op jit(solution)/shard_map/ppermute | solution.py:184
  130.6 1.4 collective-permute-done.23.d
  132.0 1.6 %kv.3 = (bf16[64,512]{1,0:T(8,128)(2,1)S(1)}, bf16[64,512]{1,0:T(8,128)(2,1)S(1)}, bf16[64,512]{1,0:T(8,128)(2,1)S(1)}, bf16[64,512]{1,0:T(8,128)(2,1)S(1)}) custom-call(s32[3]{0:T(128)S(1)} %copy-done.9, s32[1,4]{1,0:T(1,128)S(1)} %copy-done.11, s32[1,4]{1,0:T(1,128)S(1)} %copy-done.12, f32[2560]{0:T(1024)S(1)} %copy-done.10, ...), custom_call_target="tpu_custom_call" | custom-call | tf_op jit(solution)/shard_map/kv/pallas_call | solution.py:630
  135.5 3.2 %collective-permute-done.28.c = bf16[64,512]{1,0:T(8,128)(2,1)S(1)} collective-permute-done((bf16[64,512]{1,0:T(8,128)(2,1)S(1)}, bf16[64,512]{1,0:T(8,128)(2,1)S(1)}, u32[]{:S(2)}, u32[]{:S(2)}) %collective-permute-start.28) | collective-permute-done | bytes 65568 | tf_op jit(solution)/shard_map/ppermute | solution.py:655
  139.0 1.7 %hand.1 = bf16[64,4,512]{2,1,0:T(4,128)(2,1)} custom-call(s32[3]{0:T(128)S(1)} %copy-done.9, bf16[64,512]{1,0:T(8,128)(2,1)S(1)} %get-tuple-element.88.a, bf16[64,512]{1,0:T(8,128)(2,1)S(1)} %collective-permute-done.27.b, bf16[64,512]{1,0:T(8,128)(2,1)S(1)} %collective-permute-done.28.c, bf16[64,512]{1,0:T(8,128)(2,1)S(1)} %collective-permute-done.29.d), custom_call_target="tpu_custom_call" | custom-call | tf_op jit(solution)/shard_map/hand/pallas_call | solution.py:658
  (73 shorter events, 15.2 us)
Async XLA Ops:
  4.2 48.9 %collective-permute-start.2 = (bf16[272,640]{1,0:T(8,128)(2,1)}, bf16[272,640]{1,0:T(8,128)(2,1)S(1)}, u32[]{:S(2)}, u32[]{:S(2)}) collective-permute-start(bf16[272,640]{1,0:T(8,128)(2,1)} %get-tuple-element.51), channel_id=1, source_target_pairs={{0,8},{4,12},{8,0},{12,4},{1,9},{5,13},{9,1},{13,5},{2,10},{6,14},... | collective-permute-start | bytes 1044488 | tf_op jit(solution)/shard_map/ppermute | solution.py:172
  8.3 44.8 %collective-permute-start.3 = (bf16[272,640]{1,0:T(8,128)(2,1)}, bf16[272,640]{1,0:T(8,128)(2,1)S(1)}, u32[]{:S(2)}, u32[]{:S(2)}) collective-permute-start(bf16[272,640]{1,0:T(8,128)(2,1)} %get-tuple-element.52), channel_id=1, source_target_pairs={{0,4},{4,8},{8,12},{12,0},{1,5},{5,9},{9,13},{13,1},{2,6},{6,10},{... | collective-permute-start | bytes 1044488 | tf_op jit(solution)/shard_map/ppermute | solution.py:172
  9.9 43.3 %collective-permute-start.4 = (bf16[272,640]{1,0:T(8,128)(2,1)}, bf16[272,640]{1,0:T(8,128)(2,1)S(1)}, u32[]{:S(2)}, u32[]{:S(2)}) collective-permute-start(bf16[272,640]{1,0:T(8,128)(2,1)} %get-tuple-element.53), channel_id=1, source_target_pairs={{0,12},{4,0},{8,4},{12,8},{1,13},{5,1},{9,5},{13,9},{2,14},{6,2},{... | collective-permute-start | bytes 1044488 | tf_op jit(solution)/shard_map/ppermute | solution.py:172
  16.6 57.1 %copy-start.5 = (bf16[128,2560]{1,0:T(8,128)(2,1)S(1)}, bf16[128,2560]{1,0:T(8,128)(2,1)}, u32[]{:S(2)}) copy-start(bf16[128,2560]{1,0:T(8,128)(2,1)} %get-tuple-element.63.moe_in) | copy-start | bytes 1966084
  16.6 57.1 %copy-start.9 = (s32[3]{0:T(128)S(1)}, s32[3]{0:T(128)}, u32[]{:S(2)}) copy-start(s32[3]{0:T(128)} %pad_add_fusion.place) | copy-start | bytes 40
  16.7 36.5 %collective-permute-start.5 = (bf16[640,256]{1,0:T(8,128)(2,1)}, bf16[640,256]{1,0:T(8,128)(2,1)S(1)}, u32[]{:S(2)}, u32[]{:S(2)}) collective-permute-start(bf16[640,256]{1,0:T(8,128)(2,1)} %get-tuple-element.54), channel_id=1, source_target_pairs={{0,8},{4,12},{8,0},{12,4},{1,9},{5,13},{9,1},{13,5},{2,10},{6,14},... | collective-permute-start | bytes 983048 | tf_op jit(solution)/shard_map/ppermute | solution.py:172
  53.2 20.5 %collective-permute-start.10 = (bf16[432,640]{1,0:T(8,128)(2,1)S(1)}, bf16[432,640]{1,0:T(8,128)(2,1)S(1)}, u32[]{:S(2)}, u32[]{:S(2)}) collective-permute-start(bf16[432,640]{1,0:T(8,128)(2,1)S(1)} %get-tuple-element.64), channel_id=1, source_target_pairs={{0,2},{2,0},{1,3},{3,1},{4,6},{6,4},{5,7},{7,5},{8,10},{10,8},{9,1... | collective-permute-start | bytes 1658888 | tf_op jit(solution)/shard_map/ppermute | solution.py:543
  54.8 18.3 %collective-permute-start.6 = (bf16[384,640]{1,0:T(8,128)(2,1)S(1)}, bf16[384,640]{1,0:T(8,128)(2,1)S(1)}, u32[]{:S(2)}, u32[]{:S(2)}) collective-permute-start(bf16[384,640]{1,0:T(8,128)(2,1)S(1)} %get-tuple-element.58), channel_id=1, source_target_pairs={{0,16},{16,0},{1,17},{17,1},{2,18},{18,2},{3,19},{19,3},{4,20},{20... | collective-permute-start | bytes 1474568 | tf_op jit(solution)/shard_map/ppermute | solution.py:180
  56.4 12.7 %collective-permute-start = (bf16[640,256]{1,0:T(8,128)(2,1)}, bf16[640,256]{1,0:T(8,128)(2,1)S(1)}, u32[]{:S(2)}, u32[]{:S(2)}) collective-permute-start(bf16[640,256]{1,0:T(8,128)(2,1)} %get-tuple-element.49), channel_id=1, source_target_pairs={{0,4},{4,8},{8,12},{12,0},{1,5},{5,9},{9,13},{13,1},{2,6},{6,10},{... | collective-permute-start | bytes 983048 | tf_op jit(solution)/shard_map/ppermute | solution.py:172
  57.1 16.0 %collective-permute-start.1 = (bf16[640,256]{1,0:T(8,128)(2,1)}, bf16[640,256]{1,0:T(8,128)(2,1)S(1)}, u32[]{:S(2)}, u32[]{:S(2)}) collective-permute-start(bf16[640,256]{1,0:T(8,128)(2,1)} %get-tuple-element.50), channel_id=1, source_target_pairs={{0,12},{4,0},{8,4},{12,8},{1,13},{5,1},{9,5},{13,9},{2,14},{6,2},{... | collective-permute-start | bytes 983048 | tf_op jit(solution)/shard_map/ppermute | solution.py:172
  60.2 13.5 %collective-permute-start.9 = (bf16[640,256]{1,0:T(8,128)(2,1)S(1)}, bf16[640,256]{1,0:T(8,128)(2,1)S(1)}, u32[]{:S(2)}, u32[]{:S(2)}) collective-permute-start(bf16[640,256]{1,0:T(8,128)(2,1)S(1)} %collective-permute-done.5.a), channel_id=1, source_target_pairs={{0,16},{16,0},{1,17},{17,1},{2,18},{18,2},{3,19},{19,3},{4,20},{20... | collective-permute-start | bytes 983048 | tf_op jit(solution)/shard_map/ppermute | solution.py:180
  74.4 6.7 %collective-permute-start.11 = (bf16[512,1280]{1,0:T(8,128)(2,1)S(1)}, bf16[512,1280]{1,0:T(8,128)(2,1)S(1)}, u32[]{:S(2)}, u32[]{:S(2)}) collective-permute-start(bf16[512,1280]{1,0:T(8,128)(2,1)S(1)} %half.1.mine), channel_id=1, source_target_pairs={{0,1},{1,0},{2,3},{3,2},{4,5},{5,4},{6,7},{7,6},{8,9},{9,8},{10,11... | collective-permute-start | bytes 3932168 | tf_op jit(solution)/shard_map/ppermute | solution.py:550
  74.4 17.1 %collective-permute-start.12 = (bf16[1280,256]{1,0:T(8,128)(2,1)S(1)}, bf16[1280,256]{1,0:T(8,128)(2,1)S(1)}, u32[]{:S(2)}, u32[]{:S(2)}) collective-permute-start(bf16[1280,256]{1,0:T(8,128)(2,1)S(1)} %join.2), channel_id=1, source_target_pairs={{0,16},{16,0},{1,17},{17,1},{2,18},{18,2},{3,19},{19,3},{4,20},{20... | collective-permute-start | bytes 1966088 | tf_op jit(solution)/shard_map/ppermute | solution.py:180
  76.0 18.0 %collective-permute-start.7 = (bf16[640,256]{1,0:T(8,128)(2,1)}, bf16[640,256]{1,0:T(8,128)(2,1)S(1)}, u32[]{:S(2)}, u32[]{:S(2)}) collective-permute-start(bf16[640,256]{1,0:T(8,128)(2,1)} %get-tuple-element.61), channel_id=1, source_target_pairs={{0,8},{8,0},{4,12},{12,4},{1,9},{9,1},{5,13},{13,5},{2,10},{10,2},... | collective-permute-start | bytes 983048 | tf_op jit(solution)/shard_map/ppermute | solution.py:587
  76.4 17.8 %collective-permute-start.8 = (bf16[640,256]{1,0:T(8,128)(2,1)}, bf16[640,256]{1,0:T(8,128)(2,1)S(1)}, u32[]{:S(2)}, u32[]{:S(2)}) collective-permute-start(bf16[640,256]{1,0:T(8,128)(2,1)} %get-tuple-element.61), channel_id=1, source_target_pairs={{0,4},{4,0},{8,12},{12,8},{1,5},{5,1},{9,13},{13,9},{2,6},{6,2},{1... | collective-permute-start | bytes 983048 | tf_op jit(solution)/shard_map/ppermute | solution.py:588
  95.9 3.1 %collective-permute-start.13 = (bf16[512,1280]{1,0:T(8,128)(2,1)S(1)}, bf16[512,1280]{1,0:T(8,128)(2,1)S(1)}, u32[]{:S(2)}, u32[]{:S(2)}) collective-permute-start(bf16[512,1280]{1,0:T(8,128)(2,1)S(1)} %get-tuple-element.75), channel_id=1, source_target_pairs={{0,1},{1,0},{2,3},{3,2},{4,5},{5,4},{6,7},{7,6},{8,9},{9,8},{10,11... | collective-permute-start | bytes 3932168 | tf_op jit(solution)/shard_map/ppermute | solution.py:608
  96.0 18.9 %collective-permute-start.24 = (bf16[640,256]{1,0:T(8,128)(2,1)S(1)}, bf16[640,256]{1,0:T(8,128)(2,1)S(1)}, u32[]{:S(2)}, u32[]{:S(2)}) collective-permute-start(bf16[640,256]{1,0:T(8,128)(2,1)S(1)} %collective-permute-done.7.refs_0_.rest_0_), channel_id=1, source_target_pairs={{0,4},{4,0},{8,12},{12,8},{1,5},{5,1},{9,13},{13,9},{2,6},{6,2},{1... | collective-permute-start | bytes 983048 | tf_op jit(solution)/shard_map/ppermute | solution.py:589
  99.2 7.1 %collective-permute-start.19 = (bf16[128,640]{1,0:T(8,128)(2,1)S(1)}, bf16[128,640]{1,0:T(8,128)(2,1)S(1)}, u32[]{:S(2)}, u32[]{:S(2)}) collective-permute-start(bf16[128,640]{1,0:T(8,128)(2,1)S(1)} %get-tuple-element.84), channel_id=1, source_target_pairs={{0,2},{2,0},{1,3},{3,1},{4,6},{6,4},{5,7},{7,5},{8,10},{10,8},{9,1... | collective-permute-start | bytes 491528 | tf_op jit(solution)/shard_map/ppermute | solution.py:616
  99.9 9.9 %collective-permute-start.14 = (bf16[128,640]{1,0:T(8,128)(2,1)S(1)}, bf16[128,640]{1,0:T(8,128)(2,1)S(1)}, u32[]{:S(2)}, u32[]{:S(2)}) collective-permute-start(bf16[128,640]{1,0:T(8,128)(2,1)S(1)} %get-tuple-element.78), channel_id=1, source_target_pairs={{0,2},{2,0},{1,3},{3,1},{4,6},{6,4},{5,7},{7,5},{8,10},{10,8},{9,1... | collective-permute-start | bytes 491528 | tf_op jit(solution)/shard_map/ppermute | solution.py:616
  101.3 13.0 %collective-permute-start.16 = (bf16[128,640]{1,0:T(8,128)(2,1)S(1)}, bf16[128,640]{1,0:T(8,128)(2,1)S(1)}, u32[]{:S(2)}, u32[]{:S(2)}) collective-permute-start(bf16[128,640]{1,0:T(8,128)(2,1)S(1)} %get-tuple-element.81), channel_id=1, source_target_pairs={{0,2},{2,0},{1,3},{3,1},{4,6},{6,4},{5,7},{7,5},{8,10},{10,8},{9,1... | collective-permute-start | bytes 491528 | tf_op jit(solution)/shard_map/ppermute | solution.py:616
  102.0 28.6 %collective-permute-start.25 = (bf16[1280,256]{1,0:T(8,128)(2,1)S(1)}, bf16[1280,256]{1,0:T(8,128)(2,1)S(1)}, u32[]{:S(2)}, u32[]{:S(2)}) collective-permute-start(bf16[1280,256]{1,0:T(8,128)(2,1)S(1)} %join.3), channel_id=1, source_target_pairs={{0,16},{16,0},{1,17},{17,1},{2,18},{18,2},{3,19},{19,3},{4,20},{20... | collective-permute-start | bytes 1966088 | tf_op jit(solution)/shard_map/ppermute | solution.py:180
  106.4 9.0 %collective-permute-start.20 = (bf16[128,640]{1,0:T(8,128)(2,1)S(1)}, bf16[128,640]{1,0:T(8,128)(2,1)S(1)}, u32[]{:S(2)}, u32[]{:S(2)}) collective-permute-start(bf16[128,640]{1,0:T(8,128)(2,1)S(1)} %add.9), channel_id=1, source_target_pairs={{0,4},{4,8},{8,12},{12,0},{1,5},{5,9},{9,13},{13,1},{2,6},{6,10},{... | collective-permute-start | bytes 491528 | tf_op jit(solution)/shard_map/ppermute | solution.py:172
  109.9 8.3 %collective-permute-start.18 = (bf16[128,640]{1,0:T(8,128)(2,1)S(1)}, bf16[128,640]{1,0:T(8,128)(2,1)S(1)}, u32[]{:S(2)}, u32[]{:S(2)}) collective-permute-start(bf16[128,640]{1,0:T(8,128)(2,1)S(1)} %add.8), channel_id=1, source_target_pairs={{0,12},{4,0},{8,4},{12,8},{1,13},{5,1},{9,5},{13,9},{2,14},{6,2},{... | collective-permute-start | bytes 491528 | tf_op jit(solution)/shard_map/ppermute | solution.py:172
  114.4 10.0 %collective-permute-start.17 = (bf16[128,640]{1,0:T(8,128)(2,1)S(1)}, bf16[128,640]{1,0:T(8,128)(2,1)S(1)}, u32[]{:S(2)}, u32[]{:S(2)}) collective-permute-start(bf16[128,640]{1,0:T(8,128)(2,1)S(1)} %add.7), channel_id=1, source_target_pairs={{0,8},{4,12},{8,0},{12,4},{1,9},{5,13},{9,1},{13,5},{2,10},{6,14},... | collective-permute-start | bytes 491528 | tf_op jit(solution)/shard_map/ppermute | solution.py:172
  114.9 9.5 %collective-permute-start.15 = (bf16[128,640]{1,0:T(8,128)(2,1)S(1)}, bf16[128,640]{1,0:T(8,128)(2,1)S(1)}, u32[]{:S(2)}, u32[]{:S(2)}) collective-permute-start(bf16[128,640]{1,0:T(8,128)(2,1)S(1)} %get-tuple-element.79), channel_id=1, source_target_pairs={{0,2},{2,0},{1,3},{3,1},{4,6},{6,4},{5,7},{7,5},{8,10},{10,8},{9,1... | collective-permute-start | bytes 491528 | tf_op jit(solution)/shard_map/ppermute | solution.py:617
  115.4 15.1 %collective-permute-start.26 = (bf16[640,256]{1,0:T(8,128)(2,1)S(1)}, bf16[640,256]{1,0:T(8,128)(2,1)S(1)}, u32[]{:S(2)}, u32[]{:S(2)}) collective-permute-start(bf16[640,256]{1,0:T(8,128)(2,1)S(1)} %collective-permute-done.24.rest_2_), channel_id=1, source_target_pairs={{0,16},{16,0},{1,17},{17,1},{2,18},{18,2},{3,19},{19,3},{4,20},{20... | collective-permute-start | bytes 983048 | tf_op jit(solution)/shard_map/ppermute | solution.py:180
  125.2 5.3 %collective-permute-start.22 = (bf16[128,640]{1,0:T(8,128)(2,1)S(1)}, bf16[128,640]{1,0:T(8,128)(2,1)S(1)}, u32[]{:S(2)}, u32[]{:S(2)}) collective-permute-start(bf16[128,640]{1,0:T(8,128)(2,1)S(1)} %get-tuple-element.86.a), channel_id=1, source_target_pairs={{0,2},{2,0},{1,3},{3,1},{4,6},{6,4},{5,7},{7,5},{8,10},{10,8},{9,1... | collective-permute-start | bytes 491528 | tf_op jit(solution)/shard_map/ppermute | solution.py:184
  125.8 4.8 %collective-permute-start.21 = (bf16[128,640]{1,0:T(8,128)(2,1)S(1)}, bf16[128,640]{1,0:T(8,128)(2,1)S(1)}, u32[]{:S(2)}, u32[]{:S(2)}) collective-permute-start(bf16[128,640]{1,0:T(8,128)(2,1)S(1)} %get-tuple-element.86.a), channel_id=1, source_target_pairs={{0,1},{1,0},{2,3},{3,2},{4,5},{5,4},{6,7},{7,6},{8,9},{9,8},{10,11... | collective-permute-start | bytes 491528 | tf_op jit(solution)/shard_map/ppermute | solution.py:185
  130.6 1.4 collective-permute-start.23
  133.5 1.9 %collective-permute-start.27 = (bf16[64,512]{1,0:T(8,128)(2,1)S(1)}, bf16[64,512]{1,0:T(8,128)(2,1)S(1)}, u32[]{:S(2)}, u32[]{:S(2)}) collective-permute-start(bf16[64,512]{1,0:T(8,128)(2,1)S(1)} %get-tuple-element.89), channel_id=1, source_target_pairs={{0,1},{1,0},{2,3},{3,2},{4,5},{5,4},{6,7},{7,6},{8,9},{9,8},{10,11... | collective-permute-start | bytes 196616 | tf_op jit(solution)/shard_map/ppermute | solution.py:655
  133.7 4.9 %collective-permute-start.28 = (bf16[64,512]{1,0:T(8,128)(2,1)S(1)}, bf16[64,512]{1,0:T(8,128)(2,1)S(1)}, u32[]{:S(2)}, u32[]{:S(2)}) collective-permute-start(bf16[64,512]{1,0:T(8,128)(2,1)S(1)} %get-tuple-element.90), channel_id=1, source_target_pairs={{0,2},{2,0},{1,3},{3,1},{4,6},{6,4},{5,7},{7,5},{8,10},{10,8},{9,1... | collective-permute-start | bytes 196616 | tf_op jit(solution)/shard_map/ppermute | solution.py:655
  134.4 4.5 %collective-permute-start.29 = (bf16[64,512]{1,0:T(8,128)(2,1)S(1)}, bf16[64,512]{1,0:T(8,128)(2,1)S(1)}, u32[]{:S(2)}, u32[]{:S(2)}) collective-permute-start(bf16[64,512]{1,0:T(8,128)(2,1)S(1)} %get-tuple-element.91), channel_id=1, source_target_pairs={{0,3},{3,0},{1,2},{2,1},{4,7},{7,4},{5,6},{6,5},{8,11},{11,8},{9,1... | collective-permute-start | bytes 196616 | tf_op jit(solution)/shard_map/ppermute | solution.py:655
  (11 other events, 178.6 us)
